TPU v7x, 32 devices: a whole 2x2x4 slice. The times are simulated.
32 devices in a mesh: ctx: 8 (over z, y), tp: 4 (over x, core).
Axes of the slice: x: 2, y: 2, z: 4, core: 2. Of those that a mesh axis runs over, the one named last changes fastest.
Arguments:
- q_input: bfloat16 [1024, 4096], P('ctx', 'tp'), may hold values from -6 to 6
- k_input: bfloat16 [1024, 4096], P('ctx', 'tp'), may hold values from -6 to 6
- v_input: bfloat16 [1024, 4096], P('ctx', 'tp'), may hold values from -6 to 6
- resid: bfloat16 [1024, 4096], P('ctx', 'tp'), may hold values from -18 to 18
- lengths: int32 [8], replicated, may hold values from 1 to 512, 1024 in all
- short_filter: bfloat16 [3, 256, 7], P(None, 'tp'), may hold values from -2 to 2
- long_filter: bfloat16 [256, 128], P('tp'), may hold values from -0.5 to 0.5
- skip: float32 [4096], P('tp'), may hold values from -1 to 1
- gain: float32 [4096], P('tp'), may hold values from 0.1 to 1.9
- cotangent: bfloat16 [1024, 4096], P('ctx', 'tp'), may hold values from -12 to 12
Outputs:
- normed: bfloat16 [1024, 4096], P('ctx', 'tp')
- grad_q: bfloat16 [1024, 4096], P('ctx', 'tp')
- grad_k: bfloat16 [1024, 4096], P('ctx', 'tp')
- grad_v: bfloat16 [1024, 4096], P('ctx', 'tp')
- grad_short: float32 [3, 256, 7], P(None, 'tp')
- grad_long: float32 [256, 128], P('tp')
- grad_skip: float32 [4096], P('tp')
- grad_gain: float32 [4096], P('tp')
All inputs are finite; a program needn't handle non-finite values.
Results may differ from a plain program's by a relative error of at most 0.0047.
The roundings to bfloat16 on the way count: a program that leaves them out, or rounds other values in their place, can miss the bound.
Values may be sent and summed in bfloat16 or wider, within the bound.
No kernel may reach another device: no remote copies, remote signals or barrier semaphores. Data moves between devices by JAX's collectives and lax.ppermute only.
A program may use at most 128 MiB of HBM per device.

v0:
```python
import functools

import jax
import jax.numpy as jnp
from jax import lax
from jax.experimental import pallas as pl
from jax.experimental.pallas import tpu as pltpu
from jax.sharding import PartitionSpec as P

GS = 16
K = 128
KS = 7
LANES = 128
PER = LANES // GS
RIM = 16
EPS = 1e-06
F32 = jnp.float32
BF16 = jnp.bfloat16


def shifted(x, axis, by):
    count = lax.axis_size(axis)
    pairs = [(i, i + by) for i in range(count) if 0 <= i + by < count]
    return lax.ppermute(x, axis, pairs)


def iota(shape, dim):
    return lax.broadcasted_iota(jnp.int32, shape, dim)


def positions(len_ref, rows):
    begin = jnp.zeros_like(rows)
    start = jnp.int32(0)
    for n in range(len_ref.shape[0]):
        begin = jnp.where(rows >= start, start, begin)
        start = start + len_ref[n]
    return rows - begin


def first_row():
    return lax.axis_index("ctx") * K


def lanes_of(q):
    return pl.ds(pl.multiple_of(q * LANES, LANES), LANES)


def each_chunk(channels, body):
    def step(q, carry):
        body(q)
        return carry

    lax.fori_loop(0, channels // LANES, step, 0)


def as_mask(cond):
    return jnp.where(cond, 1.0, 0.0).astype(BF16)


def extended(rim_ref, which, ref, ls):
    rim = rim_ref[which * RIM : (which + 1) * RIM, ls]
    return jnp.concatenate([rim.astype(F32), ref[:, ls].astype(F32)], axis=0)


def tap_rows(taps_ref, which, ls):
    table = taps_ref[which * 8 : which * 8 + 8, ls]
    return [table[j : j + 1, :] for j in range(KS)]


def causal(ext, taps, pos):
    total = taps[0] * ext[RIM:]
    for j in range(1, KS):
        moved = ext[RIM - j : RIM - j + K]
        total = total + taps[j] * jnp.where(pos >= j, moved, 0.0)
    return total


def group_blocks(mat_ref, q, mask, right):
    left = mat_ref[pl.ds(q * PER, PER)] * mask[None]
    full = jnp.dot(
        left.reshape(PER * K, K), right, preferred_element_type=F32
    ).reshape(PER, K, LANES)
    group = iota((K, LANES), 1) // GS
    out = full[0]
    for g in range(1, PER):
        out = jnp.where(group == g, full[g], out)
    return out


def rims_kernel(q_ref, k_ref, v_ref, out_ref):
    out_ref[0:RIM] = q_ref[...]
    out_ref[RIM : 2 * RIM] = k_ref[...]
    out_ref[2 * RIM :] = v_ref[...]


def tables_kernel(short_ref, long_ref, taps_ref, fwd_ref, bwd_ref, rev_ref, for_ref):
    groups = long_ref.shape[0]
    channels = taps_ref.shape[1]
    spread = as_mask(iota((groups, channels), 1) // GS == iota((groups, channels), 0))
    for i in range(3):
        taps_ref[i * 8 : i * 8 + KS] = lax.dot_general(
            short_ref[i], spread, (((0,), (0,)), ((), ())), preferred_element_type=F32
        )
        taps_ref[i * 8 + KS : i * 8 + 8] = jnp.zeros((8 - KS, channels), F32)
    flip = as_mask((iota((K, K), 0) + iota((K, K), 1)) % K == 0)
    filt = long_ref[...]
    rev_ref[...] = jnp.dot(filt, flip, preferred_element_type=F32)
    for_ref[...] = filt.astype(F32)

    def step(g, carry):
        row = jnp.broadcast_to(rev_ref[pl.ds(g, 1), :], (K, K))
        fwd_ref[g] = pltpu.roll(row, 0, 1, stride=1, stride_axis=0).astype(BF16)
        row = jnp.broadcast_to(for_ref[pl.ds(g, 1), :], (K, K))
        bwd_ref[g] = pltpu.roll(row, 0, 1, stride=1, stride_axis=0).astype(BF16)
        return carry

    lax.fori_loop(0, groups, step, 0)


def gated_kernel(len_ref, k_ref, v_ref, rim_ref, taps_ref, gated_ref):
    pos = positions(len_ref, first_row() + iota((K, LANES), 0))

    def body(q):
        ls = lanes_of(q)
        ks = causal(extended(rim_ref, 1, k_ref, ls), tap_rows(taps_ref, 1, ls), pos)
        vs = causal(extended(rim_ref, 2, v_ref, ls), tap_rows(taps_ref, 2, ls), pos)
        gated_ref[:, ls] = (ks * vs).astype(BF16)

    each_chunk(k_ref.shape[1], body)


def current_kernel(
    len_ref, q_ref, k_ref, v_ref, rim_ref, taps_ref, gated_ref, fwd_ref, skip_ref,
    qs_ref, ks_ref, vs_ref, mixed_ref,
):
    row = iota((K, LANES), 0)
    col = iota((K, LANES), 1)
    pos = positions(len_ref, first_row() + row)
    mask = as_mask((col <= row) & (pos >= row - col))

    def body(q):
        ls = lanes_of(q)
        qs_ref[:, ls] = causal(extended(rim_ref, 0, q_ref, ls), tap_rows(taps_ref, 0, ls), pos)
        ks_ref[:, ls] = causal(extended(rim_ref, 1, k_ref, ls), tap_rows(taps_ref, 1, ls), pos)
        vs_ref[:, ls] = causal(extended(rim_ref, 2, v_ref, ls), tap_rows(taps_ref, 2, ls), pos)
        gated = gated_ref[:, ls]
        conv = group_blocks(fwd_ref, q, mask, gated)
        mixed_ref[:, ls] = conv + skip_ref[:, ls] * gated.astype(F32)

    each_chunk(q_ref.shape[1], body)


def summed_kernel(
    len_ref, before_ref, fwd_ref, part_ref, qs_ref, resid_ref, cot_ref, gain_ref,
    mixed_ref, summed_ref, sums_ref, acc_ref,
):
    row = iota((K, LANES), 0)
    col = iota((K, LANES), 1)
    pos = positions(len_ref, first_row() + row)
    mask = as_mask((col > row) & (pos >= row - col + K))
    acc_ref[...] = jnp.zeros_like(acc_ref)

    def body(q):
        ls = lanes_of(q)
        mixed = part_ref[:, ls] + group_blocks(fwd_ref, q, mask, before_ref[:, ls])
        summed = resid_ref[:, ls].astype(F32) + qs_ref[:, ls] * mixed
        mixed_ref[:, ls] = mixed
        summed_ref[:, ls] = summed
        acc_ref[0] += summed * summed
        acc_ref[1] += gain_ref[:, ls] * cot_ref[:, ls].astype(F32) * summed

    each_chunk(resid_ref.shape[1], body)
    for i in range(2):
        sums_ref[i : i + 1] = jnp.sum(acc_ref[i].T, axis=0, keepdims=True)


def by_row(line):
    return jnp.broadcast_to(line, (K, K)).T


def inverse_of(sums_ref, total):
    return by_row(lax.rsqrt(sums_ref[0:1] / total + EPS))


def grads_kernel(total, summed_ref, mixed_ref, qs_ref, cot_ref, gain_ref, sums_ref, gm_ref, gq_ref):
    inverse = inverse_of(sums_ref, total)
    scale = inverse * inverse * by_row(sums_ref[1:2] / total)

    def body(q):
        ls = lanes_of(q)
        scaled = gain_ref[:, ls] * cot_ref[:, ls].astype(F32)
        grad_sum = inverse * (scaled - summed_ref[:, ls] * scale)
        gm_ref[:, ls] = (grad_sum * qs_ref[:, ls]).astype(BF16)
        gq_ref[:, ls] = (grad_sum * mixed_ref[:, ls]).astype(BF16)

    each_chunk(cot_ref.shape[1], body)


def beside_kernel(
    total, len_ref, summed_ref, cot_ref, gain_ref, sums_ref, gm_ref, gated_ref, before_ref,
    bwd_ref, skip_ref, normed_ref, stats_ref, part_ref,
):
    groups = bwd_ref.shape[0]
    inverse = inverse_of(sums_ref, total)
    row = iota((K, LANES), 0)
    col = iota((K, LANES), 1)
    pos = positions(len_ref, first_row() + col)
    mask = as_mask((col >= row) & (pos >= col - row))
    source = K - 1 - row
    near = (col >= source) & (pos >= col - source)
    far = (col < source) & (pos >= col - source + K)
    flip = as_mask(row + col == K - 1)
    own = [as_mask(col // GS == g) for g in range(PER)]

    def body(q):
        ls = lanes_of(q)
        summed = summed_ref[:, ls]
        normed_ref[:, ls] = (gain_ref[:, ls] * summed * inverse).astype(BF16)
        gm = gm_ref[:, ls]
        gmf = gm.astype(F32)
        gated = gated_ref[:, ls]
        stats_ref[pl.ds(groups + q, 1), :] = jnp.sum(gmf * gated.astype(F32), axis=0, keepdims=True)
        stats_ref[pl.ds(groups + groups // PER + q, 1), :] = jnp.sum(
            cot_ref[:, ls].astype(F32) * summed * inverse, axis=0, keepdims=True
        )
        part_ref[:, ls] = skip_ref[:, ls] * gmf + group_blocks(bwd_ref, q, mask, gm)
        two = jnp.concatenate([before_ref[:, ls], gated], axis=1)
        flipped = jnp.dot(flip, two, preferred_element_type=F32).astype(BF16)
        left = jnp.concatenate([flipped[:, :LANES], flipped[:, LANES:]], axis=0)
        right = jnp.concatenate([gm * own[g] for g in range(PER)], axis=0)
        cross = lax.dot_general(
            left, right, (((1,), (1,)), ((), ())), preferred_element_type=F32
        )
        lines = []
        for g in range(PER):
            gs = slice(g * K, (g + 1) * K)
            square = jnp.where(near, cross[K:, gs], jnp.where(far, cross[:K, gs], 0.0))
            turned = pltpu.roll(square, 1, 1, stride=1, stride_axis=0)
            lines.append(jnp.sum(turned, axis=0, keepdims=True))
        stats_ref[pl.ds(pl.multiple_of(q * PER, PER), PER), :] = jnp.concatenate(lines, axis=0)

    each_chunk(cot_ref.shape[1], body)


def gate_kernel(
    len_ref, part_ref, after_ref, bwd_ref, ks_ref, vs_ref, gq_ref,
    gks_ref, gvs_ref, tails_ref,
):
    row = iota((K, LANES), 0)
    col = iota((K, LANES), 1)
    pos = positions(len_ref, first_row() + K + col)
    mask = as_mask((col < row) & (pos >= col - row + K))

    def body(q):
        ls = lanes_of(q)
        grad = part_ref[:, ls] + group_blocks(bwd_ref, q, mask, after_ref[:, ls])
        gks = (grad * vs_ref[:, ls]).astype(BF16)
        gvs = (grad * ks_ref[:, ls]).astype(BF16)
        gks_ref[:, ls] = gks
        gvs_ref[:, ls] = gvs
        tails_ref[0:RIM, ls] = gq_ref[0:RIM, ls]
        tails_ref[RIM : 2 * RIM, ls] = gks[:RIM]
        tails_ref[2 * RIM :, ls] = gvs[:RIM]

    each_chunk(part_ref.shape[1], body)


def shorts_kernel(
    len_ref, q_ref, k_ref, v_ref, rim_ref, taps_ref, gq_ref, gks_ref, gvs_ref, stats_ref,
    oq_ref, ok_ref, ov_ref, sums_ref, cols_ref,
):
    channels = q_ref.shape[1]
    kept = stats_ref.shape[0]
    pos = positions(len_ref, first_row() + iota((K, LANES), 0))
    pad = jnp.zeros((RIM, LANES), F32)

    def body(q):
        ls = lanes_of(q)
        for i, (x_ref, g_ref, o_ref) in enumerate(
            ((q_ref, gq_ref, oq_ref), (k_ref, gks_ref, ok_ref), (v_ref, gvs_ref, ov_ref))
        ):
            ext = extended(rim_ref, i, x_ref, ls)
            taps = tap_rows(taps_ref, i, ls)
            grad = g_ref[:, ls].astype(F32)
            total = taps[0] * grad
            lines = [jnp.sum(grad * ext[RIM:], axis=0, keepdims=True)]
            for j in range(1, KS):
                held = jnp.where(pos >= j, grad, 0.0)
                lines.append(jnp.sum(held * ext[RIM - j : RIM - j + K], axis=0, keepdims=True))
                total = total + taps[j] * jnp.concatenate([held, pad], axis=0)[j : j + K]
            o_ref[:, ls] = total.astype(BF16)
            lines.append(jnp.zeros((8 - KS, LANES), F32))
            cols_ref[i * 8 : i * 8 + 8, ls] = jnp.concatenate(lines, axis=0)

    each_chunk(channels, body)
    sums_ref[0:kept] = stats_ref[...]
    gather = jnp.where(
        iota((channels, LANES), 0) // GS == iota((channels, LANES), 1), 1.0, 0.0
    )
    sums_ref[kept:] = jnp.dot(
        cols_ref[...], gather, preferred_element_type=F32, precision=lax.Precision.HIGHEST
    )


def ends_kernel(
    len_ref, taps_ref, gq_ref, gks_ref, gvs_ref, tails_ref, sums_ref, aq_ref, ak_ref, av_ref,
    oq_ref, ok_ref, ov_ref, short_ref, long_ref, skip_ref, gain_ref,
):
    groups = long_ref.shape[0]
    rows = groups // PER
    pos = positions(len_ref, first_row() + K - RIM + iota((2 * RIM, LANES), 0))

    def body(q):
        ls = lanes_of(q)
        for i, (g_ref, o_ref) in enumerate(((gq_ref, oq_ref), (gks_ref, ok_ref), (gvs_ref, ov_ref))):
            tail = tails_ref[i * RIM : (i + 1) * RIM, ls].astype(F32)
            ext = jnp.concatenate([g_ref[:, ls].astype(F32), tail], axis=0)
            taps = tap_rows(taps_ref, i, ls)
            total = taps[0] * ext[:RIM]
            for j in range(1, KS):
                held = jnp.where(pos >= j, ext, 0.0)
                total = total + taps[j] * held[j : j + RIM]
            o_ref[:, ls] = total.astype(BF16)

    each_chunk(gq_ref.shape[1], body)
    long_ref[...] = sums_ref[:groups]
    skip_ref[...] = sums_ref[groups : groups + rows]
    gain_ref[...] = sums_ref[groups + rows : groups + 2 * rows]
    turned = jnp.concatenate(
        [sums_ref[groups + 2 * rows :], jnp.zeros((LANES - 24, LANES), F32)], axis=0
    ).T
    for i in range(3):
        short_ref[i] = turned[:groups, i * 8 : i * 8 + KS]


def shards(
    q_input, k_input, v_input, resid, lengths, short_filter, long_filter, skip, gain, cotangent
):
    length, channels = q_input.shape
    groups = channels // GS
    wide = channels * lax.axis_size("tp")
    rows = groups // PER

    def arr(shape, dtype):
        return jax.ShapeDtypeStruct(shape, dtype)

    smem = pl.BlockSpec(memory_space=pltpu.SMEM)
    vmem = pl.BlockSpec(memory_space=pltpu.VMEM)
    params = pltpu.CompilerParams(vmem_limit_bytes=32 * 1024 * 1024)
    full_bf = arr((length, channels), BF16)
    full_f = arr((length, channels), F32)

    def call(kernel, outs, ins, scratch=(), flops=0, moved=0, name=None):
        scalar = ins[0] is lengths
        return pl.pallas_call(
            kernel,
            out_shape=outs,
            in_specs=[smem if (i == 0 and scalar) else vmem for i in range(len(ins))],
            out_specs=[vmem] * len(outs),
            scratch_shapes=scratch,
            compiler_params=params,
            cost_estimate=pl.CostEstimate(flops=flops, bytes_accessed=moved, transcendentals=0),
            name=name,
        )(*ins)

    skip2 = skip.reshape(1, channels)
    gain2 = gain.reshape(1, channels)
    last = pl.BlockSpec((RIM, channels), lambda i: (length // RIM - 1, 0))
    left_rows = pl.pallas_call(
        rims_kernel,
        grid=(1,),
        out_shape=arr((3 * RIM, channels), BF16),
        in_specs=[last] * 3,
        out_specs=pl.BlockSpec((3 * RIM, channels), lambda i: (0, 0)),
        name="rims",
    )(q_input, k_input, v_input)
    rims = shifted(left_rows, "ctx", 1)
    taps, fwd, bwd = call(
        tables_kernel,
        [arr((24, channels), F32), arr((groups, K, K), BF16), arr((groups, K, K), BF16)],
        [short_filter, long_filter],
        [pltpu.VMEM((groups, K), F32), pltpu.VMEM((groups, K), F32)],
        flops=10**9, moved=4 * 10**6, name="tables",
    )
    (gated,) = call(
        gated_kernel, [full_bf], [lengths, k_input, v_input, rims, taps],
        flops=10**8, moved=10**6, name="gated",
    )
    before = shifted(gated, "ctx", 1)
    q_short, k_short, v_short, part = call(
        current_kernel, [full_f] * 4,
        [lengths, q_input, k_input, v_input, rims, taps, gated, fwd, skip2],
        flops=10**9, moved=5 * 10**6, name="current",
    )
    mixed, summed, sums = call(
        summed_kernel, [full_f, full_f, arr((2, K), F32)],
        [lengths, before, fwd, part, q_short, resid, cotangent, gain2],
        [pltpu.VMEM((2, K, LANES), F32)],
        flops=10**9, moved=5 * 10**6, name="summed",
    )
    sums = lax.psum(sums, "tp")
    grad_mixed, grad_qs = call(
        functools.partial(grads_kernel, wide), [full_bf, full_bf],
        [summed, mixed, q_short, cotangent, gain2, sums],
        flops=10**8, moved=2 * 10**6, name="grads",
    )
    after = shifted(grad_mixed, "ctx", -1)
    normed, stats, part = call(
        functools.partial(beside_kernel, wide),
        [full_bf, arr((groups + 2 * rows, LANES), F32), full_f],
        [lengths, summed, cotangent, gain2, sums, grad_mixed, gated, before, bwd, skip2],
        flops=4 * 10**9, moved=5 * 10**6, name="beside",
    )
    grad_ks, grad_vs, tails = call(
        gate_kernel, [full_bf, full_bf, arr((3 * RIM, channels), BF16)],
        [lengths, part, after, bwd, k_short, v_short, grad_qs],
        flops=10**9, moved=5 * 10**6, name="gate",
    )
    tails = shifted(tails, "ctx", -1)
    grad_q, grad_k, grad_v, packed = call(
        shorts_kernel,
        [full_bf, full_bf, full_bf, arr((groups + 2 * rows + 24, LANES), F32)],
        [lengths, q_input, k_input, v_input, rims, taps, grad_qs, grad_ks, grad_vs, stats],
        [pltpu.VMEM((24, channels), F32)],
        flops=10**9, moved=5 * 10**6, name="shorts",
    )
    packed = lax.psum(packed, "ctx")
    whole = lambda *shape: pl.BlockSpec(shape, lambda i: (0,) * len(shape))
    grad_q, grad_k, grad_v, grad_short, grad_long, grad_skip, grad_gain = pl.pallas_call(
        ends_kernel,
        grid=(1,),
        out_shape=[
            full_bf, full_bf, full_bf,
            arr((3, groups, KS), F32), arr((groups, K), F32),
            arr((rows, LANES), F32), arr((rows, LANES), F32),
        ],
        in_specs=[smem, whole(24, channels)] + [last] * 3
        + [whole(3 * RIM, channels), whole(*packed.shape)]
        + [pl.BlockSpec(memory_space=pl.ANY)] * 3,
        out_specs=[last] * 3
        + [whole(3, groups, KS), whole(groups, K), whole(rows, LANES), whole(rows, LANES)],
        input_output_aliases={7: 0, 8: 1, 9: 2},
        name="ends",
    )(lengths, taps, grad_qs, grad_ks, grad_vs, tails, packed, grad_q, grad_k, grad_v)
    return (
        normed, grad_q, grad_k, grad_v, grad_short, grad_long,
        grad_skip.reshape(channels), grad_gain.reshape(channels),
    )


def solution(mesh):
    tiled = P("ctx", "tp")
    return jax.shard_map(
        shards,
        mesh=mesh,
        in_specs=(
            tiled, tiled, tiled, tiled, P(), P(None, "tp", None), P("tp", None), P("tp"), P("tp"),
            tiled,
        ),
        out_specs=(
            tiled, tiled, tiled, tiled, P(None, "tp", None), P("tp", None), P("tp"), P("tp"),
        ),
        check_vma=False,
    )
```

profile of v0, /device:TPU:0, one launch (start us, length us, event | category | flops | bytes accessed | tf_op | source)
XLA Modules:
  0.0 104.5 jit_solution(13182316066252007826)
XLA Ops:
  0.6 1.4 %rims.1 = bf16[48,1024]{1,0:T(8,128)(2,1)} custom-call(bf16[128,1024]{1,0:T(8,128)(2,1)} %q_ref.5, bf16[128,1024]{1,0:T(8,128)(2,1)} %k_ref.7, bf16[128,1024]{1,0:T(8,128)(2,1)} %v_ref.7), custom_call_target="tpu_custom_call" | custom-call | tf_op jit(solution)/shard_map/rims/pallas_call | solution.py:369
  2.1 5.0 %collective-permute-start = (bf16[48,1024]{1,0:T(8,128)(2,1)}, bf16[48,1024]{1,0:T(8,128)(2,1)S(1)}, u32[]{:S(2)}, u32[]{:S(2)}) collective-permute-start(bf16[48,1024]{1,0:T(8,128)(2,1)} %rims.1), channel_id=1, source_target_pairs={{0,4},{4,8},{8,12},{12,16},{16,20},{20,24},{24,28},{1,5},{5,9},{9,... | collective-permute-start | bytes 294920 | tf_op jit(solution)/shard_map/ppermute | solution.py:24
  7.1 0.8 copy.21.short_ref
  7.9 0.0 copy-start.28
  7.9 0.7 copy-done.28
  8.6 5.8 %tables.1 = (f32[24,1024]{1,0:T(8,128)S(1)}, bf16[64,128,128]{2,1,0:T(8,128)(2,1)S(1)}, bf16[64,128,128]{2,1,0:T(8,128)(2,1)S(1)}) custom-call(bf16[3,64,7]{2,1,0:T(8,128)(2,1)S(1)} %copy.21.short_ref, bf16[64,128]{1,0:T(8,128)(2,1)S(1)} %copy-done.28), custom_call_target="tpu_custom_call" | custom-call | flops 1000000000 | bytes 4000000 | tf_op jit(solution)/shard_map/tables/pallas_call | solution.py:355
  14.5 1.9 %gated.1.gated_ref = bf16[128,1024]{1,0:T(8,128)(2,1)S(1)} custom-call(s32[8]{0:T(128)S(1)} %copy-done.27, bf16[128,1024]{1,0:T(8,128)(2,1)S(1)} %copy-done.1, bf16[128,1024]{1,0:T(8,128)(2,1)S(1)} %copy-done.2, bf16[48,1024]{1,0:T(8,128)(2,1)S(1)} %collective-permute-done.rim_ref, f32[24,1024]{1,0:T(8,128)S(1)} %get-tuple-element.37.taps_ref), custom_call_target="tpu_custom_call" | custom-call | flops 100000000 | bytes 1000000 | tf_op jit(solution)/shard_map/gated/pallas_call | solution.py:355
  16.4 0.6 copy-done.23
  17.1 3.6 %collective-permute-start.1 = (bf16[128,1024]{1,0:T(8,128)(2,1)S(1)}, bf16[128,1024]{1,0:T(8,128)(2,1)S(1)}, u32[]{:S(2)}, u32[]{:S(2)}) collective-permute-start(bf16[128,1024]{1,0:T(8,128)(2,1)S(1)} %gated.1.gated_ref), channel_id=1, source_target_pairs={{0,4},{4,8},{8,12},{12,16},{16,20},{20,24},{24,28},{1,5},{5,9},{9,... | collective-permute-start | bytes 786440 | tf_op jit(solution)/shard_map/ppermute | solution.py:24
  20.6 0.9 copy-done.24
  21.5 3.8 %current.1 = (f32[128,1024]{1,0:T(8,128)S(1)}, f32[128,1024]{1,0:T(8,128)S(1)}, f32[128,1024]{1,0:T(8,128)S(1)}, f32[128,1024]{1,0:T(8,128)S(1)}) custom-call(s32[8]{0:T(128)S(1)} %copy-done.27, bf16[128,1024]{1,0:T(8,128)(2,1)S(1)} %copy-done.15, bf16[128,1024]{1,0:T(8,128)(2,1)S(1)} %copy-done.1, bf16[128,1024]{1,0:T(8,128)(2,1)S(1)} %copy-done.2, ...), custom_call_target="tpu_custom_call" | custom-call | flops 1000000000 | bytes 5000000 | tf_op jit(solution)/shard_map/current/pallas_call | solution.py:355
  25.3 0.8 copy-done.6
  26.1 2.7 %summed.1 = (f32[128,1024]{1,0:T(8,128)S(1)}, f32[128,1024]{1,0:T(8,128)S(1)}, f32[2,128]{1,0:T(2,128)S(1)}) custom-call(s32[8]{0:T(128)S(1)} %copy-done.27, bf16[128,1024]{1,0:T(8,128)(2,1)S(1)} %collective-permute-done.1.before_ref, bf16[64,128,128]{2,1,0:T(8,128)(2,1)S(1)} %get-tuple-element.38.fwd_ref, f32[128,1024]{1,0:T(8,128)S(1)} %get-tuple-element.39.part_ref, ...), custom_call_target="tpu_custom_call" | custom-call | flops 1000000000 | bytes 5000000 | tf_op jit(solution)/shard_map/summed/pallas_call | solution.py:355
  28.9 0.8 copy-done.8
  29.6 0.8 copy-done.11
  30.4 6.0 %psum.14.sums_ref = f32[2,128]{1,0:T(2,128)S(1)} all-reduce(f32[2,128]{1,0:T(2,128)S(1)} %get-tuple-element.42), channel_id=1, replica_groups=mesh['ctx'=8,'tp'=4] {'tp'}, use_global_device_ids=true, to_apply=%region_0.0 | all-reduce | flops 256 | bytes 2048 | tf_op jit(solution)/shard_map/psum | solution.py:401
  36.4 1.0 copy-done.9
  37.5 1.0 copy-done.12
  38.5 0.4 grads.1
  38.9 1.3 %collective-permute-start.2 = (bf16[128,1024]{1,0:T(8,128)(2,1)S(1)}, bf16[128,1024]{1,0:T(8,128)(2,1)S(1)}, u32[]{:S(2)}, u32[]{:S(2)}) collective-permute-start(bf16[128,1024]{1,0:T(8,128)(2,1)S(1)} %get-tuple-element.44.gm_ref), channel_id=1, source_target_pairs={{4,0},{8,4},{12,8},{16,12},{20,16},{24,20},{28,24},{5,1},{9,5},{13... | collective-permute-start | bytes 786440 | tf_op jit(solution)/shard_map/ppermute | solution.py:24
  40.2 1.0 copy-done.10
  41.3 0.9 copy-done.18
  42.2 0.9 copy-done.20
  43.2 5.8 %beside.1 = (bf16[128,1024]{1,0:T(8,128)(2,1)}, f32[80,128]{1,0:T(8,128)S(1)}, f32[128,1024]{1,0:T(8,128)S(1)}) custom-call(s32[8]{0:T(128)S(1)} %copy-done.27, f32[128,1024]{1,0:T(8,128)S(1)} %copy-done.10, bf16[128,1024]{1,0:T(8,128)(2,1)S(1)} %copy-done, f32[1,1024]{1,0:T(1,128)S(1)} %bitcast.6, f32[2,128]{1,0:T(2,128)S(1)} %psum.14.sums_ref, ...), custom_call_target="tpu_custom_call" | custom-call | flops 4000000000 | bytes 5000000 | tf_op jit(solution)/shard_map/beside/pallas_call | solution.py:355
  49.0 0.1 collective-permute-done.2.after_ref
  49.0 2.5 %gate.1 = (bf16[128,1024]{1,0:T(8,128)(2,1)S(1)}, bf16[128,1024]{1,0:T(8,128)(2,1)S(1)}, bf16[48,1024]{1,0:T(8,128)(2,1)S(1)}) custom-call(s32[8]{0:T(128)S(1)} %copy-done.27, f32[128,1024]{1,0:T(8,128)S(1)} %get-tuple-element.48.part_ref, bf16[128,1024]{1,0:T(8,128)(2,1)S(1)} %collective-permute-done.2.after_ref, ...), custom_call_target="tpu_custom_call" | custom-call | flops 1000000000 | bytes 5000000 | tf_op jit(solution)/shard_map/gate/pallas_call | solution.py:355
  51.6 1.3 %collective-permute-start.3 = (bf16[48,1024]{1,0:T(8,128)(2,1)S(1)}, bf16[48,1024]{1,0:T(8,128)(2,1)S(1)}, u32[]{:S(2)}, u32[]{:S(2)}) collective-permute-start(bf16[48,1024]{1,0:T(8,128)(2,1)S(1)} %get-tuple-element.53), channel_id=1, source_target_pairs={{4,0},{8,4},{12,8},{16,12},{20,16},{24,20},{28,24},{5,1},{9,5},{13... | collective-permute-start | bytes 294920 | tf_op jit(solution)/shard_map/ppermute | solution.py:24
  52.9 5.3 %shorts.1 = (bf16[128,1024]{1,0:T(8,128)(2,1)}, bf16[128,1024]{1,0:T(8,128)(2,1)}, bf16[128,1024]{1,0:T(8,128)(2,1)}, f32[104,128]{1,0:T(8,128)S(1)}) custom-call(s32[8]{0:T(128)S(1)} %copy-done.27, bf16[128,1024]{1,0:T(8,128)(2,1)S(1)} %copy-done.16, bf16[128,1024]{1,0:T(8,128)(2,1)S(1)} %copy-done.1, bf16[128,1024]{1,0:T(8,128)(2,1)S(1)} %copy-done.2, ...), custom_call_target="tpu_custom_call" | custom-call | flops 1000000000 | bytes 5000000 | tf_op jit(solution)/shard_map/shorts/pallas_call | solution.py:355
  58.1 41.9 %psum.15.sums_ref = f32[104,128]{1,0:T(8,128)} all-reduce(f32[104,128]{1,0:T(8,128)S(1)} %get-tuple-element.55), channel_id=1, replica_groups=mesh['ctx'=8,'tp'=4] {'ctx'}, use_global_device_ids=true, to_apply=%region_1.0 | all-reduce | flops 13312 | bytes 106496 | tf_op jit(solution)/shard_map/psum | solution.py:427
  100.1 0.6 copy-done.30
  100.7 2.2 %ends.1 = (bf16[128,1024]{1,0:T(8,128)(2,1)}, bf16[128,1024]{1,0:T(8,128)(2,1)}, bf16[128,1024]{1,0:T(8,128)(2,1)}, f32[3,64,7]{2,1,0:T(8,128)}, f32[64,128]{1,0...) custom-call(s32[8]{0:T(128)} %len_ref.13, ...), custom_call_target="tpu_custom_call", output_to_operand_aliasing={{0}: (7, {}), {1}: (8, {}), {2}: (9, {})} | custom-call | tf_op jit(solution)/shard_map/ends/pallas_call | solution.py:429
  102.9 1.6 %copy.22 = f32[3,64,7]{1,2,0:T(8,128)} copy(f32[3,64,7]{2,1,0:T(8,128)} %get-tuple-element.70) | data formatting | bytes 10752
  (52 shorter events, 0.1 us)
Async XLA Ops:
  2.1 12.4 %copy-start.1 = (bf16[128,1024]{1,0:T(8,128)(2,1)S(1)}, bf16[128,1024]{1,0:T(8,128)(2,1)}, u32[]{:S(2)}) copy-start(bf16[128,1024]{1,0:T(8,128)(2,1)} %k_ref.7) | copy-start | bytes 786436
  2.1 12.4 %copy-start.2 = (bf16[128,1024]{1,0:T(8,128)(2,1)S(1)}, bf16[128,1024]{1,0:T(8,128)(2,1)}, u32[]{:S(2)}) copy-start(bf16[128,1024]{1,0:T(8,128)(2,1)} %v_ref.7) | copy-start | bytes 786436
  2.1 12.4 %copy-start.27 = (s32[8]{0:T(128)S(1)}, s32[8]{0:T(128)}, u32[]{:S(2)}) copy-start(s32[8]{0:T(128)} %len_ref.13) | copy-start | bytes 100
  2.1 12.4 %collective-permute-start = (bf16[48,1024]{1,0:T(8,128)(2,1)}, bf16[48,1024]{1,0:T(8,128)(2,1)S(1)}, u32[]{:S(2)}, u32[]{:S(2)}) collective-permute-start(bf16[48,1024]{1,0:T(8,128)(2,1)} %rims.1), channel_id=1, source_target_pairs={{0,4},{4,8},{8,12},{12,16},{16,20},{20,24},{24,28},{1,5},{5,9},{9,... | collective-permute-start | bytes 294920 | tf_op jit(solution)/shard_map/ppermute | solution.py:24
  8.6 12.0 %copy-start.15 = (bf16[128,1024]{1,0:T(8,128)(2,1)S(1)}, bf16[128,1024]{1,0:T(8,128)(2,1)}, u32[]{:S(2)}) copy-start(bf16[128,1024]{1,0:T(8,128)(2,1)} %q_ref.5) | copy-start | bytes 786436
  8.6 12.0 %copy-start.29 = (f32[1024]{0:T(1024)S(1)}, f32[1024]{0:T(1024)}, u32[]{:S(2)}) copy-start(f32[1024]{0:T(1024)} %param.17) | copy-start | bytes 12292
  14.4 38.4 %copy-start.13 = (f32[24,1024]{1,0:T(8,128)}, f32[24,1024]{1,0:T(8,128)S(1)}, u32[]{:S(2)}) copy-start(f32[24,1024]{1,0:T(8,128)S(1)} %get-tuple-element.37.taps_ref) | copy-start | bytes 294916
  14.5 11.6 %copy-start.26 = (f32[1024]{0:T(1024)S(1)}, f32[1024]{0:T(1024)}, u32[]{:S(2)}) copy-start(f32[1024]{0:T(1024)} %param.18) | copy-start | bytes 12292
  17.0 11.8 %copy-start.17 = (bf16[128,1024]{1,0:T(8,128)(2,1)}, bf16[128,1024]{1,0:T(8,128)(2,1)S(1)}, u32[]{:S(2)}) copy-start(bf16[128,1024]{1,0:T(8,128)(2,1)S(1)} %gated.1.gated_ref) | copy-start | bytes 786436
  17.0 9.1 %copy-start = (bf16[128,1024]{1,0:T(8,128)(2,1)S(1)}, bf16[128,1024]{1,0:T(8,128)(2,1)}, u32[]{:S(2)}) copy-start(bf16[128,1024]{1,0:T(8,128)(2,1)} %cot_ref.5) | copy-start | bytes 786436
  17.1 9.1 %copy-start.14 = (bf16[128,1024]{1,0:T(8,128)(2,1)S(1)}, bf16[128,1024]{1,0:T(8,128)(2,1)}, u32[]{:S(2)}) copy-start(bf16[128,1024]{1,0:T(8,128)(2,1)} %resid_ref.1) | copy-start | bytes 786436
  17.1 9.1 %collective-permute-start.1 = (bf16[128,1024]{1,0:T(8,128)(2,1)S(1)}, bf16[128,1024]{1,0:T(8,128)(2,1)S(1)}, u32[]{:S(2)}, u32[]{:S(2)}) collective-permute-start(bf16[128,1024]{1,0:T(8,128)(2,1)S(1)} %gated.1.gated_ref), channel_id=1, source_target_pairs={{0,4},{4,8},{8,12},{12,16},{16,20},{20,24},{24,28},{1,5},{5,9},{9,... | collective-permute-start | bytes 786440 | tf_op jit(solution)/shard_map/ppermute | solution.py:24
  20.6 0.9 copy-start.24
  25.3 0.8 copy-start.6
  26.1 2.7 %copy-start.4 = (f32[128,1024]{1,0:T(8,128)}, f32[128,1024]{1,0:T(8,128)S(1)}, u32[]{:S(2)}) copy-start(f32[128,1024]{1,0:T(8,128)S(1)} %get-tuple-element.49.ks_ref) | copy-start | bytes 1572868
  26.1 2.7 %copy-start.19 = (bf16[128,1024]{1,0:T(8,128)(2,1)}, bf16[128,1024]{1,0:T(8,128)(2,1)S(1)}, u32[]{:S(2)}) copy-start(bf16[128,1024]{1,0:T(8,128)(2,1)S(1)} %collective-permute-done.1.before_ref) | copy-start | bytes 786436
  28.8 0.8 copy-start.8
  29.6 0.8 copy-start.11
  36.4 1.0 copy-start.9
  37.5 1.0 copy-start.12
  38.9 13.9 %copy-start.3 = (bf16[128,1024]{1,0:T(8,128)(2,1)}, bf16[128,1024]{1,0:T(8,128)(2,1)S(1)}, u32[]{:S(2)}) copy-start(bf16[128,1024]{1,0:T(8,128)(2,1)S(1)} %get-tuple-element.47.gq_ref) | copy-start | bytes 786436
  38.9 10.1 %collective-permute-start.2 = (bf16[128,1024]{1,0:T(8,128)(2,1)S(1)}, bf16[128,1024]{1,0:T(8,128)(2,1)S(1)}, u32[]{:S(2)}, u32[]{:S(2)}) collective-permute-start(bf16[128,1024]{1,0:T(8,128)(2,1)S(1)} %get-tuple-element.44.gm_ref), channel_id=1, source_target_pairs={{4,0},{8,4},{12,8},{16,12},{20,16},{24,20},{28,24},{5,1},{9,5},{13... | collective-permute-start | bytes 786440 | tf_op jit(solution)/shard_map/ppermute | solution.py:24
  40.2 1.0 copy-start.10
  41.3 0.9 copy-start.18
  42.2 0.9 copy-start.20
  43.2 5.9 %copy-start.5 = (f32[128,1024]{1,0:T(8,128)S(1)}, f32[128,1024]{1,0:T(8,128)}, u32[]{:S(2)}) copy-start(f32[128,1024]{1,0:T(8,128)} %copy-done.4) | copy-start | bytes 1572868
  43.2 5.9 %copy-start.7 = (f32[128,1024]{1,0:T(8,128)S(1)}, f32[128,1024]{1,0:T(8,128)}, u32[]{:S(2)}) copy-start(f32[128,1024]{1,0:T(8,128)} %copy-done.6) | copy-start | bytes 1572868
  49.0 3.8 %copy-start.16 = (bf16[128,1024]{1,0:T(8,128)(2,1)S(1)}, bf16[128,1024]{1,0:T(8,128)(2,1)}, u32[]{:S(2)}) copy-start(bf16[128,1024]{1,0:T(8,128)(2,1)} %q_ref.5) | copy-start | bytes 786436
  49.0 3.9 %copy-start.25 = (bf16[48,1024]{1,0:T(8,128)(2,1)S(1)}, bf16[48,1024]{1,0:T(8,128)(2,1)}, u32[]{:S(2)}) copy-start(bf16[48,1024]{1,0:T(8,128)(2,1)} %copy-done.23) | copy-start | bytes 294916
  51.5 48.5 %copy-start.21 = (bf16[128,1024]{1,0:T(8,128)(2,1)}, bf16[128,1024]{1,0:T(8,128)(2,1)S(1)}, u32[]{:S(2)}) copy-start(bf16[128,1024]{1,0:T(8,128)(2,1)S(1)} %get-tuple-element.51.gks_ref) | copy-start | bytes 786436
  51.5 48.5 %copy-start.22 = (bf16[128,1024]{1,0:T(8,128)(2,1)}, bf16[128,1024]{1,0:T(8,128)(2,1)S(1)}, u32[]{:S(2)}) copy-start(bf16[128,1024]{1,0:T(8,128)(2,1)S(1)} %get-tuple-element.52.gvs_ref) | copy-start | bytes 786436
  51.6 48.5 %collective-permute-start.3 = (bf16[48,1024]{1,0:T(8,128)(2,1)S(1)}, bf16[48,1024]{1,0:T(8,128)(2,1)S(1)}, u32[]{:S(2)}, u32[]{:S(2)}) collective-permute-start(bf16[48,1024]{1,0:T(8,128)(2,1)S(1)} %get-tuple-element.53), channel_id=1, source_target_pairs={{4,0},{8,4},{12,8},{16,12},{20,16},{24,20},{28,24},{5,1},{9,5},{13... | collective-permute-start | bytes 294920 | tf_op jit(solution)/shard_map/ppermute | solution.py:24
  (3 other events, 2.0 us)
where the time goes:
time: 105 us; the launch traced here: 104 us
  blocking collectives  47.9 us (46%)
  Pallas kernels  31.7 us (30%)
  local copies, waits for them, and re-layouts  12.7 us (12%)
  starting transfers between devices  11.1 us (11%)
    psum x1, blocking collectives, shards(): packed = lax.psum(packed, 'ctx')  41.9 us
    pallas_call x8, Pallas kernels, call(): pl.pallas_call(kernel, out_shape=outs, in_specs=[smem if i == 0 and scala...  28.1 us
    unnamed x64, local copies, waits for them, and re-layouts  12.7 us
    ppermute x4, starting transfers between devices, shifted(): return lax.ppermute(x, axis, pairs)  11.1 us
    psum x1, blocking collectives, shards(): sums = lax.psum(sums, 'tp')  5.99 us
    pallas_call x1, Pallas kernels, shards(): pl.pallas_call(ends_kernel, grid=(1,), out_shape=[full_bf, full_bf, full_...  2.22 us
  transfers between devices with their start and end apart: 4, of which 1 were waited for; matrix products, arithmetic and copies ran while one was open for 1% of the time, Pallas kernels for 20%

commit v1 on v0

v1 whole, which is shorter than its diff:
```python
import functools

import jax
import jax.numpy as jnp
from jax import lax
from jax.experimental import pallas as pl
from jax.experimental.pallas import tpu as pltpu
from jax.sharding import PartitionSpec as P

GS = 16
K = 128
KS = 7
LANES = 128
PER = LANES // GS
RIM = 16
EPS = 1e-06
F32 = jnp.float32
BF16 = jnp.bfloat16


def shifted(x, axis, by):
    count = lax.axis_size(axis)
    pairs = [(i, i + by) for i in range(count) if 0 <= i + by < count]
    return lax.ppermute(x, axis, pairs)


def iota(shape, dim):
    return lax.broadcasted_iota(jnp.int32, shape, dim)


def positions(len_ref, rows):
    begin = jnp.zeros_like(rows)
    start = jnp.int32(0)
    for n in range(len_ref.shape[0]):
        begin = jnp.where(rows >= start, start, begin)
        start = start + len_ref[n]
    return rows - begin


def first_row():
    return lax.axis_index("ctx") * K


def lanes_of(q):
    return pl.ds(pl.multiple_of(q * LANES, LANES), LANES)


def each_chunk(channels, body, unroll=2):
    def step(q, carry):
        body(q)
        return carry

    lax.fori_loop(0, channels // LANES, step, 0, unroll=unroll)


def as_mask(cond):
    return jnp.where(cond, 1.0, 0.0).astype(BF16)


def join(*parts):
    return jnp.concatenate(parts, axis=0)


def tap_rows(taps_ref, which, ls):
    table = taps_ref[which * 8 : which * 8 + 8, ls]
    return [table[j : j + 1, :] for j in range(KS)]


def causal(ext, taps, pos):
    rows = ext.shape[0] - RIM
    total = taps[0] * ext[RIM:]
    for j in range(1, KS):
        moved = ext[RIM - j : RIM - j + rows]
        total = total + taps[j] * jnp.where(pos >= j, moved, 0.0)
    return total


def tap_lines(grad, ext, pos):
    lines = [jnp.sum(grad * ext[RIM:], axis=0, keepdims=True)]
    for j in range(1, KS):
        held = jnp.where(pos >= j, grad, 0.0)
        lines.append(jnp.sum(held * ext[RIM - j : RIM - j + K], axis=0, keepdims=True))
    lines.append(jnp.zeros((8 - KS, LANES), F32))
    return join(*lines)


def group_blocks(left, right):
    full = jnp.dot(
        left.reshape(PER * K, left.shape[2]), right, preferred_element_type=F32
    ).reshape(PER, K, LANES)
    group = iota((K, LANES), 1) // GS
    out = full[0]
    for g in range(1, PER):
        out = jnp.where(group == g, full[g], out)
    return out


BULK = K - RIM
Q_LAST, K_LAST, V_LAST, K_FIRST, V_FIRST = (BULK + i * RIM for i in range(5))
SENT = BULK + 5 * RIM


def rim_of(ref, at, ls):
    return ref[at : at + RIM, ls].astype(F32)


def first_kernel(len_ref, short_ref, q_ref, k_ref, v_ref, taps_ref, sent_ref, far_ref):
    groups = short_ref.shape[2]
    channels = taps_ref.shape[1]
    spread = as_mask(iota((groups, channels), 1) // GS == iota((groups, channels), 0))
    for i in range(3):
        taps_ref[i * 8 : i * 8 + KS] = jnp.dot(
            short_ref[i], spread, preferred_element_type=F32
        )
        taps_ref[i * 8 + KS : i * 8 + 8] = jnp.zeros((8 - KS, channels), F32)
    pos = positions(len_ref, first_row() + RIM + iota((BULK, LANES), 0))
    end = slice(K - RIM, K)

    def body(q):
        ls = lanes_of(q)
        ks = causal(k_ref[:, ls].astype(F32), tap_rows(taps_ref, 1, ls), pos)
        vs = causal(v_ref[:, ls].astype(F32), tap_rows(taps_ref, 2, ls), pos)
        sent_ref[:BULK, ls] = (ks * vs).astype(BF16)

    each_chunk(channels, body)
    sent_ref[Q_LAST : Q_LAST + RIM] = q_ref[end]
    sent_ref[K_LAST : K_LAST + RIM] = k_ref[end]
    sent_ref[V_LAST : V_LAST + RIM] = v_ref[end]
    sent_ref[K_FIRST : K_FIRST + RIM] = k_ref[:RIM]
    sent_ref[V_FIRST : V_FIRST + RIM] = v_ref[:RIM]
    far_ref[:RIM] = k_ref[end]
    far_ref[RIM:] = v_ref[end]


def circulant_kernel(turned, long_ref, out_ref, line_ref):
    groups = long_ref.shape[0]
    filt = long_ref[...]
    if turned:
        flip = as_mask((iota((K, K), 0) + iota((K, K), 1)) % K == 0)
        line_ref[...] = jnp.dot(filt, flip, preferred_element_type=F32)
    else:
        line_ref[...] = filt.astype(F32)

    def step(g, carry):
        row = jnp.broadcast_to(line_ref[pl.ds(g, 1), :], (GS, K))
        block = pltpu.roll(row, 0, 1, stride=1, stride_axis=0)
        for i in range(K // GS):
            moved = block if i == 0 else pltpu.roll(block, i * GS, 1)
            out_ref[g, i * GS : (i + 1) * GS] = moved.astype(BF16)
        return carry

    lax.fori_loop(0, groups, step, 0, unroll=8)


def current_kernel(len_ref, q_ref, taps_ref, sent_ref, fwd_ref, skip_ref, qs_ref, part_ref):
    row = iota((K, LANES), 0)
    col = iota((K, LANES), 1)
    pos = positions(len_ref, first_row() + row)
    mask = as_mask((col <= row) & (pos >= row - col))
    top = jnp.zeros((RIM, LANES), BF16)

    def body(q):
        ls = lanes_of(q)
        qs_ref[RIM:, ls] = causal(q_ref[:, ls].astype(F32), tap_rows(taps_ref, 0, ls), pos[RIM:])
        qs_ref[:RIM, ls] = jnp.zeros((RIM, LANES), F32)
        gated = join(top, sent_ref[:BULK, ls])
        left = fwd_ref[pl.ds(q * PER, PER)] * mask[None]
        part_ref[:, ls] = group_blocks(left, gated) + skip_ref[:, ls] * gated.astype(F32)

    each_chunk(q_ref.shape[1], body)


def summed_kernel(
    len_ref, came_ref, far_ref, q_ref, k_ref, v_ref, taps_ref, sent_ref, fwd_ref, bulk_ref,
    part_ref, skip_ref, resid_ref, cot_ref, gain_ref,
    qs_ref, gated_ref, before_ref, mixed_ref, summed_ref, sums_ref, acc_ref,
):
    row = iota((K, LANES), 0)
    col = iota((K, LANES), 1)
    pos = positions(len_ref, first_row() + row)
    far = as_mask((col > row) & (pos >= row - col + K))
    near = as_mask((col <= row) & (col < RIM) & (pos >= row - col))
    pos_top = pos[:RIM]
    pos_far = positions(len_ref, first_row() - K + iota((RIM, LANES), 0))
    rest = jnp.zeros((K - RIM, LANES), BF16)
    acc_ref[...] = jnp.zeros_like(acc_ref)

    def body(q):
        ls = lanes_of(q)
        kt = tap_rows(taps_ref, 1, ls)
        vt = tap_rows(taps_ref, 2, ls)
        k_last = rim_of(came_ref, K_LAST, ls)
        v_last = rim_of(came_ref, V_LAST, ls)
        top = (
            causal(join(k_last, rim_of(k_ref, 0, ls)), kt, pos_top)
            * causal(join(v_last, rim_of(v_ref, 0, ls)), vt, pos_top)
        ).astype(BF16)
        far_top = (
            causal(join(rim_of(far_ref, 0, ls), rim_of(came_ref, K_FIRST, ls)), kt, pos_far)
            * causal(join(rim_of(far_ref, RIM, ls), rim_of(came_ref, V_FIRST, ls)), vt, pos_far)
        ).astype(BF16)
        qs_top = causal(
            join(rim_of(came_ref, Q_LAST, ls), rim_of(q_ref, 0, ls)), tap_rows(taps_ref, 0, ls), pos_top
        )
        before = join(far_top, came_ref[:BULK, ls])
        before_ref[:, ls] = before
        gated_ref[:, ls] = join(top, sent_ref[:BULK, ls])
        qs = join(qs_top, bulk_ref[RIM:, ls])
        qs_ref[:, ls] = qs
        table = fwd_ref[pl.ds(q * PER, PER)]
        left = jnp.concatenate([table * far[None], table * near[None]], axis=2)
        direct = join(skip_ref[:, ls] * top.astype(F32), jnp.zeros((K - RIM, LANES), F32))
        mixed = part_ref[:, ls] + direct + group_blocks(left, join(before, top, rest))
        summed = resid_ref[:, ls].astype(F32) + qs * mixed
        mixed_ref[:, ls] = mixed
        summed_ref[:, ls] = summed
        acc_ref[0] += summed * summed
        acc_ref[1] += gain_ref[:, ls] * cot_ref[:, ls].astype(F32) * summed

    each_chunk(resid_ref.shape[1], body)
    for i in range(2):
        sums_ref[i : i + 1] = jnp.sum(acc_ref[i].T, axis=0, keepdims=True)


def by_row(line):
    return jnp.broadcast_to(line, (K, K)).T


def inverse_of(sums_ref, total):
    return by_row(lax.rsqrt(sums_ref[0:1] / total + EPS))


def grads_kernel(total, summed_ref, mixed_ref, qs_ref, cot_ref, gain_ref, sums_ref, gm_ref, gq_ref):
    inverse = inverse_of(sums_ref, total)
    scale = inverse * inverse * by_row(sums_ref[1:2] / total)

    def body(q):
        ls = lanes_of(q)
        scaled = gain_ref[:, ls] * cot_ref[:, ls].astype(F32)
        grad_sum = inverse * (scaled - summed_ref[:, ls] * scale)
        gm_ref[:, ls] = (grad_sum * qs_ref[:, ls]).astype(BF16)
        gq_ref[:, ls] = (grad_sum * mixed_ref[:, ls]).astype(BF16)

    each_chunk(cot_ref.shape[1], body)


def beside_kernel(
    total, len_ref, summed_ref, cot_ref, gain_ref, sums_ref, gm_ref, gq_ref, gated_ref, before_ref,
    bwd_ref, skip_ref, q_ref, k_ref, v_ref, came_ref, taps_ref,
    normed_ref, stats_ref, part_ref, ks_ref, vs_ref, cols_ref,
):
    groups = bwd_ref.shape[0]
    inverse = inverse_of(sums_ref, total)
    row = iota((K, LANES), 0)
    col = iota((K, LANES), 1)
    pos_row = positions(len_ref, first_row() + row)
    pos = positions(len_ref, first_row() + col)
    mask = as_mask((col >= row) & (pos >= col - row))
    source = K - 1 - row
    near = (col >= source) & (pos >= col - source)
    far = (col < source) & (pos >= col - source + K)
    flip = as_mask(row + col == K - 1)
    own = [as_mask(col // GS == g) for g in range(PER)]

    def body(q):
        ls = lanes_of(q)
        summed = summed_ref[:, ls]
        normed_ref[:, ls] = (gain_ref[:, ls] * summed * inverse).astype(BF16)
        gm = gm_ref[:, ls]
        gmf = gm.astype(F32)
        gated = gated_ref[:, ls]
        stats_ref[pl.ds(groups + q, 1), :] = jnp.sum(gmf * gated.astype(F32), axis=0, keepdims=True)
        stats_ref[pl.ds(groups + groups // PER + q, 1), :] = jnp.sum(
            cot_ref[:, ls].astype(F32) * summed * inverse, axis=0, keepdims=True
        )
        left = bwd_ref[pl.ds(q * PER, PER)] * mask[None]
        part_ref[:, ls] = skip_ref[:, ls] * gmf + group_blocks(left, gm)
        two = jnp.concatenate([before_ref[:, ls], gated], axis=1)
        flipped = jnp.dot(flip, two, preferred_element_type=F32).astype(BF16)
        left = join(flipped[:, :LANES], flipped[:, LANES:])
        right = join(*[gm * own[g] for g in range(PER)])
        cross = lax.dot_general(
            left, right, (((1,), (1,)), ((), ())), preferred_element_type=F32
        )
        lines = []
        for g in range(PER):
            gs = slice(g * K, (g + 1) * K)
            square = jnp.where(near, cross[K:, gs], jnp.where(far, cross[:K, gs], 0.0))
            turned = pltpu.roll(square, 1, 1, stride=1, stride_axis=0)
            lines.append(jnp.sum(turned, axis=0, keepdims=True))
        stats_ref[pl.ds(pl.multiple_of(q * PER, PER), PER), :] = join(*lines)
        k_ext = join(rim_of(came_ref, K_LAST, ls), k_ref[:, ls].astype(F32))
        v_ext = join(rim_of(came_ref, V_LAST, ls), v_ref[:, ls].astype(F32))
        q_ext = join(rim_of(came_ref, Q_LAST, ls), q_ref[:, ls].astype(F32))
        ks_ref[:, ls] = causal(k_ext, tap_rows(taps_ref, 1, ls), pos_row)
        vs_ref[:, ls] = causal(v_ext, tap_rows(taps_ref, 2, ls), pos_row)
        cols_ref[:, ls] = tap_lines(gq_ref[:, ls].astype(F32), q_ext, pos_row)

    each_chunk(cot_ref.shape[1], body, 1)


def gate_kernel(
    len_ref, part_ref, after_ref, bwd_ref, ks_ref, vs_ref, gq_ref, k_ref, v_ref, came_ref,
    stats_ref, qcols_ref, gks_ref, gvs_ref, tails_ref, packed_ref, cols_ref,
):
    channels = part_ref.shape[1]
    kept = stats_ref.shape[0]
    row = iota((K, LANES), 0)
    col = iota((K, LANES), 1)
    pos_row = positions(len_ref, first_row() + row)
    pos = positions(len_ref, first_row() + K + col)
    mask = as_mask((col < row) & (pos >= col - row + K))

    def body(q):
        ls = lanes_of(q)
        left = bwd_ref[pl.ds(q * PER, PER)] * mask[None]
        grad = part_ref[:, ls] + group_blocks(left, after_ref[:, ls])
        gks = (grad * vs_ref[:, ls]).astype(BF16)
        gvs = (grad * ks_ref[:, ls]).astype(BF16)
        gks_ref[:, ls] = gks
        gvs_ref[:, ls] = gvs
        tails_ref[0:RIM, ls] = gq_ref[0:RIM, ls]
        tails_ref[RIM : 2 * RIM, ls] = gks[:RIM]
        tails_ref[2 * RIM :, ls] = gvs[:RIM]
        k_ext = join(rim_of(came_ref, K_LAST, ls), k_ref[:, ls].astype(F32))
        v_ext = join(rim_of(came_ref, V_LAST, ls), v_ref[:, ls].astype(F32))
        cols_ref[0:8, ls] = qcols_ref[:, ls]
        cols_ref[8:16, ls] = tap_lines(gks.astype(F32), k_ext, pos_row)
        cols_ref[16:24, ls] = tap_lines(gvs.astype(F32), v_ext, pos_row)

    each_chunk(channels, body)
    packed_ref[0:kept] = stats_ref[...]
    gather = jnp.where(
        iota((channels, LANES), 0) // GS == iota((channels, LANES), 1), 1.0, 0.0
    )
    packed_ref[kept:] = jnp.dot(
        cols_ref[...], gather, preferred_element_type=F32, precision=lax.Precision.HIGHEST
    )


def mains_kernel(
    len_ref, taps_ref, gq_ref, gks_ref, gvs_ref, tails_ref, oq_ref, ok_ref, ov_ref
):
    pos = positions(len_ref, first_row() + iota((K + RIM, LANES), 0))

    def body(q):
        ls = lanes_of(q)
        for i, (g_ref, o_ref) in enumerate(((gq_ref, oq_ref), (gks_ref, ok_ref), (gvs_ref, ov_ref))):
            ext = join(g_ref[:, ls].astype(F32), rim_of(tails_ref, i * RIM, ls))
            taps = tap_rows(taps_ref, i, ls)
            total = taps[0] * ext[:K]
            for j in range(1, KS):
                held = jnp.where(pos >= j, ext, 0.0)
                total = total + taps[j] * held[j : j + K]
            o_ref[:, ls] = total.astype(BF16)

    each_chunk(gq_ref.shape[1], body)


def unpack_kernel(one_ref, two_ref, short_ref, long_ref, skip_ref, gain_ref):
    groups = long_ref.shape[0]
    rows = groups // PER
    total = one_ref[...] + two_ref[...]
    long_ref[...] = total[:groups]
    skip_ref[...] = total[groups : groups + rows]
    gain_ref[...] = total[groups + rows : groups + 2 * rows]
    for i in range(3):
        at = groups + 2 * rows + i * 8
        short_ref[i] = total[at : at + KS, :groups]


def shards(
    q_input, k_input, v_input, resid, lengths, short_filter, long_filter, skip, gain, cotangent
):
    length, channels = q_input.shape
    groups = channels // GS
    wide = channels * lax.axis_size("tp")
    rows = groups // PER

    def arr(shape, dtype):
        return jax.ShapeDtypeStruct(shape, dtype)

    smem = pl.BlockSpec(memory_space=pltpu.SMEM)
    vmem = pl.BlockSpec(memory_space=pltpu.VMEM)
    full_bf = arr((length, channels), BF16)
    full_f = arr((length, channels), F32)

    def call(name, kernel, outs, ins, scratch=(), flops=10**8, moved=10**6, grant=8):
        scalar = ins[0] is lengths
        return pl.pallas_call(
            kernel,
            out_shape=outs,
            in_specs=[smem if (i == 0 and scalar) else vmem for i in range(len(ins))],
            out_specs=[vmem] * len(outs),
            scratch_shapes=scratch,
            compiler_params=pltpu.CompilerParams(vmem_limit_bytes=grant * 1024 * 1024),
            cost_estimate=pl.CostEstimate(flops=flops, bytes_accessed=moved, transcendentals=0),
            name=name,
        )(*ins)

    skip2 = skip.reshape(1, channels)
    gain2 = gain.reshape(1, channels)
    taps, sent, far = call(
        "first", first_kernel,
        [arr((24, channels), F32), arr((SENT, channels), BF16), arr((2 * RIM, channels), BF16)],
        [lengths, jnp.transpose(short_filter, (0, 2, 1)), q_input, k_input, v_input],
    )
    came = shifted(sent, "ctx", 1)
    came_far = shifted(far, "ctx", 2)

    def circulants(filt, turned):
        return call(
            "circulants", functools.partial(circulant_kernel, turned),
            [arr((groups, K, K), BF16)], [filt], [pltpu.VMEM((groups, K), F32)],
            flops=10**9, moved=4 * 10**6,
        )[0]

    filt, sent = lax.optimization_barrier((long_filter, sent))
    fwd = circulants(filt, True)
    bulk, part = call(
        "current", current_kernel, [full_f] * 2,
        [lengths, q_input, taps, sent, fwd, skip2], flops=10**9, moved=5 * 10**6,
    )
    q_short, gated, before, mixed, summed, sums = call(
        "summed", summed_kernel,
        [full_f, full_bf, full_bf, full_f, full_f, arr((2, K), F32)],
        [
            lengths, came, came_far, q_input, k_input, v_input, taps, sent, fwd, bulk,
            part, skip2, resid, cotangent, gain2,
        ],
        [pltpu.VMEM((2, K, LANES), F32)], flops=10**9, moved=5 * 10**6,
    )
    sums = lax.psum(sums, "tp")
    grad_mixed, grad_qs = call(
        "grads", functools.partial(grads_kernel, wide), [full_bf, full_bf],
        [summed, mixed, q_short, cotangent, gain2, sums],
    )
    after = shifted(grad_mixed, "ctx", -1)
    filt, grad_mixed = lax.optimization_barrier((long_filter, grad_mixed))
    bwd = circulants(filt, False)
    normed, stats, part, k_short, v_short, qcols = call(
        "beside", functools.partial(beside_kernel, wide),
        [
            full_bf, arr((groups + 2 * rows, LANES), F32), full_f, full_f, full_f,
            arr((8, channels), F32),
        ],
        [
            lengths, summed, cotangent, gain2, sums, grad_mixed, grad_qs, gated, before,
            bwd, skip2, q_input, k_input, v_input, came, taps,
        ],
        flops=4 * 10**9, moved=5 * 10**6,
    )
    grad_ks, grad_vs, tails, packed = call(
        "gate", gate_kernel,
        [
            full_bf, full_bf, arr((3 * RIM, channels), BF16),
            arr((groups + 2 * rows + 24, LANES), F32),
        ],
        [
            lengths, part, after, bwd, k_short, v_short, grad_qs, k_input, v_input, came,
            stats, qcols,
        ],
        [pltpu.VMEM((24, channels), F32)], flops=10**9, moved=5 * 10**6,
    )
    tails = shifted(tails, "ctx", -1)
    grad_q, grad_k, grad_v = call(
        "mains", mains_kernel, [full_bf] * 3,
        [lengths, taps, grad_qs, grad_ks, grad_vs, tails], flops=10**9, moved=5 * 10**6,
    )
    count = lax.axis_size("ctx")
    step = 1
    while step < count:
        if step > 1:
            packed = packed + other
        other = lax.ppermute(packed, "ctx", [(i, i ^ step) for i in range(count)])
        step *= 2
    grad_short, grad_long, grad_skip, grad_gain = call(
        "unpack", unpack_kernel,
        [
            arr((3, KS, groups), F32), arr((groups, K), F32),
            arr((rows, LANES), F32), arr((rows, LANES), F32),
        ],
        [packed, other],
    )
    return (
        normed, grad_q, grad_k, grad_v, jnp.transpose(grad_short, (0, 2, 1)), grad_long,
        grad_skip.reshape(channels), grad_gain.reshape(channels),
    )


def solution(mesh):
    tiled = P("ctx", "tp")
    return jax.shard_map(
        shards,
        mesh=mesh,
        in_specs=(
            tiled, tiled, tiled, tiled, P(), P(None, "tp", None), P("tp", None), P("tp"), P("tp"),
            tiled,
        ),
        out_specs=(
            tiled, tiled, tiled, tiled, P(None, "tp", None), P("tp", None), P("tp"), P("tp"),
        ),
        check_vma=False,
    )
```

time: 105 us -> 64.9 us (0.62)
  blocking collectives: 47.9 us -> 6 us
  starting transfers between devices: 11.1 us -> 21.2 us
  local copies, waits for them, and re-layouts: 12.7 us -> 5.66 us
  Pallas kernels: 31.7 us -> 27 us
  waiting for transfers between devices: 0.07 us -> 3.65 us
    psum x1 -> x0, blocking collectives: 41.9 us -> none  [shards(): packed = lax.psum(packed, 'ctx')]
    ppermute x0 -> x3, starting transfers between devices: none -> 10.2 us  [shards(): other = lax.ppermute(packed, 'ctx', [(i, i ^ step) for i in range(count)])]
    unnamed x64 -> x34, local copies, waits for them, and re-layouts: 12.7 us -> 5.66 us
    pallas_call x2 -> x0, Pallas kernels: 3.66 us -> none  [the longest x1 2.22 us: shards(): pl.pallas_call(ends_kernel, grid=(1,), out_shape=[full_bf, full_bf, full_...]
    ppermute x0 -> x3, waiting for transfers between devices: none -> 3.64 us  [shards(): other = lax.ppermute(packed, 'ctx', [(i, i ^ step) for i in range(count)])]
    pallas_call x8 -> x10, Pallas kernels: 28.1 us -> 27 us  [call(): pl.pallas_call(kernel, out_shape=outs, in_specs=[smem if i == 0 and scala...]
  transfers between devices with their start and end apart: 4 -> 7, of which waited for: 1 -> 2; matrix products, arithmetic and copies ran while one was open for 1% -> 0% of each run, Pallas kernels for 20% -> 27%
where the time goes in v1:
time: 64.9 us; the launch traced here: 64.5 us
  Pallas kernels  27 us (42%)
  starting transfers between devices  21.2 us (33%)
  blocking collectives  6 us (9%)
  local copies, waits for them, and re-layouts  5.66 us (9%)
  waiting for transfers between devices  3.65 us (6%)
  between operations  0.91 us (1%)
    pallas_call x10, Pallas kernels, call(): pl.pallas_call(kernel, out_shape=outs, in_specs=[smem if i == 0 and scala...  27 us
    ppermute x4, starting transfers between devices, shifted(): return lax.ppermute(x, axis, pairs)  11.1 us
    ppermute x3, starting transfers between devices, shards(): other = lax.ppermute(packed, 'ctx', [(i, i ^ step) for i in range(count)])  10.2 us
    psum x1, blocking collectives, shards(): sums = lax.psum(sums, 'tp')  6 us
    unnamed x34, local copies, waits for them, and re-layouts  5.66 us
    ppermute x3, waiting for transfers between devices, shards(): other = lax.ppermute(packed, 'ctx', [(i, i ^ step) for i in range(count)])  3.64 us
  transfers between devices with their start and end apart: 7, of which 2 were waited for; matrix products, arithmetic and copies ran while one was open for 0% of the time, Pallas kernels for 27%

profile of v1, /device:TPU:0, one launch (start us, length us, event | category | flops | bytes accessed | tf_op | source)
XLA Modules:
  0.0 64.5 jit_solution(6189320265784901955)
XLA Ops:
  0.6 0.9 %copy-done = bf16[128,1024]{1,0:T(8,128)(2,1)S(1)} copy-done((bf16[128,1024]{1,0:T(8,128)(2,1)S(1)}, bf16[128,1024]{1,0:T(8,128)(2,1)}, u32[]{:S(2)}) %copy-start) | copy-done | bytes 262168
  1.6 0.9 %copy-done.2 = bf16[128,1024]{1,0:T(8,128)(2,1)S(1)} copy-done((bf16[128,1024]{1,0:T(8,128)(2,1)S(1)}, bf16[128,1024]{1,0:T(8,128)(2,1)}, u32[]{:S(2)}) %copy-start.2) | copy-done | bytes 262168
  2.5 0.9 %copy-done.5 = bf16[128,1024]{1,0:T(8,128)(2,1)S(1)} copy-done((bf16[128,1024]{1,0:T(8,128)(2,1)S(1)}, bf16[128,1024]{1,0:T(8,128)(2,1)}, u32[]{:S(2)}) %copy-start.5) | copy-done | bytes 262168
  3.5 0.7 %copy-done.9 = bf16[3,64,7]{1,2,0:T(8,128)(2,1)S(1)} copy-done((bf16[3,64,7]{1,2,0:T(8,128)(2,1)S(1)}, bf16[3,64,7]{1,2,0:T(8,128)(2,1)}, u32[]{:S(2)}) %copy-start.9) | copy-done | bytes 2712
  4.2 0.7 %copy-done.10 = s32[8]{0:T(128)S(1)} copy-done((s32[8]{0:T(128)S(1)}, s32[8]{0:T(128)}, u32[]{:S(2)}) %copy-start.10) | copy-done | bytes 56
  4.8 1.9 %first.1 = (f32[24,1024]{1,0:T(8,128)S(1)}, bf16[192,1024]{1,0:T(8,128)(2,1)S(1)}, bf16[32,1024]{1,0:T(8,128)(2,1)S(1)}) custom-call(s32[8]{0:T(128)S(1)} %copy-done.10, bf16[3,7,64]{2,1,0:T(8,128)(2,1)S(1)} %bitcast.9, bf16[128,1024]{1,0:T(8,128)(2,1)S(1)} %copy-done.5, bf16[128,1024]{1,0:T(8,128)(2,1)S(1)} %copy-done, bf16[128,1024]{1,0:T(8,128)(2,1)S(1)} %copy-done.2), custom_call_target="tpu_custom_call" | custom-call | flops 100000000 | bytes 1000000 | tf_op jit(solution)/shard_map/first/pallas_call | solution.py:390
  6.8 4.9 %collective-permute-start = (bf16[192,1024]{1,0:T(8,128)(2,1)S(1)}, bf16[192,1024]{1,0:T(8,128)(2,1)S(1)}, u32[]{:S(2)}, u32[]{:S(2)}) collective-permute-start(bf16[192,1024]{1,0:T(8,128)(2,1)S(1)} %get-tuple-element.45.sent_ref), channel_id=1, source_target_pairs={{0,4},{4,8},{8,12},{12,16},{16,20},{20,24},{24,28},{1,5},{5,9},{9,... | collective-permute-start | bytes 1179656 | tf_op jit(solution)/shard_map/ppermute | solution.py:24
  11.7 3.5 %collective-permute-start.1 = (bf16[32,1024]{1,0:T(8,128)(2,1)S(1)}, bf16[32,1024]{1,0:T(8,128)(2,1)S(1)}, u32[]{:S(2)}, u32[]{:S(2)}) collective-permute-start(bf16[32,1024]{1,0:T(8,128)(2,1)S(1)} %get-tuple-element.43), channel_id=1, source_target_pairs={{0,8},{4,12},{8,16},{12,20},{16,24},{20,28},{1,9},{5,13},{9,17},{1... | collective-permute-start | bytes 196616 | tf_op jit(solution)/shard_map/ppermute | solution.py:24
  15.2 0.7 %copy-done.15 = bf16[64,128]{1,0:T(8,128)(2,1)S(1)} copy-done((bf16[64,128]{1,0:T(8,128)(2,1)S(1)}, bf16[64,128]{1,0:T(8,128)(2,1)}, u32[]{:S(2)}) %copy-start.15) | copy-done | bytes 16408
  15.9 1.8 %circulants.2.fwd_ref = bf16[64,128,128]{2,1,0:T(8,128)(2,1)S(1)} custom-call(bf16[64,128]{1,0:T(8,128)(2,1)S(1)} %copy-done.15), custom_call_target="tpu_custom_call" | custom-call | flops 1000000000 | bytes 4000000 | tf_op jit(solution)/shard_map/circulants/pallas_call | solution.py:390
  17.7 0.0 copy-start.1
  17.7 0.0 copy-start.3
  17.7 0.0 copy-start.7
  17.7 0.0 copy-start.8
  17.7 2.4 %current.1 = (f32[128,1024]{1,0:T(8,128)S(1)}, f32[128,1024]{1,0:T(8,128)S(1)}) custom-call(s32[8]{0:T(128)S(1)} %copy-done.11, bf16[128,1024]{1,0:T(8,128)(2,1)S(1)} %copy-done.6, f32[24,1024]{1,0:T(8,128)S(1)} %get-tuple-element.44.taps_ref, bf16[192,1024]{1,0:T(8,128)(2,1)S(1)} %get-tuple-element.45.sent_ref, ...), custom_call_target="tpu_custom_call" | custom-call | flops 1000000000 | bytes 5000000 | tf_op jit(solution)/shard_map/current/pallas_call | solution.py:390
  20.2 0.0 copy-start.16
  20.2 3.0 %summed.1 = (f32[128,1024]{1,0:T(8,128)S(1)}, bf16[128,1024]{1,0:T(8,128)(2,1)S(1)}, bf16[128,1024]{1,0:T(8,128)(2,1)S(1)}, f32[128,1024]{1,0:T(8,128)S(1)}, f32...) custom-call(s32[8]{0:T(128)S(1)} %copy-done.11, bf16[192,1024]{1,0:T(8,128)(2,1)S(1)} %collective-permute-done.came_ref, ...), custom_call_target="tpu_custom_call" | custom-call | flops 1000000000 | bytes 5000000 | tf_op jit(solution)/shard_map/summed/pallas_call | solution.py:390
  23.3 0.7 %copy-done.13 = bf16[128,1024]{1,0:T(8,128)(2,1)} copy-done((bf16[128,1024]{1,0:T(8,128)(2,1)}, bf16[128,1024]{1,0:T(8,128)(2,1)S(1)}, u32[]{:S(2)}) %copy-start.13) | copy-done | bytes 262168
  24.0 6.0 %psum.7.sums_ref = f32[2,128]{1,0:T(2,128)S(1)} all-reduce(f32[2,128]{1,0:T(2,128)S(1)} %get-tuple-element.50), channel_id=1, replica_groups=mesh['ctx'=8,'tp'=4] {'tp'}, use_global_device_ids=true, to_apply=%region_0.0 | all-reduce | flops 256 | bytes 2048 | tf_op jit(solution)/shard_map/psum | solution.py:433
  30.0 0.5 grads.1
  30.5 1.4 %collective-permute-start.2 = (bf16[128,1024]{1,0:T(8,128)(2,1)S(1)}, bf16[128,1024]{1,0:T(8,128)(2,1)S(1)}, u32[]{:S(2)}, u32[]{:S(2)}) collective-permute-start(bf16[128,1024]{1,0:T(8,128)(2,1)S(1)} %get-tuple-element.54.gm_ref), channel_id=1, source_target_pairs={{4,0},{8,4},{12,8},{16,12},{20,16},{24,20},{28,24},{5,1},{9,5},{13... | collective-permute-start | bytes 786440 | tf_op jit(solution)/shard_map/ppermute | solution.py:24
  31.9 1.6 %circulants.3.bwd_ref = bf16[64,128,128]{2,1,0:T(8,128)(2,1)S(1)} custom-call(bf16[64,128]{1,0:T(8,128)(2,1)S(1)} %copy-done.16), custom_call_target="tpu_custom_call" | custom-call | flops 1000000000 | bytes 4000000 | tf_op jit(solution)/shard_map/circulants/pallas_call | solution.py:390
  33.5 7.8 %beside.1 = (bf16[128,1024]{1,0:T(8,128)(2,1)}, f32[80,128]{1,0:T(8,128)S(1)}, f32[128,1024]{1,0:T(8,128)S(1)}, f32[128,1024]{1,0:T(8,128)S(1)}, f32[128,1024]{1,0:T(8,128)S(1)}, /*index=5*/f32[8,1024]{1,0:T(8,128)S(1)}) custom-call(s32[8]{0:T(128)S(1)} %copy-done.11, f32[128,1024]{1,0:T(8,128)S(1)} %get-tuple-element.49.summed_ref, ...), custom_call_target="tpu_custom_call" | custom-call | flops 4000000000 | bytes 5000000 | tf_op jit(solution)/shard_map/beside/pallas_call | solution.py:390
  41.3 3.7 %gate.1 = (bf16[128,1024]{1,0:T(8,128)(2,1)S(1)}, bf16[128,1024]{1,0:T(8,128)(2,1)S(1)}, bf16[48,1024]{1,0:T(8,128)(2,1)S(1)}, f32[104,128]{1,0:T(8,128)S(1)}) custom-call(s32[8]{0:T(128)S(1)} %copy-done.11, f32[128,1024]{1,0:T(8,128)S(1)} %get-tuple-element.60.part_ref, bf16[128,1024]{1,0:T(8,128)(2,1)S(1)} %collective-permute-done.2.after_ref, ...), custom_call_target="tpu_custom_call" | custom-call | flops 1000000000 | bytes 5000000 | tf_op jit(solution)/shard_map/gate/pallas_call | solution.py:390
  45.0 3.1 %collective-permute-start.4 = (f32[104,128]{1,0:T(8,128)S(1)}, f32[104,128]{1,0:T(8,128)S(1)}, u32[]{:S(2)}, u32[]{:S(2)}) collective-permute-start(f32[104,128]{1,0:T(8,128)S(1)} %get-tuple-element.71), channel_id=1, source_target_pairs={{0,4},{4,0},{8,12},{12,8},{16,20},{20,16},{24,28},{28,24},{1,5},{5... | collective-permute-start | bytes 159752 | tf_op jit(solution)/shard_map/ppermute | solution.py:475
  48.1 1.3 %collective-permute-start.3 = (bf16[48,1024]{1,0:T(8,128)(2,1)S(1)}, bf16[48,1024]{1,0:T(8,128)(2,1)S(1)}, u32[]{:S(2)}, u32[]{:S(2)}) collective-permute-start(bf16[48,1024]{1,0:T(8,128)(2,1)S(1)} %get-tuple-element.67), channel_id=1, source_target_pairs={{4,0},{8,4},{12,8},{16,12},{20,16},{24,20},{28,24},{5,1},{9,5},{13... | collective-permute-start | bytes 294920 | tf_op jit(solution)/shard_map/ppermute | solution.py:24
  49.4 0.8 %collective-permute-done.4 = f32[104,128]{1,0:T(8,128)S(1)} collective-permute-done((f32[104,128]{1,0:T(8,128)S(1)}, f32[104,128]{1,0:T(8,128)S(1)}, u32[]{:S(2)}, u32[]{:S(2)}) %collective-permute-start.4) | collective-permute-done | bytes 53280 | tf_op jit(solution)/shard_map/ppermute | solution.py:475
  50.3 3.5 %collective-permute-start.5 = (f32[104,128]{1,0:T(8,128)S(1)}, f32[104,128]{1,0:T(8,128)S(1)}, u32[]{:S(2)}, u32[]{:S(2)}) collective-permute-start(f32[104,128]{1,0:T(8,128)S(1)} %add.8), channel_id=1, source_target_pairs={{0,8},{4,12},{8,0},{12,4},{16,24},{20,28},{24,16},{28,20},{1,9},{5... | collective-permute-start | bytes 159752 | tf_op jit(solution)/shard_map/ppermute | solution.py:475
  53.8 2.8 %collective-permute-done.5 = f32[104,128]{1,0:T(8,128)S(1)} collective-permute-done((f32[104,128]{1,0:T(8,128)S(1)}, f32[104,128]{1,0:T(8,128)S(1)}, u32[]{:S(2)}, u32[]{:S(2)}) %collective-permute-start.5) | collective-permute-done | bytes 53280 | tf_op jit(solution)/shard_map/ppermute | solution.py:475
  56.6 3.5 %collective-permute-start.6 = (f32[104,128]{1,0:T(8,128)S(1)}, f32[104,128]{1,0:T(8,128)S(1)}, u32[]{:S(2)}, u32[]{:S(2)}) collective-permute-start(f32[104,128]{1,0:T(8,128)S(1)} %add.9.one_ref), channel_id=1, source_target_pairs={{0,16},{4,20},{8,24},{12,28},{16,0},{20,4},{24,8},{28,12},{1,17},{... | collective-permute-start | bytes 159752 | tf_op jit(solution)/shard_map/ppermute | solution.py:475
  60.1 3.7 %mains.1 = (bf16[128,1024]{1,0:T(8,128)(2,1)}, bf16[128,1024]{1,0:T(8,128)(2,1)}, bf16[128,1024]{1,0:T(8,128)(2,1)}) custom-call(s32[8]{0:T(128)S(1)} %copy-done.11, f32[24,1024]{1,0:T(8,128)S(1)} %get-tuple-element.44.taps_ref, bf16[128,1024]{1,0:T(8,128)(2,1)S(1)} %get-tuple-element.55.gq_ref, bf16[128,1024]{1,0:T(8,128)(2,1)S(1)} %get-tuple-element.65.gks_ref, ...), custom_call_target="tpu_custom_call" | custom-call | flops 1000000000 | bytes 5000000 | tf_op jit(solution)/shard_map/mains/pallas_call | solution.py:390
  63.9 0.6 unpack.1
  (29 shorter events, 0.1 us)
Async XLA Ops:
  0.6 1.0 %copy-start = (bf16[128,1024]{1,0:T(8,128)(2,1)S(1)}, bf16[128,1024]{1,0:T(8,128)(2,1)}, u32[]{:S(2)}) copy-start(bf16[128,1024]{1,0:T(8,128)(2,1)} %k_ref.7) | copy-start | bytes 786436
  1.6 0.9 %copy-start.2 = (bf16[128,1024]{1,0:T(8,128)(2,1)S(1)}, bf16[128,1024]{1,0:T(8,128)(2,1)}, u32[]{:S(2)}) copy-start(bf16[128,1024]{1,0:T(8,128)(2,1)} %v_ref.7) | copy-start | bytes 786436
  2.5 0.9 %copy-start.5 = (bf16[128,1024]{1,0:T(8,128)(2,1)S(1)}, bf16[128,1024]{1,0:T(8,128)(2,1)}, u32[]{:S(2)}) copy-start(bf16[128,1024]{1,0:T(8,128)(2,1)} %q_ref.7) | copy-start | bytes 786436
  3.5 0.7 %copy-start.9 = (bf16[3,64,7]{1,2,0:T(8,128)(2,1)S(1)}, bf16[3,64,7]{1,2,0:T(8,128)(2,1)}, u32[]{:S(2)}) copy-start(bf16[3,64,7]{1,2,0:T(8,128)(2,1)} %param.15) | copy-start | bytes 8068
  4.2 0.7 %copy-start.10 = (s32[8]{0:T(128)S(1)}, s32[8]{0:T(128)}, u32[]{:S(2)}) copy-start(s32[8]{0:T(128)} %len_ref.11) | copy-start | bytes 100
  4.8 12.9 %copy-start.6 = (bf16[128,1024]{1,0:T(8,128)(2,1)S(1)}, bf16[128,1024]{1,0:T(8,128)(2,1)}, u32[]{:S(2)}) copy-start(bf16[128,1024]{1,0:T(8,128)(2,1)} %q_ref.7) | copy-start | bytes 786436
  4.8 12.9 %copy-start.11 = (s32[8]{0:T(128)S(1)}, s32[8]{0:T(128)}, u32[]{:S(2)}) copy-start(s32[8]{0:T(128)} %len_ref.11) | copy-start | bytes 100
  4.8 12.9 %copy-start.12 = (f32[1024]{0:T(1024)S(1)}, f32[1024]{0:T(1024)}, u32[]{:S(2)}) copy-start(f32[1024]{0:T(1024)} %param.17) | copy-start | bytes 12292
  6.8 13.4 %collective-permute-start = (bf16[192,1024]{1,0:T(8,128)(2,1)S(1)}, bf16[192,1024]{1,0:T(8,128)(2,1)S(1)}, u32[]{:S(2)}, u32[]{:S(2)}) collective-permute-start(bf16[192,1024]{1,0:T(8,128)(2,1)S(1)} %get-tuple-element.45.sent_ref), channel_id=1, source_target_pairs={{0,4},{4,8},{8,12},{12,16},{16,20},{20,24},{24,28},{1,5},{5,9},{9,... | collective-permute-start | bytes 1179656 | tf_op jit(solution)/shard_map/ppermute | solution.py:24
  11.7 8.5 %collective-permute-start.1 = (bf16[32,1024]{1,0:T(8,128)(2,1)S(1)}, bf16[32,1024]{1,0:T(8,128)(2,1)S(1)}, u32[]{:S(2)}, u32[]{:S(2)}) collective-permute-start(bf16[32,1024]{1,0:T(8,128)(2,1)S(1)} %get-tuple-element.43), channel_id=1, source_target_pairs={{0,8},{4,12},{8,16},{12,20},{16,24},{20,28},{1,9},{5,13},{9,17},{1... | collective-permute-start | bytes 196616 | tf_op jit(solution)/shard_map/ppermute | solution.py:24
  15.2 0.7 %copy-start.15 = (bf16[64,128]{1,0:T(8,128)(2,1)S(1)}, bf16[64,128]{1,0:T(8,128)(2,1)}, u32[]{:S(2)}) copy-start(bf16[64,128]{1,0:T(8,128)(2,1)} %long_ref.1) | copy-start | bytes 49156
  17.7 2.5 %copy-start.1 = (bf16[128,1024]{1,0:T(8,128)(2,1)S(1)}, bf16[128,1024]{1,0:T(8,128)(2,1)}, u32[]{:S(2)}) copy-start(bf16[128,1024]{1,0:T(8,128)(2,1)} %k_ref.7) | copy-start | bytes 786436
  17.7 2.5 %copy-start.3 = (bf16[128,1024]{1,0:T(8,128)(2,1)S(1)}, bf16[128,1024]{1,0:T(8,128)(2,1)}, u32[]{:S(2)}) copy-start(bf16[128,1024]{1,0:T(8,128)(2,1)} %v_ref.7) | copy-start | bytes 786436
  17.7 2.5 %copy-start.4 = (bf16[128,1024]{1,0:T(8,128)(2,1)S(1)}, bf16[128,1024]{1,0:T(8,128)(2,1)}, u32[]{:S(2)}) copy-start(bf16[128,1024]{1,0:T(8,128)(2,1)} %cot_ref.5) | copy-start | bytes 786436
  17.7 2.5 %copy-start.7 = (bf16[128,1024]{1,0:T(8,128)(2,1)S(1)}, bf16[128,1024]{1,0:T(8,128)(2,1)}, u32[]{:S(2)}) copy-start(bf16[128,1024]{1,0:T(8,128)(2,1)} %resid_ref.1) | copy-start | bytes 786436
  17.7 2.5 %copy-start.8 = (f32[1024]{0:T(1024)S(1)}, f32[1024]{0:T(1024)}, u32[]{:S(2)}) copy-start(f32[1024]{0:T(1024)} %param.18) | copy-start | bytes 12292
  20.2 11.7 %copy-start.16 = (bf16[64,128]{1,0:T(8,128)(2,1)S(1)}, bf16[64,128]{1,0:T(8,128)(2,1)}, u32[]{:S(2)}) copy-start(bf16[64,128]{1,0:T(8,128)(2,1)} %long_ref.1) | copy-start | bytes 49156
  23.3 0.7 %copy-start.13 = (bf16[128,1024]{1,0:T(8,128)(2,1)}, bf16[128,1024]{1,0:T(8,128)(2,1)S(1)}, u32[]{:S(2)}) copy-start(bf16[128,1024]{1,0:T(8,128)(2,1)S(1)} %get-tuple-element.57.before_ref) | copy-start | bytes 786436
  30.4 3.1 %copy-start.14 = (bf16[128,1024]{1,0:T(8,128)(2,1)S(1)}, bf16[128,1024]{1,0:T(8,128)(2,1)}, u32[]{:S(2)}) copy-start(bf16[128,1024]{1,0:T(8,128)(2,1)} %copy-done.13) | copy-start | bytes 786436
  30.5 10.9 %collective-permute-start.2 = (bf16[128,1024]{1,0:T(8,128)(2,1)S(1)}, bf16[128,1024]{1,0:T(8,128)(2,1)S(1)}, u32[]{:S(2)}, u32[]{:S(2)}) collective-permute-start(bf16[128,1024]{1,0:T(8,128)(2,1)S(1)} %get-tuple-element.54.gm_ref), channel_id=1, source_target_pairs={{4,0},{8,4},{12,8},{16,12},{20,16},{24,20},{28,24},{5,1},{9,5},{13... | collective-permute-start | bytes 786440 | tf_op jit(solution)/shard_map/ppermute | solution.py:24
  45.0 5.2 %collective-permute-start.4 = (f32[104,128]{1,0:T(8,128)S(1)}, f32[104,128]{1,0:T(8,128)S(1)}, u32[]{:S(2)}, u32[]{:S(2)}) collective-permute-start(f32[104,128]{1,0:T(8,128)S(1)} %get-tuple-element.71), channel_id=1, source_target_pairs={{0,4},{4,0},{8,12},{12,8},{16,20},{20,16},{24,28},{28,24},{1,5},{5... | collective-permute-start | bytes 159752 | tf_op jit(solution)/shard_map/ppermute | solution.py:475
  48.1 12.0 %collective-permute-start.3 = (bf16[48,1024]{1,0:T(8,128)(2,1)S(1)}, bf16[48,1024]{1,0:T(8,128)(2,1)S(1)}, u32[]{:S(2)}, u32[]{:S(2)}) collective-permute-start(bf16[48,1024]{1,0:T(8,128)(2,1)S(1)} %get-tuple-element.67), channel_id=1, source_target_pairs={{4,0},{8,4},{12,8},{16,12},{20,16},{24,20},{28,24},{5,1},{9,5},{13... | collective-permute-start | bytes 294920 | tf_op jit(solution)/shard_map/ppermute | solution.py:24
  50.3 6.4 %collective-permute-start.5 = (f32[104,128]{1,0:T(8,128)S(1)}, f32[104,128]{1,0:T(8,128)S(1)}, u32[]{:S(2)}, u32[]{:S(2)}) collective-permute-start(f32[104,128]{1,0:T(8,128)S(1)} %add.8), channel_id=1, source_target_pairs={{0,8},{4,12},{8,0},{12,4},{16,24},{20,28},{24,16},{28,20},{1,9},{5... | collective-permute-start | bytes 159752 | tf_op jit(solution)/shard_map/ppermute | solution.py:475
  56.6 7.2 %collective-permute-start.6 = (f32[104,128]{1,0:T(8,128)S(1)}, f32[104,128]{1,0:T(8,128)S(1)}, u32[]{:S(2)}, u32[]{:S(2)}) collective-permute-start(f32[104,128]{1,0:T(8,128)S(1)} %add.9.one_ref), channel_id=1, source_target_pairs={{0,16},{4,20},{8,24},{12,28},{16,0},{20,4},{24,8},{28,12},{1,17},{... | collective-permute-start | bytes 159752 | tf_op jit(solution)/shard_map/ppermute | solution.py:475

commit v2 on v1

--- a/solution.py
+++ b/solution.py
@@ -12,7 +12,8 @@
 KS = 7
 LANES = 128
 PER = LANES // GS
-RIM = 16
+RIM = 8
+PACK = 16
 EPS = 1e-06
 F32 = jnp.float32
 BF16 = jnp.bfloat16
@@ -84,52 +85,70 @@
     return join(*lines)
 
 
-def group_blocks(left, right):
-    full = jnp.dot(
-        left.reshape(PER * K, left.shape[2]), right, preferred_element_type=F32
-    ).reshape(PER, K, LANES)
-    group = iota((K, LANES), 1) // GS
-    out = full[0]
-    for g in range(1, PER):
-        out = jnp.where(group == g, full[g], out)
-    return out
-
-
-BULK = K - RIM
-Q_LAST, K_LAST, V_LAST, K_FIRST, V_FIRST = (BULK + i * RIM for i in range(5))
-SENT = BULK + 5 * RIM
+def owners():
+    lane = iota((K, LANES), 1) // GS
+    return [as_mask(lane == g) for g in range(PER)]
+
+
+def per_group(right, own):
+    return join(*[right * mask for mask in own])
+
+
+def masked(table_ref, q, mask):
+    table = table_ref[:, pl.ds(pl.multiple_of(q * PER * K, PER * K), PER * K)]
+    return [table[:, g * K : (g + 1) * K] * mask for g in range(PER)]
+
+
+def product(left, right):
+    return jnp.dot(jnp.concatenate(left, axis=1), right, preferred_element_type=F32)
+
+
+K_FIRST, Q_LAST, K_LAST, V_LAST, V_FIRST, SENT = 0, K, K + 8, K + 16, K + 24, K + 32
 
 
 def rim_of(ref, at, ls):
-    return ref[at : at + RIM, ls].astype(F32)
-
-
-def first_kernel(len_ref, short_ref, q_ref, k_ref, v_ref, taps_ref, sent_ref, far_ref):
+    base = at // PACK * PACK
+    return ref[base : base + PACK, ls].astype(F32)[at - base : at - base + RIM]
+
+
+def first_kernel(
+    len_hbm, short_hbm, q_hbm, k_hbm, v_hbm, taps_ref, sent_ref, far_ref,
+    len_ref, short_ref, q_ref, k_ref, v_ref, sems,
+):
     groups = short_ref.shape[2]
     channels = taps_ref.shape[1]
+    pairs = (
+        (short_hbm, short_ref), (len_hbm, len_ref), (k_hbm, k_ref), (v_hbm, v_ref),
+        (q_hbm.at[K - PACK : K], q_ref),
+    )
+    copies = [pltpu.make_async_copy(a, b, sems.at[i]) for i, (a, b) in enumerate(pairs)]
+    for copy in copies:
+        copy.start()
     spread = as_mask(iota((groups, channels), 1) // GS == iota((groups, channels), 0))
+    copies[0].wait()
     for i in range(3):
         taps_ref[i * 8 : i * 8 + KS] = jnp.dot(
             short_ref[i], spread, preferred_element_type=F32
         )
         taps_ref[i * 8 + KS : i * 8 + 8] = jnp.zeros((8 - KS, channels), F32)
-    pos = positions(len_ref, first_row() + RIM + iota((BULK, LANES), 0))
-    end = slice(K - RIM, K)
-
-    def body(q):
-        ls = lanes_of(q)
-        ks = causal(k_ref[:, ls].astype(F32), tap_rows(taps_ref, 1, ls), pos)
-        vs = causal(v_ref[:, ls].astype(F32), tap_rows(taps_ref, 2, ls), pos)
-        sent_ref[:BULK, ls] = (ks * vs).astype(BF16)
+    for copy in copies[1:]:
+        copy.wait()
+    pos = positions(len_ref, first_row() + RIM + iota((K - RIM, LANES), 0))
+
+    def body(q):
+        ls = lanes_of(q)
+        kx = k_ref[:, ls].astype(F32)
+        vx = v_ref[:, ls].astype(F32)
+        ks = causal(kx, tap_rows(taps_ref, 1, ls), pos)
+        vs = causal(vx, tap_rows(taps_ref, 2, ls), pos)
+        sent_ref[:K, ls] = join(kx[:RIM], ks * vs).astype(BF16)
+        q_end = q_ref[:, ls].astype(F32)[PACK - RIM :]
+        k_end = kx[K - RIM :]
+        v_end = vx[K - RIM :]
+        sent_ref[K:, ls] = join(q_end, k_end, v_end, vx[:RIM]).astype(BF16)
+        far_ref[:, ls] = join(k_end, v_end).astype(BF16)
 
     each_chunk(channels, body)
-    sent_ref[Q_LAST : Q_LAST + RIM] = q_ref[end]
-    sent_ref[K_LAST : K_LAST + RIM] = k_ref[end]
-    sent_ref[V_LAST : V_LAST + RIM] = v_ref[end]
-    sent_ref[K_FIRST : K_FIRST + RIM] = k_ref[:RIM]
-    sent_ref[V_FIRST : V_FIRST + RIM] = v_ref[:RIM]
-    far_ref[:RIM] = k_ref[end]
-    far_ref[RIM:] = v_ref[end]
 
 
 def circulant_kernel(turned, long_ref, out_ref, line_ref):
@@ -146,43 +165,54 @@
         block = pltpu.roll(row, 0, 1, stride=1, stride_axis=0)
         for i in range(K // GS):
             moved = block if i == 0 else pltpu.roll(block, i * GS, 1)
-            out_ref[g, i * GS : (i + 1) * GS] = moved.astype(BF16)
+            at = pl.ds(pl.multiple_of(g * K, K), K)
+            out_ref[i * GS : (i + 1) * GS, at] = moved.astype(BF16)
         return carry
 
     lax.fori_loop(0, groups, step, 0, unroll=8)
 
 
-def current_kernel(len_ref, q_ref, taps_ref, sent_ref, fwd_ref, skip_ref, qs_ref, part_ref):
+def current_kernel(
+    len_ref, q_ref, taps_ref, sent_ref, fwd_ref, skip_ref, qs_ref, part_ref, top_ref
+):
     row = iota((K, LANES), 0)
     col = iota((K, LANES), 1)
     pos = positions(len_ref, first_row() + row)
-    mask = as_mask((col <= row) & (pos >= row - col))
-    top = jnp.zeros((RIM, LANES), BF16)
+    near = (col <= row) & (pos >= row - col)
+    mask = as_mask(near)
+    mask_top = as_mask(near & (col < RIM))
+    picks = join(*[as_mask((col == row + g * GS) & (row < GS)) for g in range(PER)])
+    own = owners()
+    top = jnp.zeros((RIM, LANES), F32)
 
     def body(q):
         ls = lanes_of(q)
         qs_ref[RIM:, ls] = causal(q_ref[:, ls].astype(F32), tap_rows(taps_ref, 0, ls), pos[RIM:])
-        qs_ref[:RIM, ls] = jnp.zeros((RIM, LANES), F32)
-        gated = join(top, sent_ref[:BULK, ls])
-        left = fwd_ref[pl.ds(q * PER, PER)] * mask[None]
-        part_ref[:, ls] = group_blocks(left, gated) + skip_ref[:, ls] * gated.astype(F32)
+        qs_ref[:RIM, ls] = top
+        gated = join(top, sent_ref[:K, ls].astype(F32)[RIM:])
+        rest = product(masked(fwd_ref, q, mask), per_group(gated.astype(BF16), own))
+        part_ref[:, ls] = rest + skip_ref[:, ls] * gated
+        top_ref[:, ls] = product(masked(fwd_ref, q, mask_top), picks).astype(BF16)
 
     each_chunk(q_ref.shape[1], body)
 
 
 def summed_kernel(
-    len_ref, came_ref, far_ref, q_ref, k_ref, v_ref, taps_ref, sent_ref, fwd_ref, bulk_ref,
-    part_ref, skip_ref, resid_ref, cot_ref, gain_ref,
+    len_ref, came_ref, far_ref, q_ref, k_ref, v_ref, taps_ref, sent_ref, fwd_ref, top_ref,
+    bulk_ref, part_ref, skip_ref, resid_ref, cot_ref, gain_ref,
     qs_ref, gated_ref, before_ref, mixed_ref, summed_ref, sums_ref, acc_ref,
 ):
     row = iota((K, LANES), 0)
     col = iota((K, LANES), 1)
     pos = positions(len_ref, first_row() + row)
-    far = as_mask((col > row) & (pos >= row - col + K))
-    near = as_mask((col <= row) & (col < RIM) & (pos >= row - col))
+    mask = as_mask((col > row) & (pos >= row - col + K))
     pos_top = pos[:RIM]
     pos_far = positions(len_ref, first_row() - K + iota((RIM, LANES), 0))
-    rest = jnp.zeros((K - RIM, LANES), BF16)
+    own = owners()
+    own_top = [
+        as_mask((iota((PACK, LANES), 1) // GS == g) & (iota((PACK, LANES), 0) < RIM))
+        for g in range(PER)
+    ]
     acc_ref[...] = jnp.zeros_like(acc_ref)
 
     def body(q):
@@ -191,26 +221,27 @@
         vt = tap_rows(taps_ref, 2, ls)
         k_last = rim_of(came_ref, K_LAST, ls)
         v_last = rim_of(came_ref, V_LAST, ls)
-        top = (
-            causal(join(k_last, rim_of(k_ref, 0, ls)), kt, pos_top)
-            * causal(join(v_last, rim_of(v_ref, 0, ls)), vt, pos_top)
-        ).astype(BF16)
-        far_top = (
-            causal(join(rim_of(far_ref, 0, ls), rim_of(came_ref, K_FIRST, ls)), kt, pos_far)
-            * causal(join(rim_of(far_ref, RIM, ls), rim_of(came_ref, V_FIRST, ls)), vt, pos_far)
-        ).astype(BF16)
+        top = causal(join(k_last, rim_of(k_ref, 0, ls)), kt, pos_top) * causal(
+            join(v_last, rim_of(v_ref, 0, ls)), vt, pos_top
+        )
+        far_top = causal(
+            join(rim_of(far_ref, 0, ls), rim_of(came_ref, K_FIRST, ls)), kt, pos_far
+        ) * causal(join(rim_of(far_ref, RIM, ls), rim_of(came_ref, V_FIRST, ls)), vt, pos_far)
         qs_top = causal(
             join(rim_of(came_ref, Q_LAST, ls), rim_of(q_ref, 0, ls)), tap_rows(taps_ref, 0, ls), pos_top
         )
-        before = join(far_top, came_ref[:BULK, ls])
+        before = join(far_top, came_ref[:K, ls].astype(F32)[RIM:]).astype(BF16)
+        gated = join(top, sent_ref[:K, ls].astype(F32)[RIM:]).astype(BF16)
         before_ref[:, ls] = before
-        gated_ref[:, ls] = join(top, sent_ref[:BULK, ls])
+        gated_ref[:, ls] = gated
         qs = join(qs_top, bulk_ref[RIM:, ls])
         qs_ref[:, ls] = qs
-        table = fwd_ref[pl.ds(q * PER, PER)]
-        left = jnp.concatenate([table * far[None], table * near[None]], axis=2)
-        direct = join(skip_ref[:, ls] * top.astype(F32), jnp.zeros((K - RIM, LANES), F32))
-        mixed = part_ref[:, ls] + direct + group_blocks(left, join(before, top, rest))
+        first = gated[:PACK]
+        left = masked(fwd_ref, q, mask) + [top_ref[:, ls]]
+        right = join(per_group(before, own), per_group(first, own_top))
+        direct = skip_ref[:, ls] * first.astype(F32)[:RIM]
+        mixed = part_ref[:, ls] + product(left, right)
+        mixed = join(mixed[:RIM] + direct, mixed[RIM:])
         summed = resid_ref[:, ls].astype(F32) + qs * mixed
         mixed_ref[:, ls] = mixed
         summed_ref[:, ls] = summed
@@ -245,11 +276,11 @@
 
 
 def beside_kernel(
-    total, len_ref, summed_ref, cot_ref, gain_ref, sums_ref, gm_ref, gq_ref, gated_ref, before_ref,
+    total, len_ref, summed_ref, cot_ref, sums_ref, gm_ref, gq_ref, gated_ref, before_ref,
     bwd_ref, skip_ref, q_ref, k_ref, v_ref, came_ref, taps_ref,
-    normed_ref, stats_ref, part_ref, ks_ref, vs_ref, cols_ref,
-):
-    groups = bwd_ref.shape[0]
+    stats_ref, part_ref, ks_ref, vs_ref, cols_ref,
+):
+    groups = bwd_ref.shape[1] // K
     inverse = inverse_of(sums_ref, total)
     row = iota((K, LANES), 0)
     col = iota((K, LANES), 1)
@@ -260,12 +291,11 @@
     near = (col >= source) & (pos >= col - source)
     far = (col < source) & (pos >= col - source + K)
     flip = as_mask(row + col == K - 1)
-    own = [as_mask(col // GS == g) for g in range(PER)]
+    own = owners()
 
     def body(q):
         ls = lanes_of(q)
         summed = summed_ref[:, ls]
-        normed_ref[:, ls] = (gain_ref[:, ls] * summed * inverse).astype(BF16)
         gm = gm_ref[:, ls]
         gmf = gm.astype(F32)
         gated = gated_ref[:, ls]
@@ -273,12 +303,11 @@
         stats_ref[pl.ds(groups + groups // PER + q, 1), :] = jnp.sum(
             cot_ref[:, ls].astype(F32) * summed * inverse, axis=0, keepdims=True
         )
-        left = bwd_ref[pl.ds(q * PER, PER)] * mask[None]
-        part_ref[:, ls] = skip_ref[:, ls] * gmf + group_blocks(left, gm)
+        right = per_group(gm, own)
+        part_ref[:, ls] = skip_ref[:, ls] * gmf + product(masked(bwd_ref, q, mask), right)
         two = jnp.concatenate([before_ref[:, ls], gated], axis=1)
         flipped = jnp.dot(flip, two, preferred_element_type=F32).astype(BF16)
         left = join(flipped[:, :LANES], flipped[:, LANES:])
-        right = join(*[gm * own[g] for g in range(PER)])
         cross = lax.dot_general(
             left, right, (((1,), (1,)), ((), ())), preferred_element_type=F32
         )
@@ -310,18 +339,18 @@
     pos_row = positions(len_ref, first_row() + row)
     pos = positions(len_ref, first_row() + K + col)
     mask = as_mask((col < row) & (pos >= col - row + K))
-
-    def body(q):
-        ls = lanes_of(q)
-        left = bwd_ref[pl.ds(q * PER, PER)] * mask[None]
-        grad = part_ref[:, ls] + group_blocks(left, after_ref[:, ls])
+    own = owners()
+
+    def body(q):
+        ls = lanes_of(q)
+        right = per_group(after_ref[:, ls], own)
+        grad = part_ref[:, ls] + product(masked(bwd_ref, q, mask), right)
         gks = (grad * vs_ref[:, ls]).astype(BF16)
         gvs = (grad * ks_ref[:, ls]).astype(BF16)
         gks_ref[:, ls] = gks
         gvs_ref[:, ls] = gvs
-        tails_ref[0:RIM, ls] = gq_ref[0:RIM, ls]
-        tails_ref[RIM : 2 * RIM, ls] = gks[:RIM]
-        tails_ref[2 * RIM :, ls] = gvs[:RIM]
+        heads = (rim_of(gq_ref, 0, ls), gks.astype(F32)[:RIM], gvs.astype(F32)[:RIM])
+        tails_ref[:, ls] = join(*heads, jnp.zeros((RIM, LANES), F32)).astype(BF16)
         k_ext = join(rim_of(came_ref, K_LAST, ls), k_ref[:, ls].astype(F32))
         v_ext = join(rim_of(came_ref, V_LAST, ls), v_ref[:, ls].astype(F32))
         cols_ref[0:8, ls] = qcols_ref[:, ls]
@@ -339,28 +368,33 @@
 
 
 def mains_kernel(
-    len_ref, taps_ref, gq_ref, gks_ref, gvs_ref, tails_ref, oq_ref, ok_ref, ov_ref
+    total, len_ref, taps_ref, gq_ref, gks_ref, gvs_ref, tails_ref, summed_ref, gain_ref, sums_ref,
+    oq_ref, ok_ref, ov_ref, normed_ref,
 ):
     pos = positions(len_ref, first_row() + iota((K + RIM, LANES), 0))
-
-    def body(q):
-        ls = lanes_of(q)
+    inverse = inverse_of(sums_ref, total)
+
+    def body(q):
+        ls = lanes_of(q)
+        normed_ref[:, ls] = (gain_ref[:, ls] * summed_ref[:, ls] * inverse).astype(BF16)
         for i, (g_ref, o_ref) in enumerate(((gq_ref, oq_ref), (gks_ref, ok_ref), (gvs_ref, ov_ref))):
             ext = join(g_ref[:, ls].astype(F32), rim_of(tails_ref, i * RIM, ls))
             taps = tap_rows(taps_ref, i, ls)
-            total = taps[0] * ext[:K]
+            grad = taps[0] * ext[:K]
             for j in range(1, KS):
                 held = jnp.where(pos >= j, ext, 0.0)
-                total = total + taps[j] * held[j : j + K]
-            o_ref[:, ls] = total.astype(BF16)
+                grad = grad + taps[j] * held[j : j + K]
+            o_ref[:, ls] = grad.astype(BF16)
 
     each_chunk(gq_ref.shape[1], body)
 
 
-def unpack_kernel(one_ref, two_ref, short_ref, long_ref, skip_ref, gain_ref):
+def unpack_kernel(all_ref, short_ref, long_ref, skip_ref, gain_ref):
     groups = long_ref.shape[0]
     rows = groups // PER
-    total = one_ref[...] + two_ref[...]
+    total = lax.fori_loop(
+        1, all_ref.shape[0], lambda i, acc: acc + all_ref[i], all_ref[0]
+    )
     long_ref[...] = total[:groups]
     skip_ref[...] = total[groups : groups + rows]
     gain_ref[...] = total[groups + rows : groups + 2 * rows]
@@ -382,15 +416,18 @@
 
     smem = pl.BlockSpec(memory_space=pltpu.SMEM)
     vmem = pl.BlockSpec(memory_space=pltpu.VMEM)
+    far_off = pl.BlockSpec(memory_space=pltpu.HBM)
     full_bf = arr((length, channels), BF16)
     full_f = arr((length, channels), F32)
 
-    def call(name, kernel, outs, ins, scratch=(), flops=10**8, moved=10**6, grant=8):
+    def call(name, kernel, outs, ins, scratch=(), flops=10**8, moved=10**6, grant=8, hbm=False):
         scalar = ins[0] is lengths
         return pl.pallas_call(
             kernel,
             out_shape=outs,
-            in_specs=[smem if (i == 0 and scalar) else vmem for i in range(len(ins))],
+            in_specs=[far_off] * len(ins)
+            if hbm
+            else [smem if (i == 0 and scalar) else vmem for i in range(len(ins))],
             out_specs=[vmem] * len(outs),
             scratch_shapes=scratch,
             compiler_params=pltpu.CompilerParams(vmem_limit_bytes=grant * 1024 * 1024),
@@ -404,6 +441,12 @@
         "first", first_kernel,
         [arr((24, channels), F32), arr((SENT, channels), BF16), arr((2 * RIM, channels), BF16)],
         [lengths, jnp.transpose(short_filter, (0, 2, 1)), q_input, k_input, v_input],
+        [
+            pltpu.SMEM(lengths.shape, jnp.int32), pltpu.VMEM((3, KS, groups), BF16),
+            pltpu.VMEM((PACK, channels), BF16), pltpu.VMEM((length, channels), BF16),
+            pltpu.VMEM((length, channels), BF16), pltpu.SemaphoreType.DMA((5,)),
+        ],
+        hbm=True,
     )
     came = shifted(sent, "ctx", 1)
     came_far = shifted(far, "ctx", 2)
@@ -411,22 +454,22 @@
     def circulants(filt, turned):
         return call(
             "circulants", functools.partial(circulant_kernel, turned),
-            [arr((groups, K, K), BF16)], [filt], [pltpu.VMEM((groups, K), F32)],
+            [arr((K, groups * K), BF16)], [filt], [pltpu.VMEM((groups, K), F32)],
             flops=10**9, moved=4 * 10**6,
         )[0]
 
     filt, sent = lax.optimization_barrier((long_filter, sent))
     fwd = circulants(filt, True)
-    bulk, part = call(
-        "current", current_kernel, [full_f] * 2,
+    bulk, part, top = call(
+        "current", current_kernel, [full_f, full_f, full_bf],
         [lengths, q_input, taps, sent, fwd, skip2], flops=10**9, moved=5 * 10**6,
     )
     q_short, gated, before, mixed, summed, sums = call(
         "summed", summed_kernel,
         [full_f, full_bf, full_bf, full_f, full_f, arr((2, K), F32)],
         [
-            lengths, came, came_far, q_input, k_input, v_input, taps, sent, fwd, bulk,
-            part, skip2, resid, cotangent, gain2,
+            lengths, came, came_far, q_input, k_input, v_input, taps, sent, fwd, top,
+            bulk, part, skip2, resid, cotangent, gain2,
         ],
         [pltpu.VMEM((2, K, LANES), F32)], flops=10**9, moved=5 * 10**6,
     )
@@ -438,22 +481,22 @@
     after = shifted(grad_mixed, "ctx", -1)
     filt, grad_mixed = lax.optimization_barrier((long_filter, grad_mixed))
     bwd = circulants(filt, False)
-    normed, stats, part, k_short, v_short, qcols = call(
+    stats, part, k_short, v_short, qcols = call(
         "beside", functools.partial(beside_kernel, wide),
         [
-            full_bf, arr((groups + 2 * rows, LANES), F32), full_f, full_f, full_f,
+            arr((groups + 2 * rows, LANES), F32), full_f, full_f, full_f,
             arr((8, channels), F32),
         ],
         [
-            lengths, summed, cotangent, gain2, sums, grad_mixed, grad_qs, gated, before,
-            bwd, skip2, q_input, k_input, v_input, came, taps,
+            lengths, summed, cotangent, sums, grad_mixed, grad_qs, gated, before, bwd,
+            skip2, q_input, k_input, v_input, came, taps,
         ],
         flops=4 * 10**9, moved=5 * 10**6,
     )
     grad_ks, grad_vs, tails, packed = call(
         "gate", gate_kernel,
         [
-            full_bf, full_bf, arr((3 * RIM, channels), BF16),
+            full_bf, full_bf, arr((4 * RIM, channels), BF16),
             arr((groups + 2 * rows + 24, LANES), F32),
         ],
         [
@@ -463,24 +506,18 @@
         [pltpu.VMEM((24, channels), F32)], flops=10**9, moved=5 * 10**6,
     )
     tails = shifted(tails, "ctx", -1)
-    grad_q, grad_k, grad_v = call(
-        "mains", mains_kernel, [full_bf] * 3,
-        [lengths, taps, grad_qs, grad_ks, grad_vs, tails], flops=10**9, moved=5 * 10**6,
-    )
-    count = lax.axis_size("ctx")
-    step = 1
-    while step < count:
-        if step > 1:
-            packed = packed + other
-        other = lax.ppermute(packed, "ctx", [(i, i ^ step) for i in range(count)])
-        step *= 2
+    grad_q, grad_k, grad_v, normed = call(
+        "mains", functools.partial(mains_kernel, wide), [full_bf] * 4,
+        [lengths, taps, grad_qs, grad_ks, grad_vs, tails, summed, gain2, sums], flops=10**9, moved=5 * 10**6,
+    )
+    packed = lax.all_gather(packed, "ctx")
     grad_short, grad_long, grad_skip, grad_gain = call(
         "unpack", unpack_kernel,
         [
             arr((3, KS, groups), F32), arr((groups, K), F32),
             arr((rows, LANES), F32), arr((rows, LANES), F32),
         ],
-        [packed, other],
+        [packed],
     )
     return (
         normed, grad_q, grad_k, grad_v, jnp.transpose(grad_short, (0, 2, 1)), grad_long,

time: 64.9 us -> 85.1 us (1.31)
  blocking collectives: 6 us -> 40.7 us
  starting transfers between devices: 21.2 us -> 11.1 us
  waiting for transfers between devices: 3.65 us -> 0.01 us
    all_gather x0 -> x1, blocking collectives: none -> 34.7 us  [shards(): packed = lax.all_gather(packed, 'ctx')]
    ppermute x3 -> x0, starting transfers between devices: 10.2 us -> none  [shards(): other = lax.ppermute(packed, 'ctx', [(i, i ^ step) for i in range(count)])]
    ppermute x3 -> x0, waiting for transfers between devices: 3.64 us -> none  [shards(): other = lax.ppermute(packed, 'ctx', [(i, i ^ step) for i in range(count)])]
  transfers between devices with their start and end apart: 7 -> 4, of which waited for: 2 -> 0; matrix products, arithmetic and copies ran while one was open for 0% -> 0% of each run, Pallas kernels for 27% -> 17%
where the time goes in v2:
time: 85.1 us; the launch traced here: 84.7 us
  blocking collectives  40.7 us (48%)
  Pallas kernels  26.3 us (31%)
  starting transfers between devices  11.1 us (13%)
  local copies, waits for them, and re-layouts  5.66 us (7%)
  between operations  0.92 us (1%)
    all_gather x1, blocking collectives, shards(): packed = lax.all_gather(packed, 'ctx')  34.7 us
    pallas_call x10, Pallas kernels, call(): pl.pallas_call(kernel, out_shape=outs, in_specs=[far_off] * len(ins) if h...  26.3 us
    ppermute x4, starting transfers between devices, shifted(): return lax.ppermute(x, axis, pairs)  11.1 us
    psum x1, blocking collectives, shards(): sums = lax.psum(sums, 'tp')  5.98 us
    unnamed x34, local copies, waits for them, and re-layouts  5.66 us
  transfers between devices with their start and end apart: 4, of which 0 were waited for; matrix products, arithmetic and copies ran while one was open for 0% of the time, Pallas kernels for 17%

profile of v2, /device:TPU:0, one launch (start us, length us, event | category | flops | bytes accessed | tf_op | source)
XLA Modules:
  0.0 84.7 jit_solution(15671025443359099633)
XLA Ops:
  0.6 0.0 copy-start
  0.6 0.9 %copy-done = bf16[128,1024]{1,0:T(8,128)(2,1)S(1)} copy-done((bf16[128,1024]{1,0:T(8,128)(2,1)S(1)}, bf16[128,1024]{1,0:T(8,128)(2,1)}, u32[]{:S(2)}) %copy-start) | copy-done | bytes 262168
  1.6 0.9 %copy-done.2 = bf16[128,1024]{1,0:T(8,128)(2,1)S(1)} copy-done((bf16[128,1024]{1,0:T(8,128)(2,1)S(1)}, bf16[128,1024]{1,0:T(8,128)(2,1)}, u32[]{:S(2)}) %copy-start.2) | copy-done | bytes 262168
  2.5 0.9 %copy-done.5 = bf16[128,1024]{1,0:T(8,128)(2,1)S(1)} copy-done((bf16[128,1024]{1,0:T(8,128)(2,1)S(1)}, bf16[128,1024]{1,0:T(8,128)(2,1)}, u32[]{:S(2)}) %copy-start.5) | copy-done | bytes 262168
  3.5 0.7 copy-done.9
  4.2 0.7 copy-done.10
  4.8 2.0 %first.1 = (f32[24,1024]{1,0:T(8,128)S(1)}, bf16[160,1024]{1,0:T(8,128)(2,1)S(1)}, bf16[16,1024]{1,0:T(8,128)(2,1)S(1)}) custom-call(s32[8]{0:T(128)S(1)} %copy-done.10, bf16[3,7,64]{2,1,0:T(8,128)(2,1)S(1)} %bitcast.11, bf16[128,1024]{1,0:T(8,128)(2,1)S(1)} %copy-done.5, bf16[128,1024]{1,0:T(8,128)(2,1)S(1)} %copy-done, bf16[128,1024]{1,0:T(8,128)(2,1)S(1)} %copy-done.2), custom_call_target="tpu_custom_call" | custom-call | flops 100000000 | bytes 1000000 | tf_op jit(solution)/shard_map/first/pallas_call | solution.py:425
  6.8 4.9 %collective-permute-start = (bf16[160,1024]{1,0:T(8,128)(2,1)S(1)}, bf16[160,1024]{1,0:T(8,128)(2,1)S(1)}, u32[]{:S(2)}, u32[]{:S(2)}) collective-permute-start(bf16[160,1024]{1,0:T(8,128)(2,1)S(1)} %get-tuple-element.46.sent_ref), channel_id=1, source_target_pairs={{0,4},{4,8},{8,12},{12,16},{16,20},{20,24},{24,28},{1,5},{5,9},{9,... | collective-permute-start | bytes 983048 | tf_op jit(solution)/shard_map/ppermute | solution.py:25
  11.7 3.5 %collective-permute-start.1 = (bf16[16,1024]{1,0:T(8,128)(2,1)S(1)}, bf16[16,1024]{1,0:T(8,128)(2,1)S(1)}, u32[]{:S(2)}, u32[]{:S(2)}) collective-permute-start(bf16[16,1024]{1,0:T(8,128)(2,1)S(1)} %get-tuple-element.45), channel_id=1, source_target_pairs={{0,8},{4,12},{8,16},{12,20},{16,24},{20,28},{1,9},{5,13},{9,17},{1... | collective-permute-start | bytes 98312 | tf_op jit(solution)/shard_map/ppermute | solution.py:25
  15.2 0.0 copy-start.15
  15.2 0.7 copy-done.15
  15.9 1.8 %circulants.2.fwd_ref = bf16[128,8192]{1,0:T(8,128)(2,1)S(1)} custom-call(bf16[64,128]{1,0:T(8,128)(2,1)S(1)} %copy-done.15), custom_call_target="tpu_custom_call" | custom-call | flops 1000000000 | bytes 4000000 | tf_op jit(solution)/shard_map/circulants/pallas_call | solution.py:425
  17.7 0.0 copy-start.1
  17.7 0.0 copy-start.3
  17.7 0.0 copy-start.4
  17.7 0.0 copy-start.7
  17.8 0.0 copy-start.8
  17.8 2.9 %current.1 = (f32[128,1024]{1,0:T(8,128)S(1)}, f32[128,1024]{1,0:T(8,128)S(1)}, bf16[128,1024]{1,0:T(8,128)(2,1)S(1)}) custom-call(s32[8]{0:T(128)S(1)} %copy-done.11, bf16[128,1024]{1,0:T(8,128)(2,1)S(1)} %copy-done.6, f32[24,1024]{1,0:T(8,128)S(1)} %get-tuple-element.43.taps_ref, bf16[160,1024]{1,0:T(8,128)(2,1)S(1)} %get-tuple-element.46.sent_ref, ...), custom_call_target="tpu_custom_call" | custom-call | flops 1000000000 | bytes 5000000 | tf_op jit(solution)/shard_map/current/pallas_call | solution.py:425
  20.8 2.2 %summed.1 = (f32[128,1024]{1,0:T(8,128)S(1)}, bf16[128,1024]{1,0:T(8,128)(2,1)S(1)}, bf16[128,1024]{1,0:T(8,128)(2,1)S(1)}, f32[128,1024]{1,0:T(8,128)S(1)}, f32...) custom-call(s32[8]{0:T(128)S(1)} %copy-done.11, bf16[160,1024]{1,0:T(8,128)(2,1)S(1)} %collective-permute-done.came_ref, ...), custom_call_target="tpu_custom_call" | custom-call | flops 1000000000 | bytes 5000000 | tf_op jit(solution)/shard_map/summed/pallas_call | solution.py:425
  23.0 0.0 copy-start.13
  23.1 0.7 copy-done.13
  23.7 6.0 %psum.7.sums_ref = f32[2,128]{1,0:T(2,128)S(1)} all-reduce(f32[2,128]{1,0:T(2,128)S(1)} %get-tuple-element.54), channel_id=1, replica_groups=mesh['ctx'=8,'tp'=4] {'tp'}, use_global_device_ids=true, to_apply=%region_0.0 | all-reduce | flops 256 | bytes 2048 | tf_op jit(solution)/shard_map/psum | solution.py:476
  29.7 0.5 grads.1
  30.2 0.0 copy-start.14
  30.2 1.4 %collective-permute-start.2 = (bf16[128,1024]{1,0:T(8,128)(2,1)S(1)}, bf16[128,1024]{1,0:T(8,128)(2,1)S(1)}, u32[]{:S(2)}, u32[]{:S(2)}) collective-permute-start(bf16[128,1024]{1,0:T(8,128)(2,1)S(1)} %get-tuple-element.57.gm_ref), channel_id=1, source_target_pairs={{4,0},{8,4},{12,8},{16,12},{20,16},{24,20},{28,24},{5,1},{9,5},{13... | collective-permute-start | bytes 786440 | tf_op jit(solution)/shard_map/ppermute | solution.py:25
  31.7 1.7 %circulants.3.bwd_ref = bf16[128,8192]{1,0:T(8,128)(2,1)S(1)} custom-call(bf16[64,128]{1,0:T(8,128)(2,1)S(1)} %copy-done.16), custom_call_target="tpu_custom_call" | custom-call | flops 1000000000 | bytes 4000000 | tf_op jit(solution)/shard_map/circulants/pallas_call | solution.py:425
  33.4 7.4 %beside.1 = (f32[80,128]{1,0:T(8,128)S(1)}, f32[128,1024]{1,0:T(8,128)S(1)}, f32[128,1024]{1,0:T(8,128)S(1)}, f32[128,1024]{1,0:T(8,128)S(1)}, f32[8,1024]{1,0:T(8,128)S(1)}) custom-call(s32[8]{0:T(128)S(1)} %copy-done.11, f32[128,1024]{1,0:T(8,128)S(1)} %get-tuple-element.51.summed_ref, bf16[128,1024]{1,0:T(8,128)(2,1)S(1)} %copy-done.4, ...), custom_call_target="tpu_custom_call" | custom-call | flops 4000000000 | bytes 5000000 | tf_op jit(solution)/shard_map/beside/pallas_call | solution.py:425
  40.7 3.4 %gate.1 = (bf16[128,1024]{1,0:T(8,128)(2,1)S(1)}, bf16[128,1024]{1,0:T(8,128)(2,1)S(1)}, bf16[32,1024]{1,0:T(8,128)(2,1)S(1)}, f32[104,128]{1,0:T(8,128)S(1)}) custom-call(s32[8]{0:T(128)S(1)} %copy-done.11, f32[128,1024]{1,0:T(8,128)S(1)} %get-tuple-element.61.part_ref, bf16[128,1024]{1,0:T(8,128)(2,1)S(1)} %collective-permute-done.2.after_ref, ...), custom_call_target="tpu_custom_call" | custom-call | flops 1000000000 | bytes 5000000 | tf_op jit(solution)/shard_map/gate/pallas_call | solution.py:425
  44.2 1.3 %collective-permute-start.3 = (bf16[32,1024]{1,0:T(8,128)(2,1)S(1)}, bf16[32,1024]{1,0:T(8,128)(2,1)S(1)}, u32[]{:S(2)}, u32[]{:S(2)}) collective-permute-start(bf16[32,1024]{1,0:T(8,128)(2,1)S(1)} %get-tuple-element.68), channel_id=1, source_target_pairs={{4,0},{8,4},{12,8},{16,12},{20,16},{24,20},{28,24},{5,1},{9,5},{13... | collective-permute-start | bytes 196616 | tf_op jit(solution)/shard_map/ppermute | solution.py:25
  45.5 34.7 %all-gather = f32[832,128]{1,0:T(8,128)S(1)} all-gather(f32[104,128]{1,0:T(8,128)S(1)} %get-tuple-element.73), channel_id=2, replica_groups=mesh['ctx'=8,'tp'=4] {'ctx'}, dimensions={0}, use_global_device_ids=true | all-gather | bytes 479232 | tf_op jit(solution)/shard_map/all_gather | solution.py:513
  80.2 0.7 unpack.1
  80.8 3.8 %mains.1 = (bf16[128,1024]{1,0:T(8,128)(2,1)}, bf16[128,1024]{1,0:T(8,128)(2,1)}, bf16[128,1024]{1,0:T(8,128)(2,1)}, bf16[128,1024]{1,0:T(8,128)(2,1)}) custom-call(s32[8]{0:T(128)S(1)} %copy-done.11, f32[24,1024]{1,0:T(8,128)S(1)} %get-tuple-element.43.taps_ref, bf16[128,1024]{1,0:T(8,128)(2,1)S(1)} %get-tuple-element.55.gq_ref, ...), custom_call_target="tpu_custom_call" | custom-call | flops 1000000000 | bytes 5000000 | tf_op jit(solution)/shard_map/mains/pallas_call | solution.py:425
  (22 shorter events, 0.0 us)
Async XLA Ops:
  0.6 1.0 %copy-start = (bf16[128,1024]{1,0:T(8,128)(2,1)S(1)}, bf16[128,1024]{1,0:T(8,128)(2,1)}, u32[]{:S(2)}) copy-start(bf16[128,1024]{1,0:T(8,128)(2,1)} %k_ref.5) | copy-start | bytes 786436
  1.6 0.9 %copy-start.2 = (bf16[128,1024]{1,0:T(8,128)(2,1)S(1)}, bf16[128,1024]{1,0:T(8,128)(2,1)}, u32[]{:S(2)}) copy-start(bf16[128,1024]{1,0:T(8,128)(2,1)} %v_ref.5) | copy-start | bytes 786436
  2.5 0.9 %copy-start.5 = (bf16[128,1024]{1,0:T(8,128)(2,1)S(1)}, bf16[128,1024]{1,0:T(8,128)(2,1)}, u32[]{:S(2)}) copy-start(bf16[128,1024]{1,0:T(8,128)(2,1)} %q_ref.5) | copy-start | bytes 786436
  3.5 0.7 copy-start.9
  4.2 0.7 copy-start.10
  4.8 12.9 %copy-start.6 = (bf16[128,1024]{1,0:T(8,128)(2,1)S(1)}, bf16[128,1024]{1,0:T(8,128)(2,1)}, u32[]{:S(2)}) copy-start(bf16[128,1024]{1,0:T(8,128)(2,1)} %q_ref.5) | copy-start | bytes 786436
  4.8 12.9 %copy-start.11 = (s32[8]{0:T(128)S(1)}, s32[8]{0:T(128)}, u32[]{:S(2)}) copy-start(s32[8]{0:T(128)} %len_ref.9) | copy-start | bytes 100
  4.8 13.0 %copy-start.12 = (f32[1024]{0:T(1024)S(1)}, f32[1024]{0:T(1024)}, u32[]{:S(2)}) copy-start(f32[1024]{0:T(1024)} %param.17) | copy-start | bytes 12292
  6.8 13.9 %collective-permute-start = (bf16[160,1024]{1,0:T(8,128)(2,1)S(1)}, bf16[160,1024]{1,0:T(8,128)(2,1)S(1)}, u32[]{:S(2)}, u32[]{:S(2)}) collective-permute-start(bf16[160,1024]{1,0:T(8,128)(2,1)S(1)} %get-tuple-element.46.sent_ref), channel_id=1, source_target_pairs={{0,4},{4,8},{8,12},{12,16},{16,20},{20,24},{24,28},{1,5},{5,9},{9,... | collective-permute-start | bytes 983048 | tf_op jit(solution)/shard_map/ppermute | solution.py:25
  11.7 9.0 %collective-permute-start.1 = (bf16[16,1024]{1,0:T(8,128)(2,1)S(1)}, bf16[16,1024]{1,0:T(8,128)(2,1)S(1)}, u32[]{:S(2)}, u32[]{:S(2)}) collective-permute-start(bf16[16,1024]{1,0:T(8,128)(2,1)S(1)} %get-tuple-element.45), channel_id=1, source_target_pairs={{0,8},{4,12},{8,16},{12,20},{16,24},{20,28},{1,9},{5,13},{9,17},{1... | collective-permute-start | bytes 98312 | tf_op jit(solution)/shard_map/ppermute | solution.py:25
  15.2 0.7 copy-start.15
  17.7 3.0 %copy-start.1 = (bf16[128,1024]{1,0:T(8,128)(2,1)S(1)}, bf16[128,1024]{1,0:T(8,128)(2,1)}, u32[]{:S(2)}) copy-start(bf16[128,1024]{1,0:T(8,128)(2,1)} %k_ref.5) | copy-start | bytes 786436
  17.7 3.0 %copy-start.3 = (bf16[128,1024]{1,0:T(8,128)(2,1)S(1)}, bf16[128,1024]{1,0:T(8,128)(2,1)}, u32[]{:S(2)}) copy-start(bf16[128,1024]{1,0:T(8,128)(2,1)} %v_ref.5) | copy-start | bytes 786436
  17.7 3.0 %copy-start.4 = (bf16[128,1024]{1,0:T(8,128)(2,1)S(1)}, bf16[128,1024]{1,0:T(8,128)(2,1)}, u32[]{:S(2)}) copy-start(bf16[128,1024]{1,0:T(8,128)(2,1)} %cot_ref.5) | copy-start | bytes 786436
  17.7 3.0 %copy-start.7 = (bf16[128,1024]{1,0:T(8,128)(2,1)S(1)}, bf16[128,1024]{1,0:T(8,128)(2,1)}, u32[]{:S(2)}) copy-start(bf16[128,1024]{1,0:T(8,128)(2,1)} %resid_ref.1) | copy-start | bytes 786436
  17.8 3.0 %copy-start.8 = (f32[1024]{0:T(1024)S(1)}, f32[1024]{0:T(1024)}, u32[]{:S(2)}) copy-start(f32[1024]{0:T(1024)} %param.18) | copy-start | bytes 12292
  20.8 10.9 %copy-start.16 = (bf16[64,128]{1,0:T(8,128)(2,1)S(1)}, bf16[64,128]{1,0:T(8,128)(2,1)}, u32[]{:S(2)}) copy-start(bf16[64,128]{1,0:T(8,128)(2,1)} %long_ref.1) | copy-start | bytes 49156
  23.0 0.7 copy-start.13
  30.2 3.1 %copy-start.14 = (bf16[128,1024]{1,0:T(8,128)(2,1)S(1)}, bf16[128,1024]{1,0:T(8,128)(2,1)}, u32[]{:S(2)}) copy-start(bf16[128,1024]{1,0:T(8,128)(2,1)} %copy-done.13) | copy-start | bytes 786436
  30.2 10.5 %collective-permute-start.2 = (bf16[128,1024]{1,0:T(8,128)(2,1)S(1)}, bf16[128,1024]{1,0:T(8,128)(2,1)S(1)}, u32[]{:S(2)}, u32[]{:S(2)}) collective-permute-start(bf16[128,1024]{1,0:T(8,128)(2,1)S(1)} %get-tuple-element.57.gm_ref), channel_id=1, source_target_pairs={{4,0},{8,4},{12,8},{16,12},{20,16},{24,20},{28,24},{5,1},{9,5},{13... | collective-permute-start | bytes 786440 | tf_op jit(solution)/shard_map/ppermute | solution.py:25
  44.2 36.7 %collective-permute-start.3 = (bf16[32,1024]{1,0:T(8,128)(2,1)S(1)}, bf16[32,1024]{1,0:T(8,128)(2,1)S(1)}, u32[]{:S(2)}, u32[]{:S(2)}) collective-permute-start(bf16[32,1024]{1,0:T(8,128)(2,1)S(1)} %get-tuple-element.68), channel_id=1, source_target_pairs={{4,0},{8,4},{12,8},{16,12},{20,16},{24,20},{28,24},{5,1},{9,5},{13... | collective-permute-start | bytes 196616 | tf_op jit(solution)/shard_map/ppermute | solution.py:25

commit v3 on v2

--- a/solution.py
+++ b/solution.py
@@ -308,15 +308,19 @@
         two = jnp.concatenate([before_ref[:, ls], gated], axis=1)
         flipped = jnp.dot(flip, two, preferred_element_type=F32).astype(BF16)
         left = join(flipped[:, :LANES], flipped[:, LANES:])
-        cross = lax.dot_general(
-            left, right, (((1,), (1,)), ((), ())), preferred_element_type=F32
-        )
+        turned = gmf.T.astype(BF16)
+        spread = []
+        for g in range(PER):
+            pieces = [jnp.zeros((GS, K), BF16)] * PER
+            pieces[g] = turned[g * GS : (g + 1) * GS]
+            spread.append(join(*pieces))
+        cross = jnp.dot(left, jnp.concatenate(spread, axis=1), preferred_element_type=F32)
         lines = []
         for g in range(PER):
             gs = slice(g * K, (g + 1) * K)
             square = jnp.where(near, cross[K:, gs], jnp.where(far, cross[:K, gs], 0.0))
-            turned = pltpu.roll(square, 1, 1, stride=1, stride_axis=0)
-            lines.append(jnp.sum(turned, axis=0, keepdims=True))
+            square = pltpu.roll(square, 1, 1, stride=1, stride_axis=0)
+            lines.append(jnp.sum(square, axis=0, keepdims=True))
         stats_ref[pl.ds(pl.multiple_of(q * PER, PER), PER), :] = join(*lines)
         k_ext = join(rim_of(came_ref, K_LAST, ls), k_ref[:, ls].astype(F32))
         v_ext = join(rim_of(came_ref, V_LAST, ls), v_ref[:, ls].astype(F32))
@@ -362,7 +366,8 @@
     gather = jnp.where(
         iota((channels, LANES), 0) // GS == iota((channels, LANES), 1), 1.0, 0.0
     )
-    packed_ref[kept:] = jnp.dot(
+    packed_ref[kept + 24 :] = jnp.zeros((packed_ref.shape[0] - kept - 24, LANES), F32)
+    packed_ref[kept : kept + 24] = jnp.dot(
         cols_ref[...], gather, preferred_element_type=F32, precision=lax.Precision.HIGHEST
     )
 
@@ -389,18 +394,21 @@
     each_chunk(gq_ref.shape[1], body)
 
 
+def sum_kernel(all_ref, out_ref):
+    count = all_ref.shape[0]
+    total = lax.fori_loop(1, count, lambda i, acc: acc + all_ref[i], all_ref[0])
+    out_ref[...] = jnp.broadcast_to(total[None], out_ref.shape)
+
+
 def unpack_kernel(all_ref, short_ref, long_ref, skip_ref, gain_ref):
     groups = long_ref.shape[0]
     rows = groups // PER
-    total = lax.fori_loop(
-        1, all_ref.shape[0], lambda i, acc: acc + all_ref[i], all_ref[0]
-    )
-    long_ref[...] = total[:groups]
-    skip_ref[...] = total[groups : groups + rows]
-    gain_ref[...] = total[groups + rows : groups + 2 * rows]
+    long_ref[...] = all_ref[:groups]
+    skip_ref[...] = all_ref[groups : groups + rows]
+    gain_ref[...] = all_ref[groups + rows : groups + 2 * rows]
     for i in range(3):
         at = groups + 2 * rows + i * 8
-        short_ref[i] = total[at : at + KS, :groups]
+        short_ref[i] = all_ref[at : at + KS, :groups]
 
 
 def shards(
@@ -410,6 +418,9 @@
     groups = channels // GS
     wide = channels * lax.axis_size("tp")
     rows = groups // PER
+    count = lax.axis_size("ctx")
+    piece = -(-(groups + 2 * rows + 24) // (8 * count)) * 8
+    packed_rows = piece * count
 
     def arr(shape, dtype):
         return jax.ShapeDtypeStruct(shape, dtype)
@@ -446,6 +457,7 @@
             pltpu.VMEM((PACK, channels), BF16), pltpu.VMEM((length, channels), BF16),
             pltpu.VMEM((length, channels), BF16), pltpu.SemaphoreType.DMA((5,)),
         ],
+        grant=60,
         hbm=True,
     )
     came = shifted(sent, "ctx", 1)
@@ -497,7 +509,7 @@
         "gate", gate_kernel,
         [
             full_bf, full_bf, arr((4 * RIM, channels), BF16),
-            arr((groups + 2 * rows + 24, LANES), F32),
+            arr((packed_rows, LANES), F32),
         ],
         [
             lengths, part, after, bwd, k_short, v_short, grad_qs, k_input, v_input, came,
@@ -510,7 +522,9 @@
         "mains", functools.partial(mains_kernel, wide), [full_bf] * 4,
         [lengths, taps, grad_qs, grad_ks, grad_vs, tails, summed, gain2, sums], flops=10**9, moved=5 * 10**6,
     )
-    packed = lax.all_gather(packed, "ctx")
+    parts = lax.all_to_all(packed.reshape(count, piece, LANES), "ctx", 0, 0)
+    (spread,) = call("sum_rows", sum_kernel, [arr((count, piece, LANES), F32)], [parts])
+    packed = lax.all_to_all(spread, "ctx", 0, 0).reshape(packed_rows, LANES)
     grad_short, grad_long, grad_skip, grad_gain = call(
         "unpack", unpack_kernel,
         [

time: 85.1 us -> 68.8 us (0.81)
  blocking collectives: 40.7 us -> 5.99 us
  starting transfers between devices: 11.1 us -> 21.4 us
  waiting for transfers between devices: 0.01 us -> 8.61 us
  local copies, waits for them, and re-layouts: 5.66 us -> 2.19 us
  Pallas kernels: 26.3 us -> 29.1 us
    all_gather x1 -> x0, blocking collectives: 34.7 us -> none  [shards(): packed = lax.all_gather(packed, 'ctx')]
    all_to_all x0 -> x2, starting transfers between devices: none -> 10.2 us  [the longest x1 6.86 us: shards(): parts = lax.all_to_all(packed.reshape(count, piece, LANES), 'ctx', 0, 0)]
    all_to_all x0 -> x2, waiting for transfers between devices: none -> 8.6 us  [the longest x1 5.62 us: shards(): parts = lax.all_to_all(packed.reshape(count, piece, LANES), 'ctx', 0, 0)]
    unnamed x34 -> x32, local copies, waits for them, and re-layouts: 5.66 us -> 2.19 us
    pallas_call x10 -> x11, Pallas kernels: 26.3 us -> 29.1 us  [call(): pl.pallas_call(kernel, out_shape=outs, in_specs=[far_off] * len(ins) if h...]
  transfers between devices with their start and end apart: 4 -> 6, of which waited for: 0 -> 2; matrix products, arithmetic and copies ran while one was open for 0% -> 0% of each run, Pallas kernels for 17% -> 27%
where the time goes in v3:
time: 68.8 us; the launch traced here: 68.2 us
  Pallas kernels  29.1 us (42%)
  starting transfers between devices  21.4 us (31%)
  waiting for transfers between devices  8.61 us (13%)
  blocking collectives  5.99 us (9%)
  local copies, waits for them, and re-layouts  2.19 us (3%)
  between operations  0.99 us (1%)
    pallas_call x11, Pallas kernels, call(): pl.pallas_call(kernel, out_shape=outs, in_specs=[far_off] * len(ins) if h...  29.1 us
    ppermute x4, starting transfers between devices, shifted(): return lax.ppermute(x, axis, pairs)  11.2 us
    all_to_all x1, starting transfers between devices, shards(): parts = lax.all_to_all(packed.reshape(count, piece, LANES), 'ctx', 0, 0)  6.86 us
    psum x1, blocking collectives, shards(): sums = lax.psum(sums, 'tp')  5.99 us
    all_to_all x1, waiting for transfers between devices, shards(): parts = lax.all_to_all(packed.reshape(count, piece, LANES), 'ctx', 0, 0)  5.62 us
    all_to_all x1, starting transfers between devices, shards(): packed = lax.all_to_all(spread, 'ctx', 0, 0).reshape(packed_rows, LANES)  3.35 us
    all_to_all x1, waiting for transfers between devices, shards(): packed = lax.all_to_all(spread, 'ctx', 0, 0).reshape(packed_rows, LANES)  2.98 us
    unnamed x32, local copies, waits for them, and re-layouts  2.19 us
  transfers between devices with their start and end apart: 6, of which 2 were waited for; matrix products, arithmetic and copies ran while one was open for 0% of the time, Pallas kernels for 27%

profile of v3, /device:TPU:0, one launch (start us, length us, event | category | flops | bytes accessed | tf_op | source)
XLA Modules:
  0.0 68.2 jit_solution(4290465305743793722)
XLA Ops:
  0.7 3.2 %first.1 = (f32[24,1024]{1,0:T(8,128)}, bf16[160,1024]{1,0:T(8,128)(2,1)}, bf16[16,1024]{1,0:T(8,128)(2,1)}) custom-call(s32[8]{0:T(128)} %len_ref.9, bf16[3,7,64]{2,1,0:T(8,128)(2,1)} %bitcast.15, bf16[128,1024]{1,0:T(8,128)(2,1)} %q_ref.5, bf16[128,1024]{1,0:T(8,128)(2,1)} %k_ref.5, bf16[128,1024]{1,0:T(8,128)(2,1)} %v_ref.5), custom_call_target="tpu_custom_call" | custom-call | flops 100000000 | bytes 1000000 | tf_op jit(solution)/shard_map/first/pallas_call | solution.py:436
  3.9 0.0 copy-start.6
  3.9 5.0 %collective-permute-start = (bf16[160,1024]{1,0:T(8,128)(2,1)}, bf16[160,1024]{1,0:T(8,128)(2,1)S(1)}, u32[]{:S(2)}, u32[]{:S(2)}) collective-permute-start(bf16[160,1024]{1,0:T(8,128)(2,1)} %get-tuple-element.46.sent_ref), channel_id=1, source_target_pairs={{0,4},{4,8},{8,12},{12,16},{16,20},{20,24},{24,28},{1,5},{5,9},{9,... | collective-permute-start | bytes 983048 | tf_op jit(solution)/shard_map/ppermute | solution.py:25
  9.0 3.5 %collective-permute-start.1 = (bf16[16,1024]{1,0:T(8,128)(2,1)}, bf16[16,1024]{1,0:T(8,128)(2,1)S(1)}, u32[]{:S(2)}, u32[]{:S(2)}) collective-permute-start(bf16[16,1024]{1,0:T(8,128)(2,1)} %get-tuple-element.45), channel_id=1, source_target_pairs={{0,8},{4,12},{8,16},{12,20},{16,24},{20,28},{1,9},{5,13},{9,17},{1... | collective-permute-start | bytes 98312 | tf_op jit(solution)/shard_map/ppermute | solution.py:25
  12.4 0.0 copy-start.14
  12.4 0.7 %copy-done.14 = bf16[64,128]{1,0:T(8,128)(2,1)S(1)} copy-done((bf16[64,128]{1,0:T(8,128)(2,1)S(1)}, bf16[64,128]{1,0:T(8,128)(2,1)}, u32[]{:S(2)}) %copy-start.14) | copy-done | bytes 16408
  13.1 1.8 %circulants.2.fwd_ref = bf16[128,8192]{1,0:T(8,128)(2,1)S(1)} custom-call(bf16[64,128]{1,0:T(8,128)(2,1)S(1)} %copy-done.14), custom_call_target="tpu_custom_call" | custom-call | flops 1000000000 | bytes 4000000 | tf_op jit(solution)/shard_map/circulants/pallas_call | solution.py:436
  15.0 0.0 copy-start
  15.0 0.0 copy-start.1
  15.0 0.0 copy-start.2
  15.0 0.0 copy-start.5
  15.1 2.9 %current.1 = (f32[128,1024]{1,0:T(8,128)S(1)}, f32[128,1024]{1,0:T(8,128)S(1)}, bf16[128,1024]{1,0:T(8,128)(2,1)S(1)}) custom-call(s32[8]{0:T(128)S(1)} %copy-done.8, bf16[128,1024]{1,0:T(8,128)(2,1)S(1)} %copy-done.3, f32[24,1024]{1,0:T(8,128)S(1)} %copy-done.6, bf16[160,1024]{1,0:T(8,128)(2,1)S(1)} %copy-done.4, bf16[128,8192]{1,0:T(8,128)(2,1)S(1)} %circulants.2.fwd_ref, ...), custom_call_target="tpu_custom_call" | custom-call | flops 1000000000 | bytes 5000000 | tf_op jit(solution)/shard_map/current/pallas_call | solution.py:436
  18.1 0.0 copy-start.15
  18.1 2.2 %summed.1 = (f32[128,1024]{1,0:T(8,128)S(1)}, bf16[128,1024]{1,0:T(8,128)(2,1)S(1)}, bf16[128,1024]{1,0:T(8,128)(2,1)S(1)}, f32[128,1024]{1,0:T(8,128)S(1)}, f32...) custom-call(s32[8]{0:T(128)S(1)} %copy-done.8, bf16[160,1024]{1,0:T(8,128)(2,1)S(1)} %collective-permute-done.came_ref, ...), custom_call_target="tpu_custom_call" | custom-call | flops 1000000000 | bytes 5000000 | tf_op jit(solution)/shard_map/summed/pallas_call | solution.py:436
  20.3 0.7 %copy-done.10 = bf16[128,1024]{1,0:T(8,128)(2,1)} copy-done((bf16[128,1024]{1,0:T(8,128)(2,1)}, bf16[128,1024]{1,0:T(8,128)(2,1)S(1)}, u32[]{:S(2)}) %copy-start.10) | copy-done | bytes 262168
  21.0 0.7 %copy-done.12 = bf16[128,1024]{1,0:T(8,128)(2,1)} copy-done((bf16[128,1024]{1,0:T(8,128)(2,1)}, bf16[128,1024]{1,0:T(8,128)(2,1)S(1)}, u32[]{:S(2)}) %copy-start.12) | copy-done | bytes 262168
  21.7 6.0 %psum.7.sums_ref = f32[2,128]{1,0:T(2,128)S(1)} all-reduce(f32[2,128]{1,0:T(2,128)S(1)} %get-tuple-element.54), channel_id=1, replica_groups=mesh['ctx'=8,'tp'=4] {'tp'}, use_global_device_ids=true, to_apply=%region_0.0 | all-reduce | flops 256 | bytes 2048 | tf_op jit(solution)/shard_map/psum | solution.py:488
  27.7 0.5 grads.1
  28.2 0.0 copy-start.11
  28.2 0.0 copy-start.13
  28.2 1.4 %collective-permute-start.2 = (bf16[128,1024]{1,0:T(8,128)(2,1)S(1)}, bf16[128,1024]{1,0:T(8,128)(2,1)S(1)}, u32[]{:S(2)}, u32[]{:S(2)}) collective-permute-start(bf16[128,1024]{1,0:T(8,128)(2,1)S(1)} %get-tuple-element.57.gm_ref), channel_id=1, source_target_pairs={{4,0},{8,4},{12,8},{16,12},{20,16},{24,20},{28,24},{5,1},{9,5},{13... | collective-permute-start | bytes 786440 | tf_op jit(solution)/shard_map/ppermute | solution.py:25
  29.7 1.7 %circulants.3.bwd_ref = bf16[128,8192]{1,0:T(8,128)(2,1)S(1)} custom-call(bf16[64,128]{1,0:T(8,128)(2,1)S(1)} %copy-done.15), custom_call_target="tpu_custom_call" | custom-call | flops 1000000000 | bytes 4000000 | tf_op jit(solution)/shard_map/circulants/pallas_call | solution.py:436
  31.4 7.6 %beside.1 = (f32[80,128]{1,0:T(8,128)S(1)}, f32[128,1024]{1,0:T(8,128)S(1)}, f32[128,1024]{1,0:T(8,128)S(1)}, f32[128,1024]{1,0:T(8,128)S(1)}, f32[8,1024]{1,0:T(8,128)S(1)}) custom-call(s32[8]{0:T(128)S(1)} %copy-done.8, f32[128,1024]{1,0:T(8,128)S(1)} %get-tuple-element.51.summed_ref, bf16[128,1024]{1,0:T(8,128)(2,1)S(1)} %copy-done.2, ...), custom_call_target="tpu_custom_call" | custom-call | flops 4000000000 | bytes 5000000 | tf_op jit(solution)/shard_map/beside/pallas_call | solution.py:436
  38.9 4.1 %gate.1 = (bf16[128,1024]{1,0:T(8,128)(2,1)S(1)}, bf16[128,1024]{1,0:T(8,128)(2,1)S(1)}, bf16[32,1024]{1,0:T(8,128)(2,1)S(1)}, f32[128,128]{1,0:T(8,128)}) custom-call(s32[8]{0:T(128)S(1)} %copy-done.8, f32[128,1024]{1,0:T(8,128)S(1)} %get-tuple-element.61.part_ref, bf16[128,1024]{1,0:T(8,128)(2,1)S(1)} %collective-permute-done.2.after_ref, ...), custom_call_target="tpu_custom_call" | custom-call | flops 1000000000 | bytes 5000000 | tf_op jit(solution)/shard_map/gate/pallas_call | solution.py:436
  43.0 6.9 %all-to-all-start = ((f32[8,16,128]{2,1,0:T(8,128)}), f32[8,16,128]{2,1,0:T(8,128)S(1)}, u32[]{:S(2)}, u32[]{:S(2)}) async-start(f32[8,16,128]{2,1,0:T(8,128)} %bitcast.3), calls=%async_computation | async-start | bytes 131072 | tf_op jit(solution)/shard_map/all_to_all | solution.py:525
  49.9 1.3 %collective-permute-start.3 = (bf16[32,1024]{1,0:T(8,128)(2,1)S(1)}, bf16[32,1024]{1,0:T(8,128)(2,1)S(1)}, u32[]{:S(2)}, u32[]{:S(2)}) collective-permute-start(bf16[32,1024]{1,0:T(8,128)(2,1)S(1)} %get-tuple-element.68), channel_id=1, source_target_pairs={{4,0},{8,4},{12,8},{16,12},{20,16},{24,20},{28,24},{5,1},{9,5},{13... | collective-permute-start | bytes 196616 | tf_op jit(solution)/shard_map/ppermute | solution.py:25
  51.2 5.6 %all-to-all-done.all_ref = f32[8,16,128]{2,1,0:T(8,128)S(1)} async-done(((f32[8,16,128]{2,1,0:T(8,128)}), f32[8,16,128]{2,1,0:T(8,128)S(1)}, u32[]{:S(2)}, u32[]{:S(2)}) %all-to-all-start) | async-done | bytes 65568 | tf_op jit(solution)/shard_map/all_to_all | solution.py:525
  56.8 0.6 sum_rows.1
  57.4 3.3 %all-to-all-start.1 = ((f32[8,16,128]{2,1,0:T(8,128)}), f32[8,16,128]{2,1,0:T(8,128)S(1)}, u32[]{:S(2)}, u32[]{:S(2)}) async-start(f32[8,16,128]{2,1,0:T(8,128)} %sum_rows.1), calls=%async_computation.1 | async-start | bytes 131072 | tf_op jit(solution)/shard_map/all_to_all | solution.py:527
  60.8 3.8 %mains.1 = (bf16[128,1024]{1,0:T(8,128)(2,1)}, bf16[128,1024]{1,0:T(8,128)(2,1)}, bf16[128,1024]{1,0:T(8,128)(2,1)}, bf16[128,1024]{1,0:T(8,128)(2,1)}) custom-call(s32[8]{0:T(128)S(1)} %copy-done.8, f32[24,1024]{1,0:T(8,128)S(1)} %copy-done.6, bf16[128,1024]{1,0:T(8,128)(2,1)S(1)} %get-tuple-element.55.gq_ref, ...), custom_call_target="tpu_custom_call" | custom-call | flops 1000000000 | bytes 5000000 | tf_op jit(solution)/shard_map/mains/pallas_call | solution.py:436
  64.6 3.0 %all-to-all-done.1 = f32[8,16,128]{2,1,0:T(8,128)S(1)} async-done(((f32[8,16,128]{2,1,0:T(8,128)}), f32[8,16,128]{2,1,0:T(8,128)S(1)}, u32[]{:S(2)}, u32[]{:S(2)}) %all-to-all-start.1) | async-done | bytes 65568 | tf_op jit(solution)/shard_map/all_to_all | solution.py:527
  67.6 0.6 unpack.1
  (24 shorter events, 0.1 us)
Async XLA Ops:
  0.6 14.4 %copy-start.3 = (bf16[128,1024]{1,0:T(8,128)(2,1)S(1)}, bf16[128,1024]{1,0:T(8,128)(2,1)}, u32[]{:S(2)}) copy-start(bf16[128,1024]{1,0:T(8,128)(2,1)} %q_ref.5) | copy-start | bytes 786436
  0.6 14.4 %copy-start.8 = (s32[8]{0:T(128)S(1)}, s32[8]{0:T(128)}, u32[]{:S(2)}) copy-start(s32[8]{0:T(128)} %len_ref.9) | copy-start | bytes 100
  0.7 14.4 %copy-start.9 = (f32[1024]{0:T(1024)S(1)}, f32[1024]{0:T(1024)}, u32[]{:S(2)}) copy-start(f32[1024]{0:T(1024)} %param.17) | copy-start | bytes 12292
  3.9 11.1 %copy-start.4 = (bf16[160,1024]{1,0:T(8,128)(2,1)S(1)}, bf16[160,1024]{1,0:T(8,128)(2,1)}, u32[]{:S(2)}) copy-start(bf16[160,1024]{1,0:T(8,128)(2,1)} %get-tuple-element.46.sent_ref) | copy-start | bytes 983044
  3.9 11.1 %copy-start.6 = (f32[24,1024]{1,0:T(8,128)S(1)}, f32[24,1024]{1,0:T(8,128)}, u32[]{:S(2)}) copy-start(f32[24,1024]{1,0:T(8,128)} %get-tuple-element.43.taps_ref) | copy-start | bytes 294916
  3.9 14.1 %collective-permute-start = (bf16[160,1024]{1,0:T(8,128)(2,1)}, bf16[160,1024]{1,0:T(8,128)(2,1)S(1)}, u32[]{:S(2)}, u32[]{:S(2)}) collective-permute-start(bf16[160,1024]{1,0:T(8,128)(2,1)} %get-tuple-element.46.sent_ref), channel_id=1, source_target_pairs={{0,4},{4,8},{8,12},{12,16},{16,20},{20,24},{24,28},{1,5},{5,9},{9,... | collective-permute-start | bytes 983048 | tf_op jit(solution)/shard_map/ppermute | solution.py:25
  9.0 9.1 %collective-permute-start.1 = (bf16[16,1024]{1,0:T(8,128)(2,1)}, bf16[16,1024]{1,0:T(8,128)(2,1)S(1)}, u32[]{:S(2)}, u32[]{:S(2)}) collective-permute-start(bf16[16,1024]{1,0:T(8,128)(2,1)} %get-tuple-element.45), channel_id=1, source_target_pairs={{0,8},{4,12},{8,16},{12,20},{16,24},{20,28},{1,9},{5,13},{9,17},{1... | collective-permute-start | bytes 98312 | tf_op jit(solution)/shard_map/ppermute | solution.py:25
  12.4 0.7 %copy-start.14 = (bf16[64,128]{1,0:T(8,128)(2,1)S(1)}, bf16[64,128]{1,0:T(8,128)(2,1)}, u32[]{:S(2)}) copy-start(bf16[64,128]{1,0:T(8,128)(2,1)} %long_ref.1) | copy-start | bytes 49156
  15.0 3.1 %copy-start = (bf16[128,1024]{1,0:T(8,128)(2,1)S(1)}, bf16[128,1024]{1,0:T(8,128)(2,1)}, u32[]{:S(2)}) copy-start(bf16[128,1024]{1,0:T(8,128)(2,1)} %k_ref.5) | copy-start | bytes 786436
  15.0 3.1 %copy-start.1 = (bf16[128,1024]{1,0:T(8,128)(2,1)S(1)}, bf16[128,1024]{1,0:T(8,128)(2,1)}, u32[]{:S(2)}) copy-start(bf16[128,1024]{1,0:T(8,128)(2,1)} %v_ref.5) | copy-start | bytes 786436
  15.0 3.1 %copy-start.2 = (bf16[128,1024]{1,0:T(8,128)(2,1)S(1)}, bf16[128,1024]{1,0:T(8,128)(2,1)}, u32[]{:S(2)}) copy-start(bf16[128,1024]{1,0:T(8,128)(2,1)} %cot_ref.5) | copy-start | bytes 786436
  15.0 3.1 %copy-start.5 = (bf16[128,1024]{1,0:T(8,128)(2,1)S(1)}, bf16[128,1024]{1,0:T(8,128)(2,1)}, u32[]{:S(2)}) copy-start(bf16[128,1024]{1,0:T(8,128)(2,1)} %resid_ref.1) | copy-start | bytes 786436
  15.0 3.1 %copy-start.7 = (f32[1024]{0:T(1024)S(1)}, f32[1024]{0:T(1024)}, u32[]{:S(2)}) copy-start(f32[1024]{0:T(1024)} %param.18) | copy-start | bytes 12292
  18.1 11.6 %copy-start.15 = (bf16[64,128]{1,0:T(8,128)(2,1)S(1)}, bf16[64,128]{1,0:T(8,128)(2,1)}, u32[]{:S(2)}) copy-start(bf16[64,128]{1,0:T(8,128)(2,1)} %long_ref.1) | copy-start | bytes 49156
  20.3 0.7 %copy-start.10 = (bf16[128,1024]{1,0:T(8,128)(2,1)}, bf16[128,1024]{1,0:T(8,128)(2,1)S(1)}, u32[]{:S(2)}) copy-start(bf16[128,1024]{1,0:T(8,128)(2,1)S(1)} %get-tuple-element.58.gated_ref) | copy-start | bytes 786436
  21.0 0.7 %copy-start.12 = (bf16[128,1024]{1,0:T(8,128)(2,1)}, bf16[128,1024]{1,0:T(8,128)(2,1)S(1)}, u32[]{:S(2)}) copy-start(bf16[128,1024]{1,0:T(8,128)(2,1)S(1)} %get-tuple-element.59.before_ref) | copy-start | bytes 786436
  28.2 3.1 %copy-start.11 = (bf16[128,1024]{1,0:T(8,128)(2,1)S(1)}, bf16[128,1024]{1,0:T(8,128)(2,1)}, u32[]{:S(2)}) copy-start(bf16[128,1024]{1,0:T(8,128)(2,1)} %copy-done.10) | copy-start | bytes 786436
  28.2 3.1 %copy-start.13 = (bf16[128,1024]{1,0:T(8,128)(2,1)S(1)}, bf16[128,1024]{1,0:T(8,128)(2,1)}, u32[]{:S(2)}) copy-start(bf16[128,1024]{1,0:T(8,128)(2,1)} %copy-done.12) | copy-start | bytes 786436
  28.2 10.7 %collective-permute-start.2 = (bf16[128,1024]{1,0:T(8,128)(2,1)S(1)}, bf16[128,1024]{1,0:T(8,128)(2,1)S(1)}, u32[]{:S(2)}, u32[]{:S(2)}) collective-permute-start(bf16[128,1024]{1,0:T(8,128)(2,1)S(1)} %get-tuple-element.57.gm_ref), channel_id=1, source_target_pairs={{4,0},{8,4},{12,8},{16,12},{20,16},{24,20},{28,24},{5,1},{9,5},{13... | collective-permute-start | bytes 786440 | tf_op jit(solution)/shard_map/ppermute | solution.py:25
  43.0 13.8 %all-to-all-start = ((f32[8,16,128]{2,1,0:T(8,128)}), f32[8,16,128]{2,1,0:T(8,128)S(1)}, u32[]{:S(2)}, u32[]{:S(2)}) async-start(f32[8,16,128]{2,1,0:T(8,128)} %bitcast.3), calls=%async_computation | async-start | bytes 131072 | tf_op jit(solution)/shard_map/all_to_all | solution.py:525
  49.9 10.9 %collective-permute-start.3 = (bf16[32,1024]{1,0:T(8,128)(2,1)S(1)}, bf16[32,1024]{1,0:T(8,128)(2,1)S(1)}, u32[]{:S(2)}, u32[]{:S(2)}) collective-permute-start(bf16[32,1024]{1,0:T(8,128)(2,1)S(1)} %get-tuple-element.68), channel_id=1, source_target_pairs={{4,0},{8,4},{12,8},{16,12},{20,16},{24,20},{28,24},{5,1},{9,5},{13... | collective-permute-start | bytes 196616 | tf_op jit(solution)/shard_map/ppermute | solution.py:25
  57.4 10.2 %all-to-all-start.1 = ((f32[8,16,128]{2,1,0:T(8,128)}), f32[8,16,128]{2,1,0:T(8,128)S(1)}, u32[]{:S(2)}, u32[]{:S(2)}) async-start(f32[8,16,128]{2,1,0:T(8,128)} %sum_rows.1), calls=%async_computation.1 | async-start | bytes 131072 | tf_op jit(solution)/shard_map/all_to_all | solution.py:527

commit v4 on v3

--- a/solution.py
+++ b/solution.py
@@ -23,6 +23,10 @@
     count = lax.axis_size(axis)
     pairs = [(i, i + by) for i in range(count) if 0 <= i + by < count]
     return lax.ppermute(x, axis, pairs)
+
+
+def swapped(x, axis, step):
+    return lax.ppermute(x, axis, [(i, i ^ step) for i in range(lax.axis_size(axis))])
 
 
 def iota(shape, dim):
@@ -261,6 +265,19 @@
     return by_row(lax.rsqrt(sums_ref[0:1] / total + EPS))
 
 
+def gates_kernel(len_ref, k_ref, v_ref, came_ref, taps_ref, ks_ref, vs_ref):
+    pos = positions(len_ref, first_row() + iota((K, LANES), 0))
+
+    def body(q):
+        ls = lanes_of(q)
+        k_ext = join(rim_of(came_ref, K_LAST, ls), k_ref[:, ls].astype(F32))
+        v_ext = join(rim_of(came_ref, V_LAST, ls), v_ref[:, ls].astype(F32))
+        ks_ref[:, ls] = causal(k_ext, tap_rows(taps_ref, 1, ls), pos)
+        vs_ref[:, ls] = causal(v_ext, tap_rows(taps_ref, 2, ls), pos)
+
+    each_chunk(k_ref.shape[1], body)
+
+
 def grads_kernel(total, summed_ref, mixed_ref, qs_ref, cot_ref, gain_ref, sums_ref, gm_ref, gq_ref):
     inverse = inverse_of(sums_ref, total)
     scale = inverse * inverse * by_row(sums_ref[1:2] / total)
@@ -277,8 +294,7 @@
 
 def beside_kernel(
     total, len_ref, summed_ref, cot_ref, sums_ref, gm_ref, gq_ref, gated_ref, before_ref,
-    bwd_ref, skip_ref, q_ref, k_ref, v_ref, came_ref, taps_ref,
-    stats_ref, part_ref, ks_ref, vs_ref, cols_ref,
+    bwd_ref, skip_ref, q_ref, came_ref, stats_ref, part_ref, cols_ref,
 ):
     groups = bwd_ref.shape[1] // K
     inverse = inverse_of(sums_ref, total)
@@ -322,11 +338,7 @@
             square = pltpu.roll(square, 1, 1, stride=1, stride_axis=0)
             lines.append(jnp.sum(square, axis=0, keepdims=True))
         stats_ref[pl.ds(pl.multiple_of(q * PER, PER), PER), :] = join(*lines)
-        k_ext = join(rim_of(came_ref, K_LAST, ls), k_ref[:, ls].astype(F32))
-        v_ext = join(rim_of(came_ref, V_LAST, ls), v_ref[:, ls].astype(F32))
         q_ext = join(rim_of(came_ref, Q_LAST, ls), q_ref[:, ls].astype(F32))
-        ks_ref[:, ls] = causal(k_ext, tap_rows(taps_ref, 1, ls), pos_row)
-        vs_ref[:, ls] = causal(v_ext, tap_rows(taps_ref, 2, ls), pos_row)
         cols_ref[:, ls] = tap_lines(gq_ref[:, ls].astype(F32), q_ext, pos_row)
 
     each_chunk(cot_ref.shape[1], body, 1)
@@ -366,8 +378,7 @@
     gather = jnp.where(
         iota((channels, LANES), 0) // GS == iota((channels, LANES), 1), 1.0, 0.0
     )
-    packed_ref[kept + 24 :] = jnp.zeros((packed_ref.shape[0] - kept - 24, LANES), F32)
-    packed_ref[kept : kept + 24] = jnp.dot(
+    packed_ref[kept:] = jnp.dot(
         cols_ref[...], gather, preferred_element_type=F32, precision=lax.Precision.HIGHEST
     )
 
@@ -394,21 +405,16 @@
     each_chunk(gq_ref.shape[1], body)
 
 
-def sum_kernel(all_ref, out_ref):
-    count = all_ref.shape[0]
-    total = lax.fori_loop(1, count, lambda i, acc: acc + all_ref[i], all_ref[0])
-    out_ref[...] = jnp.broadcast_to(total[None], out_ref.shape)
-
-
-def unpack_kernel(all_ref, short_ref, long_ref, skip_ref, gain_ref):
+def unpack_kernel(one_ref, two_ref, short_ref, long_ref, skip_ref, gain_ref):
     groups = long_ref.shape[0]
     rows = groups // PER
-    long_ref[...] = all_ref[:groups]
-    skip_ref[...] = all_ref[groups : groups + rows]
-    gain_ref[...] = all_ref[groups + rows : groups + 2 * rows]
+    total = one_ref[...] + two_ref[...]
+    long_ref[...] = total[:groups]
+    skip_ref[...] = total[groups : groups + rows]
+    gain_ref[...] = total[groups + rows : groups + 2 * rows]
     for i in range(3):
         at = groups + 2 * rows + i * 8
-        short_ref[i] = all_ref[at : at + KS, :groups]
+        short_ref[i] = total[at : at + KS, :groups]
 
 
 def shards(
@@ -418,9 +424,7 @@
     groups = channels // GS
     wide = channels * lax.axis_size("tp")
     rows = groups // PER
-    count = lax.axis_size("ctx")
-    piece = -(-(groups + 2 * rows + 24) // (8 * count)) * 8
-    packed_rows = piece * count
+    packed_rows = groups + 2 * rows + 24
 
     def arr(shape, dtype):
         return jax.ShapeDtypeStruct(shape, dtype)
@@ -485,23 +489,31 @@
         ],
         [pltpu.VMEM((2, K, LANES), F32)], flops=10**9, moved=5 * 10**6,
     )
-    sums = lax.psum(sums, "tp")
+    own_sums = sums
+    step = 1
+    while step < lax.axis_size("tp"):
+        sums = sums + swapped(sums, "tp", step)
+        step *= 2
+    filt, came, _ = lax.optimization_barrier((long_filter, came, own_sums))
+    bwd = circulants(filt, False)
+    k_short, v_short = call(
+        "gates", gates_kernel, [full_f] * 2, [lengths, k_input, v_input, came, taps],
+        flops=10**8, moved=2 * 10**6,
+    )
+    sums, bwd, k_short, v_short = lax.optimization_barrier((sums, bwd, k_short, v_short))
     grad_mixed, grad_qs = call(
         "grads", functools.partial(grads_kernel, wide), [full_bf, full_bf],
         [summed, mixed, q_short, cotangent, gain2, sums],
     )
     after = shifted(grad_mixed, "ctx", -1)
-    filt, grad_mixed = lax.optimization_barrier((long_filter, grad_mixed))
-    bwd = circulants(filt, False)
-    stats, part, k_short, v_short, qcols = call(
+    stats, part, qcols = call(
         "beside", functools.partial(beside_kernel, wide),
         [
-            arr((groups + 2 * rows, LANES), F32), full_f, full_f, full_f,
-            arr((8, channels), F32),
+            arr((groups + 2 * rows, LANES), F32), full_f, arr((8, channels), F32),
         ],
         [
             lengths, summed, cotangent, sums, grad_mixed, grad_qs, gated, before, bwd,
-            skip2, q_input, k_input, v_input, came, taps,
+            skip2, q_input, came,
         ],
         flops=4 * 10**9, moved=5 * 10**6,
     )
@@ -522,16 +534,22 @@
         "mains", functools.partial(mains_kernel, wide), [full_bf] * 4,
         [lengths, taps, grad_qs, grad_ks, grad_vs, tails, summed, gain2, sums], flops=10**9, moved=5 * 10**6,
     )
-    parts = lax.all_to_all(packed.reshape(count, piece, LANES), "ctx", 0, 0)
-    (spread,) = call("sum_rows", sum_kernel, [arr((count, piece, LANES), F32)], [parts])
-    packed = lax.all_to_all(spread, "ctx", 0, 0).reshape(packed_rows, LANES)
+    outs = (grad_q, grad_k, grad_v, normed)
+    count = lax.axis_size("ctx")
+    step = 1
+    while 2 * step < count:
+        packed = packed + swapped(packed, "ctx", step)
+        step *= 2
+    packed, *outs = lax.optimization_barrier((packed, *outs))
+    grad_q, grad_k, grad_v, normed = outs
+    other = swapped(packed, "ctx", step)
     grad_short, grad_long, grad_skip, grad_gain = call(
         "unpack", unpack_kernel,
         [
             arr((3, KS, groups), F32), arr((groups, K), F32),
             arr((rows, LANES), F32), arr((rows, LANES), F32),
         ],
-        [packed],
+        [packed, other],
     )
     return (
         normed, grad_q, grad_k, grad_v, jnp.transpose(grad_short, (0, 2, 1)), grad_long,

time: 68.8 us -> 60.2 us (0.88)
  blocking collectives: 5.99 us -> 0 us
  local copies, waits for them, and re-layouts: 2.19 us -> 0.77 us
  Pallas kernels: 29.1 us -> 28.2 us
    all_to_all x2 -> x0, starting transfers between devices: 10.2 us -> none  [the longest x1 6.86 us: shards(): parts = lax.all_to_all(packed.reshape(count, piece, LANES), 'ctx', 0, 0)]
    ppermute x0 -> x5, starting transfers between devices: none -> 10 us  [swapped(): lax.ppermute(x, axis, [(i, i ^ step) for i in range(lax.axis_size(axis))])]
    all_to_all x2 -> x0, waiting for transfers between devices: 8.6 us -> none  [the longest x1 5.62 us: shards(): parts = lax.all_to_all(packed.reshape(count, piece, LANES), 'ctx', 0, 0)]
    psum x1 -> x0, blocking collectives: 5.99 us -> none  [shards(): sums = lax.psum(sums, 'tp')]
    ppermute x0 -> x5, waiting for transfers between devices: none -> 5.85 us  [swapped(): lax.ppermute(x, axis, [(i, i ^ step) for i in range(lax.axis_size(axis))])]
    ppermute x4, waiting for transfers between devices: 0.01 us -> 2.98 us  [shifted(): return lax.ppermute(x, axis, pairs)]
    unnamed x32 -> x24, local copies, waits for them, and re-layouts: 2.19 us -> 0.77 us
    pallas_call x11, Pallas kernels: 29.1 us -> 28.2 us  [call(): pl.pallas_call(kernel, out_shape=outs, in_specs=[far_off] * len(ins) if h...]
  transfers between devices with their start and end apart: 6 -> 9, of which waited for: 2 -> 4; matrix products, arithmetic and copies ran while one was open for 0% -> 0% of each run, Pallas kernels for 27% -> 30%
where the time goes in v4:
time: 60.2 us; the launch traced here: 59.9 us
  Pallas kernels  28.2 us (47%)
  starting transfers between devices  21.1 us (35%)
  waiting for transfers between devices  8.83 us (15%)
  between operations  0.96 us (2%)
  local copies, waits for them, and re-layouts  0.77 us (1%)
    pallas_call x11, Pallas kernels, call(): pl.pallas_call(kernel, out_shape=outs, in_specs=[far_off] * len(ins) if h...  28.2 us
    ppermute x4, starting transfers between devices, shifted(): return lax.ppermute(x, axis, pairs)  11.1 us
    ppermute x5, starting transfers between devices, swapped(): lax.ppermute(x, axis, [(i, i ^ step) for i in range(lax.axis_size(axis))])  10 us
    ppermute x5, waiting for transfers between devices, swapped(): lax.ppermute(x, axis, [(i, i ^ step) for i in range(lax.axis_size(axis))])  5.85 us
    ppermute x4, waiting for transfers between devices, shifted(): return lax.ppermute(x, axis, pairs)  2.98 us
  transfers between devices with their start and end apart: 9, of which 4 were waited for; matrix products, arithmetic and copies ran while one was open for 0% of the time, Pallas kernels for 30%

profile of v4, /device:TPU:0, one launch (start us, length us, event | category | flops | bytes accessed | tf_op | source)
XLA Modules:
  0.0 59.9 jit_solution(15751159058352140620)
XLA Ops:
  0.7 3.2 %first.1 = (f32[24,1024]{1,0:T(8,128)}, bf16[160,1024]{1,0:T(8,128)(2,1)}, bf16[16,1024]{1,0:T(8,128)(2,1)}) custom-call(s32[8]{0:T(128)} %len_ref.11, bf16[3,7,64]{2,1,0:T(8,128)(2,1)} %bitcast.12, bf16[128,1024]{1,0:T(8,128)(2,1)} %q_ref.5, bf16[128,1024]{1,0:T(8,128)(2,1)} %k_ref.5, bf16[128,1024]{1,0:T(8,128)(2,1)} %v_ref.5), custom_call_target="tpu_custom_call" | custom-call | flops 100000000 | bytes 1000000 | tf_op jit(solution)/shard_map/first/pallas_call | solution.py:440
  3.9 0.0 copy-start.4
  3.9 5.0 %collective-permute-start = (bf16[160,1024]{1,0:T(8,128)(2,1)}, bf16[160,1024]{1,0:T(8,128)(2,1)S(1)}, u32[]{:S(2)}, u32[]{:S(2)}) collective-permute-start(bf16[160,1024]{1,0:T(8,128)(2,1)} %get-tuple-element.55.sent_ref), channel_id=1, source_target_pairs={{0,4},{4,8},{8,12},{12,16},{16,20},{20,24},{24,28},{1,5},{5,9},{9,... | collective-permute-start | bytes 983048 | tf_op jit(solution)/shard_map/ppermute | solution.py:25
  9.0 3.5 %collective-permute-start.1 = (bf16[16,1024]{1,0:T(8,128)(2,1)}, bf16[16,1024]{1,0:T(8,128)(2,1)S(1)}, u32[]{:S(2)}, u32[]{:S(2)}) collective-permute-start(bf16[16,1024]{1,0:T(8,128)(2,1)} %get-tuple-element.53), channel_id=1, source_target_pairs={{0,8},{4,12},{8,16},{12,20},{16,24},{20,28},{1,9},{5,13},{9,17},{1... | collective-permute-start | bytes 98312 | tf_op jit(solution)/shard_map/ppermute | solution.py:25
  12.4 0.0 copy-start.10
  12.4 0.7 %copy-done.10 = bf16[64,128]{1,0:T(8,128)(2,1)S(1)} copy-done((bf16[64,128]{1,0:T(8,128)(2,1)S(1)}, bf16[64,128]{1,0:T(8,128)(2,1)}, u32[]{:S(2)}) %copy-start.10) | copy-done | bytes 16408
  13.1 1.8 %circulants.2.fwd_ref = bf16[128,8192]{1,0:T(8,128)(2,1)S(1)} custom-call(bf16[64,128]{1,0:T(8,128)(2,1)S(1)} %copy-done.10), custom_call_target="tpu_custom_call" | custom-call | flops 1000000000 | bytes 4000000 | tf_op jit(solution)/shard_map/circulants/pallas_call | solution.py:440
  15.0 0.0 copy-start
  15.0 0.0 copy-start.1
  15.0 0.0 copy-start.2
  15.0 0.0 copy-start.6
  15.0 0.0 copy-start.7
  15.1 2.9 %current.1 = (f32[128,1024]{1,0:T(8,128)S(1)}, f32[128,1024]{1,0:T(8,128)S(1)}, bf16[128,1024]{1,0:T(8,128)(2,1)S(1)}) custom-call(s32[8]{0:T(128)S(1)} %copy-done.8, bf16[128,1024]{1,0:T(8,128)(2,1)S(1)} %copy-done.3, f32[24,1024]{1,0:T(8,128)S(1)} %copy-done.4, bf16[160,1024]{1,0:T(8,128)(2,1)S(1)} %copy-done.5, bf16[128,8192]{1,0:T(8,128)(2,1)S(1)} %circulants.2.fwd_ref, ...), custom_call_target="tpu_custom_call" | custom-call | flops 1000000000 | bytes 5000000 | tf_op jit(solution)/shard_map/current/pallas_call | solution.py:440
  18.1 2.2 %summed.1 = (f32[128,1024]{1,0:T(8,128)S(1)}, bf16[128,1024]{1,0:T(8,128)(2,1)S(1)}, bf16[128,1024]{1,0:T(8,128)(2,1)S(1)}, f32[128,1024]{1,0:T(8,128)S(1)}, f32...) custom-call(s32[8]{0:T(128)S(1)} %copy-done.8, bf16[160,1024]{1,0:T(8,128)(2,1)S(1)} %collective-permute-done.came_ref, ...), custom_call_target="tpu_custom_call" | custom-call | flops 1000000000 | bytes 5000000 | tf_op jit(solution)/shard_map/summed/pallas_call | solution.py:440
  20.3 0.1 collective-permute-start.2
  20.4 1.7 %circulants.3.bwd_ref = bf16[128,8192]{1,0:T(8,128)(2,1)S(1)} custom-call(bf16[64,128]{1,0:T(8,128)(2,1)S(1)} %copy-done.11), custom_call_target="tpu_custom_call" | custom-call | flops 1000000000 | bytes 4000000 | tf_op jit(solution)/shard_map/circulants/pallas_call | solution.py:440
  22.1 1.6 %collective-permute-start.3 = (f32[2,128]{1,0:T(2,128)S(1)}, f32[2,128]{1,0:T(2,128)S(1)}, u32[]{:S(2)}, u32[]{:S(2)}) collective-permute-start(f32[2,128]{1,0:T(2,128)S(1)} %add.12), channel_id=1, source_target_pairs={{0,2},{1,3},{2,0},{3,1},{4,6},{5,7},{6,4},{7,5},{8,10},{9,11},{10,... | collective-permute-start | bytes 3080 | tf_op jit(solution)/shard_map/ppermute | solution.py:29
  23.7 2.0 %gates.1 = (f32[128,1024]{1,0:T(8,128)S(1)}, f32[128,1024]{1,0:T(8,128)S(1)}) custom-call(s32[8]{0:T(128)S(1)} %copy-done.8, bf16[128,1024]{1,0:T(8,128)(2,1)S(1)} %copy-done, bf16[128,1024]{1,0:T(8,128)(2,1)S(1)} %copy-done.1, bf16[160,1024]{1,0:T(8,128)(2,1)S(1)} %collective-permute-done.came_ref, f32[24,1024]{1,0:T(8,128)S(1)} %copy-done.4), custom_call_target="tpu_custom_call" | custom-call | flops 100000000 | bytes 2000000 | tf_op jit(solution)/shard_map/gates/pallas_call | solution.py:440
  25.7 0.1 collective-permute-done.3
  25.7 0.5 grads.1
  26.2 1.3 %collective-permute-start.4 = (bf16[128,1024]{1,0:T(8,128)(2,1)S(1)}, bf16[128,1024]{1,0:T(8,128)(2,1)S(1)}, u32[]{:S(2)}, u32[]{:S(2)}) collective-permute-start(bf16[128,1024]{1,0:T(8,128)(2,1)S(1)} %get-tuple-element.69.gm_ref), channel_id=1, source_target_pairs={{4,0},{8,4},{12,8},{16,12},{20,16},{24,20},{28,24},{5,1},{9,5},{13... | collective-permute-start | bytes 786440 | tf_op jit(solution)/shard_map/ppermute | solution.py:25
  27.5 6.0 %beside.1 = (f32[80,128]{1,0:T(8,128)S(1)}, f32[128,1024]{1,0:T(8,128)S(1)}, f32[8,1024]{1,0:T(8,128)S(1)}) custom-call(s32[8]{0:T(128)S(1)} %copy-done.8, f32[128,1024]{1,0:T(8,128)S(1)} %get-tuple-element.60.summed_ref, bf16[128,1024]{1,0:T(8,128)(2,1)S(1)} %copy-done.2, f32[2,128]{1,0:T(2,128)S(1)} %add.13.sums_ref, ...), custom_call_target="tpu_custom_call" | custom-call | flops 4000000000 | bytes 5000000 | tf_op jit(solution)/shard_map/beside/pallas_call | solution.py:440
  33.5 3.0 %collective-permute-done.4.after_ref = bf16[128,1024]{1,0:T(8,128)(2,1)S(1)} collective-permute-done((bf16[128,1024]{1,0:T(8,128)(2,1)S(1)}, bf16[128,1024]{1,0:T(8,128)(2,1)S(1)}, u32[]{:S(2)}, u32[]{:S(2)}) %collective-permute-start.4) | collective-permute-done | bytes 262176 | tf_op jit(solution)/shard_map/ppermute | solution.py:25
  36.5 3.4 %gate.1 = (bf16[128,1024]{1,0:T(8,128)(2,1)S(1)}, bf16[128,1024]{1,0:T(8,128)(2,1)S(1)}, bf16[32,1024]{1,0:T(8,128)(2,1)S(1)}, f32[104,128]{1,0:T(8,128)S(1)}) custom-call(s32[8]{0:T(128)S(1)} %copy-done.8, f32[128,1024]{1,0:T(8,128)S(1)} %get-tuple-element.74.part_ref, bf16[128,1024]{1,0:T(8,128)(2,1)S(1)} %collective-permute-done.4.after_ref, ...), custom_call_target="tpu_custom_call" | custom-call | flops 1000000000 | bytes 5000000 | tf_op jit(solution)/shard_map/gate/pallas_call | solution.py:440
  39.9 1.3 %collective-permute-start.7 = (bf16[32,1024]{1,0:T(8,128)(2,1)S(1)}, bf16[32,1024]{1,0:T(8,128)(2,1)S(1)}, u32[]{:S(2)}, u32[]{:S(2)}) collective-permute-start(bf16[32,1024]{1,0:T(8,128)(2,1)S(1)} %get-tuple-element.82), channel_id=1, source_target_pairs={{4,0},{8,4},{12,8},{16,12},{20,16},{24,20},{28,24},{5,1},{9,5},{13... | collective-permute-start | bytes 196616 | tf_op jit(solution)/shard_map/ppermute | solution.py:25
  41.2 3.1 %collective-permute-start.5 = (f32[104,128]{1,0:T(8,128)S(1)}, f32[104,128]{1,0:T(8,128)S(1)}, u32[]{:S(2)}, u32[]{:S(2)}) collective-permute-start(f32[104,128]{1,0:T(8,128)S(1)} %get-tuple-element.79), channel_id=1, source_target_pairs={{0,4},{4,0},{8,12},{12,8},{16,20},{20,16},{24,28},{28,24},{1,5},{5... | collective-permute-start | bytes 159752 | tf_op jit(solution)/shard_map/ppermute | solution.py:29
  44.3 2.7 %collective-permute-done.5 = f32[104,128]{1,0:T(8,128)S(1)} collective-permute-done((f32[104,128]{1,0:T(8,128)S(1)}, f32[104,128]{1,0:T(8,128)S(1)}, u32[]{:S(2)}, u32[]{:S(2)}) %collective-permute-start.5) | collective-permute-done | bytes 53280 | tf_op jit(solution)/shard_map/ppermute | solution.py:29
  47.1 2.9 %collective-permute-start.6 = (f32[104,128]{1,0:T(8,128)S(1)}, f32[104,128]{1,0:T(8,128)S(1)}, u32[]{:S(2)}, u32[]{:S(2)}) collective-permute-start(f32[104,128]{1,0:T(8,128)S(1)} %add.14), channel_id=1, source_target_pairs={{0,8},{4,12},{8,0},{12,4},{16,24},{20,28},{24,16},{28,20},{1,9},{5... | collective-permute-start | bytes 159752 | tf_op jit(solution)/shard_map/ppermute | solution.py:29
  50.0 3.8 %mains.1 = (bf16[128,1024]{1,0:T(8,128)(2,1)}, bf16[128,1024]{1,0:T(8,128)(2,1)}, bf16[128,1024]{1,0:T(8,128)(2,1)}, bf16[128,1024]{1,0:T(8,128)(2,1)}) custom-call(s32[8]{0:T(128)S(1)} %copy-done.8, f32[24,1024]{1,0:T(8,128)S(1)} %copy-done.4, bf16[128,1024]{1,0:T(8,128)(2,1)S(1)} %get-tuple-element.70.gq_ref, ...), custom_call_target="tpu_custom_call" | custom-call | flops 1000000000 | bytes 5000000 | tf_op jit(solution)/shard_map/mains/pallas_call | solution.py:440
  53.9 2.3 %collective-permute-start.8 = (f32[104,128]{1,0:T(8,128)S(1)}, f32[104,128]{1,0:T(8,128)S(1)}, u32[]{:S(2)}, u32[]{:S(2)}) collective-permute-start(f32[104,128]{1,0:T(8,128)S(1)} %add.15.one_ref), channel_id=1, source_target_pairs={{0,16},{4,20},{8,24},{12,28},{16,0},{20,4},{24,8},{28,12},{1,17},{... | collective-permute-start | bytes 159752 | tf_op jit(solution)/shard_map/ppermute | solution.py:29
  56.2 3.0 %collective-permute-done.8.two_ref = f32[104,128]{1,0:T(8,128)S(1)} collective-permute-done((f32[104,128]{1,0:T(8,128)S(1)}, f32[104,128]{1,0:T(8,128)S(1)}, u32[]{:S(2)}, u32[]{:S(2)}) %collective-permute-start.8) | collective-permute-done | bytes 53280 | tf_op jit(solution)/shard_map/ppermute | solution.py:29
  59.2 0.6 %unpack.1 = (f32[3,7,64]{2,1,0:T(8,128)}, f32[64,128]{1,0:T(8,128)}, f32[8,128]{1,0:T(8,128)}, f32[8,128]{1,0:T(8,128)}) custom-call(f32[104,128]{1,0:T(8,128)S(1)} %add.15.one_ref, f32[104,128]{1,0:T(8,128)S(1)} %collective-permute-done.8.two_ref), custom_call_target="tpu_custom_call" | custom-call | flops 100000000 | bytes 1000000 | tf_op jit(solution)/shard_map/unpack/pallas_call | solution.py:440
  (25 shorter events, 0.1 us)
Async XLA Ops:
  0.6 14.4 %copy-start.3 = (bf16[128,1024]{1,0:T(8,128)(2,1)S(1)}, bf16[128,1024]{1,0:T(8,128)(2,1)}, u32[]{:S(2)}) copy-start(bf16[128,1024]{1,0:T(8,128)(2,1)} %q_ref.5) | copy-start | bytes 786436
  0.6 14.4 %copy-start.8 = (s32[8]{0:T(128)S(1)}, s32[8]{0:T(128)}, u32[]{:S(2)}) copy-start(s32[8]{0:T(128)} %len_ref.11) | copy-start | bytes 100
  0.7 14.4 %copy-start.9 = (f32[1024]{0:T(1024)S(1)}, f32[1024]{0:T(1024)}, u32[]{:S(2)}) copy-start(f32[1024]{0:T(1024)} %param.17) | copy-start | bytes 12292
  3.9 11.1 %copy-start.4 = (f32[24,1024]{1,0:T(8,128)S(1)}, f32[24,1024]{1,0:T(8,128)}, u32[]{:S(2)}) copy-start(f32[24,1024]{1,0:T(8,128)} %get-tuple-element.54.taps_ref) | copy-start | bytes 294916
  3.9 11.1 %copy-start.5 = (bf16[160,1024]{1,0:T(8,128)(2,1)S(1)}, bf16[160,1024]{1,0:T(8,128)(2,1)}, u32[]{:S(2)}) copy-start(bf16[160,1024]{1,0:T(8,128)(2,1)} %get-tuple-element.55.sent_ref) | copy-start | bytes 983044
  3.9 14.1 %collective-permute-start = (bf16[160,1024]{1,0:T(8,128)(2,1)}, bf16[160,1024]{1,0:T(8,128)(2,1)S(1)}, u32[]{:S(2)}, u32[]{:S(2)}) collective-permute-start(bf16[160,1024]{1,0:T(8,128)(2,1)} %get-tuple-element.55.sent_ref), channel_id=1, source_target_pairs={{0,4},{4,8},{8,12},{12,16},{16,20},{20,24},{24,28},{1,5},{5,9},{9,... | collective-permute-start | bytes 983048 | tf_op jit(solution)/shard_map/ppermute | solution.py:25
  9.0 9.0 %collective-permute-start.1 = (bf16[16,1024]{1,0:T(8,128)(2,1)}, bf16[16,1024]{1,0:T(8,128)(2,1)S(1)}, u32[]{:S(2)}, u32[]{:S(2)}) collective-permute-start(bf16[16,1024]{1,0:T(8,128)(2,1)} %get-tuple-element.53), channel_id=1, source_target_pairs={{0,8},{4,12},{8,16},{12,20},{16,24},{20,28},{1,9},{5,13},{9,17},{1... | collective-permute-start | bytes 98312 | tf_op jit(solution)/shard_map/ppermute | solution.py:25
  12.4 0.7 %copy-start.10 = (bf16[64,128]{1,0:T(8,128)(2,1)S(1)}, bf16[64,128]{1,0:T(8,128)(2,1)}, u32[]{:S(2)}) copy-start(bf16[64,128]{1,0:T(8,128)(2,1)} %long_ref.1) | copy-start | bytes 49156
  15.0 3.0 %copy-start = (bf16[128,1024]{1,0:T(8,128)(2,1)S(1)}, bf16[128,1024]{1,0:T(8,128)(2,1)}, u32[]{:S(2)}) copy-start(bf16[128,1024]{1,0:T(8,128)(2,1)} %k_ref.5) | copy-start | bytes 786436
  15.0 3.0 %copy-start.1 = (bf16[128,1024]{1,0:T(8,128)(2,1)S(1)}, bf16[128,1024]{1,0:T(8,128)(2,1)}, u32[]{:S(2)}) copy-start(bf16[128,1024]{1,0:T(8,128)(2,1)} %v_ref.5) | copy-start | bytes 786436
  15.0 3.0 %copy-start.2 = (bf16[128,1024]{1,0:T(8,128)(2,1)S(1)}, bf16[128,1024]{1,0:T(8,128)(2,1)}, u32[]{:S(2)}) copy-start(bf16[128,1024]{1,0:T(8,128)(2,1)} %cot_ref.5) | copy-start | bytes 786436
  15.0 3.0 %copy-start.6 = (bf16[128,1024]{1,0:T(8,128)(2,1)S(1)}, bf16[128,1024]{1,0:T(8,128)(2,1)}, u32[]{:S(2)}) copy-start(bf16[128,1024]{1,0:T(8,128)(2,1)} %resid_ref.1) | copy-start | bytes 786436
  15.0 3.0 %copy-start.7 = (f32[1024]{0:T(1024)S(1)}, f32[1024]{0:T(1024)}, u32[]{:S(2)}) copy-start(f32[1024]{0:T(1024)} %param.18) | copy-start | bytes 12292
  18.0 2.4 %copy-start.11 = (bf16[64,128]{1,0:T(8,128)(2,1)S(1)}, bf16[64,128]{1,0:T(8,128)(2,1)}, u32[]{:S(2)}) copy-start(bf16[64,128]{1,0:T(8,128)(2,1)} %long_ref.1) | copy-start | bytes 49156
  20.3 1.8 %collective-permute-start.2 = (f32[2,128]{1,0:T(2,128)S(1)}, f32[2,128]{1,0:T(2,128)S(1)}, u32[]{:S(2)}, u32[]{:S(2)}) collective-permute-start(f32[2,128]{1,0:T(2,128)S(1)} %get-tuple-element.61), channel_id=1, source_target_pairs={{0,1},{1,0},{2,3},{3,2},{4,5},{5,4},{6,7},{7,6},{8,9},{9,8},{10,11... | collective-permute-start | bytes 3080 | tf_op jit(solution)/shard_map/ppermute | solution.py:29
  22.1 3.6 %collective-permute-start.3 = (f32[2,128]{1,0:T(2,128)S(1)}, f32[2,128]{1,0:T(2,128)S(1)}, u32[]{:S(2)}, u32[]{:S(2)}) collective-permute-start(f32[2,128]{1,0:T(2,128)S(1)} %add.12), channel_id=1, source_target_pairs={{0,2},{1,3},{2,0},{3,1},{4,6},{5,7},{6,4},{7,5},{8,10},{9,11},{10,... | collective-permute-start | bytes 3080 | tf_op jit(solution)/shard_map/ppermute | solution.py:29
  26.2 10.3 %collective-permute-start.4 = (bf16[128,1024]{1,0:T(8,128)(2,1)S(1)}, bf16[128,1024]{1,0:T(8,128)(2,1)S(1)}, u32[]{:S(2)}, u32[]{:S(2)}) collective-permute-start(bf16[128,1024]{1,0:T(8,128)(2,1)S(1)} %get-tuple-element.69.gm_ref), channel_id=1, source_target_pairs={{4,0},{8,4},{12,8},{16,12},{20,16},{24,20},{28,24},{5,1},{9,5},{13... | collective-permute-start | bytes 786440 | tf_op jit(solution)/shard_map/ppermute | solution.py:25
  39.9 10.1 %collective-permute-start.7 = (bf16[32,1024]{1,0:T(8,128)(2,1)S(1)}, bf16[32,1024]{1,0:T(8,128)(2,1)S(1)}, u32[]{:S(2)}, u32[]{:S(2)}) collective-permute-start(bf16[32,1024]{1,0:T(8,128)(2,1)S(1)} %get-tuple-element.82), channel_id=1, source_target_pairs={{4,0},{8,4},{12,8},{16,12},{20,16},{24,20},{28,24},{5,1},{9,5},{13... | collective-permute-start | bytes 196616 | tf_op jit(solution)/shard_map/ppermute | solution.py:25
  41.2 5.8 %collective-permute-start.5 = (f32[104,128]{1,0:T(8,128)S(1)}, f32[104,128]{1,0:T(8,128)S(1)}, u32[]{:S(2)}, u32[]{:S(2)}) collective-permute-start(f32[104,128]{1,0:T(8,128)S(1)} %get-tuple-element.79), channel_id=1, source_target_pairs={{0,4},{4,0},{8,12},{12,8},{16,20},{20,16},{24,28},{28,24},{1,5},{5... | collective-permute-start | bytes 159752 | tf_op jit(solution)/shard_map/ppermute | solution.py:29
  47.1 6.8 %collective-permute-start.6 = (f32[104,128]{1,0:T(8,128)S(1)}, f32[104,128]{1,0:T(8,128)S(1)}, u32[]{:S(2)}, u32[]{:S(2)}) collective-permute-start(f32[104,128]{1,0:T(8,128)S(1)} %add.14), channel_id=1, source_target_pairs={{0,8},{4,12},{8,0},{12,4},{16,24},{20,28},{24,16},{28,20},{1,9},{5... | collective-permute-start | bytes 159752 | tf_op jit(solution)/shard_map/ppermute | solution.py:29
  53.9 5.4 %collective-permute-start.8 = (f32[104,128]{1,0:T(8,128)S(1)}, f32[104,128]{1,0:T(8,128)S(1)}, u32[]{:S(2)}, u32[]{:S(2)}) collective-permute-start(f32[104,128]{1,0:T(8,128)S(1)} %add.15.one_ref), channel_id=1, source_target_pairs={{0,16},{4,20},{8,24},{12,28},{16,0},{20,4},{24,8},{28,12},{1,17},{... | collective-permute-start | bytes 159752 | tf_op jit(solution)/shard_map/ppermute | solution.py:29

commit v5 on v4

--- a/solution.py
+++ b/solution.py
@@ -21,8 +21,7 @@
 
 def shifted(x, axis, by):
     count = lax.axis_size(axis)
-    pairs = [(i, i + by) for i in range(count) if 0 <= i + by < count]
-    return lax.ppermute(x, axis, pairs)
+    return lax.ppermute(x, axis, [(i, (i + by) % count) for i in range(count)])
 
 
 def swapped(x, axis, step):
@@ -39,7 +38,7 @@
     for n in range(len_ref.shape[0]):
         begin = jnp.where(rows >= start, start, begin)
         start = start + len_ref[n]
-    return rows - begin
+    return jnp.where(rows < start, rows - begin, -1)
 
 
 def first_row():

time: 60.2 us -> 57.4 us (0.953)
  starting transfers between devices: 21.1 us -> 13.2 us
  waiting for transfers between devices: 8.83 us -> 14 us
    ppermute x5, starting transfers between devices: 10 us -> 1.77 us  [swapped(): lax.ppermute(x, axis, [(i, i ^ step) for i in range(lax.axis_size(axis))])]
    ppermute x5, waiting for transfers between devices: 5.85 us -> 9.49 us  [swapped(): lax.ppermute(x, axis, [(i, i ^ step) for i in range(lax.axis_size(axis))])]
    ppermute x4, waiting for transfers between devices: 2.98 us -> 4.49 us  [shifted(): return lax.ppermute(x, axis, [(i, (i + by) % count) for i in range(count)])]
  transfers between devices with their start and end apart: 9 -> 9, of which waited for: 4 -> 6; matrix products, arithmetic and copies ran while one was open for 0% -> 0% of each run, Pallas kernels for 30% -> 32%
where the time goes in v5:
time: 57.4 us; the launch traced here: 57.2 us
  Pallas kernels  28.2 us (49%)
  waiting for transfers between devices  14 us (24%)
  starting transfers between devices  13.2 us (23%)
  between operations  0.92 us (2%)
  local copies, waits for them, and re-layouts  0.78 us (1%)
    pallas_call x11, Pallas kernels, call(): pl.pallas_call(kernel, out_shape=outs, in_specs=[far_off] * len(ins) if h...  28.2 us
    ppermute x4, starting transfers between devices, shifted(): return lax.ppermute(x, axis, [(i, (i + by) % count) for i in range(count)])  11.5 us
    ppermute x5, waiting for transfers between devices, swapped(): lax.ppermute(x, axis, [(i, i ^ step) for i in range(lax.axis_size(axis))])  9.49 us
    ppermute x4, waiting for transfers between devices, shifted(): return lax.ppermute(x, axis, [(i, (i + by) % count) for i in range(count)])  4.49 us
    ppermute x5, starting transfers between devices, swapped(): lax.ppermute(x, axis, [(i, i ^ step) for i in range(lax.axis_size(axis))])  1.77 us
  transfers between devices with their start and end apart: 9, of which 6 were waited for; matrix products, arithmetic and copies ran while one was open for 0% of the time, Pallas kernels for 32%

profile of v5, /device:TPU:0, one launch (start us, length us, event | category | flops | bytes accessed | tf_op | source)
XLA Modules:
  0.0 57.2 jit_solution(17870670547198736686)
XLA Ops:
  0.7 3.2 %first.1 = (f32[24,1024]{1,0:T(8,128)}, bf16[160,1024]{1,0:T(8,128)(2,1)}, bf16[16,1024]{1,0:T(8,128)(2,1)}) custom-call(s32[8]{0:T(128)} %len_ref.11, bf16[3,7,64]{2,1,0:T(8,128)(2,1)} %bitcast.12, bf16[128,1024]{1,0:T(8,128)(2,1)} %q_ref.5, bf16[128,1024]{1,0:T(8,128)(2,1)} %k_ref.5, bf16[128,1024]{1,0:T(8,128)(2,1)} %v_ref.5), custom_call_target="tpu_custom_call" | custom-call | flops 100000000 | bytes 1000000 | tf_op jit(solution)/shard_map/first/pallas_call | solution.py:439
  3.9 0.0 copy-start.4
  3.9 3.0 %collective-permute-start = (bf16[160,1024]{1,0:T(8,128)(2,1)}, bf16[160,1024]{1,0:T(8,128)(2,1)S(1)}, u32[]{:S(2)}, u32[]{:S(2)}) collective-permute-start(bf16[160,1024]{1,0:T(8,128)(2,1)} %get-tuple-element.55.sent_ref), channel_id=1, source_target_pairs={{0,4},{4,8},{8,12},{12,16},{16,20},{20,24},{24,28},{28,0},{1,5},{5... | collective-permute-start | bytes 983048 | tf_op jit(solution)/shard_map/ppermute | solution.py:24
  6.9 1.6 %collective-permute-start.1 = (bf16[16,1024]{1,0:T(8,128)(2,1)}, bf16[16,1024]{1,0:T(8,128)(2,1)S(1)}, u32[]{:S(2)}, u32[]{:S(2)}) collective-permute-start(bf16[16,1024]{1,0:T(8,128)(2,1)} %get-tuple-element.53), channel_id=1, source_target_pairs={{0,8},{4,12},{8,16},{12,20},{16,24},{20,28},{24,0},{28,4},{1,9},{5... | collective-permute-start | bytes 98312 | tf_op jit(solution)/shard_map/ppermute | solution.py:24
  8.5 0.7 %copy-done.10 = bf16[64,128]{1,0:T(8,128)(2,1)S(1)} copy-done((bf16[64,128]{1,0:T(8,128)(2,1)S(1)}, bf16[64,128]{1,0:T(8,128)(2,1)}, u32[]{:S(2)}) %copy-start.10) | copy-done | bytes 16408
  9.2 1.8 %circulants.2.fwd_ref = bf16[128,8192]{1,0:T(8,128)(2,1)S(1)} custom-call(bf16[64,128]{1,0:T(8,128)(2,1)S(1)} %copy-done.10), custom_call_target="tpu_custom_call" | custom-call | flops 1000000000 | bytes 4000000 | tf_op jit(solution)/shard_map/circulants/pallas_call | solution.py:439
  11.0 0.0 copy-start
  11.1 0.0 copy-start.1
  11.1 0.0 copy-start.2
  11.1 0.0 copy-start.6
  11.2 2.9 %current.1 = (f32[128,1024]{1,0:T(8,128)S(1)}, f32[128,1024]{1,0:T(8,128)S(1)}, bf16[128,1024]{1,0:T(8,128)(2,1)S(1)}) custom-call(s32[8]{0:T(128)S(1)} %copy-done.8, bf16[128,1024]{1,0:T(8,128)(2,1)S(1)} %copy-done.3, f32[24,1024]{1,0:T(8,128)S(1)} %copy-done.4, bf16[160,1024]{1,0:T(8,128)(2,1)S(1)} %copy-done.5, bf16[128,8192]{1,0:T(8,128)(2,1)S(1)} %circulants.2.fwd_ref, ...), custom_call_target="tpu_custom_call" | custom-call | flops 1000000000 | bytes 5000000 | tf_op jit(solution)/shard_map/current/pallas_call | solution.py:439
  14.1 4.2 %collective-permute-done.came_ref = bf16[160,1024]{1,0:T(8,128)(2,1)S(1)} collective-permute-done((bf16[160,1024]{1,0:T(8,128)(2,1)}, bf16[160,1024]{1,0:T(8,128)(2,1)S(1)}, u32[]{:S(2)}, u32[]{:S(2)}) %collective-permute-start) | collective-permute-done | bytes 327712 | tf_op jit(solution)/shard_map/ppermute | solution.py:24
  18.3 0.0 copy-start.11
  18.3 2.2 %summed.1 = (f32[128,1024]{1,0:T(8,128)S(1)}, bf16[128,1024]{1,0:T(8,128)(2,1)S(1)}, bf16[128,1024]{1,0:T(8,128)(2,1)S(1)}, f32[128,1024]{1,0:T(8,128)S(1)}, f32...) custom-call(s32[8]{0:T(128)S(1)} %copy-done.8, bf16[160,1024]{1,0:T(8,128)(2,1)S(1)} %collective-permute-done.came_ref, ...), custom_call_target="tpu_custom_call" | custom-call | flops 1000000000 | bytes 5000000 | tf_op jit(solution)/shard_map/summed/pallas_call | solution.py:439
  20.5 0.1 collective-permute-start.2
  20.6 1.7 %circulants.3.bwd_ref = bf16[128,8192]{1,0:T(8,128)(2,1)S(1)} custom-call(bf16[64,128]{1,0:T(8,128)(2,1)S(1)} %copy-done.11), custom_call_target="tpu_custom_call" | custom-call | flops 1000000000 | bytes 4000000 | tf_op jit(solution)/shard_map/circulants/pallas_call | solution.py:439
  22.3 1.6 %collective-permute-start.3 = (f32[2,128]{1,0:T(2,128)S(1)}, f32[2,128]{1,0:T(2,128)S(1)}, u32[]{:S(2)}, u32[]{:S(2)}) collective-permute-start(f32[2,128]{1,0:T(2,128)S(1)} %add.12), channel_id=1, source_target_pairs={{0,2},{1,3},{2,0},{3,1},{4,6},{5,7},{6,4},{7,5},{8,10},{9,11},{10,... | collective-permute-start | bytes 3080 | tf_op jit(solution)/shard_map/ppermute | solution.py:28
  23.9 2.0 %gates.1 = (f32[128,1024]{1,0:T(8,128)S(1)}, f32[128,1024]{1,0:T(8,128)S(1)}) custom-call(s32[8]{0:T(128)S(1)} %copy-done.8, bf16[128,1024]{1,0:T(8,128)(2,1)S(1)} %copy-done, bf16[128,1024]{1,0:T(8,128)(2,1)S(1)} %copy-done.1, bf16[160,1024]{1,0:T(8,128)(2,1)S(1)} %collective-permute-done.came_ref, f32[24,1024]{1,0:T(8,128)S(1)} %copy-done.4), custom_call_target="tpu_custom_call" | custom-call | flops 100000000 | bytes 2000000 | tf_op jit(solution)/shard_map/gates/pallas_call | solution.py:439
  25.9 0.1 collective-permute-done.3
  26.0 0.5 grads.1
  26.5 2.1 %collective-permute-start.4 = (bf16[128,1024]{1,0:T(8,128)(2,1)S(1)}, bf16[128,1024]{1,0:T(8,128)(2,1)S(1)}, u32[]{:S(2)}, u32[]{:S(2)}) collective-permute-start(bf16[128,1024]{1,0:T(8,128)(2,1)S(1)} %get-tuple-element.69.gm_ref), channel_id=1, source_target_pairs={{0,28},{4,0},{8,4},{12,8},{16,12},{20,16},{24,20},{28,24},{1,29},{... | collective-permute-start | bytes 786440 | tf_op jit(solution)/shard_map/ppermute | solution.py:24
  28.5 6.0 %beside.1 = (f32[80,128]{1,0:T(8,128)S(1)}, f32[128,1024]{1,0:T(8,128)S(1)}, f32[8,1024]{1,0:T(8,128)S(1)}) custom-call(s32[8]{0:T(128)S(1)} %copy-done.8, f32[128,1024]{1,0:T(8,128)S(1)} %get-tuple-element.60.summed_ref, bf16[128,1024]{1,0:T(8,128)(2,1)S(1)} %copy-done.2, f32[2,128]{1,0:T(2,128)S(1)} %add.13.sums_ref, ...), custom_call_target="tpu_custom_call" | custom-call | flops 4000000000 | bytes 5000000 | tf_op jit(solution)/shard_map/beside/pallas_call | solution.py:439
  34.5 0.3 collective-permute-done.4.after_ref
  34.9 3.4 %gate.1 = (bf16[128,1024]{1,0:T(8,128)(2,1)S(1)}, bf16[128,1024]{1,0:T(8,128)(2,1)S(1)}, bf16[32,1024]{1,0:T(8,128)(2,1)S(1)}, f32[104,128]{1,0:T(8,128)S(1)}) custom-call(s32[8]{0:T(128)S(1)} %copy-done.8, f32[128,1024]{1,0:T(8,128)S(1)} %get-tuple-element.74.part_ref, bf16[128,1024]{1,0:T(8,128)(2,1)S(1)} %collective-permute-done.4.after_ref, ...), custom_call_target="tpu_custom_call" | custom-call | flops 1000000000 | bytes 5000000 | tf_op jit(solution)/shard_map/gate/pallas_call | solution.py:439
  38.3 4.8 %collective-permute-start.7 = (bf16[32,1024]{1,0:T(8,128)(2,1)S(1)}, bf16[32,1024]{1,0:T(8,128)(2,1)S(1)}, u32[]{:S(2)}, u32[]{:S(2)}) collective-permute-start(bf16[32,1024]{1,0:T(8,128)(2,1)S(1)} %get-tuple-element.82), channel_id=1, source_target_pairs={{0,28},{4,0},{8,4},{12,8},{16,12},{20,16},{24,20},{28,24},{1,29},{... | collective-permute-start | bytes 196616 | tf_op jit(solution)/shard_map/ppermute | solution.py:24
  43.1 4.1 %collective-permute-done.5 = f32[104,128]{1,0:T(8,128)S(1)} collective-permute-done((f32[104,128]{1,0:T(8,128)S(1)}, f32[104,128]{1,0:T(8,128)S(1)}, u32[]{:S(2)}, u32[]{:S(2)}) %collective-permute-start.5) | collective-permute-done | bytes 53280 | tf_op jit(solution)/shard_map/ppermute | solution.py:28
  47.2 0.1 collective-permute-start.6
  47.3 3.8 %mains.1 = (bf16[128,1024]{1,0:T(8,128)(2,1)}, bf16[128,1024]{1,0:T(8,128)(2,1)}, bf16[128,1024]{1,0:T(8,128)(2,1)}, bf16[128,1024]{1,0:T(8,128)(2,1)}) custom-call(s32[8]{0:T(128)S(1)} %copy-done.8, f32[24,1024]{1,0:T(8,128)S(1)} %copy-done.4, bf16[128,1024]{1,0:T(8,128)(2,1)S(1)} %get-tuple-element.70.gq_ref, ...), custom_call_target="tpu_custom_call" | custom-call | flops 1000000000 | bytes 5000000 | tf_op jit(solution)/shard_map/mains/pallas_call | solution.py:439
  51.2 0.3 collective-permute-done.6
  51.4 0.1 collective-permute-start.8
  51.5 5.0 %collective-permute-done.8.two_ref = f32[104,128]{1,0:T(8,128)S(1)} collective-permute-done((f32[104,128]{1,0:T(8,128)S(1)}, f32[104,128]{1,0:T(8,128)S(1)}, u32[]{:S(2)}, u32[]{:S(2)}) %collective-permute-start.8) | collective-permute-done | bytes 53280 | tf_op jit(solution)/shard_map/ppermute | solution.py:28
  56.5 0.6 %unpack.1 = (f32[3,7,64]{2,1,0:T(8,128)}, f32[64,128]{1,0:T(8,128)}, f32[8,128]{1,0:T(8,128)}, f32[8,128]{1,0:T(8,128)}) custom-call(f32[104,128]{1,0:T(8,128)S(1)} %add.15.one_ref, f32[104,128]{1,0:T(8,128)S(1)} %collective-permute-done.8.two_ref), custom_call_target="tpu_custom_call" | custom-call | flops 100000000 | bytes 1000000 | tf_op jit(solution)/shard_map/unpack/pallas_call | solution.py:439
  (25 shorter events, 0.1 us)
Async XLA Ops:
  0.6 10.5 %copy-start.3 = (bf16[128,1024]{1,0:T(8,128)(2,1)S(1)}, bf16[128,1024]{1,0:T(8,128)(2,1)}, u32[]{:S(2)}) copy-start(bf16[128,1024]{1,0:T(8,128)(2,1)} %q_ref.5) | copy-start | bytes 786436
  0.6 10.5 %copy-start.8 = (s32[8]{0:T(128)S(1)}, s32[8]{0:T(128)}, u32[]{:S(2)}) copy-start(s32[8]{0:T(128)} %len_ref.11) | copy-start | bytes 100
  0.7 10.5 %copy-start.9 = (f32[1024]{0:T(1024)S(1)}, f32[1024]{0:T(1024)}, u32[]{:S(2)}) copy-start(f32[1024]{0:T(1024)} %param.17) | copy-start | bytes 12292
  3.9 7.2 %copy-start.4 = (f32[24,1024]{1,0:T(8,128)S(1)}, f32[24,1024]{1,0:T(8,128)}, u32[]{:S(2)}) copy-start(f32[24,1024]{1,0:T(8,128)} %get-tuple-element.54.taps_ref) | copy-start | bytes 294916
  3.9 7.2 %copy-start.5 = (bf16[160,1024]{1,0:T(8,128)(2,1)S(1)}, bf16[160,1024]{1,0:T(8,128)(2,1)}, u32[]{:S(2)}) copy-start(bf16[160,1024]{1,0:T(8,128)(2,1)} %get-tuple-element.55.sent_ref) | copy-start | bytes 983044
  3.9 14.3 %collective-permute-start = (bf16[160,1024]{1,0:T(8,128)(2,1)}, bf16[160,1024]{1,0:T(8,128)(2,1)S(1)}, u32[]{:S(2)}, u32[]{:S(2)}) collective-permute-start(bf16[160,1024]{1,0:T(8,128)(2,1)} %get-tuple-element.55.sent_ref), channel_id=1, source_target_pairs={{0,4},{4,8},{8,12},{12,16},{16,20},{20,24},{24,28},{28,0},{1,5},{5... | collective-permute-start | bytes 983048 | tf_op jit(solution)/shard_map/ppermute | solution.py:24
  6.9 7.1 %collective-permute-start.1 = (bf16[16,1024]{1,0:T(8,128)(2,1)}, bf16[16,1024]{1,0:T(8,128)(2,1)S(1)}, u32[]{:S(2)}, u32[]{:S(2)}) collective-permute-start(bf16[16,1024]{1,0:T(8,128)(2,1)} %get-tuple-element.53), channel_id=1, source_target_pairs={{0,8},{4,12},{8,16},{12,20},{16,24},{20,28},{24,0},{28,4},{1,9},{5... | collective-permute-start | bytes 98312 | tf_op jit(solution)/shard_map/ppermute | solution.py:24
  8.5 0.7 %copy-start.10 = (bf16[64,128]{1,0:T(8,128)(2,1)S(1)}, bf16[64,128]{1,0:T(8,128)(2,1)}, u32[]{:S(2)}) copy-start(bf16[64,128]{1,0:T(8,128)(2,1)} %long_ref.1) | copy-start | bytes 49156
  11.0 7.2 %copy-start = (bf16[128,1024]{1,0:T(8,128)(2,1)S(1)}, bf16[128,1024]{1,0:T(8,128)(2,1)}, u32[]{:S(2)}) copy-start(bf16[128,1024]{1,0:T(8,128)(2,1)} %k_ref.5) | copy-start | bytes 786436
  11.1 7.2 %copy-start.1 = (bf16[128,1024]{1,0:T(8,128)(2,1)S(1)}, bf16[128,1024]{1,0:T(8,128)(2,1)}, u32[]{:S(2)}) copy-start(bf16[128,1024]{1,0:T(8,128)(2,1)} %v_ref.5) | copy-start | bytes 786436
  11.1 7.2 %copy-start.2 = (bf16[128,1024]{1,0:T(8,128)(2,1)S(1)}, bf16[128,1024]{1,0:T(8,128)(2,1)}, u32[]{:S(2)}) copy-start(bf16[128,1024]{1,0:T(8,128)(2,1)} %cot_ref.5) | copy-start | bytes 786436
  11.1 7.2 %copy-start.6 = (bf16[128,1024]{1,0:T(8,128)(2,1)S(1)}, bf16[128,1024]{1,0:T(8,128)(2,1)}, u32[]{:S(2)}) copy-start(bf16[128,1024]{1,0:T(8,128)(2,1)} %resid_ref.1) | copy-start | bytes 786436
  11.1 7.2 %copy-start.7 = (f32[1024]{0:T(1024)S(1)}, f32[1024]{0:T(1024)}, u32[]{:S(2)}) copy-start(f32[1024]{0:T(1024)} %param.18) | copy-start | bytes 12292
  18.3 2.3 %copy-start.11 = (bf16[64,128]{1,0:T(8,128)(2,1)S(1)}, bf16[64,128]{1,0:T(8,128)(2,1)}, u32[]{:S(2)}) copy-start(bf16[64,128]{1,0:T(8,128)(2,1)} %long_ref.1) | copy-start | bytes 49156
  20.5 1.8 %collective-permute-start.2 = (f32[2,128]{1,0:T(2,128)S(1)}, f32[2,128]{1,0:T(2,128)S(1)}, u32[]{:S(2)}, u32[]{:S(2)}) collective-permute-start(f32[2,128]{1,0:T(2,128)S(1)} %get-tuple-element.61), channel_id=1, source_target_pairs={{0,1},{1,0},{2,3},{3,2},{4,5},{5,4},{6,7},{7,6},{8,9},{9,8},{10,11... | collective-permute-start | bytes 3080 | tf_op jit(solution)/shard_map/ppermute | solution.py:28
  22.3 3.6 %collective-permute-start.3 = (f32[2,128]{1,0:T(2,128)S(1)}, f32[2,128]{1,0:T(2,128)S(1)}, u32[]{:S(2)}, u32[]{:S(2)}) collective-permute-start(f32[2,128]{1,0:T(2,128)S(1)} %add.12), channel_id=1, source_target_pairs={{0,2},{1,3},{2,0},{3,1},{4,6},{5,7},{6,4},{7,5},{8,10},{9,11},{10,... | collective-permute-start | bytes 3080 | tf_op jit(solution)/shard_map/ppermute | solution.py:28
  26.5 8.4 %collective-permute-start.4 = (bf16[128,1024]{1,0:T(8,128)(2,1)S(1)}, bf16[128,1024]{1,0:T(8,128)(2,1)S(1)}, u32[]{:S(2)}, u32[]{:S(2)}) collective-permute-start(bf16[128,1024]{1,0:T(8,128)(2,1)S(1)} %get-tuple-element.69.gm_ref), channel_id=1, source_target_pairs={{0,28},{4,0},{8,4},{12,8},{16,12},{20,16},{24,20},{28,24},{1,29},{... | collective-permute-start | bytes 786440 | tf_op jit(solution)/shard_map/ppermute | solution.py:24
  38.3 9.0 %collective-permute-start.7 = (bf16[32,1024]{1,0:T(8,128)(2,1)S(1)}, bf16[32,1024]{1,0:T(8,128)(2,1)S(1)}, u32[]{:S(2)}, u32[]{:S(2)}) collective-permute-start(bf16[32,1024]{1,0:T(8,128)(2,1)S(1)} %get-tuple-element.82), channel_id=1, source_target_pairs={{0,28},{4,0},{8,4},{12,8},{16,12},{20,16},{24,20},{28,24},{1,29},{... | collective-permute-start | bytes 196616 | tf_op jit(solution)/shard_map/ppermute | solution.py:24
  43.1 4.1 %collective-permute-start.5 = (f32[104,128]{1,0:T(8,128)S(1)}, f32[104,128]{1,0:T(8,128)S(1)}, u32[]{:S(2)}, u32[]{:S(2)}) collective-permute-start(f32[104,128]{1,0:T(8,128)S(1)} %get-tuple-element.79), channel_id=1, source_target_pairs={{0,4},{4,0},{8,12},{12,8},{16,20},{20,16},{24,28},{28,24},{1,5},{5... | collective-permute-start | bytes 159752 | tf_op jit(solution)/shard_map/ppermute | solution.py:28
  47.2 4.2 %collective-permute-start.6 = (f32[104,128]{1,0:T(8,128)S(1)}, f32[104,128]{1,0:T(8,128)S(1)}, u32[]{:S(2)}, u32[]{:S(2)}) collective-permute-start(f32[104,128]{1,0:T(8,128)S(1)} %add.14), channel_id=1, source_target_pairs={{0,8},{4,12},{8,0},{12,4},{16,24},{20,28},{24,16},{28,20},{1,9},{5... | collective-permute-start | bytes 159752 | tf_op jit(solution)/shard_map/ppermute | solution.py:28
  51.4 5.1 %collective-permute-start.8 = (f32[104,128]{1,0:T(8,128)S(1)}, f32[104,128]{1,0:T(8,128)S(1)}, u32[]{:S(2)}, u32[]{:S(2)}) collective-permute-start(f32[104,128]{1,0:T(8,128)S(1)} %add.15.one_ref), channel_id=1, source_target_pairs={{0,16},{4,20},{8,24},{12,28},{16,0},{20,4},{24,8},{28,12},{1,17},{... | collective-permute-start | bytes 159752 | tf_op jit(solution)/shard_map/ppermute | solution.py:28

commit v6 on v5

--- a/solution.py
+++ b/solution.py
@@ -256,6 +256,18 @@
         sums_ref[i : i + 1] = jnp.sum(acc_ref[i].T, axis=0, keepdims=True)
 
 
+def group_sums(cols):
+    count, channels = cols.shape
+    gather = as_mask(iota((channels, LANES), 0) // GS == iota((channels, LANES), 1))
+    high = cols.astype(BF16)
+    rest = cols - high.astype(F32)
+    mid = rest.astype(BF16)
+    low = (rest - mid.astype(F32)).astype(BF16)
+    parts = join(high.astype(F32), mid.astype(F32), low.astype(F32)).astype(BF16)
+    sums = jnp.dot(parts, gather, preferred_element_type=F32)
+    return sums[:count] + sums[count : 2 * count] + sums[2 * count :]
+
+
 def by_row(line):
     return jnp.broadcast_to(line, (K, K)).T
 
@@ -277,7 +289,7 @@
     each_chunk(k_ref.shape[1], body)
 
 
-def grads_kernel(total, summed_ref, mixed_ref, qs_ref, cot_ref, gain_ref, sums_ref, gm_ref, gq_ref):
+def grads_kernel(total, summed_ref, mixed_ref, qs_ref, cot_ref, gain_ref, sums_ref, gm_ref, gq_ref, head_ref):
     inverse = inverse_of(sums_ref, total)
     scale = inverse * inverse * by_row(sums_ref[1:2] / total)
 
@@ -286,7 +298,9 @@
         scaled = gain_ref[:, ls] * cot_ref[:, ls].astype(F32)
         grad_sum = inverse * (scaled - summed_ref[:, ls] * scale)
         gm_ref[:, ls] = (grad_sum * qs_ref[:, ls]).astype(BF16)
-        gq_ref[:, ls] = (grad_sum * mixed_ref[:, ls]).astype(BF16)
+        gq = (grad_sum * mixed_ref[:, ls]).astype(BF16)
+        gq_ref[:, ls] = gq
+        head_ref[:, ls] = gq[:PACK]
 
     each_chunk(cot_ref.shape[1], body)
 
@@ -341,14 +355,14 @@
         cols_ref[:, ls] = tap_lines(gq_ref[:, ls].astype(F32), q_ext, pos_row)
 
     each_chunk(cot_ref.shape[1], body, 1)
+    stats_ref[groups + 2 * (groups // PER) :] = group_sums(cols_ref[...])
 
 
 def gate_kernel(
-    len_ref, part_ref, after_ref, bwd_ref, ks_ref, vs_ref, gq_ref, k_ref, v_ref, came_ref,
-    stats_ref, qcols_ref, gks_ref, gvs_ref, tails_ref, packed_ref, cols_ref,
+    len_ref, part_ref, after_ref, bwd_ref, ks_ref, vs_ref, k_ref, v_ref, came_ref,
+    gks_ref, gvs_ref, tails_ref, short_ref, cols_ref,
 ):
     channels = part_ref.shape[1]
-    kept = stats_ref.shape[0]
     row = iota((K, LANES), 0)
     col = iota((K, LANES), 1)
     pos_row = positions(len_ref, first_row() + row)
@@ -364,56 +378,63 @@
         gvs = (grad * ks_ref[:, ls]).astype(BF16)
         gks_ref[:, ls] = gks
         gvs_ref[:, ls] = gvs
-        heads = (rim_of(gq_ref, 0, ls), gks.astype(F32)[:RIM], gvs.astype(F32)[:RIM])
-        tails_ref[:, ls] = join(*heads, jnp.zeros((RIM, LANES), F32)).astype(BF16)
+        tails_ref[:, ls] = join(gks.astype(F32)[:RIM], gvs.astype(F32)[:RIM]).astype(BF16)
         k_ext = join(rim_of(came_ref, K_LAST, ls), k_ref[:, ls].astype(F32))
         v_ext = join(rim_of(came_ref, V_LAST, ls), v_ref[:, ls].astype(F32))
-        cols_ref[0:8, ls] = qcols_ref[:, ls]
-        cols_ref[8:16, ls] = tap_lines(gks.astype(F32), k_ext, pos_row)
-        cols_ref[16:24, ls] = tap_lines(gvs.astype(F32), v_ext, pos_row)
+        cols_ref[:8, ls] = tap_lines(gks.astype(F32), k_ext, pos_row)
+        cols_ref[8:, ls] = tap_lines(gvs.astype(F32), v_ext, pos_row)
 
     each_chunk(channels, body)
-    packed_ref[0:kept] = stats_ref[...]
-    gather = jnp.where(
-        iota((channels, LANES), 0) // GS == iota((channels, LANES), 1), 1.0, 0.0
-    )
-    packed_ref[kept:] = jnp.dot(
-        cols_ref[...], gather, preferred_element_type=F32, precision=lax.Precision.HIGHEST
-    )
-
-
-def mains_kernel(
-    total, len_ref, taps_ref, gq_ref, gks_ref, gvs_ref, tails_ref, summed_ref, gain_ref, sums_ref,
-    oq_ref, ok_ref, ov_ref, normed_ref,
-):
+    short_ref[...] = group_sums(cols_ref[...])
+
+
+def back_short(which, at, pos, ls, taps_ref, grad_ref, tail_ref):
+    ext = join(grad_ref[:, ls].astype(F32), rim_of(tail_ref, at, ls))
+    taps = tap_rows(taps_ref, which, ls)
+    grad = taps[0] * ext[:K]
+    for j in range(1, KS):
+        held = jnp.where(pos >= j, ext, 0.0)
+        grad = grad + taps[j] * held[j : j + K]
+    return grad.astype(BF16)
+
+
+def main_kernel(which, at, len_ref, taps_ref, grad_ref, tail_ref, out_ref):
     pos = positions(len_ref, first_row() + iota((K + RIM, LANES), 0))
+
+    def body(q):
+        ls = lanes_of(q)
+        out_ref[:, ls] = back_short(which, at, pos, ls, taps_ref, grad_ref, tail_ref)
+
+    each_chunk(grad_ref.shape[1], body)
+
+
+def main_q_kernel(
+    total, len_ref, taps_ref, grad_ref, tail_ref, summed_ref, gain_ref, sums_ref, out_ref, normed_ref
+):
     inverse = inverse_of(sums_ref, total)
-
-    def body(q):
-        ls = lanes_of(q)
+    pos = positions(len_ref, first_row() + iota((K + RIM, LANES), 0))
+
+    def body(q):
+        ls = lanes_of(q)
+        out_ref[:, ls] = back_short(0, 0, pos, ls, taps_ref, grad_ref, tail_ref)
         normed_ref[:, ls] = (gain_ref[:, ls] * summed_ref[:, ls] * inverse).astype(BF16)
-        for i, (g_ref, o_ref) in enumerate(((gq_ref, oq_ref), (gks_ref, ok_ref), (gvs_ref, ov_ref))):
-            ext = join(g_ref[:, ls].astype(F32), rim_of(tails_ref, i * RIM, ls))
-            taps = tap_rows(taps_ref, i, ls)
-            grad = taps[0] * ext[:K]
-            for j in range(1, KS):
-                held = jnp.where(pos >= j, ext, 0.0)
-                grad = grad + taps[j] * held[j : j + K]
-            o_ref[:, ls] = grad.astype(BF16)
-
-    each_chunk(gq_ref.shape[1], body)
-
-
-def unpack_kernel(one_ref, two_ref, short_ref, long_ref, skip_ref, gain_ref):
+
+    each_chunk(grad_ref.shape[1], body)
+
+
+def unpack_kernel(
+    stats_ref, stats2_ref, last_ref, last2_ref, short_ref, long_ref, skip_ref, gain_ref
+):
     groups = long_ref.shape[0]
     rows = groups // PER
-    total = one_ref[...] + two_ref[...]
-    long_ref[...] = total[:groups]
-    skip_ref[...] = total[groups : groups + rows]
-    gain_ref[...] = total[groups + rows : groups + 2 * rows]
-    for i in range(3):
-        at = groups + 2 * rows + i * 8
-        short_ref[i] = total[at : at + KS, :groups]
+    stats = stats_ref[...] + stats2_ref[...]
+    last = last_ref[...] + last2_ref[...]
+    long_ref[...] = stats[:groups]
+    skip_ref[...] = stats[groups : groups + rows]
+    gain_ref[...] = stats[groups + rows : groups + 2 * rows]
+    short_ref[0] = stats[groups + 2 * rows :][:KS, :groups]
+    short_ref[1] = last[:KS, :groups]
+    short_ref[2] = last[8 : 8 + KS, :groups]
 
 
 def shards(
@@ -423,7 +444,6 @@
     groups = channels // GS
     wide = channels * lax.axis_size("tp")
     rows = groups // PER
-    packed_rows = groups + 2 * rows + 24
 
     def arr(shape, dtype):
         return jax.ShapeDtypeStruct(shape, dtype)
@@ -500,55 +520,70 @@
         flops=10**8, moved=2 * 10**6,
     )
     sums, bwd, k_short, v_short = lax.optimization_barrier((sums, bwd, k_short, v_short))
-    grad_mixed, grad_qs = call(
-        "grads", functools.partial(grads_kernel, wide), [full_bf, full_bf],
+    grad_mixed, grad_qs, head = call(
+        "grads", functools.partial(grads_kernel, wide),
+        [full_bf, full_bf, arr((PACK, channels), BF16)],
         [summed, mixed, q_short, cotangent, gain2, sums],
     )
     after = shifted(grad_mixed, "ctx", -1)
-    stats, part, qcols = call(
+    tails_q = shifted(head, "ctx", -1)
+    stats, part = call(
         "beside", functools.partial(beside_kernel, wide),
         [
-            arr((groups + 2 * rows, LANES), F32), full_f, arr((8, channels), F32),
+            arr((groups + 2 * rows + 8, LANES), F32), full_f,
         ],
         [
             lengths, summed, cotangent, sums, grad_mixed, grad_qs, gated, before, bwd,
             skip2, q_input, came,
         ],
+        [pltpu.VMEM((8, channels), F32)],
         flops=4 * 10**9, moved=5 * 10**6,
     )
-    grad_ks, grad_vs, tails, packed = call(
+    count = lax.axis_size("ctx")
+    steps = [1 << i for i in range(count.bit_length() - 1)]
+    others = swapped(stats, "ctx", steps[0])
+    grad_ks, grad_vs, tails, last = call(
         "gate", gate_kernel,
-        [
-            full_bf, full_bf, arr((4 * RIM, channels), BF16),
-            arr((packed_rows, LANES), F32),
-        ],
-        [
-            lengths, part, after, bwd, k_short, v_short, grad_qs, k_input, v_input, came,
-            stats, qcols,
-        ],
-        [pltpu.VMEM((24, channels), F32)], flops=10**9, moved=5 * 10**6,
-    )
-    tails = shifted(tails, "ctx", -1)
-    grad_q, grad_k, grad_v, normed = call(
-        "mains", functools.partial(mains_kernel, wide), [full_bf] * 4,
-        [lengths, taps, grad_qs, grad_ks, grad_vs, tails, summed, gain2, sums], flops=10**9, moved=5 * 10**6,
-    )
-    outs = (grad_q, grad_k, grad_v, normed)
-    count = lax.axis_size("ctx")
-    step = 1
-    while 2 * step < count:
-        packed = packed + swapped(packed, "ctx", step)
-        step *= 2
-    packed, *outs = lax.optimization_barrier((packed, *outs))
-    grad_q, grad_k, grad_v, normed = outs
-    other = swapped(packed, "ctx", step)
+        [full_bf, full_bf, arr((2 * RIM, channels), BF16), arr((16, LANES), F32)],
+        [lengths, part, after, bwd, k_short, v_short, k_input, v_input, came],
+        [pltpu.VMEM((16, channels), F32)], flops=10**9, moved=5 * 10**6,
+    )
+    others, last = lax.optimization_barrier((others, last))
+    outs = []
+    for i, step in enumerate(steps):
+        if i:
+            last, *outs = lax.optimization_barrier((last + other, *outs))
+        other = swapped(last, "ctx", step)
+        if i == 0:
+            stats = stats + others
+            others = swapped(stats, "ctx", steps[1])
+            tails = shifted(tails, "ctx", -1)
+            outs += call(
+                "main_q", functools.partial(main_q_kernel, wide), [full_bf] * 2,
+                [lengths, taps, grad_qs, tails_q, summed, gain2, sums],
+            )
+        if i == 1:
+            outs += call(
+                "main_k", functools.partial(main_kernel, 1, 0), [full_bf],
+                [lengths, taps, grad_ks, tails],
+            )
+        if i == 2:
+            outs += call(
+                "main_v", functools.partial(main_kernel, 2, RIM), [full_bf],
+                [lengths, taps, grad_vs, tails],
+            )
+        if 0 < i < len(steps) - 1:
+            others, *outs = lax.optimization_barrier((others, *outs))
+            stats = stats + others
+            others = swapped(stats, "ctx", steps[i + 1])
+    grad_q, normed, grad_k, grad_v = outs
     grad_short, grad_long, grad_skip, grad_gain = call(
         "unpack", unpack_kernel,
         [
             arr((3, KS, groups), F32), arr((groups, K), F32),
             arr((rows, LANES), F32), arr((rows, LANES), F32),
         ],
-        [packed, other],
+        [stats, others, last, other],
     )
     return (
         normed, grad_q, grad_k, grad_v, jnp.transpose(grad_short, (0, 2, 1)), grad_long,

time: 57.4 us -> 59.7 us (1.040)
  waiting for transfers between devices: 14 us -> 7.39 us
  starting transfers between devices: 13.2 us -> 19.6 us
  Pallas kernels: 28.2 us -> 30.7 us
    ppermute x5 -> x8, waiting for transfers between devices: 9.49 us -> 3.2 us  [swapped(): lax.ppermute(x, axis, [(i, i ^ step) for i in range(lax.axis_size(axis))])]
    ppermute x5 -> x8, starting transfers between devices: 1.77 us -> 8.02 us  [swapped(): lax.ppermute(x, axis, [(i, i ^ step) for i in range(lax.axis_size(axis))])]
    pallas_call x11 -> x13, Pallas kernels: 28.2 us -> 30.7 us  [call(): pl.pallas_call(kernel, out_shape=outs, in_specs=[far_off] * len(ins) if h...]
    ppermute x4 -> x5, waiting for transfers between devices: 4.49 us -> 4.18 us  [shifted(): return lax.ppermute(x, axis, [(i, (i + by) % count) for i in range(count)])]
    ppermute x4 -> x5, starting transfers between devices: 11.5 us -> 11.6 us  [shifted(): return lax.ppermute(x, axis, [(i, (i + by) % count) for i in range(count)])]
  transfers between devices with their start and end apart: 9 -> 13, of which waited for: 6 -> 5; matrix products, arithmetic and copies ran while one was open for 0% -> 0% of each run, Pallas kernels for 32% -> 41%
where the time goes in v6:
time: 59.7 us; the launch traced here: 59.4 us
  Pallas kernels  30.7 us (51%)
  starting transfers between devices  19.6 us (33%)
  waiting for transfers between devices  7.39 us (12%)
  between operations  0.93 us (2%)
  local copies, waits for them, and re-layouts  0.78 us (1%)
    pallas_call x13, Pallas kernels, call(): pl.pallas_call(kernel, out_shape=outs, in_specs=[far_off] * len(ins) if h...  30.7 us
    ppermute x5, starting transfers between devices, shifted(): return lax.ppermute(x, axis, [(i, (i + by) % count) for i in range(count)])  11.6 us
    ppermute x8, starting transfers between devices, swapped(): lax.ppermute(x, axis, [(i, i ^ step) for i in range(lax.axis_size(axis))])  8.02 us
    ppermute x5, waiting for transfers between devices, shifted(): return lax.ppermute(x, axis, [(i, (i + by) % count) for i in range(count)])  4.18 us
    ppermute x8, waiting for transfers between devices, swapped(): lax.ppermute(x, axis, [(i, i ^ step) for i in range(lax.axis_size(axis))])  3.2 us
  transfers between devices with their start and end apart: 13, of which 5 were waited for; matrix products, arithmetic and copies ran while one was open for 0% of the time, Pallas kernels for 41%

profile of v6, /device:TPU:0, one launch (start us, length us, event | category | flops | bytes accessed | tf_op | source)
XLA Modules:
  0.0 59.4 jit_solution(15231937147680807112)
XLA Ops:
  0.7 3.2 %first.1 = (f32[24,1024]{1,0:T(8,128)}, bf16[160,1024]{1,0:T(8,128)(2,1)}, bf16[16,1024]{1,0:T(8,128)(2,1)}) custom-call(s32[8]{0:T(128)} %len_ref.15, bf16[3,7,64]{2,1,0:T(8,128)(2,1)} %bitcast.12, bf16[128,1024]{1,0:T(8,128)(2,1)} %q_ref.5, bf16[128,1024]{1,0:T(8,128)(2,1)} %k_ref.5, bf16[128,1024]{1,0:T(8,128)(2,1)} %v_ref.5), custom_call_target="tpu_custom_call" | custom-call | flops 100000000 | bytes 1000000 | tf_op jit(solution)/shard_map/first/pallas_call | solution.py:459
  3.9 3.0 %collective-permute-start = (bf16[160,1024]{1,0:T(8,128)(2,1)}, bf16[160,1024]{1,0:T(8,128)(2,1)S(1)}, u32[]{:S(2)}, u32[]{:S(2)}) collective-permute-start(bf16[160,1024]{1,0:T(8,128)(2,1)} %get-tuple-element.61.sent_ref), channel_id=1, source_target_pairs={{0,4},{4,8},{8,12},{12,16},{16,20},{20,24},{24,28},{28,0},{1,5},{5... | collective-permute-start | bytes 983048 | tf_op jit(solution)/shard_map/ppermute | solution.py:24
  6.9 1.6 %collective-permute-start.1 = (bf16[16,1024]{1,0:T(8,128)(2,1)}, bf16[16,1024]{1,0:T(8,128)(2,1)S(1)}, u32[]{:S(2)}, u32[]{:S(2)}) collective-permute-start(bf16[16,1024]{1,0:T(8,128)(2,1)} %get-tuple-element.59), channel_id=1, source_target_pairs={{0,8},{4,12},{8,16},{12,20},{16,24},{20,28},{24,0},{28,4},{1,9},{5... | collective-permute-start | bytes 98312 | tf_op jit(solution)/shard_map/ppermute | solution.py:24
  8.5 0.7 %copy-done.10 = bf16[64,128]{1,0:T(8,128)(2,1)S(1)} copy-done((bf16[64,128]{1,0:T(8,128)(2,1)S(1)}, bf16[64,128]{1,0:T(8,128)(2,1)}, u32[]{:S(2)}) %copy-start.10) | copy-done | bytes 16408
  9.2 1.8 %circulants.2.fwd_ref = bf16[128,8192]{1,0:T(8,128)(2,1)S(1)} custom-call(bf16[64,128]{1,0:T(8,128)(2,1)S(1)} %copy-done.10), custom_call_target="tpu_custom_call" | custom-call | flops 1000000000 | bytes 4000000 | tf_op jit(solution)/shard_map/circulants/pallas_call | solution.py:459
  11.0 0.0 copy-start
  11.2 2.9 %current.1 = (f32[128,1024]{1,0:T(8,128)S(1)}, f32[128,1024]{1,0:T(8,128)S(1)}, bf16[128,1024]{1,0:T(8,128)(2,1)S(1)}) custom-call(s32[8]{0:T(128)S(1)} %copy-done.8, bf16[128,1024]{1,0:T(8,128)(2,1)S(1)} %copy-done.4, f32[24,1024]{1,0:T(8,128)S(1)} %copy-done.2, bf16[160,1024]{1,0:T(8,128)(2,1)S(1)} %copy-done.5, bf16[128,8192]{1,0:T(8,128)(2,1)S(1)} %circulants.2.fwd_ref, ...), custom_call_target="tpu_custom_call" | custom-call | flops 1000000000 | bytes 5000000 | tf_op jit(solution)/shard_map/current/pallas_call | solution.py:459
  14.1 4.2 %collective-permute-done.came_ref = bf16[160,1024]{1,0:T(8,128)(2,1)S(1)} collective-permute-done((bf16[160,1024]{1,0:T(8,128)(2,1)}, bf16[160,1024]{1,0:T(8,128)(2,1)S(1)}, u32[]{:S(2)}, u32[]{:S(2)}) %collective-permute-start) | collective-permute-done | bytes 327712 | tf_op jit(solution)/shard_map/ppermute | solution.py:24
  18.3 2.2 %summed.1 = (f32[128,1024]{1,0:T(8,128)S(1)}, bf16[128,1024]{1,0:T(8,128)(2,1)S(1)}, bf16[128,1024]{1,0:T(8,128)(2,1)S(1)}, f32[128,1024]{1,0:T(8,128)S(1)}, f32...) custom-call(s32[8]{0:T(128)S(1)} %copy-done.8, bf16[160,1024]{1,0:T(8,128)(2,1)S(1)} %collective-permute-done.came_ref, ...), custom_call_target="tpu_custom_call" | custom-call | flops 1000000000 | bytes 5000000 | tf_op jit(solution)/shard_map/summed/pallas_call | solution.py:459
  20.5 0.1 collective-permute-start.2
  20.6 1.7 %circulants.3.bwd_ref = bf16[128,8192]{1,0:T(8,128)(2,1)S(1)} custom-call(bf16[64,128]{1,0:T(8,128)(2,1)S(1)} %copy-done.11), custom_call_target="tpu_custom_call" | custom-call | flops 1000000000 | bytes 4000000 | tf_op jit(solution)/shard_map/circulants/pallas_call | solution.py:459
  22.3 1.6 %collective-permute-start.3 = (f32[2,128]{1,0:T(2,128)S(1)}, f32[2,128]{1,0:T(2,128)S(1)}, u32[]{:S(2)}, u32[]{:S(2)}) collective-permute-start(f32[2,128]{1,0:T(2,128)S(1)} %add.18), channel_id=1, source_target_pairs={{0,2},{1,3},{2,0},{3,1},{4,6},{5,7},{6,4},{7,5},{8,10},{9,11},{10,... | collective-permute-start | bytes 3080 | tf_op jit(solution)/shard_map/ppermute | solution.py:28
  23.9 2.0 %gates.1 = (f32[128,1024]{1,0:T(8,128)S(1)}, f32[128,1024]{1,0:T(8,128)S(1)}) custom-call(s32[8]{0:T(128)S(1)} %copy-done.8, bf16[128,1024]{1,0:T(8,128)(2,1)S(1)} %copy-done, bf16[128,1024]{1,0:T(8,128)(2,1)S(1)} %copy-done.1, bf16[160,1024]{1,0:T(8,128)(2,1)S(1)} %collective-permute-done.came_ref, f32[24,1024]{1,0:T(8,128)S(1)} %copy-done.2), custom_call_target="tpu_custom_call" | custom-call | flops 100000000 | bytes 2000000 | tf_op jit(solution)/shard_map/gates/pallas_call | solution.py:459
  25.9 0.1 collective-permute-done.3
  26.0 0.5 grads.1
  26.5 2.1 %collective-permute-start.7 = (bf16[16,1024]{1,0:T(8,128)(2,1)S(1)}, bf16[16,1024]{1,0:T(8,128)(2,1)S(1)}, u32[]{:S(2)}, u32[]{:S(2)}) collective-permute-start(bf16[16,1024]{1,0:T(8,128)(2,1)S(1)} %get-tuple-element.86), channel_id=1, source_target_pairs={{0,28},{4,0},{8,4},{12,8},{16,12},{20,16},{24,20},{28,24},{1,29},{... | collective-permute-start | bytes 98312 | tf_op jit(solution)/shard_map/ppermute | solution.py:24
  28.5 1.1 %collective-permute-start.5 = (bf16[128,1024]{1,0:T(8,128)(2,1)S(1)}, bf16[128,1024]{1,0:T(8,128)(2,1)S(1)}, u32[]{:S(2)}, u32[]{:S(2)}) collective-permute-start(bf16[128,1024]{1,0:T(8,128)(2,1)S(1)} %get-tuple-element.75.gm_ref), channel_id=1, source_target_pairs={{0,28},{4,0},{8,4},{12,8},{16,12},{20,16},{24,20},{28,24},{1,29},{... | collective-permute-start | bytes 786440 | tf_op jit(solution)/shard_map/ppermute | solution.py:24
  29.6 6.2 %beside.1 = (f32[88,128]{1,0:T(8,128)S(1)}, f32[128,1024]{1,0:T(8,128)S(1)}) custom-call(s32[8]{0:T(128)S(1)} %copy-done.8, f32[128,1024]{1,0:T(8,128)S(1)} %get-tuple-element.66.summed_ref, bf16[128,1024]{1,0:T(8,128)(2,1)S(1)} %copy-done.3, f32[2,128]{1,0:T(2,128)S(1)} %add.19.sums_ref, bf16[128,1024]{1,0:T(8,128)(2,1)S(1)} %get-tuple-element.75.gm_ref, ...), custom_call_target="tpu_custom_call" | custom-call | flops 4000000000 | bytes 5000000 | tf_op jit(solution)/shard_map/beside/pallas_call | solution.py:459
  35.8 1.0 %collective-permute-start.4 = (f32[88,128]{1,0:T(8,128)S(1)}, f32[88,128]{1,0:T(8,128)S(1)}, u32[]{:S(2)}, u32[]{:S(2)}) collective-permute-start(f32[88,128]{1,0:T(8,128)S(1)} %get-tuple-element.80), channel_id=1, source_target_pairs={{0,4},{4,0},{8,12},{12,8},{16,20},{20,16},{24,28},{28,24},{1,5},{5... | collective-permute-start | bytes 135176 | tf_op jit(solution)/shard_map/ppermute | solution.py:28
  36.8 3.3 %gate.1 = (bf16[128,1024]{1,0:T(8,128)(2,1)S(1)}, bf16[128,1024]{1,0:T(8,128)(2,1)S(1)}, bf16[16,1024]{1,0:T(8,128)(2,1)S(1)}, f32[16,128]{1,0:T(8,128)S(1)}) custom-call(s32[8]{0:T(128)S(1)} %copy-done.8, f32[128,1024]{1,0:T(8,128)S(1)} %get-tuple-element.81.part_ref, bf16[128,1024]{1,0:T(8,128)(2,1)S(1)} %collective-permute-done.5.after_ref, ...), custom_call_target="tpu_custom_call" | custom-call | flops 1000000000 | bytes 5000000 | tf_op jit(solution)/shard_map/gate/pallas_call | solution.py:459
  40.1 0.4 collective-permute-start.9
  40.5 3.8 %collective-permute-start.10 = (bf16[16,1024]{1,0:T(8,128)(2,1)S(1)}, bf16[16,1024]{1,0:T(8,128)(2,1)S(1)}, u32[]{:S(2)}, u32[]{:S(2)}) collective-permute-start(bf16[16,1024]{1,0:T(8,128)(2,1)S(1)} %get-tuple-element.94), channel_id=1, source_target_pairs={{0,28},{4,0},{8,4},{12,8},{16,12},{20,16},{24,20},{28,24},{1,29},{... | collective-permute-start | bytes 98312 | tf_op jit(solution)/shard_map/ppermute | solution.py:24
  44.3 2.2 %main_q.1 = (bf16[128,1024]{1,0:T(8,128)(2,1)}, bf16[128,1024]{1,0:T(8,128)(2,1)}) custom-call(s32[8]{0:T(128)S(1)} %copy-done.8, f32[24,1024]{1,0:T(8,128)S(1)} %copy-done.2, bf16[128,1024]{1,0:T(8,128)(2,1)S(1)} %get-tuple-element.76.gq_ref.grad_ref, bf16[16,1024]{1,0:T(8,128)(2,1)S(1)} %collective-permute-done.7.tail_ref, ...), custom_call_target="tpu_custom_call" | custom-call | flops 100000000 | bytes 1000000 | tf_op jit(solution)/shard_map/main_q/pallas_call | solution.py:459
  46.5 1.4 %collective-permute-done.6 = f32[16,128]{1,0:T(8,128)S(1)} collective-permute-done((f32[16,128]{1,0:T(8,128)S(1)}, f32[16,128]{1,0:T(8,128)S(1)}, u32[]{:S(2)}, u32[]{:S(2)}) %collective-permute-start.6) | collective-permute-done | bytes 8224 | tf_op jit(solution)/shard_map/ppermute | solution.py:28
  47.9 2.0 %main_k.1 = bf16[128,1024]{1,0:T(8,128)(2,1)} custom-call(s32[8]{0:T(128)S(1)} %copy-done.8, f32[24,1024]{1,0:T(8,128)S(1)} %copy-done.2, bf16[128,1024]{1,0:T(8,128)(2,1)S(1)} %get-tuple-element.93.grad_ref, bf16[16,1024]{1,0:T(8,128)(2,1)S(1)} %collective-permute-done.10.tail_ref), custom_call_target="tpu_custom_call" | custom-call | flops 100000000 | bytes 1000000 | tf_op jit(solution)/shard_map/main_k/pallas_call | solution.py:459
  50.0 0.1 collective-permute-start.11
  50.1 2.5 %collective-permute-start.8 = (f32[16,128]{1,0:T(8,128)S(1)}, f32[16,128]{1,0:T(8,128)S(1)}, u32[]{:S(2)}, u32[]{:S(2)}) collective-permute-start(f32[16,128]{1,0:T(8,128)S(1)} %add.20), channel_id=1, source_target_pairs={{0,8},{4,12},{8,0},{12,4},{16,24},{20,28},{24,16},{28,20},{1,9},{5... | collective-permute-start | bytes 24584 | tf_op jit(solution)/shard_map/ppermute | solution.py:28
  52.6 1.6 %collective-permute-done.8 = f32[16,128]{1,0:T(8,128)S(1)} collective-permute-done((f32[16,128]{1,0:T(8,128)S(1)}, f32[16,128]{1,0:T(8,128)S(1)}, u32[]{:S(2)}, u32[]{:S(2)}) %collective-permute-start.8) | collective-permute-done | bytes 8224 | tf_op jit(solution)/shard_map/ppermute | solution.py:28
  54.2 2.4 %collective-permute-start.12 = (f32[16,128]{1,0:T(8,128)S(1)}, f32[16,128]{1,0:T(8,128)S(1)}, u32[]{:S(2)}, u32[]{:S(2)}) collective-permute-start(f32[16,128]{1,0:T(8,128)S(1)} %add.21.last_ref), channel_id=1, source_target_pairs={{0,16},{4,20},{8,24},{12,28},{16,0},{20,4},{24,8},{28,12},{1,17},{... | collective-permute-start | bytes 24584 | tf_op jit(solution)/shard_map/ppermute | solution.py:28
  56.6 2.0 %main_v.1 = bf16[128,1024]{1,0:T(8,128)(2,1)} custom-call(s32[8]{0:T(128)S(1)} %copy-done.8, f32[24,1024]{1,0:T(8,128)S(1)} %copy-done.2, bf16[128,1024]{1,0:T(8,128)(2,1)S(1)} %get-tuple-element.101.grad_ref, bf16[16,1024]{1,0:T(8,128)(2,1)S(1)} %collective-permute-done.10.tail_ref), custom_call_target="tpu_custom_call" | custom-call | flops 100000000 | bytes 1000000 | tf_op jit(solution)/shard_map/main_v/pallas_call | solution.py:459
  58.7 0.1 collective-permute-done.12.last2_ref
  58.8 0.6 %unpack.1 = (f32[3,7,64]{2,1,0:T(8,128)}, f32[64,128]{1,0:T(8,128)}, f32[8,128]{1,0:T(8,128)}, f32[8,128]{1,0:T(8,128)}) custom-call(f32[88,128]{1,0:T(8,128)S(1)} %add.23.stats_ref, f32[88,128]{1,0:T(8,128)S(1)} %collective-permute-done.11.stats2_ref, f32[16,128]{1,0:T(8,128)S(1)} %add.21.last_ref, f32[16,128]{1,0:T(8,128)S(1)} %collective-permute-done.12.last2_ref), custom_call_target="tpu_custom_call" | custom-call | flops 100000000 | bytes 1000000 | tf_op jit(solution)/shard_map/unpack/pallas_call | solution.py:459
  (37 shorter events, 0.1 us)
Async XLA Ops:
  0.6 10.5 %copy-start.4 = (bf16[128,1024]{1,0:T(8,128)(2,1)S(1)}, bf16[128,1024]{1,0:T(8,128)(2,1)}, u32[]{:S(2)}) copy-start(bf16[128,1024]{1,0:T(8,128)(2,1)} %q_ref.5) | copy-start | bytes 786436
  0.6 10.5 %copy-start.8 = (s32[8]{0:T(128)S(1)}, s32[8]{0:T(128)}, u32[]{:S(2)}) copy-start(s32[8]{0:T(128)} %len_ref.15) | copy-start | bytes 100
  0.7 10.5 %copy-start.9 = (f32[1024]{0:T(1024)S(1)}, f32[1024]{0:T(1024)}, u32[]{:S(2)}) copy-start(f32[1024]{0:T(1024)} %param.17) | copy-start | bytes 12292
  3.9 7.2 %copy-start.2 = (f32[24,1024]{1,0:T(8,128)S(1)}, f32[24,1024]{1,0:T(8,128)}, u32[]{:S(2)}) copy-start(f32[24,1024]{1,0:T(8,128)} %get-tuple-element.60.taps_ref) | copy-start | bytes 294916
  3.9 7.2 %copy-start.5 = (bf16[160,1024]{1,0:T(8,128)(2,1)S(1)}, bf16[160,1024]{1,0:T(8,128)(2,1)}, u32[]{:S(2)}) copy-start(bf16[160,1024]{1,0:T(8,128)(2,1)} %get-tuple-element.61.sent_ref) | copy-start | bytes 983044
  3.9 14.3 %collective-permute-start = (bf16[160,1024]{1,0:T(8,128)(2,1)}, bf16[160,1024]{1,0:T(8,128)(2,1)S(1)}, u32[]{:S(2)}, u32[]{:S(2)}) collective-permute-start(bf16[160,1024]{1,0:T(8,128)(2,1)} %get-tuple-element.61.sent_ref), channel_id=1, source_target_pairs={{0,4},{4,8},{8,12},{12,16},{16,20},{20,24},{24,28},{28,0},{1,5},{5... | collective-permute-start | bytes 983048 | tf_op jit(solution)/shard_map/ppermute | solution.py:24
  6.9 7.1 %collective-permute-start.1 = (bf16[16,1024]{1,0:T(8,128)(2,1)}, bf16[16,1024]{1,0:T(8,128)(2,1)S(1)}, u32[]{:S(2)}, u32[]{:S(2)}) collective-permute-start(bf16[16,1024]{1,0:T(8,128)(2,1)} %get-tuple-element.59), channel_id=1, source_target_pairs={{0,8},{4,12},{8,16},{12,20},{16,24},{20,28},{24,0},{28,4},{1,9},{5... | collective-permute-start | bytes 98312 | tf_op jit(solution)/shard_map/ppermute | solution.py:24
  8.5 0.7 %copy-start.10 = (bf16[64,128]{1,0:T(8,128)(2,1)S(1)}, bf16[64,128]{1,0:T(8,128)(2,1)}, u32[]{:S(2)}) copy-start(bf16[64,128]{1,0:T(8,128)(2,1)} %long_ref.1) | copy-start | bytes 49156
  11.0 7.2 %copy-start = (bf16[128,1024]{1,0:T(8,128)(2,1)S(1)}, bf16[128,1024]{1,0:T(8,128)(2,1)}, u32[]{:S(2)}) copy-start(bf16[128,1024]{1,0:T(8,128)(2,1)} %k_ref.5) | copy-start | bytes 786436
  11.1 7.2 %copy-start.1 = (bf16[128,1024]{1,0:T(8,128)(2,1)S(1)}, bf16[128,1024]{1,0:T(8,128)(2,1)}, u32[]{:S(2)}) copy-start(bf16[128,1024]{1,0:T(8,128)(2,1)} %v_ref.5) | copy-start | bytes 786436
  11.1 7.2 %copy-start.3 = (bf16[128,1024]{1,0:T(8,128)(2,1)S(1)}, bf16[128,1024]{1,0:T(8,128)(2,1)}, u32[]{:S(2)}) copy-start(bf16[128,1024]{1,0:T(8,128)(2,1)} %cot_ref.5) | copy-start | bytes 786436
  11.1 7.2 %copy-start.6 = (bf16[128,1024]{1,0:T(8,128)(2,1)S(1)}, bf16[128,1024]{1,0:T(8,128)(2,1)}, u32[]{:S(2)}) copy-start(bf16[128,1024]{1,0:T(8,128)(2,1)} %resid_ref.1) | copy-start | bytes 786436
  11.1 7.2 %copy-start.7 = (f32[1024]{0:T(1024)S(1)}, f32[1024]{0:T(1024)}, u32[]{:S(2)}) copy-start(f32[1024]{0:T(1024)} %param.18) | copy-start | bytes 12292
  18.3 2.3 %copy-start.11 = (bf16[64,128]{1,0:T(8,128)(2,1)S(1)}, bf16[64,128]{1,0:T(8,128)(2,1)}, u32[]{:S(2)}) copy-start(bf16[64,128]{1,0:T(8,128)(2,1)} %long_ref.1) | copy-start | bytes 49156
  20.5 1.8 %collective-permute-start.2 = (f32[2,128]{1,0:T(2,128)S(1)}, f32[2,128]{1,0:T(2,128)S(1)}, u32[]{:S(2)}, u32[]{:S(2)}) collective-permute-start(f32[2,128]{1,0:T(2,128)S(1)} %get-tuple-element.67), channel_id=1, source_target_pairs={{0,1},{1,0},{2,3},{3,2},{4,5},{5,4},{6,7},{7,6},{8,9},{9,8},{10,11... | collective-permute-start | bytes 3080 | tf_op jit(solution)/shard_map/ppermute | solution.py:28
  22.3 3.6 %collective-permute-start.3 = (f32[2,128]{1,0:T(2,128)S(1)}, f32[2,128]{1,0:T(2,128)S(1)}, u32[]{:S(2)}, u32[]{:S(2)}) collective-permute-start(f32[2,128]{1,0:T(2,128)S(1)} %add.18), channel_id=1, source_target_pairs={{0,2},{1,3},{2,0},{3,1},{4,6},{5,7},{6,4},{7,5},{8,10},{9,11},{10,... | collective-permute-start | bytes 3080 | tf_op jit(solution)/shard_map/ppermute | solution.py:28
  26.5 17.8 %collective-permute-start.7 = (bf16[16,1024]{1,0:T(8,128)(2,1)S(1)}, bf16[16,1024]{1,0:T(8,128)(2,1)S(1)}, u32[]{:S(2)}, u32[]{:S(2)}) collective-permute-start(bf16[16,1024]{1,0:T(8,128)(2,1)S(1)} %get-tuple-element.86), channel_id=1, source_target_pairs={{0,28},{4,0},{8,4},{12,8},{16,12},{20,16},{24,20},{28,24},{1,29},{... | collective-permute-start | bytes 98312 | tf_op jit(solution)/shard_map/ppermute | solution.py:24
  28.5 8.3 %collective-permute-start.5 = (bf16[128,1024]{1,0:T(8,128)(2,1)S(1)}, bf16[128,1024]{1,0:T(8,128)(2,1)S(1)}, u32[]{:S(2)}, u32[]{:S(2)}) collective-permute-start(bf16[128,1024]{1,0:T(8,128)(2,1)S(1)} %get-tuple-element.75.gm_ref), channel_id=1, source_target_pairs={{0,28},{4,0},{8,4},{12,8},{16,12},{20,16},{24,20},{28,24},{1,29},{... | collective-permute-start | bytes 786440 | tf_op jit(solution)/shard_map/ppermute | solution.py:24
  35.8 4.2 %collective-permute-start.4 = (f32[88,128]{1,0:T(8,128)S(1)}, f32[88,128]{1,0:T(8,128)S(1)}, u32[]{:S(2)}, u32[]{:S(2)}) collective-permute-start(f32[88,128]{1,0:T(8,128)S(1)} %get-tuple-element.80), channel_id=1, source_target_pairs={{0,4},{4,0},{8,12},{12,8},{16,20},{20,16},{24,28},{28,24},{1,5},{5... | collective-permute-start | bytes 135176 | tf_op jit(solution)/shard_map/ppermute | solution.py:28
  40.1 9.9 %collective-permute-start.9 = (f32[88,128]{1,0:T(8,128)S(1)}, f32[88,128]{1,0:T(8,128)S(1)}, u32[]{:S(2)}, u32[]{:S(2)}) collective-permute-start(f32[88,128]{1,0:T(8,128)S(1)} %add.22), channel_id=1, source_target_pairs={{0,8},{4,12},{8,0},{12,4},{16,24},{20,28},{24,16},{28,20},{1,9},{5... | collective-permute-start | bytes 135176 | tf_op jit(solution)/shard_map/ppermute | solution.py:28
  40.5 7.4 %collective-permute-start.10 = (bf16[16,1024]{1,0:T(8,128)(2,1)S(1)}, bf16[16,1024]{1,0:T(8,128)(2,1)S(1)}, u32[]{:S(2)}, u32[]{:S(2)}) collective-permute-start(bf16[16,1024]{1,0:T(8,128)(2,1)S(1)} %get-tuple-element.94), channel_id=1, source_target_pairs={{0,28},{4,0},{8,4},{12,8},{16,12},{20,16},{24,20},{28,24},{1,29},{... | collective-permute-start | bytes 98312 | tf_op jit(solution)/shard_map/ppermute | solution.py:24
  44.3 3.7 %collective-permute-start.6 = (f32[16,128]{1,0:T(8,128)S(1)}, f32[16,128]{1,0:T(8,128)S(1)}, u32[]{:S(2)}, u32[]{:S(2)}) collective-permute-start(f32[16,128]{1,0:T(8,128)S(1)} %get-tuple-element.85), channel_id=1, source_target_pairs={{0,4},{4,0},{8,12},{12,8},{16,20},{20,16},{24,28},{28,24},{1,5},{5... | collective-permute-start | bytes 24584 | tf_op jit(solution)/shard_map/ppermute | solution.py:28
  50.0 8.8 %collective-permute-start.11 = (f32[88,128]{1,0:T(8,128)S(1)}, f32[88,128]{1,0:T(8,128)S(1)}, u32[]{:S(2)}, u32[]{:S(2)}) collective-permute-start(f32[88,128]{1,0:T(8,128)S(1)} %add.23.stats_ref), channel_id=1, source_target_pairs={{0,16},{4,20},{8,24},{12,28},{16,0},{20,4},{24,8},{28,12},{1,17},{... | collective-permute-start | bytes 135176 | tf_op jit(solution)/shard_map/ppermute | solution.py:28
  50.1 4.1 %collective-permute-start.8 = (f32[16,128]{1,0:T(8,128)S(1)}, f32[16,128]{1,0:T(8,128)S(1)}, u32[]{:S(2)}, u32[]{:S(2)}) collective-permute-start(f32[16,128]{1,0:T(8,128)S(1)} %add.20), channel_id=1, source_target_pairs={{0,8},{4,12},{8,0},{12,4},{16,24},{20,28},{24,16},{28,20},{1,9},{5... | collective-permute-start | bytes 24584 | tf_op jit(solution)/shard_map/ppermute | solution.py:28
  54.2 4.5 %collective-permute-start.12 = (f32[16,128]{1,0:T(8,128)S(1)}, f32[16,128]{1,0:T(8,128)S(1)}, u32[]{:S(2)}, u32[]{:S(2)}) collective-permute-start(f32[16,128]{1,0:T(8,128)S(1)} %add.21.last_ref), channel_id=1, source_target_pairs={{0,16},{4,20},{8,24},{12,28},{16,0},{20,4},{24,8},{28,12},{1,17},{... | collective-permute-start | bytes 24584 | tf_op jit(solution)/shard_map/ppermute | solution.py:28

commit v7 on v6

--- a/solution.py
+++ b/solution.py
@@ -398,14 +398,15 @@
     return grad.astype(BF16)
 
 
-def main_kernel(which, at, len_ref, taps_ref, grad_ref, tail_ref, out_ref):
+def main_kv_kernel(len_ref, taps_ref, gks_ref, gvs_ref, tail_ref, ok_ref, ov_ref):
     pos = positions(len_ref, first_row() + iota((K + RIM, LANES), 0))
 
     def body(q):
         ls = lanes_of(q)
-        out_ref[:, ls] = back_short(which, at, pos, ls, taps_ref, grad_ref, tail_ref)
-
-    each_chunk(grad_ref.shape[1], body)
+        ok_ref[:, ls] = back_short(1, 0, pos, ls, taps_ref, gks_ref, tail_ref)
+        ov_ref[:, ls] = back_short(2, RIM, pos, ls, taps_ref, gvs_ref, tail_ref)
+
+    each_chunk(gks_ref.shape[1], body)
 
 
 def main_q_kernel(
@@ -549,34 +550,24 @@
         [pltpu.VMEM((16, channels), F32)], flops=10**9, moved=5 * 10**6,
     )
     others, last = lax.optimization_barrier((others, last))
-    outs = []
     for i, step in enumerate(steps):
-        if i:
-            last, *outs = lax.optimization_barrier((last + other, *outs))
         other = swapped(last, "ctx", step)
         if i == 0:
             stats = stats + others
             others = swapped(stats, "ctx", steps[1])
             tails = shifted(tails, "ctx", -1)
-            outs += call(
+            grad_q, normed = call(
                 "main_q", functools.partial(main_q_kernel, wide), [full_bf] * 2,
                 [lengths, taps, grad_qs, tails_q, summed, gain2, sums],
             )
-        if i == 1:
-            outs += call(
-                "main_k", functools.partial(main_kernel, 1, 0), [full_bf],
-                [lengths, taps, grad_ks, tails],
-            )
-        if i == 2:
-            outs += call(
-                "main_v", functools.partial(main_kernel, 2, RIM), [full_bf],
-                [lengths, taps, grad_vs, tails],
-            )
-        if 0 < i < len(steps) - 1:
-            others, *outs = lax.optimization_barrier((others, *outs))
-            stats = stats + others
+            last, grad_q, normed = lax.optimization_barrier((last + other, grad_q, normed))
+        elif i < len(steps) - 1:
+            last, stats, tails = lax.optimization_barrier((last + other, stats + others, tails))
             others = swapped(stats, "ctx", steps[i + 1])
-    grad_q, normed, grad_k, grad_v = outs
+    grad_ks, grad_vs, last = lax.optimization_barrier((grad_ks, grad_vs, last))
+    grad_k, grad_v = call(
+        "main_kv", main_kv_kernel, [full_bf] * 2, [lengths, taps, grad_ks, grad_vs, tails]
+    )
     grad_short, grad_long, grad_skip, grad_gain = call(
         "unpack", unpack_kernel,
         [

time: 59.7 us -> 58.4 us (0.978)
  starting transfers between devices: 19.6 us -> 17.6 us
  waiting for transfers between devices: 7.39 us -> 9.31 us
  Pallas kernels: 30.7 us -> 29.5 us
    ppermute x8, starting transfers between devices: 8.02 us -> 6.05 us  [swapped(): lax.ppermute(x, axis, [(i, i ^ step) for i in range(lax.axis_size(axis))])]
    ppermute x8, waiting for transfers between devices: 3.2 us -> 5.13 us  [swapped(): lax.ppermute(x, axis, [(i, i ^ step) for i in range(lax.axis_size(axis))])]
    pallas_call x13 -> x12, Pallas kernels: 30.7 us -> 29.5 us  [call(): pl.pallas_call(kernel, out_shape=outs, in_specs=[far_off] * len(ins) if h...]
  transfers between devices with their start and end apart: 13 -> 13, of which waited for: 5 -> 4; matrix products, arithmetic and copies ran while one was open for 0% -> 0% of each run, Pallas kernels for 41% -> 39%
where the time goes in v7:
time: 58.4 us; the launch traced here: 58.1 us
  Pallas kernels  29.5 us (51%)
  starting transfers between devices  17.6 us (30%)
  waiting for transfers between devices  9.31 us (16%)
  between operations  0.93 us (2%)
  local copies, waits for them, and re-layouts  0.78 us (1%)
    pallas_call x12, Pallas kernels, call(): pl.pallas_call(kernel, out_shape=outs, in_specs=[far_off] * len(ins) if h...  29.5 us
    ppermute x5, starting transfers between devices, shifted(): return lax.ppermute(x, axis, [(i, (i + by) % count) for i in range(count)])  11.6 us
    ppermute x8, starting transfers between devices, swapped(): lax.ppermute(x, axis, [(i, i ^ step) for i in range(lax.axis_size(axis))])  6.05 us
    ppermute x8, waiting for transfers between devices, swapped(): lax.ppermute(x, axis, [(i, i ^ step) for i in range(lax.axis_size(axis))])  5.13 us
    ppermute x5, waiting for transfers between devices, shifted(): return lax.ppermute(x, axis, [(i, (i + by) % count) for i in range(count)])  4.18 us
  transfers between devices with their start and end apart: 13, of which 4 were waited for; matrix products, arithmetic and copies ran while one was open for 0% of the time, Pallas kernels for 39%

profile of v7, /device:TPU:0, one launch (start us, length us, event | category | flops | bytes accessed | tf_op | source)
XLA Modules:
  0.0 58.1 jit_solution(10260009299597760854)
XLA Ops:
  0.7 3.2 %first.1 = (f32[24,1024]{1,0:T(8,128)}, bf16[160,1024]{1,0:T(8,128)(2,1)}, bf16[16,1024]{1,0:T(8,128)(2,1)}) custom-call(s32[8]{0:T(128)} %len_ref.13, bf16[3,7,64]{2,1,0:T(8,128)(2,1)} %bitcast.12, bf16[128,1024]{1,0:T(8,128)(2,1)} %q_ref.5, bf16[128,1024]{1,0:T(8,128)(2,1)} %k_ref.5, bf16[128,1024]{1,0:T(8,128)(2,1)} %v_ref.5), custom_call_target="tpu_custom_call" | custom-call | flops 100000000 | bytes 1000000 | tf_op jit(solution)/shard_map/first/pallas_call | solution.py:460
  3.9 0.0 copy-start.2
  3.9 3.0 %collective-permute-start = (bf16[160,1024]{1,0:T(8,128)(2,1)}, bf16[160,1024]{1,0:T(8,128)(2,1)S(1)}, u32[]{:S(2)}, u32[]{:S(2)}) collective-permute-start(bf16[160,1024]{1,0:T(8,128)(2,1)} %get-tuple-element.61.sent_ref), channel_id=1, source_target_pairs={{0,4},{4,8},{8,12},{12,16},{16,20},{20,24},{24,28},{28,0},{1,5},{5... | collective-permute-start | bytes 983048 | tf_op jit(solution)/shard_map/ppermute | solution.py:24
  7.0 1.6 %collective-permute-start.1 = (bf16[16,1024]{1,0:T(8,128)(2,1)}, bf16[16,1024]{1,0:T(8,128)(2,1)S(1)}, u32[]{:S(2)}, u32[]{:S(2)}) collective-permute-start(bf16[16,1024]{1,0:T(8,128)(2,1)} %get-tuple-element.59), channel_id=1, source_target_pairs={{0,8},{4,12},{8,16},{12,20},{16,24},{20,28},{24,0},{28,4},{1,9},{5... | collective-permute-start | bytes 98312 | tf_op jit(solution)/shard_map/ppermute | solution.py:24
  8.5 0.7 %copy-done.10 = bf16[64,128]{1,0:T(8,128)(2,1)S(1)} copy-done((bf16[64,128]{1,0:T(8,128)(2,1)S(1)}, bf16[64,128]{1,0:T(8,128)(2,1)}, u32[]{:S(2)}) %copy-start.10) | copy-done | bytes 16408
  9.2 1.8 %circulants.2.fwd_ref = bf16[128,8192]{1,0:T(8,128)(2,1)S(1)} custom-call(bf16[64,128]{1,0:T(8,128)(2,1)S(1)} %copy-done.10), custom_call_target="tpu_custom_call" | custom-call | flops 1000000000 | bytes 4000000 | tf_op jit(solution)/shard_map/circulants/pallas_call | solution.py:460
  11.1 0.0 copy-start
  11.1 0.0 copy-start.6
  11.1 0.0 copy-start.7
  11.2 2.9 %current.1 = (f32[128,1024]{1,0:T(8,128)S(1)}, f32[128,1024]{1,0:T(8,128)S(1)}, bf16[128,1024]{1,0:T(8,128)(2,1)S(1)}) custom-call(s32[8]{0:T(128)S(1)} %copy-done.8, bf16[128,1024]{1,0:T(8,128)(2,1)S(1)} %copy-done.4, f32[24,1024]{1,0:T(8,128)S(1)} %copy-done.2, bf16[160,1024]{1,0:T(8,128)(2,1)S(1)} %copy-done.5, bf16[128,8192]{1,0:T(8,128)(2,1)S(1)} %circulants.2.fwd_ref, ...), custom_call_target="tpu_custom_call" | custom-call | flops 1000000000 | bytes 5000000 | tf_op jit(solution)/shard_map/current/pallas_call | solution.py:460
  14.1 4.2 %collective-permute-done.came_ref = bf16[160,1024]{1,0:T(8,128)(2,1)S(1)} collective-permute-done((bf16[160,1024]{1,0:T(8,128)(2,1)}, bf16[160,1024]{1,0:T(8,128)(2,1)S(1)}, u32[]{:S(2)}, u32[]{:S(2)}) %collective-permute-start) | collective-permute-done | bytes 327712 | tf_op jit(solution)/shard_map/ppermute | solution.py:24
  18.3 2.2 %summed.1 = (f32[128,1024]{1,0:T(8,128)S(1)}, bf16[128,1024]{1,0:T(8,128)(2,1)S(1)}, bf16[128,1024]{1,0:T(8,128)(2,1)S(1)}, f32[128,1024]{1,0:T(8,128)S(1)}, f32...) custom-call(s32[8]{0:T(128)S(1)} %copy-done.8, bf16[160,1024]{1,0:T(8,128)(2,1)S(1)} %collective-permute-done.came_ref, ...), custom_call_target="tpu_custom_call" | custom-call | flops 1000000000 | bytes 5000000 | tf_op jit(solution)/shard_map/summed/pallas_call | solution.py:460
  20.5 0.1 collective-permute-start.2
  20.6 1.7 %circulants.3.bwd_ref = bf16[128,8192]{1,0:T(8,128)(2,1)S(1)} custom-call(bf16[64,128]{1,0:T(8,128)(2,1)S(1)} %copy-done.11), custom_call_target="tpu_custom_call" | custom-call | flops 1000000000 | bytes 4000000 | tf_op jit(solution)/shard_map/circulants/pallas_call | solution.py:460
  22.3 1.6 %collective-permute-start.3 = (f32[2,128]{1,0:T(2,128)S(1)}, f32[2,128]{1,0:T(2,128)S(1)}, u32[]{:S(2)}, u32[]{:S(2)}) collective-permute-start(f32[2,128]{1,0:T(2,128)S(1)} %add.18), channel_id=1, source_target_pairs={{0,2},{1,3},{2,0},{3,1},{4,6},{5,7},{6,4},{7,5},{8,10},{9,11},{10,... | collective-permute-start | bytes 3080 | tf_op jit(solution)/shard_map/ppermute | solution.py:28
  23.9 2.0 %gates.1 = (f32[128,1024]{1,0:T(8,128)S(1)}, f32[128,1024]{1,0:T(8,128)S(1)}) custom-call(s32[8]{0:T(128)S(1)} %copy-done.8, bf16[128,1024]{1,0:T(8,128)(2,1)S(1)} %copy-done, bf16[128,1024]{1,0:T(8,128)(2,1)S(1)} %copy-done.1, bf16[160,1024]{1,0:T(8,128)(2,1)S(1)} %collective-permute-done.came_ref, f32[24,1024]{1,0:T(8,128)S(1)} %copy-done.2), custom_call_target="tpu_custom_call" | custom-call | flops 100000000 | bytes 2000000 | tf_op jit(solution)/shard_map/gates/pallas_call | solution.py:460
  25.9 0.1 collective-permute-done.3
  26.0 0.5 grads.1
  26.5 2.1 %collective-permute-start.7 = (bf16[16,1024]{1,0:T(8,128)(2,1)S(1)}, bf16[16,1024]{1,0:T(8,128)(2,1)S(1)}, u32[]{:S(2)}, u32[]{:S(2)}) collective-permute-start(bf16[16,1024]{1,0:T(8,128)(2,1)S(1)} %get-tuple-element.86), channel_id=1, source_target_pairs={{0,28},{4,0},{8,4},{12,8},{16,12},{20,16},{24,20},{28,24},{1,29},{... | collective-permute-start | bytes 98312 | tf_op jit(solution)/shard_map/ppermute | solution.py:24
  28.5 1.1 %collective-permute-start.5 = (bf16[128,1024]{1,0:T(8,128)(2,1)S(1)}, bf16[128,1024]{1,0:T(8,128)(2,1)S(1)}, u32[]{:S(2)}, u32[]{:S(2)}) collective-permute-start(bf16[128,1024]{1,0:T(8,128)(2,1)S(1)} %get-tuple-element.75.gm_ref), channel_id=1, source_target_pairs={{0,28},{4,0},{8,4},{12,8},{16,12},{20,16},{24,20},{28,24},{1,29},{... | collective-permute-start | bytes 786440 | tf_op jit(solution)/shard_map/ppermute | solution.py:24
  29.7 6.2 %beside.1 = (f32[88,128]{1,0:T(8,128)S(1)}, f32[128,1024]{1,0:T(8,128)S(1)}) custom-call(s32[8]{0:T(128)S(1)} %copy-done.8, f32[128,1024]{1,0:T(8,128)S(1)} %get-tuple-element.66.summed_ref, bf16[128,1024]{1,0:T(8,128)(2,1)S(1)} %copy-done.3, f32[2,128]{1,0:T(2,128)S(1)} %add.19.sums_ref, bf16[128,1024]{1,0:T(8,128)(2,1)S(1)} %get-tuple-element.75.gm_ref, ...), custom_call_target="tpu_custom_call" | custom-call | flops 4000000000 | bytes 5000000 | tf_op jit(solution)/shard_map/beside/pallas_call | solution.py:460
  35.8 1.0 %collective-permute-start.4 = (f32[88,128]{1,0:T(8,128)S(1)}, f32[88,128]{1,0:T(8,128)S(1)}, u32[]{:S(2)}, u32[]{:S(2)}) collective-permute-start(f32[88,128]{1,0:T(8,128)S(1)} %get-tuple-element.80), channel_id=1, source_target_pairs={{0,4},{4,0},{8,12},{12,8},{16,20},{20,16},{24,28},{28,24},{1,5},{5... | collective-permute-start | bytes 135176 | tf_op jit(solution)/shard_map/ppermute | solution.py:28
  36.8 3.3 %gate.1 = (bf16[128,1024]{1,0:T(8,128)(2,1)S(1)}, bf16[128,1024]{1,0:T(8,128)(2,1)S(1)}, bf16[16,1024]{1,0:T(8,128)(2,1)S(1)}, f32[16,128]{1,0:T(8,128)S(1)}) custom-call(s32[8]{0:T(128)S(1)} %copy-done.8, f32[128,1024]{1,0:T(8,128)S(1)} %get-tuple-element.81.part_ref, bf16[128,1024]{1,0:T(8,128)(2,1)S(1)} %collective-permute-done.5.after_ref, ...), custom_call_target="tpu_custom_call" | custom-call | flops 1000000000 | bytes 5000000 | tf_op jit(solution)/shard_map/gate/pallas_call | solution.py:460
  40.1 0.4 collective-permute-start.9
  40.5 3.8 %collective-permute-start.10 = (bf16[16,1024]{1,0:T(8,128)(2,1)S(1)}, bf16[16,1024]{1,0:T(8,128)(2,1)S(1)}, u32[]{:S(2)}, u32[]{:S(2)}) collective-permute-start(bf16[16,1024]{1,0:T(8,128)(2,1)S(1)} %get-tuple-element.95), channel_id=1, source_target_pairs={{0,28},{4,0},{8,4},{12,8},{16,12},{20,16},{24,20},{28,24},{1,29},{... | collective-permute-start | bytes 98312 | tf_op jit(solution)/shard_map/ppermute | solution.py:24
  44.3 2.2 %main_q.1 = (bf16[128,1024]{1,0:T(8,128)(2,1)}, bf16[128,1024]{1,0:T(8,128)(2,1)}) custom-call(s32[8]{0:T(128)S(1)} %copy-done.8, f32[24,1024]{1,0:T(8,128)S(1)} %copy-done.2, bf16[128,1024]{1,0:T(8,128)(2,1)S(1)} %get-tuple-element.76.gq_ref.grad_ref, bf16[16,1024]{1,0:T(8,128)(2,1)S(1)} %collective-permute-done.7.tail_ref, ...), custom_call_target="tpu_custom_call" | custom-call | flops 100000000 | bytes 1000000 | tf_op jit(solution)/shard_map/main_q/pallas_call | solution.py:460
  46.6 1.4 %collective-permute-done.6 = f32[16,128]{1,0:T(8,128)S(1)} collective-permute-done((f32[16,128]{1,0:T(8,128)S(1)}, f32[16,128]{1,0:T(8,128)S(1)}, u32[]{:S(2)}, u32[]{:S(2)}) %collective-permute-start.6) | collective-permute-done | bytes 8224 | tf_op jit(solution)/shard_map/ppermute | solution.py:28
  48.0 3.6 %collective-permute-done.8 = f32[16,128]{1,0:T(8,128)S(1)} collective-permute-done((f32[16,128]{1,0:T(8,128)S(1)}, f32[16,128]{1,0:T(8,128)S(1)}, u32[]{:S(2)}, u32[]{:S(2)}) %collective-permute-start.8) | collective-permute-done | bytes 8224 | tf_op jit(solution)/shard_map/ppermute | solution.py:28
  51.6 0.6 collective-permute-start.11
  52.2 2.4 %collective-permute-start.12 = (f32[16,128]{1,0:T(8,128)S(1)}, f32[16,128]{1,0:T(8,128)S(1)}, u32[]{:S(2)}, u32[]{:S(2)}) collective-permute-start(f32[16,128]{1,0:T(8,128)S(1)} %add.21.last_ref), channel_id=1, source_target_pairs={{0,16},{4,20},{8,24},{12,28},{16,0},{20,4},{24,8},{28,12},{1,17},{... | collective-permute-start | bytes 24584 | tf_op jit(solution)/shard_map/ppermute | solution.py:28
  54.6 2.9 %main_kv.1 = (bf16[128,1024]{1,0:T(8,128)(2,1)}, bf16[128,1024]{1,0:T(8,128)(2,1)}) custom-call(s32[8]{0:T(128)S(1)} %copy-done.8, f32[24,1024]{1,0:T(8,128)S(1)} %copy-done.2, bf16[128,1024]{1,0:T(8,128)(2,1)S(1)} %get-tuple-element.97.gks_ref, bf16[128,1024]{1,0:T(8,128)(2,1)S(1)} %get-tuple-element.98.gvs_ref, ...), custom_call_target="tpu_custom_call" | custom-call | flops 100000000 | bytes 1000000 | tf_op jit(solution)/shard_map/main_kv/pallas_call | solution.py:460
  57.5 0.6 %unpack.1 = (f32[3,7,64]{2,1,0:T(8,128)}, f32[64,128]{1,0:T(8,128)}, f32[8,128]{1,0:T(8,128)}, f32[8,128]{1,0:T(8,128)}) custom-call(f32[88,128]{1,0:T(8,128)S(1)} %add.23.stats_ref, f32[88,128]{1,0:T(8,128)S(1)} %collective-permute-done.11.stats2_ref, f32[16,128]{1,0:T(8,128)S(1)} %add.21.last_ref, f32[16,128]{1,0:T(8,128)S(1)} %collective-permute-done.12.last2_ref), custom_call_target="tpu_custom_call" | custom-call | flops 100000000 | bytes 1000000 | tf_op jit(solution)/shard_map/unpack/pallas_call | solution.py:460
  (36 shorter events, 0.1 us)
Async XLA Ops:
  0.6 10.5 %copy-start.4 = (bf16[128,1024]{1,0:T(8,128)(2,1)S(1)}, bf16[128,1024]{1,0:T(8,128)(2,1)}, u32[]{:S(2)}) copy-start(bf16[128,1024]{1,0:T(8,128)(2,1)} %q_ref.5) | copy-start | bytes 786436
  0.6 10.5 %copy-start.8 = (s32[8]{0:T(128)S(1)}, s32[8]{0:T(128)}, u32[]{:S(2)}) copy-start(s32[8]{0:T(128)} %len_ref.13) | copy-start | bytes 100
  0.7 10.5 %copy-start.9 = (f32[1024]{0:T(1024)S(1)}, f32[1024]{0:T(1024)}, u32[]{:S(2)}) copy-start(f32[1024]{0:T(1024)} %param.17) | copy-start | bytes 12292
  3.9 7.2 %copy-start.2 = (f32[24,1024]{1,0:T(8,128)S(1)}, f32[24,1024]{1,0:T(8,128)}, u32[]{:S(2)}) copy-start(f32[24,1024]{1,0:T(8,128)} %get-tuple-element.60.taps_ref) | copy-start | bytes 294916
  3.9 7.2 %copy-start.5 = (bf16[160,1024]{1,0:T(8,128)(2,1)S(1)}, bf16[160,1024]{1,0:T(8,128)(2,1)}, u32[]{:S(2)}) copy-start(bf16[160,1024]{1,0:T(8,128)(2,1)} %get-tuple-element.61.sent_ref) | copy-start | bytes 983044
  3.9 14.3 %collective-permute-start = (bf16[160,1024]{1,0:T(8,128)(2,1)}, bf16[160,1024]{1,0:T(8,128)(2,1)S(1)}, u32[]{:S(2)}, u32[]{:S(2)}) collective-permute-start(bf16[160,1024]{1,0:T(8,128)(2,1)} %get-tuple-element.61.sent_ref), channel_id=1, source_target_pairs={{0,4},{4,8},{8,12},{12,16},{16,20},{20,24},{24,28},{28,0},{1,5},{5... | collective-permute-start | bytes 983048 | tf_op jit(solution)/shard_map/ppermute | solution.py:24
  7.0 7.1 %collective-permute-start.1 = (bf16[16,1024]{1,0:T(8,128)(2,1)}, bf16[16,1024]{1,0:T(8,128)(2,1)S(1)}, u32[]{:S(2)}, u32[]{:S(2)}) collective-permute-start(bf16[16,1024]{1,0:T(8,128)(2,1)} %get-tuple-element.59), channel_id=1, source_target_pairs={{0,8},{4,12},{8,16},{12,20},{16,24},{20,28},{24,0},{28,4},{1,9},{5... | collective-permute-start | bytes 98312 | tf_op jit(solution)/shard_map/ppermute | solution.py:24
  8.5 0.7 %copy-start.10 = (bf16[64,128]{1,0:T(8,128)(2,1)S(1)}, bf16[64,128]{1,0:T(8,128)(2,1)}, u32[]{:S(2)}) copy-start(bf16[64,128]{1,0:T(8,128)(2,1)} %long_ref.1) | copy-start | bytes 49156
  11.1 7.2 %copy-start = (bf16[128,1024]{1,0:T(8,128)(2,1)S(1)}, bf16[128,1024]{1,0:T(8,128)(2,1)}, u32[]{:S(2)}) copy-start(bf16[128,1024]{1,0:T(8,128)(2,1)} %k_ref.5) | copy-start | bytes 786436
  11.1 7.2 %copy-start.1 = (bf16[128,1024]{1,0:T(8,128)(2,1)S(1)}, bf16[128,1024]{1,0:T(8,128)(2,1)}, u32[]{:S(2)}) copy-start(bf16[128,1024]{1,0:T(8,128)(2,1)} %v_ref.5) | copy-start | bytes 786436
  11.1 7.2 %copy-start.3 = (bf16[128,1024]{1,0:T(8,128)(2,1)S(1)}, bf16[128,1024]{1,0:T(8,128)(2,1)}, u32[]{:S(2)}) copy-start(bf16[128,1024]{1,0:T(8,128)(2,1)} %cot_ref.5) | copy-start | bytes 786436
  11.1 7.2 %copy-start.6 = (bf16[128,1024]{1,0:T(8,128)(2,1)S(1)}, bf16[128,1024]{1,0:T(8,128)(2,1)}, u32[]{:S(2)}) copy-start(bf16[128,1024]{1,0:T(8,128)(2,1)} %resid_ref.1) | copy-start | bytes 786436
  11.1 7.2 %copy-start.7 = (f32[1024]{0:T(1024)S(1)}, f32[1024]{0:T(1024)}, u32[]{:S(2)}) copy-start(f32[1024]{0:T(1024)} %param.18) | copy-start | bytes 12292
  18.3 2.3 %copy-start.11 = (bf16[64,128]{1,0:T(8,128)(2,1)S(1)}, bf16[64,128]{1,0:T(8,128)(2,1)}, u32[]{:S(2)}) copy-start(bf16[64,128]{1,0:T(8,128)(2,1)} %long_ref.1) | copy-start | bytes 49156
  20.5 1.8 %collective-permute-start.2 = (f32[2,128]{1,0:T(2,128)S(1)}, f32[2,128]{1,0:T(2,128)S(1)}, u32[]{:S(2)}, u32[]{:S(2)}) collective-permute-start(f32[2,128]{1,0:T(2,128)S(1)} %get-tuple-element.67), channel_id=1, source_target_pairs={{0,1},{1,0},{2,3},{3,2},{4,5},{5,4},{6,7},{7,6},{8,9},{9,8},{10,11... | collective-permute-start | bytes 3080 | tf_op jit(solution)/shard_map/ppermute | solution.py:28
  22.3 3.6 %collective-permute-start.3 = (f32[2,128]{1,0:T(2,128)S(1)}, f32[2,128]{1,0:T(2,128)S(1)}, u32[]{:S(2)}, u32[]{:S(2)}) collective-permute-start(f32[2,128]{1,0:T(2,128)S(1)} %add.18), channel_id=1, source_target_pairs={{0,2},{1,3},{2,0},{3,1},{4,6},{5,7},{6,4},{7,5},{8,10},{9,11},{10,... | collective-permute-start | bytes 3080 | tf_op jit(solution)/shard_map/ppermute | solution.py:28
  26.5 17.9 %collective-permute-start.7 = (bf16[16,1024]{1,0:T(8,128)(2,1)S(1)}, bf16[16,1024]{1,0:T(8,128)(2,1)S(1)}, u32[]{:S(2)}, u32[]{:S(2)}) collective-permute-start(bf16[16,1024]{1,0:T(8,128)(2,1)S(1)} %get-tuple-element.86), channel_id=1, source_target_pairs={{0,28},{4,0},{8,4},{12,8},{16,12},{20,16},{24,20},{28,24},{1,29},{... | collective-permute-start | bytes 98312 | tf_op jit(solution)/shard_map/ppermute | solution.py:24
  28.5 8.3 %collective-permute-start.5 = (bf16[128,1024]{1,0:T(8,128)(2,1)S(1)}, bf16[128,1024]{1,0:T(8,128)(2,1)S(1)}, u32[]{:S(2)}, u32[]{:S(2)}) collective-permute-start(bf16[128,1024]{1,0:T(8,128)(2,1)S(1)} %get-tuple-element.75.gm_ref), channel_id=1, source_target_pairs={{0,28},{4,0},{8,4},{12,8},{16,12},{20,16},{24,20},{28,24},{1,29},{... | collective-permute-start | bytes 786440 | tf_op jit(solution)/shard_map/ppermute | solution.py:24
  35.8 4.3 %collective-permute-start.4 = (f32[88,128]{1,0:T(8,128)S(1)}, f32[88,128]{1,0:T(8,128)S(1)}, u32[]{:S(2)}, u32[]{:S(2)}) collective-permute-start(f32[88,128]{1,0:T(8,128)S(1)} %get-tuple-element.80), channel_id=1, source_target_pairs={{0,4},{4,0},{8,12},{12,8},{16,20},{20,16},{24,28},{28,24},{1,5},{5... | collective-permute-start | bytes 135176 | tf_op jit(solution)/shard_map/ppermute | solution.py:28
  40.1 11.5 %collective-permute-start.9 = (f32[88,128]{1,0:T(8,128)S(1)}, f32[88,128]{1,0:T(8,128)S(1)}, u32[]{:S(2)}, u32[]{:S(2)}) collective-permute-start(f32[88,128]{1,0:T(8,128)S(1)} %add.22), channel_id=1, source_target_pairs={{0,8},{4,12},{8,0},{12,4},{16,24},{20,28},{24,16},{28,20},{1,9},{5... | collective-permute-start | bytes 135176 | tf_op jit(solution)/shard_map/ppermute | solution.py:28
  40.5 11.1 %collective-permute-start.10 = (bf16[16,1024]{1,0:T(8,128)(2,1)S(1)}, bf16[16,1024]{1,0:T(8,128)(2,1)S(1)}, u32[]{:S(2)}, u32[]{:S(2)}) collective-permute-start(bf16[16,1024]{1,0:T(8,128)(2,1)S(1)} %get-tuple-element.95), channel_id=1, source_target_pairs={{0,28},{4,0},{8,4},{12,8},{16,12},{20,16},{24,20},{28,24},{1,29},{... | collective-permute-start | bytes 98312 | tf_op jit(solution)/shard_map/ppermute | solution.py:24
  44.3 3.7 %collective-permute-start.6 = (f32[16,128]{1,0:T(8,128)S(1)}, f32[16,128]{1,0:T(8,128)S(1)}, u32[]{:S(2)}, u32[]{:S(2)}) collective-permute-start(f32[16,128]{1,0:T(8,128)S(1)} %get-tuple-element.85), channel_id=1, source_target_pairs={{0,4},{4,0},{8,12},{12,8},{16,20},{20,16},{24,28},{28,24},{1,5},{5... | collective-permute-start | bytes 24584 | tf_op jit(solution)/shard_map/ppermute | solution.py:28
  48.0 3.7 %collective-permute-start.8 = (f32[16,128]{1,0:T(8,128)S(1)}, f32[16,128]{1,0:T(8,128)S(1)}, u32[]{:S(2)}, u32[]{:S(2)}) collective-permute-start(f32[16,128]{1,0:T(8,128)S(1)} %add.20), channel_id=1, source_target_pairs={{0,8},{4,12},{8,0},{12,4},{16,24},{20,28},{24,16},{28,20},{1,9},{5... | collective-permute-start | bytes 24584 | tf_op jit(solution)/shard_map/ppermute | solution.py:28
  51.6 5.8 %collective-permute-start.11 = (f32[88,128]{1,0:T(8,128)S(1)}, f32[88,128]{1,0:T(8,128)S(1)}, u32[]{:S(2)}, u32[]{:S(2)}) collective-permute-start(f32[88,128]{1,0:T(8,128)S(1)} %add.23.stats_ref), channel_id=1, source_target_pairs={{0,16},{4,20},{8,24},{12,28},{16,0},{20,4},{24,8},{28,12},{1,17},{... | collective-permute-start | bytes 135176 | tf_op jit(solution)/shard_map/ppermute | solution.py:28
  52.2 5.3 %collective-permute-start.12 = (f32[16,128]{1,0:T(8,128)S(1)}, f32[16,128]{1,0:T(8,128)S(1)}, u32[]{:S(2)}, u32[]{:S(2)}) collective-permute-start(f32[16,128]{1,0:T(8,128)S(1)} %add.21.last_ref), channel_id=1, source_target_pairs={{0,16},{4,20},{8,24},{12,28},{16,0},{20,4},{24,8},{28,12},{1,17},{... | collective-permute-start | bytes 24584 | tf_op jit(solution)/shard_map/ppermute | solution.py:28

commit v8 on v5

v8 whole, which is shorter than its diff:
```python
import functools

import jax
import jax.numpy as jnp
from jax import lax
from jax.experimental import pallas as pl
from jax.experimental.pallas import tpu as pltpu
from jax.sharding import PartitionSpec as P

GS = 16
K = 128
KS = 7
LANES = 128
PER = LANES // GS
RIM = 8
PACK = 16
EPS = 1e-06
F32 = jnp.float32
BF16 = jnp.bfloat16


def shifted(x, axis, by):
    count = lax.axis_size(axis)
    return lax.ppermute(x, axis, [(i, (i + by) % count) for i in range(count)])


def swapped(x, axis, step):
    return lax.ppermute(x, axis, [(i, i ^ step) for i in range(lax.axis_size(axis))])


def iota(shape, dim):
    return lax.broadcasted_iota(jnp.int32, shape, dim)


def positions(len_ref, rows):
    begin = jnp.zeros_like(rows)
    start = jnp.int32(0)
    for n in range(len_ref.shape[0]):
        begin = jnp.where(rows >= start, start, begin)
        start = start + len_ref[n]
    return jnp.where(rows < start, rows - begin, -1)


def first_row():
    return lax.axis_index("ctx") * K


def lanes_of(q):
    return pl.ds(pl.multiple_of(q * LANES, LANES), LANES)


def each_chunk(channels, body, unroll=2):
    def step(q, carry):
        body(q)
        return carry

    lax.fori_loop(0, channels // LANES, step, 0, unroll=unroll)


def each_part(part, channels, body, unroll=2):
    count = channels // LANES // 2

    def step(q, carry):
        body(part * count + q, lanes_of(part * count + q), lanes_of(q))
        return carry

    lax.fori_loop(0, count, step, 0, unroll=unroll)


def as_mask(cond):
    return jnp.where(cond, 1.0, 0.0).astype(BF16)


def join(*parts):
    return jnp.concatenate(parts, axis=0)


def tap_rows(taps_ref, which, ls):
    table = taps_ref[which * 8 : which * 8 + 8, ls]
    return [table[j : j + 1, :] for j in range(KS)]


def causal(ext, taps, pos):
    rows = ext.shape[0] - RIM
    total = taps[0] * ext[RIM:]
    for j in range(1, KS):
        moved = ext[RIM - j : RIM - j + rows]
        total = total + taps[j] * jnp.where(pos >= j, moved, 0.0)
    return total


def tap_lines(grad, ext, pos):
    lines = [jnp.sum(grad * ext[RIM:], axis=0, keepdims=True)]
    for j in range(1, KS):
        held = jnp.where(pos >= j, grad, 0.0)
        lines.append(jnp.sum(held * ext[RIM - j : RIM - j + K], axis=0, keepdims=True))
    lines.append(jnp.zeros((8 - KS, LANES), F32))
    return join(*lines)


def owners():
    lane = iota((K, LANES), 1) // GS
    return [as_mask(lane == g) for g in range(PER)]


def per_group(right, own):
    return join(*[right * mask for mask in own])


def masked(table_ref, q, mask):
    table = table_ref[:, pl.ds(pl.multiple_of(q * PER * K, PER * K), PER * K)]
    return [table[:, g * K : (g + 1) * K] * mask for g in range(PER)]


def product(left, right):
    return jnp.dot(jnp.concatenate(left, axis=1), right, preferred_element_type=F32)


K_FIRST, Q_LAST, K_LAST, V_LAST, V_FIRST, SENT = 0, K, K + 8, K + 16, K + 24, K + 32


def rim_of(ref, at, ls):
    base = at // PACK * PACK
    return ref[base : base + PACK, ls].astype(F32)[at - base : at - base + RIM]


def load_all(pairs, sems):
    copies = [pltpu.make_async_copy(a, b, sems.at[i]) for i, (a, b) in enumerate(pairs)]
    for copy in copies:
        copy.start()
    return copies


def send_part(part, channels, len_ref, q_ref, k_ref, v_ref, taps_ref, taps_part, sent_ref):
    pos = positions(len_ref, first_row() + RIM + iota((K - RIM, LANES), 0))

    def body(q, ls, hs):
        at = hs if taps_part else ls
        kx = k_ref[:, hs].astype(F32)
        vx = v_ref[:, hs].astype(F32)
        ks = causal(kx, tap_rows(taps_ref, 1, at), pos)
        vs = causal(vx, tap_rows(taps_ref, 2, at), pos)
        sent_ref[:K, hs] = join(kx[:RIM], ks * vs).astype(BF16)
        q_end = q_ref[:, hs].astype(F32)[PACK - RIM :]
        sent_ref[K:, hs] = join(q_end, kx[K - RIM :], vx[K - RIM :], vx[:RIM]).astype(BF16)

    each_part(part, channels, body)


def first_kernel(
    len_hbm, short_hbm, q_hbm, k_hbm, v_hbm, taps_ref, sent_ref,
    len_ref, short_ref, q_ref, k_ref, v_ref, sems,
):
    groups = short_ref.shape[2]
    channels = taps_ref.shape[1]
    part = slice(0, channels // 2)
    copies = load_all(
        (
            (short_hbm, short_ref), (len_hbm, len_ref), (k_hbm.at[:, part], k_ref),
            (v_hbm.at[:, part], v_ref), (q_hbm.at[K - PACK : K, part], q_ref),
        ),
        sems,
    )
    spread = as_mask(iota((groups, channels), 1) // GS == iota((groups, channels), 0))
    copies[0].wait()
    for i in range(3):
        taps_ref[i * 8 : i * 8 + KS] = jnp.dot(
            short_ref[i], spread, preferred_element_type=F32
        )
        taps_ref[i * 8 + KS : i * 8 + 8] = jnp.zeros((8 - KS, channels), F32)
    for copy in copies[1:]:
        copy.wait()
    send_part(0, channels, len_ref, q_ref, k_ref, v_ref, taps_ref, False, sent_ref)


def second_kernel(
    len_hbm, taps_hbm, q_hbm, k_hbm, v_hbm, sent_ref, far_ref,
    len_ref, taps_ref, q_ref, k_ref, v_ref, k_end, v_end, sems,
):
    channels = far_ref.shape[1]
    part = slice(channels // 2, channels)
    end = slice(K - PACK, K)
    copies = load_all(
        (
            (taps_hbm.at[:, part], taps_ref), (len_hbm, len_ref), (k_hbm.at[:, part], k_ref),
            (v_hbm.at[:, part], v_ref), (q_hbm.at[end, part], q_ref),
            (k_hbm.at[end], k_end), (v_hbm.at[end], v_end),
        ),
        sems,
    )
    for copy in copies:
        copy.wait()
    send_part(1, channels, len_ref, q_ref, k_ref, v_ref, taps_ref, True, sent_ref)
    k_rows = k_end[...].astype(F32)[PACK - RIM :]
    v_rows = v_end[...].astype(F32)[PACK - RIM :]
    far_ref[...] = join(k_rows, v_rows).astype(BF16)


def circulant_kernel(turned, long_ref, out_ref, line_ref):
    groups = long_ref.shape[0]
    filt = long_ref[...]
    if turned:
        flip = as_mask((iota((K, K), 0) + iota((K, K), 1)) % K == 0)
        line_ref[...] = jnp.dot(filt, flip, preferred_element_type=F32)
    else:
        line_ref[...] = filt.astype(F32)

    def step(g, carry):
        row = jnp.broadcast_to(line_ref[pl.ds(g, 1), :], (GS, K))
        block = pltpu.roll(row, 0, 1, stride=1, stride_axis=0)
        for i in range(K // GS):
            moved = block if i == 0 else pltpu.roll(block, i * GS, 1)
            at = pl.ds(pl.multiple_of(g * K, K), K)
            out_ref[i * GS : (i + 1) * GS, at] = moved.astype(BF16)
        return carry

    lax.fori_loop(0, groups, step, 0, unroll=8)


def current_kernel(
    len_ref, q_ref, k_ref, v_ref, taps_ref, sent0_ref, sent1_ref, fwd_ref, skip_ref,
    qs_ref, ks_ref, vs_ref, part_ref, top_ref,
):
    row = iota((K, LANES), 0)
    col = iota((K, LANES), 1)
    pos = positions(len_ref, first_row() + row)
    near = (col <= row) & (pos >= row - col)
    mask = as_mask(near)
    mask_top = as_mask(near & (col < RIM))
    picks = join(*[as_mask((col == row + g * GS) & (row < GS)) for g in range(PER)])
    own = owners()
    top = jnp.zeros((RIM, LANES), F32)

    def body(sent_ref, q, ls, hs):
        for i, (x_ref, o_ref) in enumerate(((q_ref, qs_ref), (k_ref, ks_ref), (v_ref, vs_ref))):
            short = causal(x_ref[:, ls].astype(F32), tap_rows(taps_ref, i, ls), pos[RIM:])
            o_ref[:, ls] = join(top, short)
        gated = join(top, sent_ref[:K, hs].astype(F32)[RIM:])
        rest = product(masked(fwd_ref, q, mask), per_group(gated.astype(BF16), own))
        part_ref[:, ls] = rest + skip_ref[:, ls] * gated
        top_ref[:, ls] = product(masked(fwd_ref, q, mask_top), picks).astype(BF16)

    for part, sent_ref in enumerate((sent0_ref, sent1_ref)):
        each_part(part, q_ref.shape[1], functools.partial(body, sent_ref))


def summed_kernel(
    part, len_ref, came_ref, far_ref, q_ref, k_ref, v_ref, taps_ref, sent_ref, fwd_ref, top_ref,
    qbulk_ref, kbulk_ref, vbulk_ref, part_ref, skip_ref, resid_ref, cot_ref, gain_ref, so_far_ref,
    qs_ref, ks_ref, vs_ref, gated_ref, before_ref, mixed_ref, summed_ref, sums_ref, acc_ref,
):
    row = iota((K, LANES), 0)
    col = iota((K, LANES), 1)
    pos = positions(len_ref, first_row() + row)
    mask = as_mask((col > row) & (pos >= row - col + K))
    pos_top = pos[:RIM]
    pos_far = positions(len_ref, first_row() - K + iota((RIM, LANES), 0))
    own = owners()
    own_top = [
        as_mask((iota((PACK, LANES), 1) // GS == g) & (iota((PACK, LANES), 0) < RIM))
        for g in range(PER)
    ]
    acc_ref[...] = jnp.zeros_like(acc_ref)

    def body(q, ls, hs):
        kt = tap_rows(taps_ref, 1, ls)
        vt = tap_rows(taps_ref, 2, ls)
        k_last = rim_of(came_ref, K_LAST, hs)
        v_last = rim_of(came_ref, V_LAST, hs)
        ks_top = causal(join(k_last, rim_of(k_ref, 0, ls)), kt, pos_top)
        vs_top = causal(join(v_last, rim_of(v_ref, 0, ls)), vt, pos_top)
        ks_ref[:, hs] = join(ks_top, kbulk_ref[RIM:, ls])
        vs_ref[:, hs] = join(vs_top, vbulk_ref[RIM:, ls])
        far_top = causal(
            join(rim_of(far_ref, 0, ls), rim_of(came_ref, K_FIRST, hs)), kt, pos_far
        ) * causal(join(rim_of(far_ref, RIM, ls), rim_of(came_ref, V_FIRST, hs)), vt, pos_far)
        qs_top = causal(
            join(rim_of(came_ref, Q_LAST, hs), rim_of(q_ref, 0, ls)), tap_rows(taps_ref, 0, ls), pos_top
        )
        before = join(far_top, came_ref[:K, hs].astype(F32)[RIM:]).astype(BF16)
        gated = join(ks_top * vs_top, sent_ref[:K, hs].astype(F32)[RIM:]).astype(BF16)
        before_ref[:, hs] = before
        gated_ref[:, hs] = gated
        qs = join(qs_top, qbulk_ref[RIM:, ls])
        qs_ref[:, hs] = qs
        first = gated[:PACK]
        left = masked(fwd_ref, q, mask) + [top_ref[:, ls]]
        right = join(per_group(before, own), per_group(first, own_top))
        direct = skip_ref[:, ls] * first.astype(F32)[:RIM]
        mixed = part_ref[:, ls] + product(left, right)
        mixed = join(mixed[:RIM] + direct, mixed[RIM:])
        summed = resid_ref[:, ls].astype(F32) + qs * mixed
        mixed_ref[:, hs] = mixed
        summed_ref[:, hs] = summed
        acc_ref[0] += summed * summed
        acc_ref[1] += gain_ref[:, ls] * cot_ref[:, ls].astype(F32) * summed

    each_part(part, resid_ref.shape[1], body)
    for i in range(2):
        own_sum = jnp.sum(acc_ref[i].T, axis=0, keepdims=True)
        sums_ref[i : i + 1] = own_sum + so_far_ref[i : i + 1]


def group_sums(cols):
    count, channels = cols.shape
    gather = as_mask(iota((channels, LANES), 0) // GS == iota((channels, LANES), 1))
    high = cols.astype(BF16)
    rest = cols - high.astype(F32)
    mid = rest.astype(BF16)
    low = (rest - mid.astype(F32)).astype(BF16)
    parts = join(high.astype(F32), mid.astype(F32), low.astype(F32)).astype(BF16)
    sums = jnp.dot(parts, gather, preferred_element_type=F32)
    return sums[:count] + sums[count : 2 * count] + sums[2 * count :]


def by_row(line):
    return jnp.broadcast_to(line, (K, K)).T


def inverse_of(sums_ref, total):
    return by_row(lax.rsqrt(sums_ref[0:1] / total + EPS))


def grads_kernel(
    total, part, summed_ref, mixed_ref, qs_ref, cot_ref, gain_ref, sums_ref, gm_ref, gq_ref
):
    inverse = inverse_of(sums_ref, total)
    scale = inverse * inverse * by_row(sums_ref[1:2] / total)

    def body(q, ls, hs):
        scaled = gain_ref[:, ls] * cot_ref[:, ls].astype(F32)
        grad_sum = inverse * (scaled - summed_ref[:, hs] * scale)
        gm_ref[:, hs] = (grad_sum * qs_ref[:, hs]).astype(BF16)
        gq_ref[:, hs] = (grad_sum * mixed_ref[:, hs]).astype(BF16)

    each_part(part, cot_ref.shape[1], body)


def beside_kernel(
    total, len_ref, cot_ref, sums_ref, bwd_ref, skip_ref, q_ref, *refs
):
    halves = refs[:6], refs[6:12]
    stats_ref, part_ref, cols_ref = refs[12:]
    groups = bwd_ref.shape[1] // K
    inverse = inverse_of(sums_ref, total)
    row = iota((K, LANES), 0)
    col = iota((K, LANES), 1)
    pos_row = positions(len_ref, first_row() + row)
    pos = positions(len_ref, first_row() + col)
    mask = as_mask((col >= row) & (pos >= col - row))
    source = K - 1 - row
    near = (col >= source) & (pos >= col - source)
    far = (col < source) & (pos >= col - source + K)
    flip = as_mask(row + col == K - 1)
    own = owners()

    def body(half, q, ls, hs):
        summed_ref, gm_ref, gq_ref, gated_ref, before_ref, came_ref = half
        summed = summed_ref[:, hs]
        gm = gm_ref[:, hs]
        gmf = gm.astype(F32)
        gated = gated_ref[:, hs]
        stats_ref[pl.ds(groups + q, 1), :] = jnp.sum(gmf * gated.astype(F32), axis=0, keepdims=True)
        stats_ref[pl.ds(groups + groups // PER + q, 1), :] = jnp.sum(
            cot_ref[:, ls].astype(F32) * summed * inverse, axis=0, keepdims=True
        )
        right = per_group(gm, own)
        part_ref[:, ls] = skip_ref[:, ls] * gmf + product(masked(bwd_ref, q, mask), right)
        two = jnp.concatenate([before_ref[:, hs], gated], axis=1)
        flipped = jnp.dot(flip, two, preferred_element_type=F32).astype(BF16)
        left = join(flipped[:, :LANES], flipped[:, LANES:])
        turned = gmf.T.astype(BF16)
        spread = []
        for g in range(PER):
            pieces = [jnp.zeros((GS, K), BF16)] * PER
            pieces[g] = turned[g * GS : (g + 1) * GS]
            spread.append(join(*pieces))
        cross = jnp.dot(left, jnp.concatenate(spread, axis=1), preferred_element_type=F32)
        lines = []
        for g in range(PER):
            gs = slice(g * K, (g + 1) * K)
            square = jnp.where(near, cross[K:, gs], jnp.where(far, cross[:K, gs], 0.0))
            square = pltpu.roll(square, 1, 1, stride=1, stride_axis=0)
            lines.append(jnp.sum(square, axis=0, keepdims=True))
        stats_ref[pl.ds(pl.multiple_of(q * PER, PER), PER), :] = join(*lines)
        q_ext = join(rim_of(came_ref, Q_LAST, hs), q_ref[:, ls].astype(F32))
        cols_ref[:, ls] = tap_lines(gq_ref[:, hs].astype(F32), q_ext, pos_row)

    for part, half in enumerate(halves):
        each_part(part, cot_ref.shape[1], functools.partial(body, half), 1)


def gate_kernel(
    part, len_ref, part_ref, bwd_ref, k_ref, v_ref, after_ref, ks_ref, vs_ref, gq_ref, came_ref, *refs
):
    if part:
        stats_ref, qcols_ref, cols0_ref, tails0_ref = refs[:4]
        gks_ref, gvs_ref, tails_ref, packed_ref, cols_ref = refs[4:]
    else:
        gks_ref, gvs_ref, tails_ref, cols_ref = refs
    channels = part_ref.shape[1]
    row = iota((K, LANES), 0)
    col = iota((K, LANES), 1)
    pos_row = positions(len_ref, first_row() + row)
    pos = positions(len_ref, first_row() + K + col)
    mask = as_mask((col < row) & (pos >= col - row + K))
    own = owners()

    def body(q, ls, hs):
        right = per_group(after_ref[:, hs], own)
        grad = part_ref[:, ls] + product(masked(bwd_ref, q, mask), right)
        gks = (grad * vs_ref[:, hs]).astype(BF16)
        gvs = (grad * ks_ref[:, hs]).astype(BF16)
        gks_ref[:, hs] = gks
        gvs_ref[:, hs] = gvs
        heads = (rim_of(gq_ref, 0, hs), gks.astype(F32)[:RIM], gvs.astype(F32)[:RIM])
        at = ls if part else hs
        tails_ref[:, at] = join(*heads, jnp.zeros((RIM, LANES), F32)).astype(BF16)
        k_ext = join(rim_of(came_ref, K_LAST, hs), k_ref[:, ls].astype(F32))
        v_ext = join(rim_of(came_ref, V_LAST, hs), v_ref[:, ls].astype(F32))
        base = 8 if part else 0
        cols_ref[base : base + 8, at] = tap_lines(gks.astype(F32), k_ext, pos_row)
        cols_ref[base + 8 : base + 16, at] = tap_lines(gvs.astype(F32), v_ext, pos_row)

    each_part(part, channels, body)
    if part:
        half = channels // 2
        kept = stats_ref.shape[0]
        tails_ref[:, :half] = tails0_ref[...]
        cols_ref[8:, :half] = cols0_ref[...]
        cols_ref[:8] = qcols_ref[...]
        packed_ref[0:kept] = stats_ref[...]
        packed_ref[kept:] = group_sums(cols_ref[...])


def mains_kernel(total, len_ref, taps_ref, tails_ref, gain_ref, sums_ref, *refs):
    halves = refs[:4], refs[4:8]
    normed_ref, *out_refs = refs[8:]
    pos = positions(len_ref, first_row() + iota((K + RIM, LANES), 0))
    inverse = inverse_of(sums_ref, total)

    def body(half, q, ls, hs):
        normed_ref[:, ls] = (gain_ref[:, ls] * half[0][:, hs] * inverse).astype(BF16)
        for i, (g_ref, o_ref) in enumerate(zip(half[1:], out_refs)):
            ext = join(g_ref[:, hs].astype(F32), rim_of(tails_ref, i * RIM, ls))
            taps = tap_rows(taps_ref, i, ls)
            grad = taps[0] * ext[:K]
            for j in range(1, KS):
                held = jnp.where(pos >= j, ext, 0.0)
                grad = grad + taps[j] * held[j : j + K]
            o_ref[:, ls] = grad.astype(BF16)

    for part, half in enumerate(halves):
        each_part(part, gain_ref.shape[1], functools.partial(body, half))


def unpack_kernel(one_ref, two_ref, short_ref, long_ref, skip_ref, gain_ref):
    groups = long_ref.shape[0]
    rows = groups // PER
    total = one_ref[...] + two_ref[...]
    long_ref[...] = total[:groups]
    skip_ref[...] = total[groups : groups + rows]
    gain_ref[...] = total[groups + rows : groups + 2 * rows]
    for i in range(3):
        at = groups + 2 * rows + i * 8
        short_ref[i] = total[at : at + KS, :groups]


def shards(
    q_input, k_input, v_input, resid, lengths, short_filter, long_filter, skip, gain, cotangent
):
    length, channels = q_input.shape
    groups = channels // GS
    wide = channels * lax.axis_size("tp")
    rows = groups // PER

    def arr(shape, dtype):
        return jax.ShapeDtypeStruct(shape, dtype)

    smem = pl.BlockSpec(memory_space=pltpu.SMEM)
    vmem = pl.BlockSpec(memory_space=pltpu.VMEM)
    far_off = pl.BlockSpec(memory_space=pltpu.HBM)
    full_bf = arr((length, channels), BF16)
    full_f = arr((length, channels), F32)

    def call(name, kernel, outs, ins, scratch=(), flops=10**8, moved=10**6, grant=8, hbm=False):
        scalar = ins[0] is lengths
        return pl.pallas_call(
            kernel,
            out_shape=outs,
            in_specs=[far_off] * len(ins)
            if hbm
            else [smem if (i == 0 and scalar) else vmem for i in range(len(ins))],
            out_specs=[vmem] * len(outs),
            scratch_shapes=scratch,
            compiler_params=pltpu.CompilerParams(vmem_limit_bytes=grant * 1024 * 1024),
            cost_estimate=pl.CostEstimate(flops=flops, bytes_accessed=moved, transcendentals=0),
            name=name,
        )(*ins)

    skip2 = skip.reshape(1, channels)
    gain2 = gain.reshape(1, channels)
    half_bf = arr((length, channels // 2), BF16)
    half_f = arr((length, channels // 2), F32)
    sent_half = arr((SENT, channels // 2), BF16)
    loads = [
        pltpu.VMEM((PACK, channels // 2), BF16), pltpu.VMEM((length, channels // 2), BF16),
        pltpu.VMEM((length, channels // 2), BF16),
    ]
    taps, sent0 = call(
        "first", first_kernel, [arr((24, channels), F32), sent_half],
        [lengths, jnp.transpose(short_filter, (0, 2, 1)), q_input, k_input, v_input],
        [pltpu.SMEM(lengths.shape, jnp.int32), pltpu.VMEM((3, KS, groups), BF16)]
        + loads + [pltpu.SemaphoreType.DMA((5,))],
        grant=60, hbm=True,
    )
    came0 = shifted(sent0, "ctx", 1)
    sent1, far = call(
        "second", second_kernel, [sent_half, arr((2 * RIM, channels), BF16)],
        [lengths, taps, q_input, k_input, v_input],
        [pltpu.SMEM(lengths.shape, jnp.int32), pltpu.VMEM((24, channels // 2), F32)]
        + loads + [pltpu.VMEM((PACK, channels), BF16)] * 2 + [pltpu.SemaphoreType.DMA((7,))],
        flops=10**9, moved=5 * 10**6, grant=60, hbm=True,
    )
    came1 = shifted(sent1, "ctx", 1)
    came_far = shifted(far, "ctx", 2)
    sent, came = (sent0, sent1), (came0, came1)

    def circulants(filt, turned):
        return call(
            "circulants", functools.partial(circulant_kernel, turned),
            [arr((K, groups * K), BF16)], [filt], [pltpu.VMEM((groups, K), F32)],
            flops=10**3, moved=10**3,
        )[0]

    filt, filt2, sent = lax.optimization_barrier((long_filter, long_filter, sent))
    fwd = circulants(filt, True)
    qbulk, kbulk, vbulk, part, top = call(
        "current", current_kernel, [full_f] * 4 + [full_bf],
        [lengths, q_input, k_input, v_input, taps, *sent, fwd, skip2],
        flops=10**3, moved=10**3,
    )
    bwd = circulants(filt2, False)
    made = []
    sums = jnp.zeros((2, K), F32)
    for i in range(2):
        *some, sums = call(
            "summed", functools.partial(summed_kernel, i),
            [half_f] * 3 + [half_bf] * 2 + [half_f] * 2 + [arr((2, K), F32)],
            [
                lengths, came[i], came_far, q_input, k_input, v_input, taps, sent[i], fwd, top,
                qbulk, kbulk, vbulk, part, skip2, resid, cotangent, gain2, sums,
            ],
            [pltpu.VMEM((2, K, LANES), F32)], flops=10**9, moved=5 * 10**6,
        )
        made.append(some)
    q_short, k_short, v_short, gated, before, mixed, summed = zip(*made)
    sums, bwd = lax.optimization_barrier((sums, bwd))
    step = 1
    while step < lax.axis_size("tp"):
        sums = sums + swapped(sums, "tp", step)
        step *= 2
    grads = [
        call(
            "grads", functools.partial(grads_kernel, wide, i), [half_bf, half_bf],
            [summed[i], mixed[i], q_short[i], cotangent, gain2, sums],
        )
        for i in range(2)
    ]
    after = [shifted(grads[i][0], "ctx", -1) for i in range(2)]
    pairs = [
        (summed[i], *grads[i], gated[i], before[i], came[i]) for i in range(2)
    ]
    stats, part, qcols = call(
        "beside", functools.partial(beside_kernel, wide),
        [arr((groups + 2 * rows, LANES), F32), full_f, arr((8, channels), F32)],
        [lengths, cotangent, sums, bwd, skip2, q_input, *pairs[0], *pairs[1]],
        flops=4 * 10**9, moved=5 * 10**6,
    )
    half_cols = arr((16, channels // 2), F32)
    grad_ks0, grad_vs0, tails, cols = call(
        "gate", functools.partial(gate_kernel, 0),
        [half_bf, half_bf, arr((4 * RIM, channels // 2), BF16), half_cols],
        [
            lengths, part, bwd, k_input, v_input, after[0], k_short[0], v_short[0], grads[0][1],
            came[0],
        ],
        flops=10**9, moved=5 * 10**6,
    )
    grad_ks1, grad_vs1, tails, packed = call(
        "gate", functools.partial(gate_kernel, 1),
        [
            half_bf, half_bf, arr((4 * RIM, channels), BF16),
            arr((groups + 2 * rows + 24, LANES), F32),
        ],
        [
            lengths, part, bwd, k_input, v_input, after[1], k_short[1], v_short[1], grads[1][1],
            came[1], stats, qcols, cols, tails,
        ],
        [pltpu.VMEM((24, channels), F32)], flops=10**9, moved=5 * 10**6,
    )
    tails = shifted(tails, "ctx", -1)
    normed, grad_q, grad_k, grad_v = call(
        "mains", functools.partial(mains_kernel, wide), [full_bf] * 4,
        [
            lengths, taps, tails, gain2, sums, summed[0], grads[0][1], grad_ks0, grad_vs0,
            summed[1], grads[1][1], grad_ks1, grad_vs1,
        ],
        flops=10**9, moved=5 * 10**6,
    )
    outs = (grad_q, grad_k, grad_v, normed)
    count = lax.axis_size("ctx")
    step = 1
    while 2 * step < count:
        packed = packed + swapped(packed, "ctx", step)
        step *= 2
    packed, *outs = lax.optimization_barrier((packed, *outs))
    grad_q, grad_k, grad_v, normed = outs
    other = swapped(packed, "ctx", step)
    grad_short, grad_long, grad_skip, grad_gain = call(
        "unpack", unpack_kernel,
        [
            arr((3, KS, groups), F32), arr((groups, K), F32),
            arr((rows, LANES), F32), arr((rows, LANES), F32),
        ],
        [packed, other],
    )
    return (
        normed, grad_q, grad_k, grad_v, jnp.transpose(grad_short, (0, 2, 1)), grad_long,
        grad_skip.reshape(channels), grad_gain.reshape(channels),
    )


def solution(mesh):
    tiled = P("ctx", "tp")
    return jax.shard_map(
        shards,
        mesh=mesh,
        in_specs=(
            tiled, tiled, tiled, tiled, P(), P(None, "tp", None), P("tp", None), P("tp"), P("tp"),
            tiled,
        ),
        out_specs=(
            tiled, tiled, tiled, tiled, P(None, "tp", None), P("tp", None), P("tp"), P("tp"),
        ),
        check_vma=False,
    )
```

time: 57.4 us -> 59.5 us (1.037)
  starting transfers between devices: 13.2 us -> 15.8 us
  Pallas kernels: 28.2 us -> 30.6 us
  waiting for transfers between devices: 14 us -> 11.9 us
  local copies, waits for them, and re-layouts: 0.78 us -> 0.06 us
    ppermute x4 -> x6, waiting for transfers between devices: 4.49 us -> 0.02 us  [shifted(): return lax.ppermute(x, axis, [(i, (i + by) % count) for i in range(count)])]
    ppermute x5, waiting for transfers between devices: 9.49 us -> 11.9 us  [swapped(): lax.ppermute(x, axis, [(i, i ^ step) for i in range(lax.axis_size(axis))])]
    pallas_call x11 -> x14, Pallas kernels: 28.2 us -> 30.6 us  [call(): pl.pallas_call(kernel, out_shape=outs, in_specs=[far_off] * len(ins) if h...]
    ppermute x5, starting transfers between devices: 1.77 us -> 3.92 us  [swapped(): lax.ppermute(x, axis, [(i, i ^ step) for i in range(lax.axis_size(axis))])]
    unnamed x24, local copies, waits for them, and re-layouts: 0.78 us -> 0.06 us
    ppermute x4 -> x6, starting transfers between devices: 11.5 us -> 11.9 us  [shifted(): return lax.ppermute(x, axis, [(i, (i + by) % count) for i in range(count)])]
  transfers between devices with their start and end apart: 9 -> 11, of which waited for: 6 -> 4; matrix products, arithmetic and copies ran while one was open for 0% -> 0% of each run, Pallas kernels for 32% -> 40%
where the time goes in v8:
time: 59.5 us; the launch traced here: 59.4 us
  Pallas kernels  30.6 us (51%)
  starting transfers between devices  15.8 us (27%)
  waiting for transfers between devices  11.9 us (20%)
  between operations  0.94 us (2%)
    pallas_call x14, Pallas kernels, call(): pl.pallas_call(kernel, out_shape=outs, in_specs=[far_off] * len(ins) if h...  30.6 us
    ppermute x5, waiting for transfers between devices, swapped(): lax.ppermute(x, axis, [(i, i ^ step) for i in range(lax.axis_size(axis))])  11.9 us
    ppermute x6, starting transfers between devices, shifted(): return lax.ppermute(x, axis, [(i, (i + by) % count) for i in range(count)])  11.9 us
    ppermute x5, starting transfers between devices, swapped(): lax.ppermute(x, axis, [(i, i ^ step) for i in range(lax.axis_size(axis))])  3.92 us
  transfers between devices with their start and end apart: 11, of which 4 were waited for; matrix products, arithmetic and copies ran while one was open for 0% of the time, Pallas kernels for 40%

profile of v8, /device:TPU:0, one launch (start us, length us, event | category | flops | bytes accessed | tf_op | source)
XLA Modules:
  0.0 59.4 jit_solution(915611531892744875)
XLA Ops:
  0.6 2.4 %first.1 = (f32[24,1024]{1,0:T(8,128)}, bf16[160,512]{1,0:T(8,128)(2,1)}) custom-call(s32[8]{0:T(128)} %len_ref.13, bf16[3,7,64]{2,1,0:T(8,128)(2,1)} %bitcast.15, bf16[128,1024]{1,0:T(8,128)(2,1)} %q_ref.7, bf16[128,1024]{1,0:T(8,128)(2,1)} %k_ref.9, bf16[128,1024]{1,0:T(8,128)(2,1)} %v_ref.9), custom_call_target="tpu_custom_call" | custom-call | flops 100000000 | bytes 1000000 | tf_op jit(solution)/shard_map/first/pallas_call | solution.py:488
  3.0 3.0 %collective-permute-start.2 = (bf16[160,512]{1,0:T(8,128)(2,1)}, bf16[160,512]{1,0:T(8,128)(2,1)S(1)}, u32[]{:S(2)}, u32[]{:S(2)}) collective-permute-start(bf16[160,512]{1,0:T(8,128)(2,1)} %get-tuple-element.73.sent0_ref.sent_ref), channel_id=1, source_target_pairs={{0,4},{4,8},{8,12},{12,16},{16,20},{20,24},{24,28},{28,0},{1,5},{5... | collective-permute-start | bytes 491528 | tf_op jit(solution)/shard_map/ppermute | solution.py:24
  6.1 2.4 %second.1 = (bf16[160,512]{1,0:T(8,128)(2,1)}, bf16[16,1024]{1,0:T(8,128)(2,1)}) custom-call(s32[8]{0:T(128)} %len_ref.13, f32[24,1024]{1,0:T(8,128)} %get-tuple-element.67.taps_hbm.taps_ref, bf16[128,1024]{1,0:T(8,128)(2,1)} %q_ref.7, bf16[128,1024]{1,0:T(8,128)(2,1)} %k_ref.9, bf16[128,1024]{1,0:T(8,128)(2,1)} %v_ref.9), custom_call_target="tpu_custom_call" | custom-call | flops 1000000000 | bytes 5000000 | tf_op jit(solution)/shard_map/second/pallas_call | solution.py:488
  8.5 1.6 %collective-permute-start = (bf16[160,512]{1,0:T(8,128)(2,1)}, bf16[160,512]{1,0:T(8,128)(2,1)S(1)}, u32[]{:S(2)}, u32[]{:S(2)}) collective-permute-start(bf16[160,512]{1,0:T(8,128)(2,1)} %get-tuple-element.71.sent1_ref.sent_ref), channel_id=1, source_target_pairs={{0,4},{4,8},{8,12},{12,16},{16,20},{20,24},{24,28},{28,0},{1,5},{5... | collective-permute-start | bytes 491528 | tf_op jit(solution)/shard_map/ppermute | solution.py:24
  10.1 0.0 copy-start.10
  10.1 0.0 copy-start.11
  10.1 1.6 %collective-permute-start.1 = (bf16[16,1024]{1,0:T(8,128)(2,1)}, bf16[16,1024]{1,0:T(8,128)(2,1)S(1)}, u32[]{:S(2)}, u32[]{:S(2)}) collective-permute-start(bf16[16,1024]{1,0:T(8,128)(2,1)} %get-tuple-element.69), channel_id=1, source_target_pairs={{0,8},{4,12},{8,16},{12,20},{16,24},{20,28},{24,0},{28,4},{1,9},{5... | collective-permute-start | bytes 98312 | tf_op jit(solution)/shard_map/ppermute | solution.py:24
  11.8 1.8 %circulants.2.fwd_ref = bf16[128,8192]{1,0:T(8,128)(2,1)S(1)} custom-call(bf16[64,128]{1,0:T(8,128)(2,1)S(1)} %copy-done.8), custom_call_target="tpu_custom_call" | custom-call | flops 1000 | bytes 1000 | tf_op jit(solution)/shard_map/circulants/pallas_call | solution.py:488
  13.6 1.7 %circulants.3.bwd_ref = bf16[128,8192]{1,0:T(8,128)(2,1)S(1)} custom-call(bf16[64,128]{1,0:T(8,128)(2,1)S(1)} %copy-done.8), custom_call_target="tpu_custom_call" | custom-call | flops 1000 | bytes 1000 | tf_op jit(solution)/shard_map/circulants/pallas_call | solution.py:488
  15.3 0.0 copy-start.9
  15.4 4.4 %current.1 = (f32[128,1024]{1,0:T(8,128)S(1)}, f32[128,1024]{1,0:T(8,128)S(1)}, f32[128,1024]{1,0:T(8,128)S(1)}, f32[128,1024]{1,0:T(8,128)S(1)}, bf16[128,1024]{1,0:T(8,128)(2,1)S(1)}) custom-call(s32[8]{0:T(128)S(1)} %copy-done.11, bf16[128,1024]{1,0:T(8,128)(2,1)S(1)} %copy-done.3, bf16[128,1024]{1,0:T(8,128)(2,1)S(1)} %copy-done, ...), custom_call_target="tpu_custom_call" | custom-call | flops 1000 | bytes 1000 | tf_op jit(solution)/shard_map/current/pallas_call | solution.py:488
  19.9 1.5 %summed.2 = (f32[128,512]{1,0:T(8,128)S(1)}, f32[128,512]{1,0:T(8,128)S(1)}, f32[128,512]{1,0:T(8,128)S(1)}, bf16[128,512]{1,0:T(8,128)(2,1)S(1)}, bf16[128,512]...) custom-call(s32[8]{0:T(128)S(1)} %copy-done.11, ...), custom_call_target="tpu_custom_call" | custom-call | flops 1000000000 | bytes 5000000 | tf_op jit(solution)/shard_map/summed/pallas_call | solution.py:488
  21.4 1.5 %summed.3 = (f32[128,512]{1,0:T(8,128)S(1)}, f32[128,512]{1,0:T(8,128)S(1)}, f32[128,512]{1,0:T(8,128)S(1)}, bf16[128,512]{1,0:T(8,128)(2,1)S(1)}, bf16[128,512]...) custom-call(s32[8]{0:T(128)S(1)} %copy-done.11, ...), custom_call_target="tpu_custom_call" | custom-call | flops 1000000000 | bytes 5000000 | tf_op jit(solution)/shard_map/summed/pallas_call | solution.py:488
  23.0 0.1 collective-permute-start.3
  23.0 1.1 %collective-permute-done.3 = f32[2,128]{1,0:T(2,128)S(1)} collective-permute-done((f32[2,128]{1,0:T(2,128)S(1)}, f32[2,128]{1,0:T(2,128)S(1)}, u32[]{:S(2)}, u32[]{:S(2)}) %collective-permute-start.3) | collective-permute-done | bytes 1056 | tf_op jit(solution)/shard_map/ppermute | solution.py:28
  24.2 1.5 %collective-permute-start.4 = (f32[2,128]{1,0:T(2,128)S(1)}, f32[2,128]{1,0:T(2,128)S(1)}, u32[]{:S(2)}, u32[]{:S(2)}) collective-permute-start(f32[2,128]{1,0:T(2,128)S(1)} %add.12), channel_id=1, source_target_pairs={{0,2},{1,3},{2,0},{3,1},{4,6},{5,7},{6,4},{7,5},{8,10},{9,11},{10,... | collective-permute-start | bytes 3080 | tf_op jit(solution)/shard_map/ppermute | solution.py:28
  25.7 2.1 %collective-permute-done.4 = f32[2,128]{1,0:T(2,128)S(1)} collective-permute-done((f32[2,128]{1,0:T(2,128)S(1)}, f32[2,128]{1,0:T(2,128)S(1)}, u32[]{:S(2)}, u32[]{:S(2)}) %collective-permute-start.4) | collective-permute-done | bytes 1056 | tf_op jit(solution)/shard_map/ppermute | solution.py:28
  27.7 0.3 grads.2
  28.0 3.3 %collective-permute-start.6 = (bf16[128,512]{1,0:T(8,128)(2,1)S(1)}, bf16[128,512]{1,0:T(8,128)(2,1)S(1)}, u32[]{:S(2)}, u32[]{:S(2)}) collective-permute-start(bf16[128,512]{1,0:T(8,128)(2,1)S(1)} %get-tuple-element.87.refs_1_), channel_id=1, source_target_pairs={{0,28},{4,0},{8,4},{12,8},{16,12},{20,16},{24,20},{28,24},{1,29},{... | collective-permute-start | bytes 393224 | tf_op jit(solution)/shard_map/ppermute | solution.py:24
  31.3 0.3 grads.3
  31.6 0.6 collective-permute-start.5
  32.2 5.9 %beside.1 = (f32[80,128]{1,0:T(8,128)S(1)}, f32[128,1024]{1,0:T(8,128)S(1)}, f32[8,1024]{1,0:T(8,128)S(1)}) custom-call(s32[8]{0:T(128)S(1)} %copy-done.11, bf16[128,1024]{1,0:T(8,128)(2,1)S(1)} %copy-done.2, f32[2,128]{1,0:T(2,128)S(1)} %add.13.sums_ref, bf16[128,8192]{1,0:T(8,128)(2,1)S(1)} %circulants.3.bwd_ref, f32[1,1024]{1,0:T(1,128)S(1)} %bitcast.14, ...), custom_call_target="tpu_custom_call" | custom-call | flops 4000000000 | bytes 5000000 | tf_op jit(solution)/shard_map/beside/pallas_call | solution.py:488
  38.0 1.9 %gate.2 = (bf16[128,512]{1,0:T(8,128)(2,1)S(1)}, bf16[128,512]{1,0:T(8,128)(2,1)S(1)}, bf16[32,512]{1,0:T(8,128)(2,1)S(1)}, f32[16,512]{1,0:T(8,128)S(1)}) custom-call(s32[8]{0:T(128)S(1)} %copy-done.11, f32[128,1024]{1,0:T(8,128)S(1)} %get-tuple-element.98.part_ref, bf16[128,8192]{1,0:T(8,128)(2,1)S(1)} %circulants.3.bwd_ref, ...), custom_call_target="tpu_custom_call" | custom-call | flops 1000000000 | bytes 5000000 | tf_op jit(solution)/shard_map/gate/pallas_call | solution.py:488
  39.9 2.1 %gate.3 = (bf16[128,512]{1,0:T(8,128)(2,1)S(1)}, bf16[128,512]{1,0:T(8,128)(2,1)S(1)}, bf16[32,1024]{1,0:T(8,128)(2,1)S(1)}, f32[104,128]{1,0:T(8,128)S(1)}) custom-call(s32[8]{0:T(128)S(1)} %copy-done.11, f32[128,1024]{1,0:T(8,128)S(1)} %get-tuple-element.98.part_ref, bf16[128,8192]{1,0:T(8,128)(2,1)S(1)} %circulants.3.bwd_ref, ...), custom_call_target="tpu_custom_call" | custom-call | flops 1000000000 | bytes 5000000 | tf_op jit(solution)/shard_map/gate/pallas_call | solution.py:488
  42.0 1.8 %collective-permute-start.9 = (bf16[32,1024]{1,0:T(8,128)(2,1)S(1)}, bf16[32,1024]{1,0:T(8,128)(2,1)S(1)}, u32[]{:S(2)}, u32[]{:S(2)}) collective-permute-start(bf16[32,1024]{1,0:T(8,128)(2,1)S(1)} %get-tuple-element.108), channel_id=1, source_target_pairs={{0,28},{4,0},{8,4},{12,8},{16,12},{20,16},{24,20},{28,24},{1,29},{... | collective-permute-start | bytes 196616 | tf_op jit(solution)/shard_map/ppermute | solution.py:24
  43.8 0.2 collective-permute-start.7
  44.1 3.9 %collective-permute-done.7 = f32[104,128]{1,0:T(8,128)S(1)} collective-permute-done((f32[104,128]{1,0:T(8,128)S(1)}, f32[104,128]{1,0:T(8,128)S(1)}, u32[]{:S(2)}, u32[]{:S(2)}) %collective-permute-start.7) | collective-permute-done | bytes 53280 | tf_op jit(solution)/shard_map/ppermute | solution.py:28
  48.0 1.3 %collective-permute-start.8 = (f32[104,128]{1,0:T(8,128)S(1)}, f32[104,128]{1,0:T(8,128)S(1)}, u32[]{:S(2)}, u32[]{:S(2)}) collective-permute-start(f32[104,128]{1,0:T(8,128)S(1)} %add.14), channel_id=1, source_target_pairs={{0,8},{4,12},{8,0},{12,4},{16,24},{20,28},{24,16},{28,20},{1,9},{5... | collective-permute-start | bytes 159752 | tf_op jit(solution)/shard_map/ppermute | solution.py:28
  49.2 3.8 %mains.1 = (bf16[128,1024]{1,0:T(8,128)(2,1)}, bf16[128,1024]{1,0:T(8,128)(2,1)}, bf16[128,1024]{1,0:T(8,128)(2,1)}, bf16[128,1024]{1,0:T(8,128)(2,1)}) custom-call(s32[8]{0:T(128)S(1)} %copy-done.11, f32[24,1024]{1,0:T(8,128)S(1)} %copy-done.5, bf16[32,1024]{1,0:T(8,128)(2,1)S(1)} %collective-permute-done.9.tails_ref, f32[1,1024]{1,0:T(1,128)S(1)} %bitcast.10, ...), custom_call_target="tpu_custom_call" | custom-call | flops 1000000000 | bytes 5000000 | tf_op jit(solution)/shard_map/mains/pallas_call | solution.py:488
  53.1 0.9 %collective-permute-start.10 = (f32[104,128]{1,0:T(8,128)S(1)}, f32[104,128]{1,0:T(8,128)S(1)}, u32[]{:S(2)}, u32[]{:S(2)}) collective-permute-start(f32[104,128]{1,0:T(8,128)S(1)} %add.15.one_ref), channel_id=1, source_target_pairs={{0,16},{4,20},{8,24},{12,28},{16,0},{20,4},{24,8},{28,12},{1,17},{... | collective-permute-start | bytes 159752 | tf_op jit(solution)/shard_map/ppermute | solution.py:28
  53.9 4.8 %collective-permute-done.10.two_ref = f32[104,128]{1,0:T(8,128)S(1)} collective-permute-done((f32[104,128]{1,0:T(8,128)S(1)}, f32[104,128]{1,0:T(8,128)S(1)}, u32[]{:S(2)}, u32[]{:S(2)}) %collective-permute-start.10) | collective-permute-done | bytes 53280 | tf_op jit(solution)/shard_map/ppermute | solution.py:28
  58.7 0.6 %unpack.1 = (f32[3,7,64]{2,1,0:T(8,128)}, f32[64,128]{1,0:T(8,128)}, f32[8,128]{1,0:T(8,128)}, f32[8,128]{1,0:T(8,128)}) custom-call(f32[104,128]{1,0:T(8,128)S(1)} %add.15.one_ref, f32[104,128]{1,0:T(8,128)S(1)} %collective-permute-done.10.two_ref), custom_call_target="tpu_custom_call" | custom-call | flops 100000000 | bytes 1000000 | tf_op jit(solution)/shard_map/unpack/pallas_call | solution.py:488
  (33 shorter events, 0.1 us)
Async XLA Ops:
  0.6 11.1 %copy-start.8 = (bf16[64,128]{1,0:T(8,128)(2,1)S(1)}, bf16[64,128]{1,0:T(8,128)(2,1)}, u32[]{:S(2)}) copy-start(bf16[64,128]{1,0:T(8,128)(2,1)} %long_ref.1) | copy-start | bytes 49156
  3.0 16.8 %collective-permute-start.2 = (bf16[160,512]{1,0:T(8,128)(2,1)}, bf16[160,512]{1,0:T(8,128)(2,1)S(1)}, u32[]{:S(2)}, u32[]{:S(2)}) collective-permute-start(bf16[160,512]{1,0:T(8,128)(2,1)} %get-tuple-element.73.sent0_ref.sent_ref), channel_id=1, source_target_pairs={{0,4},{4,8},{8,12},{12,16},{16,20},{20,24},{24,28},{28,0},{1,5},{5... | collective-permute-start | bytes 491528 | tf_op jit(solution)/shard_map/ppermute | solution.py:24
  8.5 12.9 %collective-permute-start = (bf16[160,512]{1,0:T(8,128)(2,1)}, bf16[160,512]{1,0:T(8,128)(2,1)S(1)}, u32[]{:S(2)}, u32[]{:S(2)}) collective-permute-start(bf16[160,512]{1,0:T(8,128)(2,1)} %get-tuple-element.71.sent1_ref.sent_ref), channel_id=1, source_target_pairs={{0,4},{4,8},{8,12},{12,16},{16,20},{20,24},{24,28},{28,0},{1,5},{5... | collective-permute-start | bytes 491528 | tf_op jit(solution)/shard_map/ppermute | solution.py:24
  10.1 5.2 %copy-start = (bf16[128,1024]{1,0:T(8,128)(2,1)S(1)}, bf16[128,1024]{1,0:T(8,128)(2,1)}, u32[]{:S(2)}) copy-start(bf16[128,1024]{1,0:T(8,128)(2,1)} %k_ref.9) | copy-start | bytes 786436
  10.1 5.2 %copy-start.1 = (bf16[128,1024]{1,0:T(8,128)(2,1)S(1)}, bf16[128,1024]{1,0:T(8,128)(2,1)}, u32[]{:S(2)}) copy-start(bf16[128,1024]{1,0:T(8,128)(2,1)} %v_ref.9) | copy-start | bytes 786436
  10.1 5.2 %copy-start.3 = (bf16[128,1024]{1,0:T(8,128)(2,1)S(1)}, bf16[128,1024]{1,0:T(8,128)(2,1)}, u32[]{:S(2)}) copy-start(bf16[128,1024]{1,0:T(8,128)(2,1)} %q_ref.7) | copy-start | bytes 786436
  10.1 5.2 %copy-start.5 = (f32[24,1024]{1,0:T(8,128)S(1)}, f32[24,1024]{1,0:T(8,128)}, u32[]{:S(2)}) copy-start(f32[24,1024]{1,0:T(8,128)} %get-tuple-element.67.taps_hbm.taps_ref) | copy-start | bytes 294916
  10.1 5.2 %copy-start.6 = (bf16[160,512]{1,0:T(8,128)(2,1)S(1)}, bf16[160,512]{1,0:T(8,128)(2,1)}, u32[]{:S(2)}) copy-start(bf16[160,512]{1,0:T(8,128)(2,1)} %get-tuple-element.71.sent1_ref.sent_ref) | copy-start | bytes 491524
  10.1 5.2 %copy-start.7 = (bf16[160,512]{1,0:T(8,128)(2,1)S(1)}, bf16[160,512]{1,0:T(8,128)(2,1)}, u32[]{:S(2)}) copy-start(bf16[160,512]{1,0:T(8,128)(2,1)} %get-tuple-element.73.sent0_ref.sent_ref) | copy-start | bytes 491524
  10.1 5.2 %copy-start.10 = (f32[1024]{0:T(1024)S(1)}, f32[1024]{0:T(1024)}, u32[]{:S(2)}) copy-start(f32[1024]{0:T(1024)} %param.17) | copy-start | bytes 12292
  10.1 5.2 %copy-start.11 = (s32[8]{0:T(128)S(1)}, s32[8]{0:T(128)}, u32[]{:S(2)}) copy-start(s32[8]{0:T(128)} %len_ref.13) | copy-start | bytes 100
  10.1 9.7 %collective-permute-start.1 = (bf16[16,1024]{1,0:T(8,128)(2,1)}, bf16[16,1024]{1,0:T(8,128)(2,1)S(1)}, u32[]{:S(2)}, u32[]{:S(2)}) collective-permute-start(bf16[16,1024]{1,0:T(8,128)(2,1)} %get-tuple-element.69), channel_id=1, source_target_pairs={{0,8},{4,12},{8,16},{12,20},{16,24},{20,28},{24,0},{28,4},{1,9},{5... | collective-permute-start | bytes 98312 | tf_op jit(solution)/shard_map/ppermute | solution.py:24
  15.3 4.6 %copy-start.2 = (bf16[128,1024]{1,0:T(8,128)(2,1)S(1)}, bf16[128,1024]{1,0:T(8,128)(2,1)}, u32[]{:S(2)}) copy-start(bf16[128,1024]{1,0:T(8,128)(2,1)} %cot_ref.9) | copy-start | bytes 786436
  15.3 4.6 %copy-start.4 = (bf16[128,1024]{1,0:T(8,128)(2,1)S(1)}, bf16[128,1024]{1,0:T(8,128)(2,1)}, u32[]{:S(2)}) copy-start(bf16[128,1024]{1,0:T(8,128)(2,1)} %resid_ref.3) | copy-start | bytes 786436
  15.3 4.6 %copy-start.9 = (f32[1024]{0:T(1024)S(1)}, f32[1024]{0:T(1024)}, u32[]{:S(2)}) copy-start(f32[1024]{0:T(1024)} %param.18) | copy-start | bytes 12292
  23.0 1.2 %collective-permute-start.3 = (f32[2,128]{1,0:T(2,128)S(1)}, f32[2,128]{1,0:T(2,128)S(1)}, u32[]{:S(2)}, u32[]{:S(2)}) collective-permute-start(f32[2,128]{1,0:T(2,128)S(1)} %get-tuple-element.82), channel_id=1, source_target_pairs={{0,1},{1,0},{2,3},{3,2},{4,5},{5,4},{6,7},{7,6},{8,9},{9,8},{10,11... | collective-permute-start | bytes 3080 | tf_op jit(solution)/shard_map/ppermute | solution.py:28
  24.2 3.6 %collective-permute-start.4 = (f32[2,128]{1,0:T(2,128)S(1)}, f32[2,128]{1,0:T(2,128)S(1)}, u32[]{:S(2)}, u32[]{:S(2)}) collective-permute-start(f32[2,128]{1,0:T(2,128)S(1)} %add.12), channel_id=1, source_target_pairs={{0,2},{1,3},{2,0},{3,1},{4,6},{5,7},{6,4},{7,5},{8,10},{9,11},{10,... | collective-permute-start | bytes 3080 | tf_op jit(solution)/shard_map/ppermute | solution.py:28
  28.0 10.0 %collective-permute-start.6 = (bf16[128,512]{1,0:T(8,128)(2,1)S(1)}, bf16[128,512]{1,0:T(8,128)(2,1)S(1)}, u32[]{:S(2)}, u32[]{:S(2)}) collective-permute-start(bf16[128,512]{1,0:T(8,128)(2,1)S(1)} %get-tuple-element.87.refs_1_), channel_id=1, source_target_pairs={{0,28},{4,0},{8,4},{12,8},{16,12},{20,16},{24,20},{28,24},{1,29},{... | collective-permute-start | bytes 393224 | tf_op jit(solution)/shard_map/ppermute | solution.py:24
  31.6 8.3 %collective-permute-start.5 = (bf16[128,512]{1,0:T(8,128)(2,1)S(1)}, bf16[128,512]{1,0:T(8,128)(2,1)S(1)}, u32[]{:S(2)}, u32[]{:S(2)}) collective-permute-start(bf16[128,512]{1,0:T(8,128)(2,1)S(1)} %get-tuple-element.94.refs_7_), channel_id=1, source_target_pairs={{0,28},{4,0},{8,4},{12,8},{16,12},{20,16},{24,20},{28,24},{1,29},{... | collective-permute-start | bytes 393224 | tf_op jit(solution)/shard_map/ppermute | solution.py:24
  42.0 7.2 %collective-permute-start.9 = (bf16[32,1024]{1,0:T(8,128)(2,1)S(1)}, bf16[32,1024]{1,0:T(8,128)(2,1)S(1)}, u32[]{:S(2)}, u32[]{:S(2)}) collective-permute-start(bf16[32,1024]{1,0:T(8,128)(2,1)S(1)} %get-tuple-element.108), channel_id=1, source_target_pairs={{0,28},{4,0},{8,4},{12,8},{16,12},{20,16},{24,20},{28,24},{1,29},{... | collective-permute-start | bytes 196616 | tf_op jit(solution)/shard_map/ppermute | solution.py:24
  43.8 4.1 %collective-permute-start.7 = (f32[104,128]{1,0:T(8,128)S(1)}, f32[104,128]{1,0:T(8,128)S(1)}, u32[]{:S(2)}, u32[]{:S(2)}) collective-permute-start(f32[104,128]{1,0:T(8,128)S(1)} %get-tuple-element.107), channel_id=1, source_target_pairs={{0,4},{4,0},{8,12},{12,8},{16,20},{20,16},{24,28},{28,24},{1,5},{5... | collective-permute-start | bytes 159752 | tf_op jit(solution)/shard_map/ppermute | solution.py:28
  48.0 5.1 %collective-permute-start.8 = (f32[104,128]{1,0:T(8,128)S(1)}, f32[104,128]{1,0:T(8,128)S(1)}, u32[]{:S(2)}, u32[]{:S(2)}) collective-permute-start(f32[104,128]{1,0:T(8,128)S(1)} %add.14), channel_id=1, source_target_pairs={{0,8},{4,12},{8,0},{12,4},{16,24},{20,28},{24,16},{28,20},{1,9},{5... | collective-permute-start | bytes 159752 | tf_op jit(solution)/shard_map/ppermute | solution.py:28
  53.1 5.7 %collective-permute-start.10 = (f32[104,128]{1,0:T(8,128)S(1)}, f32[104,128]{1,0:T(8,128)S(1)}, u32[]{:S(2)}, u32[]{:S(2)}) collective-permute-start(f32[104,128]{1,0:T(8,128)S(1)} %add.15.one_ref), channel_id=1, source_target_pairs={{0,16},{4,20},{8,24},{12,28},{16,0},{20,4},{24,8},{28,12},{1,17},{... | collective-permute-start | bytes 159752 | tf_op jit(solution)/shard_map/ppermute | solution.py:28

commit v9 on v5

--- a/solution.py
+++ b/solution.py
@@ -19,9 +19,10 @@
 BF16 = jnp.bfloat16
 
 
-def shifted(x, axis, by):
+def shifted(x, axis, by, wrap=True):
     count = lax.axis_size(axis)
-    return lax.ppermute(x, axis, [(i, (i + by) % count) for i in range(count)])
+    pairs = [(i, (i + by) % count) for i in range(count)]
+    return lax.ppermute(x, axis, [p for p in pairs if wrap or p[1] - p[0] == by])
 
 
 def swapped(x, axis, step):
@@ -49,7 +50,7 @@
     return pl.ds(pl.multiple_of(q * LANES, LANES), LANES)
 
 
-def each_chunk(channels, body, unroll=2):
+def each_chunk(channels, body, unroll=4):
     def step(q, carry):
         body(q)
         return carry
@@ -256,6 +257,18 @@
         sums_ref[i : i + 1] = jnp.sum(acc_ref[i].T, axis=0, keepdims=True)
 
 
+def group_sums(cols):
+    count, channels = cols.shape
+    gather = as_mask(iota((channels, LANES), 0) // GS == iota((channels, LANES), 1))
+    high = cols.astype(BF16)
+    rest = cols - high.astype(F32)
+    mid = rest.astype(BF16)
+    low = (rest - mid.astype(F32)).astype(BF16)
+    parts = join(high.astype(F32), mid.astype(F32), low.astype(F32)).astype(BF16)
+    sums = jnp.dot(parts, gather, preferred_element_type=F32)
+    return sums[:count] + sums[count : 2 * count] + sums[2 * count :]
+
+
 def by_row(line):
     return jnp.broadcast_to(line, (K, K)).T
 
@@ -340,7 +353,7 @@
         q_ext = join(rim_of(came_ref, Q_LAST, ls), q_ref[:, ls].astype(F32))
         cols_ref[:, ls] = tap_lines(gq_ref[:, ls].astype(F32), q_ext, pos_row)
 
-    each_chunk(cot_ref.shape[1], body, 1)
+    each_chunk(cot_ref.shape[1], body, 2)
 
 
 def gate_kernel(
@@ -374,12 +387,7 @@
 
     each_chunk(channels, body)
     packed_ref[0:kept] = stats_ref[...]
-    gather = jnp.where(
-        iota((channels, LANES), 0) // GS == iota((channels, LANES), 1), 1.0, 0.0
-    )
-    packed_ref[kept:] = jnp.dot(
-        cols_ref[...], gather, preferred_element_type=F32, precision=lax.Precision.HIGHEST
-    )
+    packed_ref[kept:] = group_sums(cols_ref[...])
 
 
 def mains_kernel(
@@ -473,12 +481,14 @@
             flops=10**9, moved=4 * 10**6,
         )[0]
 
-    filt, sent = lax.optimization_barrier((long_filter, sent))
+    filt, filt2, sent = lax.optimization_barrier((long_filter, long_filter, sent))
     fwd = circulants(filt, True)
     bulk, part, top = call(
         "current", current_kernel, [full_f, full_f, full_bf],
         [lengths, q_input, taps, sent, fwd, skip2], flops=10**9, moved=5 * 10**6,
     )
+    bwd = circulants(filt2, False)
+    came, bwd = lax.optimization_barrier((came, bwd))
     q_short, gated, before, mixed, summed, sums = call(
         "summed", summed_kernel,
         [full_f, full_bf, full_bf, full_f, full_f, arr((2, K), F32)],
@@ -493,18 +503,17 @@
     while step < lax.axis_size("tp"):
         sums = sums + swapped(sums, "tp", step)
         step *= 2
-    filt, came, _ = lax.optimization_barrier((long_filter, came, own_sums))
-    bwd = circulants(filt, False)
+    came, _ = lax.optimization_barrier((came, own_sums))
     k_short, v_short = call(
         "gates", gates_kernel, [full_f] * 2, [lengths, k_input, v_input, came, taps],
         flops=10**8, moved=2 * 10**6,
     )
-    sums, bwd, k_short, v_short = lax.optimization_barrier((sums, bwd, k_short, v_short))
+    sums, k_short, v_short = lax.optimization_barrier((sums, k_short, v_short))
     grad_mixed, grad_qs = call(
         "grads", functools.partial(grads_kernel, wide), [full_bf, full_bf],
         [summed, mixed, q_short, cotangent, gain2, sums],
     )
-    after = shifted(grad_mixed, "ctx", -1)
+    after = shifted(grad_mixed, "ctx", -1, wrap=False)
     stats, part, qcols = call(
         "beside", functools.partial(beside_kernel, wide),
         [

time: 57.4 us -> 56.6 us (0.986)
  Pallas kernels: 28.2 us -> 26.8 us
  waiting for transfers between devices: 14 us -> 15 us
    ppermute x4, starting transfers between devices: 11.5 us -> 6.61 us  [shifted(): lax.ppermute(x, axis, [p for p in pairs if wrap or p[1] - p[0] == by])]
    ppermute x5, starting transfers between devices: 1.77 us -> 6.28 us  [swapped(): lax.ppermute(x, axis, [(i, i ^ step) for i in range(lax.axis_size(axis))])]
    ppermute x4, waiting for transfers between devices: 4.49 us -> 6.42 us  [shifted(): lax.ppermute(x, axis, [p for p in pairs if wrap or p[1] - p[0] == by])]
    pallas_call x11, Pallas kernels: 28.2 us -> 26.8 us  [call(): pl.pallas_call(kernel, out_shape=outs, in_specs=[far_off] * len(ins) if h...]
    ppermute x5, waiting for transfers between devices: 9.49 us -> 8.6 us  [swapped(): lax.ppermute(x, axis, [(i, i ^ step) for i in range(lax.axis_size(axis))])]
  transfers between devices with their start and end apart: 9 -> 9, of which waited for: 6 -> 6; matrix products, arithmetic and copies ran while one was open for 0% -> 0% of each run, Pallas kernels for 32% -> 30%
where the time goes in v9:
time: 56.6 us; the launch traced here: 56.4 us
  Pallas kernels  26.8 us (47%)
  waiting for transfers between devices  15 us (27%)
  starting transfers between devices  12.9 us (23%)
  between operations  0.89 us (2%)
  local copies, waits for them, and re-layouts  0.78 us (1%)
    pallas_call x11, Pallas kernels, call(): pl.pallas_call(kernel, out_shape=outs, in_specs=[far_off] * len(ins) if h...  26.8 us
    ppermute x5, waiting for transfers between devices, swapped(): lax.ppermute(x, axis, [(i, i ^ step) for i in range(lax.axis_size(axis))])  8.6 us
    ppermute x4, starting transfers between devices, shifted(): lax.ppermute(x, axis, [p for p in pairs if wrap or p[1] - p[0] == by])  6.61 us
    ppermute x4, waiting for transfers between devices, shifted(): lax.ppermute(x, axis, [p for p in pairs if wrap or p[1] - p[0] == by])  6.42 us
    ppermute x5, starting transfers between devices, swapped(): lax.ppermute(x, axis, [(i, i ^ step) for i in range(lax.axis_size(axis))])  6.28 us
  transfers between devices with their start and end apart: 9, of which 6 were waited for; matrix products, arithmetic and copies ran while one was open for 0% of the time, Pallas kernels for 30%

profile of v9, /device:TPU:0, one launch (start us, length us, event | category | flops | bytes accessed | tf_op | source)
XLA Modules:
  0.0 56.4 jit_solution(16066092755394206835)
XLA Ops:
  0.6 0.0 copy-start.11
  0.6 3.2 %first.1 = (f32[24,1024]{1,0:T(8,128)}, bf16[160,1024]{1,0:T(8,128)(2,1)}, bf16[16,1024]{1,0:T(8,128)(2,1)}) custom-call(s32[8]{0:T(128)} %len_ref.11, bf16[3,7,64]{2,1,0:T(8,128)(2,1)} %bitcast.12, bf16[128,1024]{1,0:T(8,128)(2,1)} %q_ref.5, bf16[128,1024]{1,0:T(8,128)(2,1)} %k_ref.5, bf16[128,1024]{1,0:T(8,128)(2,1)} %v_ref.5), custom_call_target="tpu_custom_call" | custom-call | flops 100000000 | bytes 1000000 | tf_op jit(solution)/shard_map/first/pallas_call | solution.py:447
  3.9 3.0 %collective-permute-start = (bf16[160,1024]{1,0:T(8,128)(2,1)}, bf16[160,1024]{1,0:T(8,128)(2,1)S(1)}, u32[]{:S(2)}, u32[]{:S(2)}) collective-permute-start(bf16[160,1024]{1,0:T(8,128)(2,1)} %get-tuple-element.58.sent_ref), channel_id=1, source_target_pairs={{0,4},{4,8},{8,12},{12,16},{16,20},{20,24},{24,28},{28,0},{1,5},{5... | collective-permute-start | bytes 983048 | tf_op jit(solution)/shard_map/ppermute | solution.py:25
  6.9 1.6 %collective-permute-start.1 = (bf16[16,1024]{1,0:T(8,128)(2,1)}, bf16[16,1024]{1,0:T(8,128)(2,1)S(1)}, u32[]{:S(2)}, u32[]{:S(2)}) collective-permute-start(bf16[16,1024]{1,0:T(8,128)(2,1)} %get-tuple-element.56), channel_id=1, source_target_pairs={{0,8},{4,12},{8,16},{12,20},{16,24},{20,28},{24,0},{28,4},{1,9},{5... | collective-permute-start | bytes 98312 | tf_op jit(solution)/shard_map/ppermute | solution.py:25
  8.5 0.7 %copy-done.10 = bf16[64,128]{1,0:T(8,128)(2,1)S(1)} copy-done((bf16[64,128]{1,0:T(8,128)(2,1)S(1)}, bf16[64,128]{1,0:T(8,128)(2,1)}, u32[]{:S(2)}) %copy-start.10) | copy-done | bytes 16408
  9.2 1.8 %circulants.3.fwd_ref = bf16[128,8192]{1,0:T(8,128)(2,1)S(1)} custom-call(bf16[64,128]{1,0:T(8,128)(2,1)S(1)} %copy-done.10), custom_call_target="tpu_custom_call" | custom-call | flops 1000000000 | bytes 4000000 | tf_op jit(solution)/shard_map/circulants/pallas_call | solution.py:447
  11.0 0.0 copy-start.3
  11.0 0.0 copy-start.4
  11.1 0.0 copy-start.9
  11.1 1.7 %circulants.2.bwd_ref = bf16[128,8192]{1,0:T(8,128)(2,1)S(1)} custom-call(bf16[64,128]{1,0:T(8,128)(2,1)S(1)} %copy-done.11), custom_call_target="tpu_custom_call" | custom-call | flops 1000000000 | bytes 4000000 | tf_op jit(solution)/shard_map/circulants/pallas_call | solution.py:447
  12.8 0.0 copy-start
  12.9 2.7 %current.1 = (f32[128,1024]{1,0:T(8,128)S(1)}, f32[128,1024]{1,0:T(8,128)S(1)}, bf16[128,1024]{1,0:T(8,128)(2,1)S(1)}) custom-call(s32[8]{0:T(128)S(1)} %copy-done.8, bf16[128,1024]{1,0:T(8,128)(2,1)S(1)} %copy-done.3, f32[24,1024]{1,0:T(8,128)S(1)} %copy-done.4, bf16[160,1024]{1,0:T(8,128)(2,1)S(1)} %copy-done.5, bf16[128,8192]{1,0:T(8,128)(2,1)S(1)} %circulants.3.fwd_ref, ...), custom_call_target="tpu_custom_call" | custom-call | flops 1000000000 | bytes 5000000 | tf_op jit(solution)/shard_map/current/pallas_call | solution.py:447
  15.5 2.7 %collective-permute-done.came_ref = bf16[160,1024]{1,0:T(8,128)(2,1)S(1)} collective-permute-done((bf16[160,1024]{1,0:T(8,128)(2,1)}, bf16[160,1024]{1,0:T(8,128)(2,1)S(1)}, u32[]{:S(2)}, u32[]{:S(2)}) %collective-permute-start) | collective-permute-done | bytes 327712 | tf_op jit(solution)/shard_map/ppermute | solution.py:25
  18.3 2.1 %summed.1 = (f32[128,1024]{1,0:T(8,128)S(1)}, bf16[128,1024]{1,0:T(8,128)(2,1)S(1)}, bf16[128,1024]{1,0:T(8,128)(2,1)S(1)}, f32[128,1024]{1,0:T(8,128)S(1)}, f32...) custom-call(s32[8]{0:T(128)S(1)} %copy-done.8, bf16[160,1024]{1,0:T(8,128)(2,1)S(1)} %collective-permute-done.came_ref, ...), custom_call_target="tpu_custom_call" | custom-call | flops 1000000000 | bytes 5000000 | tf_op jit(solution)/shard_map/summed/pallas_call | solution.py:447
  20.4 0.1 collective-permute-start.2
  20.5 1.1 %collective-permute-done.2 = f32[2,128]{1,0:T(2,128)S(1)} collective-permute-done((f32[2,128]{1,0:T(2,128)S(1)}, f32[2,128]{1,0:T(2,128)S(1)}, u32[]{:S(2)}, u32[]{:S(2)}) %collective-permute-start.2) | collective-permute-done | bytes 1056 | tf_op jit(solution)/shard_map/ppermute | solution.py:29
  21.6 1.5 %collective-permute-start.3 = (f32[2,128]{1,0:T(2,128)S(1)}, f32[2,128]{1,0:T(2,128)S(1)}, u32[]{:S(2)}, u32[]{:S(2)}) collective-permute-start(f32[2,128]{1,0:T(2,128)S(1)} %add.12), channel_id=1, source_target_pairs={{0,2},{1,3},{2,0},{3,1},{4,6},{5,7},{6,4},{7,5},{8,10},{9,11},{10,... | collective-permute-start | bytes 3080 | tf_op jit(solution)/shard_map/ppermute | solution.py:29
  23.1 2.0 %gates.1 = (f32[128,1024]{1,0:T(8,128)S(1)}, f32[128,1024]{1,0:T(8,128)S(1)}) custom-call(s32[8]{0:T(128)S(1)} %copy-done.8, bf16[128,1024]{1,0:T(8,128)(2,1)S(1)} %copy-done, bf16[128,1024]{1,0:T(8,128)(2,1)S(1)} %copy-done.1, bf16[160,1024]{1,0:T(8,128)(2,1)S(1)} %collective-permute-done.came_ref, f32[24,1024]{1,0:T(8,128)S(1)} %copy-done.4), custom_call_target="tpu_custom_call" | custom-call | flops 100000000 | bytes 2000000 | tf_op jit(solution)/shard_map/gates/pallas_call | solution.py:447
  25.1 0.1 collective-permute-done.3
  25.2 0.5 grads.1
  25.7 1.3 %collective-permute-start.4 = (bf16[128,1024]{1,0:T(8,128)(2,1)S(1)}, bf16[128,1024]{1,0:T(8,128)(2,1)S(1)}, u32[]{:S(2)}, u32[]{:S(2)}) collective-permute-start(bf16[128,1024]{1,0:T(8,128)(2,1)S(1)} %get-tuple-element.71.gm_ref), channel_id=1, source_target_pairs={{4,0},{8,4},{12,8},{16,12},{20,16},{24,20},{28,24},{5,1},{9,5},{13... | collective-permute-start | bytes 786440 | tf_op jit(solution)/shard_map/ppermute | solution.py:25
  27.0 4.9 %beside.1 = (f32[80,128]{1,0:T(8,128)S(1)}, f32[128,1024]{1,0:T(8,128)S(1)}, f32[8,1024]{1,0:T(8,128)S(1)}) custom-call(s32[8]{0:T(128)S(1)} %copy-done.8, f32[128,1024]{1,0:T(8,128)S(1)} %get-tuple-element.63.summed_ref, bf16[128,1024]{1,0:T(8,128)(2,1)S(1)} %copy-done.2, f32[2,128]{1,0:T(2,128)S(1)} %add.13.sums_ref, ...), custom_call_target="tpu_custom_call" | custom-call | flops 4000000000 | bytes 5000000 | tf_op jit(solution)/shard_map/beside/pallas_call | solution.py:447
  31.9 3.7 %collective-permute-done.4.after_ref = bf16[128,1024]{1,0:T(8,128)(2,1)S(1)} collective-permute-done((bf16[128,1024]{1,0:T(8,128)(2,1)S(1)}, bf16[128,1024]{1,0:T(8,128)(2,1)S(1)}, u32[]{:S(2)}, u32[]{:S(2)}) %collective-permute-start.4) | collective-permute-done | bytes 262176 | tf_op jit(solution)/shard_map/ppermute | solution.py:25
  35.7 3.3 %gate.1 = (bf16[128,1024]{1,0:T(8,128)(2,1)S(1)}, bf16[128,1024]{1,0:T(8,128)(2,1)S(1)}, bf16[32,1024]{1,0:T(8,128)(2,1)S(1)}, f32[104,128]{1,0:T(8,128)S(1)}) custom-call(s32[8]{0:T(128)S(1)} %copy-done.8, f32[128,1024]{1,0:T(8,128)S(1)} %get-tuple-element.76.part_ref, bf16[128,1024]{1,0:T(8,128)(2,1)S(1)} %collective-permute-done.4.after_ref, ...), custom_call_target="tpu_custom_call" | custom-call | flops 1000000000 | bytes 5000000 | tf_op jit(solution)/shard_map/gate/pallas_call | solution.py:447
  39.0 0.7 %collective-permute-start.7 = (bf16[32,1024]{1,0:T(8,128)(2,1)S(1)}, bf16[32,1024]{1,0:T(8,128)(2,1)S(1)}, u32[]{:S(2)}, u32[]{:S(2)}) collective-permute-start(bf16[32,1024]{1,0:T(8,128)(2,1)S(1)} %get-tuple-element.84), channel_id=1, source_target_pairs={{0,28},{4,0},{8,4},{12,8},{16,12},{20,16},{24,20},{28,24},{1,29},{... | collective-permute-start | bytes 196616 | tf_op jit(solution)/shard_map/ppermute | solution.py:25
  39.7 1.4 %collective-permute-start.5 = (f32[104,128]{1,0:T(8,128)S(1)}, f32[104,128]{1,0:T(8,128)S(1)}, u32[]{:S(2)}, u32[]{:S(2)}) collective-permute-start(f32[104,128]{1,0:T(8,128)S(1)} %get-tuple-element.81), channel_id=1, source_target_pairs={{0,4},{4,0},{8,12},{12,8},{16,20},{20,16},{24,28},{28,24},{1,5},{5... | collective-permute-start | bytes 159752 | tf_op jit(solution)/shard_map/ppermute | solution.py:29
  41.0 2.8 %collective-permute-done.5 = f32[104,128]{1,0:T(8,128)S(1)} collective-permute-done((f32[104,128]{1,0:T(8,128)S(1)}, f32[104,128]{1,0:T(8,128)S(1)}, u32[]{:S(2)}, u32[]{:S(2)}) %collective-permute-start.5) | collective-permute-done | bytes 53280 | tf_op jit(solution)/shard_map/ppermute | solution.py:29
  43.9 2.6 %collective-permute-start.6 = (f32[104,128]{1,0:T(8,128)S(1)}, f32[104,128]{1,0:T(8,128)S(1)}, u32[]{:S(2)}, u32[]{:S(2)}) collective-permute-start(f32[104,128]{1,0:T(8,128)S(1)} %add.14), channel_id=1, source_target_pairs={{0,8},{4,12},{8,0},{12,4},{16,24},{20,28},{24,16},{28,20},{1,9},{5... | collective-permute-start | bytes 159752 | tf_op jit(solution)/shard_map/ppermute | solution.py:29
  46.5 3.9 %mains.1 = (bf16[128,1024]{1,0:T(8,128)(2,1)}, bf16[128,1024]{1,0:T(8,128)(2,1)}, bf16[128,1024]{1,0:T(8,128)(2,1)}, bf16[128,1024]{1,0:T(8,128)(2,1)}) custom-call(s32[8]{0:T(128)S(1)} %copy-done.8, f32[24,1024]{1,0:T(8,128)S(1)} %copy-done.4, bf16[128,1024]{1,0:T(8,128)(2,1)S(1)} %get-tuple-element.72.gq_ref, ...), custom_call_target="tpu_custom_call" | custom-call | flops 1000000000 | bytes 5000000 | tf_op jit(solution)/shard_map/mains/pallas_call | solution.py:447
  50.4 0.7 %collective-permute-start.8 = (f32[104,128]{1,0:T(8,128)S(1)}, f32[104,128]{1,0:T(8,128)S(1)}, u32[]{:S(2)}, u32[]{:S(2)}) collective-permute-start(f32[104,128]{1,0:T(8,128)S(1)} %add.15.one_ref), channel_id=1, source_target_pairs={{0,16},{4,20},{8,24},{12,28},{16,0},{20,4},{24,8},{28,12},{1,17},{... | collective-permute-start | bytes 159752 | tf_op jit(solution)/shard_map/ppermute | solution.py:29
  51.2 4.6 %collective-permute-done.8.two_ref = f32[104,128]{1,0:T(8,128)S(1)} collective-permute-done((f32[104,128]{1,0:T(8,128)S(1)}, f32[104,128]{1,0:T(8,128)S(1)}, u32[]{:S(2)}, u32[]{:S(2)}) %collective-permute-start.8) | collective-permute-done | bytes 53280 | tf_op jit(solution)/shard_map/ppermute | solution.py:29
  55.7 0.6 %unpack.1 = (f32[3,7,64]{2,1,0:T(8,128)}, f32[64,128]{1,0:T(8,128)}, f32[8,128]{1,0:T(8,128)}, f32[8,128]{1,0:T(8,128)}) custom-call(f32[104,128]{1,0:T(8,128)S(1)} %add.15.one_ref, f32[104,128]{1,0:T(8,128)S(1)} %collective-permute-done.8.two_ref), custom_call_target="tpu_custom_call" | custom-call | flops 100000000 | bytes 1000000 | tf_op jit(solution)/shard_map/unpack/pallas_call | solution.py:447
  (25 shorter events, 0.1 us)
Async XLA Ops:
  0.6 10.4 %copy-start.11 = (bf16[64,128]{1,0:T(8,128)(2,1)S(1)}, bf16[64,128]{1,0:T(8,128)(2,1)}, u32[]{:S(2)}) copy-start(bf16[64,128]{1,0:T(8,128)(2,1)} %long_ref.1) | copy-start | bytes 49156
  3.9 14.3 %collective-permute-start = (bf16[160,1024]{1,0:T(8,128)(2,1)}, bf16[160,1024]{1,0:T(8,128)(2,1)S(1)}, u32[]{:S(2)}, u32[]{:S(2)}) collective-permute-start(bf16[160,1024]{1,0:T(8,128)(2,1)} %get-tuple-element.58.sent_ref), channel_id=1, source_target_pairs={{0,4},{4,8},{8,12},{12,16},{16,20},{20,24},{24,28},{28,0},{1,5},{5... | collective-permute-start | bytes 983048 | tf_op jit(solution)/shard_map/ppermute | solution.py:25
  6.9 11.3 %collective-permute-start.1 = (bf16[16,1024]{1,0:T(8,128)(2,1)}, bf16[16,1024]{1,0:T(8,128)(2,1)S(1)}, u32[]{:S(2)}, u32[]{:S(2)}) collective-permute-start(bf16[16,1024]{1,0:T(8,128)(2,1)} %get-tuple-element.56), channel_id=1, source_target_pairs={{0,8},{4,12},{8,16},{12,20},{16,24},{20,28},{24,0},{28,4},{1,9},{5... | collective-permute-start | bytes 98312 | tf_op jit(solution)/shard_map/ppermute | solution.py:25
  8.5 0.7 %copy-start.10 = (bf16[64,128]{1,0:T(8,128)(2,1)S(1)}, bf16[64,128]{1,0:T(8,128)(2,1)}, u32[]{:S(2)}) copy-start(bf16[64,128]{1,0:T(8,128)(2,1)} %long_ref.1) | copy-start | bytes 49156
  11.0 1.8 %copy-start.3 = (bf16[128,1024]{1,0:T(8,128)(2,1)S(1)}, bf16[128,1024]{1,0:T(8,128)(2,1)}, u32[]{:S(2)}) copy-start(bf16[128,1024]{1,0:T(8,128)(2,1)} %q_ref.5) | copy-start | bytes 786436
  11.0 1.8 %copy-start.4 = (f32[24,1024]{1,0:T(8,128)S(1)}, f32[24,1024]{1,0:T(8,128)}, u32[]{:S(2)}) copy-start(f32[24,1024]{1,0:T(8,128)} %get-tuple-element.57.taps_ref) | copy-start | bytes 294916
  11.0 1.8 %copy-start.5 = (bf16[160,1024]{1,0:T(8,128)(2,1)S(1)}, bf16[160,1024]{1,0:T(8,128)(2,1)}, u32[]{:S(2)}) copy-start(bf16[160,1024]{1,0:T(8,128)(2,1)} %get-tuple-element.58.sent_ref) | copy-start | bytes 983044
  11.1 1.8 %copy-start.8 = (s32[8]{0:T(128)S(1)}, s32[8]{0:T(128)}, u32[]{:S(2)}) copy-start(s32[8]{0:T(128)} %len_ref.11) | copy-start | bytes 100
  11.1 1.8 %copy-start.9 = (f32[1024]{0:T(1024)S(1)}, f32[1024]{0:T(1024)}, u32[]{:S(2)}) copy-start(f32[1024]{0:T(1024)} %param.17) | copy-start | bytes 12292
  12.8 5.5 %copy-start = (bf16[128,1024]{1,0:T(8,128)(2,1)S(1)}, bf16[128,1024]{1,0:T(8,128)(2,1)}, u32[]{:S(2)}) copy-start(bf16[128,1024]{1,0:T(8,128)(2,1)} %k_ref.5) | copy-start | bytes 786436
  12.8 5.5 %copy-start.1 = (bf16[128,1024]{1,0:T(8,128)(2,1)S(1)}, bf16[128,1024]{1,0:T(8,128)(2,1)}, u32[]{:S(2)}) copy-start(bf16[128,1024]{1,0:T(8,128)(2,1)} %v_ref.5) | copy-start | bytes 786436
  12.8 5.5 %copy-start.2 = (bf16[128,1024]{1,0:T(8,128)(2,1)S(1)}, bf16[128,1024]{1,0:T(8,128)(2,1)}, u32[]{:S(2)}) copy-start(bf16[128,1024]{1,0:T(8,128)(2,1)} %cot_ref.5) | copy-start | bytes 786436
  12.8 5.5 %copy-start.6 = (bf16[128,1024]{1,0:T(8,128)(2,1)S(1)}, bf16[128,1024]{1,0:T(8,128)(2,1)}, u32[]{:S(2)}) copy-start(bf16[128,1024]{1,0:T(8,128)(2,1)} %resid_ref.1) | copy-start | bytes 786436
  12.8 5.4 %copy-start.7 = (f32[1024]{0:T(1024)S(1)}, f32[1024]{0:T(1024)}, u32[]{:S(2)}) copy-start(f32[1024]{0:T(1024)} %param.18) | copy-start | bytes 12292
  20.4 1.2 %collective-permute-start.2 = (f32[2,128]{1,0:T(2,128)S(1)}, f32[2,128]{1,0:T(2,128)S(1)}, u32[]{:S(2)}, u32[]{:S(2)}) collective-permute-start(f32[2,128]{1,0:T(2,128)S(1)} %get-tuple-element.64), channel_id=1, source_target_pairs={{0,1},{1,0},{2,3},{3,2},{4,5},{5,4},{6,7},{7,6},{8,9},{9,8},{10,11... | collective-permute-start | bytes 3080 | tf_op jit(solution)/shard_map/ppermute | solution.py:29
  21.6 3.6 %collective-permute-start.3 = (f32[2,128]{1,0:T(2,128)S(1)}, f32[2,128]{1,0:T(2,128)S(1)}, u32[]{:S(2)}, u32[]{:S(2)}) collective-permute-start(f32[2,128]{1,0:T(2,128)S(1)} %add.12), channel_id=1, source_target_pairs={{0,2},{1,3},{2,0},{3,1},{4,6},{5,7},{6,4},{7,5},{8,10},{9,11},{10,... | collective-permute-start | bytes 3080 | tf_op jit(solution)/shard_map/ppermute | solution.py:29
  25.7 10.0 %collective-permute-start.4 = (bf16[128,1024]{1,0:T(8,128)(2,1)S(1)}, bf16[128,1024]{1,0:T(8,128)(2,1)S(1)}, u32[]{:S(2)}, u32[]{:S(2)}) collective-permute-start(bf16[128,1024]{1,0:T(8,128)(2,1)S(1)} %get-tuple-element.71.gm_ref), channel_id=1, source_target_pairs={{4,0},{8,4},{12,8},{16,12},{20,16},{24,20},{28,24},{5,1},{9,5},{13... | collective-permute-start | bytes 786440 | tf_op jit(solution)/shard_map/ppermute | solution.py:25
  39.0 7.5 %collective-permute-start.7 = (bf16[32,1024]{1,0:T(8,128)(2,1)S(1)}, bf16[32,1024]{1,0:T(8,128)(2,1)S(1)}, u32[]{:S(2)}, u32[]{:S(2)}) collective-permute-start(bf16[32,1024]{1,0:T(8,128)(2,1)S(1)} %get-tuple-element.84), channel_id=1, source_target_pairs={{0,28},{4,0},{8,4},{12,8},{16,12},{20,16},{24,20},{28,24},{1,29},{... | collective-permute-start | bytes 196616 | tf_op jit(solution)/shard_map/ppermute | solution.py:25
  39.7 4.2 %collective-permute-start.5 = (f32[104,128]{1,0:T(8,128)S(1)}, f32[104,128]{1,0:T(8,128)S(1)}, u32[]{:S(2)}, u32[]{:S(2)}) collective-permute-start(f32[104,128]{1,0:T(8,128)S(1)} %get-tuple-element.81), channel_id=1, source_target_pairs={{0,4},{4,0},{8,12},{12,8},{16,20},{20,16},{24,28},{28,24},{1,5},{5... | collective-permute-start | bytes 159752 | tf_op jit(solution)/shard_map/ppermute | solution.py:29
  43.9 6.5 %collective-permute-start.6 = (f32[104,128]{1,0:T(8,128)S(1)}, f32[104,128]{1,0:T(8,128)S(1)}, u32[]{:S(2)}, u32[]{:S(2)}) collective-permute-start(f32[104,128]{1,0:T(8,128)S(1)} %add.14), channel_id=1, source_target_pairs={{0,8},{4,12},{8,0},{12,4},{16,24},{20,28},{24,16},{28,20},{1,9},{5... | collective-permute-start | bytes 159752 | tf_op jit(solution)/shard_map/ppermute | solution.py:29
  50.4 5.3 %collective-permute-start.8 = (f32[104,128]{1,0:T(8,128)S(1)}, f32[104,128]{1,0:T(8,128)S(1)}, u32[]{:S(2)}, u32[]{:S(2)}) collective-permute-start(f32[104,128]{1,0:T(8,128)S(1)} %add.15.one_ref), channel_id=1, source_target_pairs={{0,16},{4,20},{8,24},{12,28},{16,0},{20,4},{24,8},{28,12},{1,17},{... | collective-permute-start | bytes 159752 | tf_op jit(solution)/shard_map/ppermute | solution.py:29

commit v10 on v9

--- a/solution.py
+++ b/solution.py
@@ -277,19 +277,6 @@
     return by_row(lax.rsqrt(sums_ref[0:1] / total + EPS))
 
 
-def gates_kernel(len_ref, k_ref, v_ref, came_ref, taps_ref, ks_ref, vs_ref):
-    pos = positions(len_ref, first_row() + iota((K, LANES), 0))
-
-    def body(q):
-        ls = lanes_of(q)
-        k_ext = join(rim_of(came_ref, K_LAST, ls), k_ref[:, ls].astype(F32))
-        v_ext = join(rim_of(came_ref, V_LAST, ls), v_ref[:, ls].astype(F32))
-        ks_ref[:, ls] = causal(k_ext, tap_rows(taps_ref, 1, ls), pos)
-        vs_ref[:, ls] = causal(v_ext, tap_rows(taps_ref, 2, ls), pos)
-
-    each_chunk(k_ref.shape[1], body)
-
-
 def grads_kernel(total, summed_ref, mixed_ref, qs_ref, cot_ref, gain_ref, sums_ref, gm_ref, gq_ref):
     inverse = inverse_of(sums_ref, total)
     scale = inverse * inverse * by_row(sums_ref[1:2] / total)
@@ -306,7 +293,8 @@
 
 def beside_kernel(
     total, len_ref, summed_ref, cot_ref, sums_ref, gm_ref, gq_ref, gated_ref, before_ref,
-    bwd_ref, skip_ref, q_ref, came_ref, stats_ref, part_ref, cols_ref,
+    bwd_ref, skip_ref, q_ref, k_ref, v_ref, came_ref, taps_ref,
+    stats_ref, part_ref, cols_ref, ks_ref, vs_ref,
 ):
     groups = bwd_ref.shape[1] // K
     inverse = inverse_of(sums_ref, total)
@@ -352,6 +340,10 @@
         stats_ref[pl.ds(pl.multiple_of(q * PER, PER), PER), :] = join(*lines)
         q_ext = join(rim_of(came_ref, Q_LAST, ls), q_ref[:, ls].astype(F32))
         cols_ref[:, ls] = tap_lines(gq_ref[:, ls].astype(F32), q_ext, pos_row)
+        k_ext = join(rim_of(came_ref, K_LAST, ls), k_ref[:, ls].astype(F32))
+        v_ext = join(rim_of(came_ref, V_LAST, ls), v_ref[:, ls].astype(F32))
+        ks_ref[:, ls] = causal(k_ext, tap_rows(taps_ref, 1, ls), pos_row)
+        vs_ref[:, ls] = causal(v_ext, tap_rows(taps_ref, 2, ls), pos_row)
 
     each_chunk(cot_ref.shape[1], body, 2)
 
@@ -390,9 +382,29 @@
     packed_ref[kept:] = group_sums(cols_ref[...])
 
 
-def mains_kernel(
-    total, len_ref, taps_ref, gq_ref, gks_ref, gvs_ref, tails_ref, summed_ref, gain_ref, sums_ref,
-    oq_ref, ok_ref, ov_ref, normed_ref,
+def back_short(which, pos, ls, taps_ref, grad_ref, tails_ref):
+    ext = join(grad_ref[:, ls].astype(F32), rim_of(tails_ref, which * RIM, ls))
+    taps = tap_rows(taps_ref, which, ls)
+    grad = taps[0] * ext[:K]
+    for j in range(1, KS):
+        held = jnp.where(pos >= j, ext, 0.0)
+        grad = grad + taps[j] * held[j : j + K]
+    return grad.astype(BF16)
+
+
+def main_qk_kernel(len_ref, taps_ref, tails_ref, gq_ref, gks_ref, oq_ref, ok_ref):
+    pos = positions(len_ref, first_row() + iota((K + RIM, LANES), 0))
+
+    def body(q):
+        ls = lanes_of(q)
+        oq_ref[:, ls] = back_short(0, pos, ls, taps_ref, gq_ref, tails_ref)
+        ok_ref[:, ls] = back_short(1, pos, ls, taps_ref, gks_ref, tails_ref)
+
+    each_chunk(gq_ref.shape[1], body)
+
+
+def main_v_kernel(
+    total, len_ref, taps_ref, tails_ref, gvs_ref, summed_ref, gain_ref, sums_ref, ov_ref, normed_ref
 ):
     pos = positions(len_ref, first_row() + iota((K + RIM, LANES), 0))
     inverse = inverse_of(sums_ref, total)
@@ -400,16 +412,9 @@
     def body(q):
         ls = lanes_of(q)
         normed_ref[:, ls] = (gain_ref[:, ls] * summed_ref[:, ls] * inverse).astype(BF16)
-        for i, (g_ref, o_ref) in enumerate(((gq_ref, oq_ref), (gks_ref, ok_ref), (gvs_ref, ov_ref))):
-            ext = join(g_ref[:, ls].astype(F32), rim_of(tails_ref, i * RIM, ls))
-            taps = tap_rows(taps_ref, i, ls)
-            grad = taps[0] * ext[:K]
-            for j in range(1, KS):
-                held = jnp.where(pos >= j, ext, 0.0)
-                grad = grad + taps[j] * held[j : j + K]
-            o_ref[:, ls] = grad.astype(BF16)
-
-    each_chunk(gq_ref.shape[1], body)
+        ov_ref[:, ls] = back_short(2, pos, ls, taps_ref, gvs_ref, tails_ref)
+
+    each_chunk(gvs_ref.shape[1], body)
 
 
 def unpack_kernel(one_ref, two_ref, short_ref, long_ref, skip_ref, gain_ref):
@@ -498,30 +503,24 @@
         ],
         [pltpu.VMEM((2, K, LANES), F32)], flops=10**9, moved=5 * 10**6,
     )
-    own_sums = sums
     step = 1
     while step < lax.axis_size("tp"):
         sums = sums + swapped(sums, "tp", step)
         step *= 2
-    came, _ = lax.optimization_barrier((came, own_sums))
-    k_short, v_short = call(
-        "gates", gates_kernel, [full_f] * 2, [lengths, k_input, v_input, came, taps],
-        flops=10**8, moved=2 * 10**6,
-    )
-    sums, k_short, v_short = lax.optimization_barrier((sums, k_short, v_short))
     grad_mixed, grad_qs = call(
         "grads", functools.partial(grads_kernel, wide), [full_bf, full_bf],
         [summed, mixed, q_short, cotangent, gain2, sums],
     )
     after = shifted(grad_mixed, "ctx", -1, wrap=False)
-    stats, part, qcols = call(
+    stats, part, qcols, k_short, v_short = call(
         "beside", functools.partial(beside_kernel, wide),
         [
             arr((groups + 2 * rows, LANES), F32), full_f, arr((8, channels), F32),
+            full_f, full_f,
         ],
         [
             lengths, summed, cotangent, sums, grad_mixed, grad_qs, gated, before, bwd,
-            skip2, q_input, came,
+            skip2, q_input, k_input, v_input, came, taps,
         ],
         flops=4 * 10**9, moved=5 * 10**6,
     )
@@ -538,18 +537,20 @@
         [pltpu.VMEM((24, channels), F32)], flops=10**9, moved=5 * 10**6,
     )
     tails = shifted(tails, "ctx", -1)
-    grad_q, grad_k, grad_v, normed = call(
-        "mains", functools.partial(mains_kernel, wide), [full_bf] * 4,
-        [lengths, taps, grad_qs, grad_ks, grad_vs, tails, summed, gain2, sums], flops=10**9, moved=5 * 10**6,
-    )
-    outs = (grad_q, grad_k, grad_v, normed)
+    grad_q, grad_k = call(
+        "main_qk", main_qk_kernel, [full_bf] * 2, [lengths, taps, tails, grad_qs, grad_ks],
+        flops=10**9, moved=5 * 10**6,
+    )
     count = lax.axis_size("ctx")
     step = 1
     while 2 * step < count:
         packed = packed + swapped(packed, "ctx", step)
         step *= 2
-    packed, *outs = lax.optimization_barrier((packed, *outs))
-    grad_q, grad_k, grad_v, normed = outs
+    packed, grad_q, grad_k, grad_vs = lax.optimization_barrier((packed, grad_q, grad_k, grad_vs))
+    grad_v, normed = call(
+        "main_v", functools.partial(main_v_kernel, wide), [full_bf] * 2,
+        [lengths, taps, tails, grad_vs, summed, gain2, sums], flops=10**9, moved=5 * 10**6,
+    )
     other = swapped(packed, "ctx", step)
     grad_short, grad_long, grad_skip, grad_gain = call(
         "unpack", unpack_kernel,

time: 56.6 us -> 55.2 us (0.975)
  starting transfers between devices: 12.9 us -> 10.9 us
  Pallas kernels: 26.8 us -> 27.8 us
    ppermute x5, starting transfers between devices: 6.28 us -> 2.32 us  [swapped(): lax.ppermute(x, axis, [(i, i ^ step) for i in range(lax.axis_size(axis))])]
    ppermute x4, waiting for transfers between devices: 6.42 us -> 3.81 us  [shifted(): lax.ppermute(x, axis, [p for p in pairs if wrap or p[1] - p[0] == by])]
    ppermute x5, waiting for transfers between devices: 8.6 us -> 10.8 us  [swapped(): lax.ppermute(x, axis, [(i, i ^ step) for i in range(lax.axis_size(axis))])]
    ppermute x4, starting transfers between devices: 6.61 us -> 8.59 us  [shifted(): lax.ppermute(x, axis, [p for p in pairs if wrap or p[1] - p[0] == by])]
    pallas_call x11, Pallas kernels: 26.8 us -> 27.8 us  [call(): pl.pallas_call(kernel, out_shape=outs, in_specs=[far_off] * len(ins) if h...]
  transfers between devices with their start and end apart: 9 -> 9, of which waited for: 6 -> 7; matrix products, arithmetic and copies ran while one was open for 0% -> 0% of each run, Pallas kernels for 30% -> 33%
where the time goes in v10:
time: 55.2 us; the launch traced here: 54.9 us
  Pallas kernels  27.8 us (50%)
  waiting for transfers between devices  14.6 us (26%)
  starting transfers between devices  10.9 us (20%)
  between operations  0.88 us (2%)
  local copies, waits for them, and re-layouts  0.78 us (1%)
    pallas_call x11, Pallas kernels, call(): pl.pallas_call(kernel, out_shape=outs, in_specs=[far_off] * len(ins) if h...  27.8 us
    ppermute x5, waiting for transfers between devices, swapped(): lax.ppermute(x, axis, [(i, i ^ step) for i in range(lax.axis_size(axis))])  10.8 us
    ppermute x4, starting transfers between devices, shifted(): lax.ppermute(x, axis, [p for p in pairs if wrap or p[1] - p[0] == by])  8.59 us
    ppermute x4, waiting for transfers between devices, shifted(): lax.ppermute(x, axis, [p for p in pairs if wrap or p[1] - p[0] == by])  3.81 us
    ppermute x5, starting transfers between devices, swapped(): lax.ppermute(x, axis, [(i, i ^ step) for i in range(lax.axis_size(axis))])  2.32 us
  transfers between devices with their start and end apart: 9, of which 7 were waited for; matrix products, arithmetic and copies ran while one was open for 0% of the time, Pallas kernels for 33%

profile of v10, /device:TPU:0, one launch (start us, length us, event | category | flops | bytes accessed | tf_op | source)
XLA Modules:
  0.0 54.9 jit_solution(5338108126525877852)
XLA Ops:
  0.6 3.2 %first.1 = (f32[24,1024]{1,0:T(8,128)}, bf16[160,1024]{1,0:T(8,128)(2,1)}, bf16[16,1024]{1,0:T(8,128)(2,1)}) custom-call(s32[8]{0:T(128)} %len_ref.11, bf16[3,7,64]{2,1,0:T(8,128)(2,1)} %bitcast.12, bf16[128,1024]{1,0:T(8,128)(2,1)} %q_ref.5, bf16[128,1024]{1,0:T(8,128)(2,1)} %k_ref.5, bf16[128,1024]{1,0:T(8,128)(2,1)} %v_ref.5), custom_call_target="tpu_custom_call" | custom-call | flops 100000000 | bytes 1000000 | tf_op jit(solution)/shard_map/first/pallas_call | solution.py:452
  3.9 3.0 %collective-permute-start = (bf16[160,1024]{1,0:T(8,128)(2,1)}, bf16[160,1024]{1,0:T(8,128)(2,1)S(1)}, u32[]{:S(2)}, u32[]{:S(2)}) collective-permute-start(bf16[160,1024]{1,0:T(8,128)(2,1)} %get-tuple-element.53.sent_ref), channel_id=1, source_target_pairs={{0,4},{4,8},{8,12},{12,16},{16,20},{20,24},{24,28},{28,0},{1,5},{5... | collective-permute-start | bytes 983048 | tf_op jit(solution)/shard_map/ppermute | solution.py:25
  6.9 1.6 %collective-permute-start.1 = (bf16[16,1024]{1,0:T(8,128)(2,1)}, bf16[16,1024]{1,0:T(8,128)(2,1)S(1)}, u32[]{:S(2)}, u32[]{:S(2)}) collective-permute-start(bf16[16,1024]{1,0:T(8,128)(2,1)} %get-tuple-element.52), channel_id=1, source_target_pairs={{0,8},{4,12},{8,16},{12,20},{16,24},{20,28},{24,0},{28,4},{1,9},{5... | collective-permute-start | bytes 98312 | tf_op jit(solution)/shard_map/ppermute | solution.py:25
  8.5 0.7 %copy-done.10 = bf16[64,128]{1,0:T(8,128)(2,1)S(1)} copy-done((bf16[64,128]{1,0:T(8,128)(2,1)S(1)}, bf16[64,128]{1,0:T(8,128)(2,1)}, u32[]{:S(2)}) %copy-start.10) | copy-done | bytes 16408
  9.2 1.8 %circulants.3.fwd_ref = bf16[128,8192]{1,0:T(8,128)(2,1)S(1)} custom-call(bf16[64,128]{1,0:T(8,128)(2,1)S(1)} %copy-done.10), custom_call_target="tpu_custom_call" | custom-call | flops 1000000000 | bytes 4000000 | tf_op jit(solution)/shard_map/circulants/pallas_call | solution.py:452
  11.0 0.0 copy-start.3
  11.0 0.0 copy-start.6
  11.0 0.0 copy-start.8
  11.1 1.7 %circulants.2.bwd_ref = bf16[128,8192]{1,0:T(8,128)(2,1)S(1)} custom-call(bf16[64,128]{1,0:T(8,128)(2,1)S(1)} %copy-done.10), custom_call_target="tpu_custom_call" | custom-call | flops 1000000000 | bytes 4000000 | tf_op jit(solution)/shard_map/circulants/pallas_call | solution.py:452
  12.8 0.0 copy-start.2
  12.8 0.0 copy-start.5
  12.8 2.7 %current.1 = (f32[128,1024]{1,0:T(8,128)S(1)}, f32[128,1024]{1,0:T(8,128)S(1)}, bf16[128,1024]{1,0:T(8,128)(2,1)S(1)}) custom-call(s32[8]{0:T(128)S(1)} %copy-done.8, bf16[128,1024]{1,0:T(8,128)(2,1)S(1)} %copy-done.3, f32[24,1024]{1,0:T(8,128)S(1)} %copy-done.6, bf16[160,1024]{1,0:T(8,128)(2,1)S(1)} %copy-done.4, bf16[128,8192]{1,0:T(8,128)(2,1)S(1)} %circulants.3.fwd_ref, ...), custom_call_target="tpu_custom_call" | custom-call | flops 1000000000 | bytes 5000000 | tf_op jit(solution)/shard_map/current/pallas_call | solution.py:452
  15.6 2.7 %collective-permute-done.came_ref = bf16[160,1024]{1,0:T(8,128)(2,1)S(1)} collective-permute-done((bf16[160,1024]{1,0:T(8,128)(2,1)}, bf16[160,1024]{1,0:T(8,128)(2,1)S(1)}, u32[]{:S(2)}, u32[]{:S(2)}) %collective-permute-start) | collective-permute-done | bytes 327712 | tf_op jit(solution)/shard_map/ppermute | solution.py:25
  18.3 2.1 %summed.1 = (f32[128,1024]{1,0:T(8,128)S(1)}, bf16[128,1024]{1,0:T(8,128)(2,1)S(1)}, bf16[128,1024]{1,0:T(8,128)(2,1)S(1)}, f32[128,1024]{1,0:T(8,128)S(1)}, f32...) custom-call(s32[8]{0:T(128)S(1)} %copy-done.8, bf16[160,1024]{1,0:T(8,128)(2,1)S(1)} %collective-permute-done.came_ref, ...), custom_call_target="tpu_custom_call" | custom-call | flops 1000000000 | bytes 5000000 | tf_op jit(solution)/shard_map/summed/pallas_call | solution.py:452
  20.4 0.1 collective-permute-start.2
  20.5 1.1 %collective-permute-done.2 = f32[2,128]{1,0:T(2,128)S(1)} collective-permute-done((f32[2,128]{1,0:T(2,128)S(1)}, f32[2,128]{1,0:T(2,128)S(1)}, u32[]{:S(2)}, u32[]{:S(2)}) %collective-permute-start.2) | collective-permute-done | bytes 1056 | tf_op jit(solution)/shard_map/ppermute | solution.py:29
  21.6 1.5 %collective-permute-start.3 = (f32[2,128]{1,0:T(2,128)S(1)}, f32[2,128]{1,0:T(2,128)S(1)}, u32[]{:S(2)}, u32[]{:S(2)}) collective-permute-start(f32[2,128]{1,0:T(2,128)S(1)} %add.12), channel_id=1, source_target_pairs={{0,2},{1,3},{2,0},{3,1},{4,6},{5,7},{6,4},{7,5},{8,10},{9,11},{10,... | collective-permute-start | bytes 3080 | tf_op jit(solution)/shard_map/ppermute | solution.py:29
  23.1 2.1 %collective-permute-done.3 = f32[2,128]{1,0:T(2,128)S(1)} collective-permute-done((f32[2,128]{1,0:T(2,128)S(1)}, f32[2,128]{1,0:T(2,128)S(1)}, u32[]{:S(2)}, u32[]{:S(2)}) %collective-permute-start.3) | collective-permute-done | bytes 1056 | tf_op jit(solution)/shard_map/ppermute | solution.py:29
  25.2 0.5 grads.1
  25.7 1.3 %collective-permute-start.4 = (bf16[128,1024]{1,0:T(8,128)(2,1)S(1)}, bf16[128,1024]{1,0:T(8,128)(2,1)S(1)}, u32[]{:S(2)}, u32[]{:S(2)}) collective-permute-start(bf16[128,1024]{1,0:T(8,128)(2,1)S(1)} %get-tuple-element.62.gm_ref), channel_id=1, source_target_pairs={{4,0},{8,4},{12,8},{16,12},{20,16},{24,20},{28,24},{5,1},{9,5},{13... | collective-permute-start | bytes 786440 | tf_op jit(solution)/shard_map/ppermute | solution.py:25
  27.0 6.7 %beside.1 = (f32[80,128]{1,0:T(8,128)S(1)}, f32[128,1024]{1,0:T(8,128)S(1)}, f32[8,1024]{1,0:T(8,128)S(1)}, f32[128,1024]{1,0:T(8,128)S(1)}, f32[128,1024]{1,0:T(8,128)S(1)}) custom-call(s32[8]{0:T(128)S(1)} %copy-done.8, f32[128,1024]{1,0:T(8,128)S(1)} %get-tuple-element.58.summed_ref, bf16[128,1024]{1,0:T(8,128)(2,1)S(1)} %copy-done.2, ...), custom_call_target="tpu_custom_call" | custom-call | flops 4000000000 | bytes 5000000 | tf_op jit(solution)/shard_map/beside/pallas_call | solution.py:452
  33.7 1.2 %collective-permute-done.4.after_ref = bf16[128,1024]{1,0:T(8,128)(2,1)S(1)} collective-permute-done((bf16[128,1024]{1,0:T(8,128)(2,1)S(1)}, bf16[128,1024]{1,0:T(8,128)(2,1)S(1)}, u32[]{:S(2)}, u32[]{:S(2)}) %collective-permute-start.4) | collective-permute-done | bytes 262176 | tf_op jit(solution)/shard_map/ppermute | solution.py:25
  34.8 3.3 %gate.1 = (bf16[128,1024]{1,0:T(8,128)(2,1)S(1)}, bf16[128,1024]{1,0:T(8,128)(2,1)S(1)}, bf16[32,1024]{1,0:T(8,128)(2,1)S(1)}, f32[104,128]{1,0:T(8,128)S(1)}) custom-call(s32[8]{0:T(128)S(1)} %copy-done.8, f32[128,1024]{1,0:T(8,128)S(1)} %get-tuple-element.67.part_ref, bf16[128,1024]{1,0:T(8,128)(2,1)S(1)} %collective-permute-done.4.after_ref, ...), custom_call_target="tpu_custom_call" | custom-call | flops 1000000000 | bytes 5000000 | tf_op jit(solution)/shard_map/gate/pallas_call | solution.py:452
  38.1 2.7 %collective-permute-start.5 = (bf16[32,1024]{1,0:T(8,128)(2,1)S(1)}, bf16[32,1024]{1,0:T(8,128)(2,1)S(1)}, u32[]{:S(2)}, u32[]{:S(2)}) collective-permute-start(bf16[32,1024]{1,0:T(8,128)(2,1)S(1)} %get-tuple-element.72), channel_id=1, source_target_pairs={{0,28},{4,0},{8,4},{12,8},{16,12},{20,16},{24,20},{28,24},{1,29},{... | collective-permute-start | bytes 196616 | tf_op jit(solution)/shard_map/ppermute | solution.py:25
  40.8 4.1 %collective-permute-done.6 = f32[104,128]{1,0:T(8,128)S(1)} collective-permute-done((f32[104,128]{1,0:T(8,128)S(1)}, f32[104,128]{1,0:T(8,128)S(1)}, u32[]{:S(2)}, u32[]{:S(2)}) %collective-permute-start.6) | collective-permute-done | bytes 53280 | tf_op jit(solution)/shard_map/ppermute | solution.py:29
  45.0 0.7 %collective-permute-start.7 = (f32[104,128]{1,0:T(8,128)S(1)}, f32[104,128]{1,0:T(8,128)S(1)}, u32[]{:S(2)}, u32[]{:S(2)}) collective-permute-start(f32[104,128]{1,0:T(8,128)S(1)} %add.14), channel_id=1, source_target_pairs={{0,8},{4,12},{8,0},{12,4},{16,24},{20,28},{24,16},{28,20},{1,9},{5... | collective-permute-start | bytes 159752 | tf_op jit(solution)/shard_map/ppermute | solution.py:29
  45.7 2.8 %main_qk.1 = (bf16[128,1024]{1,0:T(8,128)(2,1)}, bf16[128,1024]{1,0:T(8,128)(2,1)}) custom-call(s32[8]{0:T(128)S(1)} %copy-done.8, f32[24,1024]{1,0:T(8,128)S(1)} %copy-done.6, bf16[32,1024]{1,0:T(8,128)(2,1)S(1)} %collective-permute-done.5.tails_ref, bf16[128,1024]{1,0:T(8,128)(2,1)S(1)} %get-tuple-element.63.gq_ref, ...), custom_call_target="tpu_custom_call" | custom-call | flops 1000000000 | bytes 5000000 | tf_op jit(solution)/shard_map/main_qk/pallas_call | solution.py:452
  48.5 0.7 %collective-permute-done.7 = f32[104,128]{1,0:T(8,128)S(1)} collective-permute-done((f32[104,128]{1,0:T(8,128)S(1)}, f32[104,128]{1,0:T(8,128)S(1)}, u32[]{:S(2)}, u32[]{:S(2)}) %collective-permute-start.7) | collective-permute-done | bytes 53280 | tf_op jit(solution)/shard_map/ppermute | solution.py:29
  49.2 0.1 collective-permute-start.8
  49.3 2.3 %main_v.1 = (bf16[128,1024]{1,0:T(8,128)(2,1)}, bf16[128,1024]{1,0:T(8,128)(2,1)}) custom-call(s32[8]{0:T(128)S(1)} %copy-done.8, f32[24,1024]{1,0:T(8,128)S(1)} %copy-done.6, bf16[32,1024]{1,0:T(8,128)(2,1)S(1)} %collective-permute-done.5.tails_ref, bf16[128,1024]{1,0:T(8,128)(2,1)S(1)} %get-tuple-element.78.gvs_ref, ...), custom_call_target="tpu_custom_call" | custom-call | flops 1000000000 | bytes 5000000 | tf_op jit(solution)/shard_map/main_v/pallas_call | solution.py:452
  51.5 2.8 %collective-permute-done.8.two_ref = f32[104,128]{1,0:T(8,128)S(1)} collective-permute-done((f32[104,128]{1,0:T(8,128)S(1)}, f32[104,128]{1,0:T(8,128)S(1)}, u32[]{:S(2)}, u32[]{:S(2)}) %collective-permute-start.8) | collective-permute-done | bytes 53280 | tf_op jit(solution)/shard_map/ppermute | solution.py:29
  54.3 0.6 %unpack.1 = (f32[3,7,64]{2,1,0:T(8,128)}, f32[64,128]{1,0:T(8,128)}, f32[8,128]{1,0:T(8,128)}, f32[8,128]{1,0:T(8,128)}) custom-call(f32[104,128]{1,0:T(8,128)S(1)} %add.15.one_ref, f32[104,128]{1,0:T(8,128)S(1)} %collective-permute-done.8.two_ref), custom_call_target="tpu_custom_call" | custom-call | flops 100000000 | bytes 1000000 | tf_op jit(solution)/shard_map/unpack/pallas_call | solution.py:452
  (23 shorter events, 0.1 us)
Async XLA Ops:
  3.9 14.3 %collective-permute-start = (bf16[160,1024]{1,0:T(8,128)(2,1)}, bf16[160,1024]{1,0:T(8,128)(2,1)S(1)}, u32[]{:S(2)}, u32[]{:S(2)}) collective-permute-start(bf16[160,1024]{1,0:T(8,128)(2,1)} %get-tuple-element.53.sent_ref), channel_id=1, source_target_pairs={{0,4},{4,8},{8,12},{12,16},{16,20},{20,24},{24,28},{28,0},{1,5},{5... | collective-permute-start | bytes 983048 | tf_op jit(solution)/shard_map/ppermute | solution.py:25
  6.9 11.3 %collective-permute-start.1 = (bf16[16,1024]{1,0:T(8,128)(2,1)}, bf16[16,1024]{1,0:T(8,128)(2,1)S(1)}, u32[]{:S(2)}, u32[]{:S(2)}) collective-permute-start(bf16[16,1024]{1,0:T(8,128)(2,1)} %get-tuple-element.52), channel_id=1, source_target_pairs={{0,8},{4,12},{8,16},{12,20},{16,24},{20,28},{24,0},{28,4},{1,9},{5... | collective-permute-start | bytes 98312 | tf_op jit(solution)/shard_map/ppermute | solution.py:25
  8.5 0.7 %copy-start.10 = (bf16[64,128]{1,0:T(8,128)(2,1)S(1)}, bf16[64,128]{1,0:T(8,128)(2,1)}, u32[]{:S(2)}) copy-start(bf16[64,128]{1,0:T(8,128)(2,1)} %long_ref.1) | copy-start | bytes 49156
  11.0 1.8 %copy-start.3 = (bf16[128,1024]{1,0:T(8,128)(2,1)S(1)}, bf16[128,1024]{1,0:T(8,128)(2,1)}, u32[]{:S(2)}) copy-start(bf16[128,1024]{1,0:T(8,128)(2,1)} %q_ref.5) | copy-start | bytes 786436
  11.0 1.8 %copy-start.4 = (bf16[160,1024]{1,0:T(8,128)(2,1)S(1)}, bf16[160,1024]{1,0:T(8,128)(2,1)}, u32[]{:S(2)}) copy-start(bf16[160,1024]{1,0:T(8,128)(2,1)} %get-tuple-element.53.sent_ref) | copy-start | bytes 983044
  11.0 1.8 %copy-start.6 = (f32[24,1024]{1,0:T(8,128)S(1)}, f32[24,1024]{1,0:T(8,128)}, u32[]{:S(2)}) copy-start(f32[24,1024]{1,0:T(8,128)} %get-tuple-element.48.taps_ref) | copy-start | bytes 294916
  11.0 1.8 %copy-start.8 = (s32[8]{0:T(128)S(1)}, s32[8]{0:T(128)}, u32[]{:S(2)}) copy-start(s32[8]{0:T(128)} %len_ref.11) | copy-start | bytes 100
  11.1 1.8 %copy-start.9 = (f32[1024]{0:T(1024)S(1)}, f32[1024]{0:T(1024)}, u32[]{:S(2)}) copy-start(f32[1024]{0:T(1024)} %param.17) | copy-start | bytes 12292
  12.7 5.5 %copy-start = (bf16[128,1024]{1,0:T(8,128)(2,1)S(1)}, bf16[128,1024]{1,0:T(8,128)(2,1)}, u32[]{:S(2)}) copy-start(bf16[128,1024]{1,0:T(8,128)(2,1)} %k_ref.5) | copy-start | bytes 786436
  12.8 5.5 %copy-start.1 = (bf16[128,1024]{1,0:T(8,128)(2,1)S(1)}, bf16[128,1024]{1,0:T(8,128)(2,1)}, u32[]{:S(2)}) copy-start(bf16[128,1024]{1,0:T(8,128)(2,1)} %v_ref.5) | copy-start | bytes 786436
  12.8 5.5 %copy-start.2 = (bf16[128,1024]{1,0:T(8,128)(2,1)S(1)}, bf16[128,1024]{1,0:T(8,128)(2,1)}, u32[]{:S(2)}) copy-start(bf16[128,1024]{1,0:T(8,128)(2,1)} %cot_ref.5) | copy-start | bytes 786436
  12.8 5.5 %copy-start.5 = (bf16[128,1024]{1,0:T(8,128)(2,1)S(1)}, bf16[128,1024]{1,0:T(8,128)(2,1)}, u32[]{:S(2)}) copy-start(bf16[128,1024]{1,0:T(8,128)(2,1)} %resid_ref.1) | copy-start | bytes 786436
  12.8 5.5 %copy-start.7 = (f32[1024]{0:T(1024)S(1)}, f32[1024]{0:T(1024)}, u32[]{:S(2)}) copy-start(f32[1024]{0:T(1024)} %param.18) | copy-start | bytes 12292
  20.4 1.2 %collective-permute-start.2 = (f32[2,128]{1,0:T(2,128)S(1)}, f32[2,128]{1,0:T(2,128)S(1)}, u32[]{:S(2)}, u32[]{:S(2)}) collective-permute-start(f32[2,128]{1,0:T(2,128)S(1)} %get-tuple-element.59), channel_id=1, source_target_pairs={{0,1},{1,0},{2,3},{3,2},{4,5},{5,4},{6,7},{7,6},{8,9},{9,8},{10,11... | collective-permute-start | bytes 3080 | tf_op jit(solution)/shard_map/ppermute | solution.py:29
  21.6 3.6 %collective-permute-start.3 = (f32[2,128]{1,0:T(2,128)S(1)}, f32[2,128]{1,0:T(2,128)S(1)}, u32[]{:S(2)}, u32[]{:S(2)}) collective-permute-start(f32[2,128]{1,0:T(2,128)S(1)} %add.12), channel_id=1, source_target_pairs={{0,2},{1,3},{2,0},{3,1},{4,6},{5,7},{6,4},{7,5},{8,10},{9,11},{10,... | collective-permute-start | bytes 3080 | tf_op jit(solution)/shard_map/ppermute | solution.py:29
  25.7 9.1 %collective-permute-start.4 = (bf16[128,1024]{1,0:T(8,128)(2,1)S(1)}, bf16[128,1024]{1,0:T(8,128)(2,1)S(1)}, u32[]{:S(2)}, u32[]{:S(2)}) collective-permute-start(bf16[128,1024]{1,0:T(8,128)(2,1)S(1)} %get-tuple-element.62.gm_ref), channel_id=1, source_target_pairs={{4,0},{8,4},{12,8},{16,12},{20,16},{24,20},{28,24},{5,1},{9,5},{13... | collective-permute-start | bytes 786440 | tf_op jit(solution)/shard_map/ppermute | solution.py:25
  38.1 7.5 %collective-permute-start.5 = (bf16[32,1024]{1,0:T(8,128)(2,1)S(1)}, bf16[32,1024]{1,0:T(8,128)(2,1)S(1)}, u32[]{:S(2)}, u32[]{:S(2)}) collective-permute-start(bf16[32,1024]{1,0:T(8,128)(2,1)S(1)} %get-tuple-element.72), channel_id=1, source_target_pairs={{0,28},{4,0},{8,4},{12,8},{16,12},{20,16},{24,20},{28,24},{1,29},{... | collective-permute-start | bytes 196616 | tf_op jit(solution)/shard_map/ppermute | solution.py:25
  40.8 4.1 %collective-permute-start.6 = (f32[104,128]{1,0:T(8,128)S(1)}, f32[104,128]{1,0:T(8,128)S(1)}, u32[]{:S(2)}, u32[]{:S(2)}) collective-permute-start(f32[104,128]{1,0:T(8,128)S(1)} %get-tuple-element.73), channel_id=1, source_target_pairs={{0,4},{4,0},{8,12},{12,8},{16,20},{20,16},{24,28},{28,24},{1,5},{5... | collective-permute-start | bytes 159752 | tf_op jit(solution)/shard_map/ppermute | solution.py:29
  45.0 4.2 %collective-permute-start.7 = (f32[104,128]{1,0:T(8,128)S(1)}, f32[104,128]{1,0:T(8,128)S(1)}, u32[]{:S(2)}, u32[]{:S(2)}) collective-permute-start(f32[104,128]{1,0:T(8,128)S(1)} %add.14), channel_id=1, source_target_pairs={{0,8},{4,12},{8,0},{12,4},{16,24},{20,28},{24,16},{28,20},{1,9},{5... | collective-permute-start | bytes 159752 | tf_op jit(solution)/shard_map/ppermute | solution.py:29
  49.2 5.1 %collective-permute-start.8 = (f32[104,128]{1,0:T(8,128)S(1)}, f32[104,128]{1,0:T(8,128)S(1)}, u32[]{:S(2)}, u32[]{:S(2)}) collective-permute-start(f32[104,128]{1,0:T(8,128)S(1)} %add.15.one_ref), channel_id=1, source_target_pairs={{0,16},{4,20},{8,24},{12,28},{16,0},{20,4},{24,8},{28,12},{1,17},{... | collective-permute-start | bytes 159752 | tf_op jit(solution)/shard_map/ppermute | solution.py:29

commit v11 on v10

--- a/solution.py
+++ b/solution.py
@@ -71,20 +71,28 @@
     return [table[j : j + 1, :] for j in range(KS)]
 
 
-def causal(ext, taps, pos):
-    rows = ext.shape[0] - RIM
+def follows(len_ref, start, count):
+    pos = positions(len_ref, start + iota((count, LANES), 0))
+    return jnp.where(pos >= 1, 1.0, 0.0)
+
+
+def moved_on(x, after):
+    return pltpu.roll(x, 1, 0) * after
+
+
+def causal(ext, taps, after):
     total = taps[0] * ext[RIM:]
     for j in range(1, KS):
-        moved = ext[RIM - j : RIM - j + rows]
-        total = total + taps[j] * jnp.where(pos >= j, moved, 0.0)
+        ext = moved_on(ext, after)
+        total = total + taps[j] * ext[RIM:]
     return total
 
 
-def tap_lines(grad, ext, pos):
+def tap_lines(grad, ext, after):
     lines = [jnp.sum(grad * ext[RIM:], axis=0, keepdims=True)]
     for j in range(1, KS):
-        held = jnp.where(pos >= j, grad, 0.0)
-        lines.append(jnp.sum(held * ext[RIM - j : RIM - j + K], axis=0, keepdims=True))
+        ext = moved_on(ext, after)
+        lines.append(jnp.sum(grad * ext[RIM:], axis=0, keepdims=True))
     lines.append(jnp.zeros((8 - KS, LANES), F32))
     return join(*lines)
 
@@ -137,14 +145,14 @@
         taps_ref[i * 8 + KS : i * 8 + 8] = jnp.zeros((8 - KS, channels), F32)
     for copy in copies[1:]:
         copy.wait()
-    pos = positions(len_ref, first_row() + RIM + iota((K - RIM, LANES), 0))
+    after = follows(len_ref, first_row(), K)
 
     def body(q):
         ls = lanes_of(q)
         kx = k_ref[:, ls].astype(F32)
         vx = v_ref[:, ls].astype(F32)
-        ks = causal(kx, tap_rows(taps_ref, 1, ls), pos)
-        vs = causal(vx, tap_rows(taps_ref, 2, ls), pos)
+        ks = causal(kx, tap_rows(taps_ref, 1, ls), after)
+        vs = causal(vx, tap_rows(taps_ref, 2, ls), after)
         sent_ref[:K, ls] = join(kx[:RIM], ks * vs).astype(BF16)
         q_end = q_ref[:, ls].astype(F32)[PACK - RIM :]
         k_end = kx[K - RIM :]
@@ -188,10 +196,11 @@
     picks = join(*[as_mask((col == row + g * GS) & (row < GS)) for g in range(PER)])
     own = owners()
     top = jnp.zeros((RIM, LANES), F32)
-
-    def body(q):
-        ls = lanes_of(q)
-        qs_ref[RIM:, ls] = causal(q_ref[:, ls].astype(F32), tap_rows(taps_ref, 0, ls), pos[RIM:])
+    after = follows(len_ref, first_row(), K)
+
+    def body(q):
+        ls = lanes_of(q)
+        qs_ref[RIM:, ls] = causal(q_ref[:, ls].astype(F32), tap_rows(taps_ref, 0, ls), after)
         qs_ref[:RIM, ls] = top
         gated = join(top, sent_ref[:K, ls].astype(F32)[RIM:])
         rest = product(masked(fwd_ref, q, mask), per_group(gated.astype(BF16), own))
@@ -210,8 +219,8 @@
     col = iota((K, LANES), 1)
     pos = positions(len_ref, first_row() + row)
     mask = as_mask((col > row) & (pos >= row - col + K))
-    pos_top = pos[:RIM]
-    pos_far = positions(len_ref, first_row() - K + iota((RIM, LANES), 0))
+    after = follows(len_ref, first_row() - RIM, 2 * RIM)
+    after_far = follows(len_ref, first_row() - K - RIM, 2 * RIM)
     own = owners()
     own_top = [
         as_mask((iota((PACK, LANES), 1) // GS == g) & (iota((PACK, LANES), 0) < RIM))
@@ -225,14 +234,14 @@
         vt = tap_rows(taps_ref, 2, ls)
         k_last = rim_of(came_ref, K_LAST, ls)
         v_last = rim_of(came_ref, V_LAST, ls)
-        top = causal(join(k_last, rim_of(k_ref, 0, ls)), kt, pos_top) * causal(
-            join(v_last, rim_of(v_ref, 0, ls)), vt, pos_top
+        top = causal(join(k_last, rim_of(k_ref, 0, ls)), kt, after) * causal(
+            join(v_last, rim_of(v_ref, 0, ls)), vt, after
         )
         far_top = causal(
-            join(rim_of(far_ref, 0, ls), rim_of(came_ref, K_FIRST, ls)), kt, pos_far
-        ) * causal(join(rim_of(far_ref, RIM, ls), rim_of(came_ref, V_FIRST, ls)), vt, pos_far)
+            join(rim_of(far_ref, 0, ls), rim_of(came_ref, K_FIRST, ls)), kt, after_far
+        ) * causal(join(rim_of(far_ref, RIM, ls), rim_of(came_ref, V_FIRST, ls)), vt, after_far)
         qs_top = causal(
-            join(rim_of(came_ref, Q_LAST, ls), rim_of(q_ref, 0, ls)), tap_rows(taps_ref, 0, ls), pos_top
+            join(rim_of(came_ref, Q_LAST, ls), rim_of(q_ref, 0, ls)), tap_rows(taps_ref, 0, ls), after
         )
         before = join(far_top, came_ref[:K, ls].astype(F32)[RIM:]).astype(BF16)
         gated = join(top, sent_ref[:K, ls].astype(F32)[RIM:]).astype(BF16)
@@ -277,6 +286,19 @@
     return by_row(lax.rsqrt(sums_ref[0:1] / total + EPS))
 
 
+def gates_kernel(len_ref, k_ref, v_ref, came_ref, taps_ref, ks_ref, vs_ref):
+    after = follows(len_ref, first_row() - RIM, K + RIM)
+
+    def body(q):
+        ls = lanes_of(q)
+        k_ext = join(rim_of(came_ref, K_LAST, ls), k_ref[:, ls].astype(F32))
+        v_ext = join(rim_of(came_ref, V_LAST, ls), v_ref[:, ls].astype(F32))
+        ks_ref[:, ls] = causal(k_ext, tap_rows(taps_ref, 1, ls), after)
+        vs_ref[:, ls] = causal(v_ext, tap_rows(taps_ref, 2, ls), after)
+
+    each_chunk(k_ref.shape[1], body)
+
+
 def grads_kernel(total, summed_ref, mixed_ref, qs_ref, cot_ref, gain_ref, sums_ref, gm_ref, gq_ref):
     inverse = inverse_of(sums_ref, total)
     scale = inverse * inverse * by_row(sums_ref[1:2] / total)
@@ -293,14 +315,13 @@
 
 def beside_kernel(
     total, len_ref, summed_ref, cot_ref, sums_ref, gm_ref, gq_ref, gated_ref, before_ref,
-    bwd_ref, skip_ref, q_ref, k_ref, v_ref, came_ref, taps_ref,
-    stats_ref, part_ref, cols_ref, ks_ref, vs_ref,
+    bwd_ref, skip_ref, q_ref, came_ref, stats_ref, part_ref, cols_ref,
 ):
     groups = bwd_ref.shape[1] // K
     inverse = inverse_of(sums_ref, total)
     row = iota((K, LANES), 0)
     col = iota((K, LANES), 1)
-    pos_row = positions(len_ref, first_row() + row)
+    after = follows(len_ref, first_row() - RIM, K + RIM)
     pos = positions(len_ref, first_row() + col)
     mask = as_mask((col >= row) & (pos >= col - row))
     source = K - 1 - row
@@ -339,11 +360,7 @@
             lines.append(jnp.sum(square, axis=0, keepdims=True))
         stats_ref[pl.ds(pl.multiple_of(q * PER, PER), PER), :] = join(*lines)
         q_ext = join(rim_of(came_ref, Q_LAST, ls), q_ref[:, ls].astype(F32))
-        cols_ref[:, ls] = tap_lines(gq_ref[:, ls].astype(F32), q_ext, pos_row)
-        k_ext = join(rim_of(came_ref, K_LAST, ls), k_ref[:, ls].astype(F32))
-        v_ext = join(rim_of(came_ref, V_LAST, ls), v_ref[:, ls].astype(F32))
-        ks_ref[:, ls] = causal(k_ext, tap_rows(taps_ref, 1, ls), pos_row)
-        vs_ref[:, ls] = causal(v_ext, tap_rows(taps_ref, 2, ls), pos_row)
+        cols_ref[:, ls] = tap_lines(gq_ref[:, ls].astype(F32), q_ext, after)
 
     each_chunk(cot_ref.shape[1], body, 2)
 
@@ -356,7 +373,7 @@
     kept = stats_ref.shape[0]
     row = iota((K, LANES), 0)
     col = iota((K, LANES), 1)
-    pos_row = positions(len_ref, first_row() + row)
+    after = follows(len_ref, first_row() - RIM, K + RIM)
     pos = positions(len_ref, first_row() + K + col)
     mask = as_mask((col < row) & (pos >= col - row + K))
     own = owners()
@@ -374,31 +391,31 @@
         k_ext = join(rim_of(came_ref, K_LAST, ls), k_ref[:, ls].astype(F32))
         v_ext = join(rim_of(came_ref, V_LAST, ls), v_ref[:, ls].astype(F32))
         cols_ref[0:8, ls] = qcols_ref[:, ls]
-        cols_ref[8:16, ls] = tap_lines(gks.astype(F32), k_ext, pos_row)
-        cols_ref[16:24, ls] = tap_lines(gvs.astype(F32), v_ext, pos_row)
+        cols_ref[8:16, ls] = tap_lines(gks.astype(F32), k_ext, after)
+        cols_ref[16:24, ls] = tap_lines(gvs.astype(F32), v_ext, after)
 
     each_chunk(channels, body)
     packed_ref[0:kept] = stats_ref[...]
     packed_ref[kept:] = group_sums(cols_ref[...])
 
 
-def back_short(which, pos, ls, taps_ref, grad_ref, tails_ref):
+def back_short(which, after, ls, taps_ref, grad_ref, tails_ref):
     ext = join(grad_ref[:, ls].astype(F32), rim_of(tails_ref, which * RIM, ls))
     taps = tap_rows(taps_ref, which, ls)
     grad = taps[0] * ext[:K]
     for j in range(1, KS):
-        held = jnp.where(pos >= j, ext, 0.0)
-        grad = grad + taps[j] * held[j : j + K]
+        ext = pltpu.roll(ext * after, K + RIM - 1, 0)
+        grad = grad + taps[j] * ext[:K]
     return grad.astype(BF16)
 
 
 def main_qk_kernel(len_ref, taps_ref, tails_ref, gq_ref, gks_ref, oq_ref, ok_ref):
-    pos = positions(len_ref, first_row() + iota((K + RIM, LANES), 0))
-
-    def body(q):
-        ls = lanes_of(q)
-        oq_ref[:, ls] = back_short(0, pos, ls, taps_ref, gq_ref, tails_ref)
-        ok_ref[:, ls] = back_short(1, pos, ls, taps_ref, gks_ref, tails_ref)
+    after = follows(len_ref, first_row(), K + RIM)
+
+    def body(q):
+        ls = lanes_of(q)
+        oq_ref[:, ls] = back_short(0, after, ls, taps_ref, gq_ref, tails_ref)
+        ok_ref[:, ls] = back_short(1, after, ls, taps_ref, gks_ref, tails_ref)
 
     each_chunk(gq_ref.shape[1], body)
 
@@ -406,13 +423,13 @@
 def main_v_kernel(
     total, len_ref, taps_ref, tails_ref, gvs_ref, summed_ref, gain_ref, sums_ref, ov_ref, normed_ref
 ):
-    pos = positions(len_ref, first_row() + iota((K + RIM, LANES), 0))
+    after = follows(len_ref, first_row(), K + RIM)
     inverse = inverse_of(sums_ref, total)
 
     def body(q):
         ls = lanes_of(q)
         normed_ref[:, ls] = (gain_ref[:, ls] * summed_ref[:, ls] * inverse).astype(BF16)
-        ov_ref[:, ls] = back_short(2, pos, ls, taps_ref, gvs_ref, tails_ref)
+        ov_ref[:, ls] = back_short(2, after, ls, taps_ref, gvs_ref, tails_ref)
 
     each_chunk(gvs_ref.shape[1], body)
 
@@ -503,24 +520,30 @@
         ],
         [pltpu.VMEM((2, K, LANES), F32)], flops=10**9, moved=5 * 10**6,
     )
+    own_sums = sums
     step = 1
     while step < lax.axis_size("tp"):
         sums = sums + swapped(sums, "tp", step)
         step *= 2
+    came, _ = lax.optimization_barrier((came, own_sums))
+    k_short, v_short = call(
+        "gates", gates_kernel, [full_f] * 2, [lengths, k_input, v_input, came, taps],
+        flops=10**8, moved=2 * 10**6,
+    )
+    sums, k_short, v_short = lax.optimization_barrier((sums, k_short, v_short))
     grad_mixed, grad_qs = call(
         "grads", functools.partial(grads_kernel, wide), [full_bf, full_bf],
         [summed, mixed, q_short, cotangent, gain2, sums],
     )
     after = shifted(grad_mixed, "ctx", -1, wrap=False)
-    stats, part, qcols, k_short, v_short = call(
+    stats, part, qcols = call(
         "beside", functools.partial(beside_kernel, wide),
         [
             arr((groups + 2 * rows, LANES), F32), full_f, arr((8, channels), F32),
-            full_f, full_f,
         ],
         [
             lengths, summed, cotangent, sums, grad_mixed, grad_qs, gated, before, bwd,
-            skip2, q_input, k_input, v_input, came, taps,
+            skip2, q_input, came,
         ],
         flops=4 * 10**9, moved=5 * 10**6,
     )

time: 55.2 us -> 54.8 us (level)
  starting transfers between devices: 10.9 us -> 12.9 us
  waiting for transfers between devices: 14.6 us -> 12.7 us
  Pallas kernels: 27.8 us -> 27.2 us
    ppermute x5, waiting for transfers between devices: 10.8 us -> 6.32 us  [swapped(): lax.ppermute(x, axis, [(i, i ^ step) for i in range(lax.axis_size(axis))])]
    ppermute x5, starting transfers between devices: 2.32 us -> 6.28 us  [swapped(): lax.ppermute(x, axis, [(i, i ^ step) for i in range(lax.axis_size(axis))])]
    ppermute x4, waiting for transfers between devices: 3.81 us -> 6.41 us  [shifted(): lax.ppermute(x, axis, [p for p in pairs if wrap or p[1] - p[0] == by])]
    ppermute x4, starting transfers between devices: 8.59 us -> 6.61 us  [shifted(): lax.ppermute(x, axis, [p for p in pairs if wrap or p[1] - p[0] == by])]
    pallas_call x11 -> x12, Pallas kernels: 27.8 us -> 27.2 us  [call(): pl.pallas_call(kernel, out_shape=outs, in_specs=[far_off] * len(ins) if h...]
  transfers between devices with their start and end apart: 9 -> 9, of which waited for: 7 -> 6; matrix products, arithmetic and copies ran while one was open for 0% -> 0% of each run, Pallas kernels for 33% -> 32%
where the time goes in v11:
time: 54.8 us; the launch traced here: 54.5 us
  Pallas kernels  27.2 us (50%)
  starting transfers between devices  12.9 us (24%)
  waiting for transfers between devices  12.7 us (23%)
  between operations  0.89 us (2%)
  local copies, waits for them, and re-layouts  0.78 us (1%)
    pallas_call x12, Pallas kernels, call(): pl.pallas_call(kernel, out_shape=outs, in_specs=[far_off] * len(ins) if h...  27.2 us
    ppermute x4, starting transfers between devices, shifted(): lax.ppermute(x, axis, [p for p in pairs if wrap or p[1] - p[0] == by])  6.61 us
    ppermute x4, waiting for transfers between devices, shifted(): lax.ppermute(x, axis, [p for p in pairs if wrap or p[1] - p[0] == by])  6.41 us
    ppermute x5, waiting for transfers between devices, swapped(): lax.ppermute(x, axis, [(i, i ^ step) for i in range(lax.axis_size(axis))])  6.32 us
    ppermute x5, starting transfers between devices, swapped(): lax.ppermute(x, axis, [(i, i ^ step) for i in range(lax.axis_size(axis))])  6.28 us
  transfers between devices with their start and end apart: 9, of which 6 were waited for; matrix products, arithmetic and copies ran while one was open for 0% of the time, Pallas kernels for 32%

profile of v11, /device:TPU:0, one launch (start us, length us, event | category | flops | bytes accessed | tf_op | source)
XLA Modules:
  0.0 54.5 jit_solution(10423106387135073797)
XLA Ops:
  0.6 0.0 copy-start.11
  0.6 3.1 %first.1 = (f32[24,1024]{1,0:T(8,128)}, bf16[160,1024]{1,0:T(8,128)(2,1)}, bf16[16,1024]{1,0:T(8,128)(2,1)}) custom-call(s32[8]{0:T(128)} %len_ref.13, bf16[3,7,64]{2,1,0:T(8,128)(2,1)} %bitcast.12, bf16[128,1024]{1,0:T(8,128)(2,1)} %q_ref.5, bf16[128,1024]{1,0:T(8,128)(2,1)} %k_ref.5, bf16[128,1024]{1,0:T(8,128)(2,1)} %v_ref.5), custom_call_target="tpu_custom_call" | custom-call | flops 100000000 | bytes 1000000 | tf_op jit(solution)/shard_map/first/pallas_call | solution.py:469
  3.8 3.0 %collective-permute-start = (bf16[160,1024]{1,0:T(8,128)(2,1)}, bf16[160,1024]{1,0:T(8,128)(2,1)S(1)}, u32[]{:S(2)}, u32[]{:S(2)}) collective-permute-start(bf16[160,1024]{1,0:T(8,128)(2,1)} %get-tuple-element.57.sent_ref), channel_id=1, source_target_pairs={{0,4},{4,8},{8,12},{12,16},{16,20},{20,24},{24,28},{28,0},{1,5},{5... | collective-permute-start | bytes 983048 | tf_op jit(solution)/shard_map/ppermute | solution.py:25
  6.8 1.6 %collective-permute-start.1 = (bf16[16,1024]{1,0:T(8,128)(2,1)}, bf16[16,1024]{1,0:T(8,128)(2,1)S(1)}, u32[]{:S(2)}, u32[]{:S(2)}) collective-permute-start(bf16[16,1024]{1,0:T(8,128)(2,1)} %get-tuple-element.56), channel_id=1, source_target_pairs={{0,8},{4,12},{8,16},{12,20},{16,24},{20,28},{24,0},{28,4},{1,9},{5... | collective-permute-start | bytes 98312 | tf_op jit(solution)/shard_map/ppermute | solution.py:25
  8.4 0.7 %copy-done.10 = bf16[64,128]{1,0:T(8,128)(2,1)S(1)} copy-done((bf16[64,128]{1,0:T(8,128)(2,1)S(1)}, bf16[64,128]{1,0:T(8,128)(2,1)}, u32[]{:S(2)}) %copy-start.10) | copy-done | bytes 16408
  9.1 1.8 %circulants.3.fwd_ref = bf16[128,8192]{1,0:T(8,128)(2,1)S(1)} custom-call(bf16[64,128]{1,0:T(8,128)(2,1)S(1)} %copy-done.10), custom_call_target="tpu_custom_call" | custom-call | flops 1000000000 | bytes 4000000 | tf_op jit(solution)/shard_map/circulants/pallas_call | solution.py:469
  10.9 0.0 copy-start.4
  11.0 0.0 copy-start.8
  11.0 1.7 %circulants.2.bwd_ref = bf16[128,8192]{1,0:T(8,128)(2,1)S(1)} custom-call(bf16[64,128]{1,0:T(8,128)(2,1)S(1)} %copy-done.11), custom_call_target="tpu_custom_call" | custom-call | flops 1000000000 | bytes 4000000 | tf_op jit(solution)/shard_map/circulants/pallas_call | solution.py:469
  12.7 0.0 copy-start.2
  12.8 2.6 %current.1 = (f32[128,1024]{1,0:T(8,128)S(1)}, f32[128,1024]{1,0:T(8,128)S(1)}, bf16[128,1024]{1,0:T(8,128)(2,1)S(1)}) custom-call(s32[8]{0:T(128)S(1)} %copy-done.8, bf16[128,1024]{1,0:T(8,128)(2,1)S(1)} %copy-done.3, f32[24,1024]{1,0:T(8,128)S(1)} %copy-done.4, bf16[160,1024]{1,0:T(8,128)(2,1)S(1)} %copy-done.5, bf16[128,8192]{1,0:T(8,128)(2,1)S(1)} %circulants.3.fwd_ref, ...), custom_call_target="tpu_custom_call" | custom-call | flops 1000000000 | bytes 5000000 | tf_op jit(solution)/shard_map/current/pallas_call | solution.py:469
  15.4 2.8 %collective-permute-done.came_ref = bf16[160,1024]{1,0:T(8,128)(2,1)S(1)} collective-permute-done((bf16[160,1024]{1,0:T(8,128)(2,1)}, bf16[160,1024]{1,0:T(8,128)(2,1)S(1)}, u32[]{:S(2)}, u32[]{:S(2)}) %collective-permute-start) | collective-permute-done | bytes 327712 | tf_op jit(solution)/shard_map/ppermute | solution.py:25
  18.2 2.2 %summed.1 = (f32[128,1024]{1,0:T(8,128)S(1)}, bf16[128,1024]{1,0:T(8,128)(2,1)S(1)}, bf16[128,1024]{1,0:T(8,128)(2,1)S(1)}, f32[128,1024]{1,0:T(8,128)S(1)}, f32...) custom-call(s32[8]{0:T(128)S(1)} %copy-done.8, bf16[160,1024]{1,0:T(8,128)(2,1)S(1)} %collective-permute-done.came_ref, ...), custom_call_target="tpu_custom_call" | custom-call | flops 1000000000 | bytes 5000000 | tf_op jit(solution)/shard_map/summed/pallas_call | solution.py:469
  20.3 0.1 collective-permute-start.2
  20.4 1.1 %collective-permute-done.2 = f32[2,128]{1,0:T(2,128)S(1)} collective-permute-done((f32[2,128]{1,0:T(2,128)S(1)}, f32[2,128]{1,0:T(2,128)S(1)}, u32[]{:S(2)}, u32[]{:S(2)}) %collective-permute-start.2) | collective-permute-done | bytes 1056 | tf_op jit(solution)/shard_map/ppermute | solution.py:29
  21.5 1.5 %collective-permute-start.3 = (f32[2,128]{1,0:T(2,128)S(1)}, f32[2,128]{1,0:T(2,128)S(1)}, u32[]{:S(2)}, u32[]{:S(2)}) collective-permute-start(f32[2,128]{1,0:T(2,128)S(1)} %add.12), channel_id=1, source_target_pairs={{0,2},{1,3},{2,0},{3,1},{4,6},{5,7},{6,4},{7,5},{8,10},{9,11},{10,... | collective-permute-start | bytes 3080 | tf_op jit(solution)/shard_map/ppermute | solution.py:29
  23.0 1.9 %gates.1 = (f32[128,1024]{1,0:T(8,128)S(1)}, f32[128,1024]{1,0:T(8,128)S(1)}) custom-call(s32[8]{0:T(128)S(1)} %copy-done.8, bf16[128,1024]{1,0:T(8,128)(2,1)S(1)} %copy-done, bf16[128,1024]{1,0:T(8,128)(2,1)S(1)} %copy-done.1, bf16[160,1024]{1,0:T(8,128)(2,1)S(1)} %collective-permute-done.came_ref, f32[24,1024]{1,0:T(8,128)S(1)} %copy-done.4), custom_call_target="tpu_custom_call" | custom-call | flops 100000000 | bytes 2000000 | tf_op jit(solution)/shard_map/gates/pallas_call | solution.py:469
  24.9 0.2 collective-permute-done.3
  25.1 0.5 grads.1
  25.6 1.3 %collective-permute-start.4 = (bf16[128,1024]{1,0:T(8,128)(2,1)S(1)}, bf16[128,1024]{1,0:T(8,128)(2,1)S(1)}, u32[]{:S(2)}, u32[]{:S(2)}) collective-permute-start(bf16[128,1024]{1,0:T(8,128)(2,1)S(1)} %get-tuple-element.70.gm_ref), channel_id=1, source_target_pairs={{4,0},{8,4},{12,8},{16,12},{20,16},{24,20},{28,24},{5,1},{9,5},{13... | collective-permute-start | bytes 786440 | tf_op jit(solution)/shard_map/ppermute | solution.py:25
  26.9 4.9 %beside.1 = (f32[80,128]{1,0:T(8,128)S(1)}, f32[128,1024]{1,0:T(8,128)S(1)}, f32[8,1024]{1,0:T(8,128)S(1)}) custom-call(s32[8]{0:T(128)S(1)} %copy-done.8, f32[128,1024]{1,0:T(8,128)S(1)} %get-tuple-element.62.summed_ref, bf16[128,1024]{1,0:T(8,128)(2,1)S(1)} %copy-done.2, f32[2,128]{1,0:T(2,128)S(1)} %add.13.sums_ref, ...), custom_call_target="tpu_custom_call" | custom-call | flops 4000000000 | bytes 5000000 | tf_op jit(solution)/shard_map/beside/pallas_call | solution.py:469
  31.8 3.6 %collective-permute-done.4.after_ref = bf16[128,1024]{1,0:T(8,128)(2,1)S(1)} collective-permute-done((bf16[128,1024]{1,0:T(8,128)(2,1)S(1)}, bf16[128,1024]{1,0:T(8,128)(2,1)S(1)}, u32[]{:S(2)}, u32[]{:S(2)}) %collective-permute-start.4) | collective-permute-done | bytes 262176 | tf_op jit(solution)/shard_map/ppermute | solution.py:25
  35.5 3.2 %gate.1 = (bf16[128,1024]{1,0:T(8,128)(2,1)S(1)}, bf16[128,1024]{1,0:T(8,128)(2,1)S(1)}, bf16[32,1024]{1,0:T(8,128)(2,1)S(1)}, f32[104,128]{1,0:T(8,128)S(1)}) custom-call(s32[8]{0:T(128)S(1)} %copy-done.8, f32[128,1024]{1,0:T(8,128)S(1)} %get-tuple-element.75.part_ref, bf16[128,1024]{1,0:T(8,128)(2,1)S(1)} %collective-permute-done.4.after_ref, ...), custom_call_target="tpu_custom_call" | custom-call | flops 1000000000 | bytes 5000000 | tf_op jit(solution)/shard_map/gate/pallas_call | solution.py:469
  38.7 0.7 %collective-permute-start.5 = (bf16[32,1024]{1,0:T(8,128)(2,1)S(1)}, bf16[32,1024]{1,0:T(8,128)(2,1)S(1)}, u32[]{:S(2)}, u32[]{:S(2)}) collective-permute-start(bf16[32,1024]{1,0:T(8,128)(2,1)S(1)} %get-tuple-element.80), channel_id=1, source_target_pairs={{0,28},{4,0},{8,4},{12,8},{16,12},{20,16},{24,20},{28,24},{1,29},{... | collective-permute-start | bytes 196616 | tf_op jit(solution)/shard_map/ppermute | solution.py:25
  39.4 1.4 %collective-permute-start.6 = (f32[104,128]{1,0:T(8,128)S(1)}, f32[104,128]{1,0:T(8,128)S(1)}, u32[]{:S(2)}, u32[]{:S(2)}) collective-permute-start(f32[104,128]{1,0:T(8,128)S(1)} %get-tuple-element.81), channel_id=1, source_target_pairs={{0,4},{4,0},{8,12},{12,8},{16,20},{20,16},{24,28},{28,24},{1,5},{5... | collective-permute-start | bytes 159752 | tf_op jit(solution)/shard_map/ppermute | solution.py:29
  40.7 2.8 %collective-permute-done.6 = f32[104,128]{1,0:T(8,128)S(1)} collective-permute-done((f32[104,128]{1,0:T(8,128)S(1)}, f32[104,128]{1,0:T(8,128)S(1)}, u32[]{:S(2)}, u32[]{:S(2)}) %collective-permute-start.6) | collective-permute-done | bytes 53280 | tf_op jit(solution)/shard_map/ppermute | solution.py:29
  43.6 2.6 %collective-permute-start.7 = (f32[104,128]{1,0:T(8,128)S(1)}, f32[104,128]{1,0:T(8,128)S(1)}, u32[]{:S(2)}, u32[]{:S(2)}) collective-permute-start(f32[104,128]{1,0:T(8,128)S(1)} %add.14), channel_id=1, source_target_pairs={{0,8},{4,12},{8,0},{12,4},{16,24},{20,28},{24,16},{28,20},{1,9},{5... | collective-permute-start | bytes 159752 | tf_op jit(solution)/shard_map/ppermute | solution.py:29
  46.2 2.6 %main_qk.1 = (bf16[128,1024]{1,0:T(8,128)(2,1)}, bf16[128,1024]{1,0:T(8,128)(2,1)}) custom-call(s32[8]{0:T(128)S(1)} %copy-done.8, f32[24,1024]{1,0:T(8,128)S(1)} %copy-done.4, bf16[32,1024]{1,0:T(8,128)(2,1)S(1)} %collective-permute-done.5.tails_ref, bf16[128,1024]{1,0:T(8,128)(2,1)S(1)} %get-tuple-element.71.gq_ref, ...), custom_call_target="tpu_custom_call" | custom-call | flops 1000000000 | bytes 5000000 | tf_op jit(solution)/shard_map/main_qk/pallas_call | solution.py:469
  48.8 0.7 %collective-permute-start.8 = (f32[104,128]{1,0:T(8,128)S(1)}, f32[104,128]{1,0:T(8,128)S(1)}, u32[]{:S(2)}, u32[]{:S(2)}) collective-permute-start(f32[104,128]{1,0:T(8,128)S(1)} %add.15.one_ref), channel_id=1, source_target_pairs={{0,16},{4,20},{8,24},{12,28},{16,0},{20,4},{24,8},{28,12},{1,17},{... | collective-permute-start | bytes 159752 | tf_op jit(solution)/shard_map/ppermute | solution.py:29
  49.6 2.2 %main_v.1 = (bf16[128,1024]{1,0:T(8,128)(2,1)}, bf16[128,1024]{1,0:T(8,128)(2,1)}) custom-call(s32[8]{0:T(128)S(1)} %copy-done.8, f32[24,1024]{1,0:T(8,128)S(1)} %copy-done.4, bf16[32,1024]{1,0:T(8,128)(2,1)S(1)} %collective-permute-done.5.tails_ref, bf16[128,1024]{1,0:T(8,128)(2,1)S(1)} %get-tuple-element.86.gvs_ref, ...), custom_call_target="tpu_custom_call" | custom-call | flops 1000000000 | bytes 5000000 | tf_op jit(solution)/shard_map/main_v/pallas_call | solution.py:469
  51.7 2.2 %collective-permute-done.8.two_ref = f32[104,128]{1,0:T(8,128)S(1)} collective-permute-done((f32[104,128]{1,0:T(8,128)S(1)}, f32[104,128]{1,0:T(8,128)S(1)}, u32[]{:S(2)}, u32[]{:S(2)}) %collective-permute-start.8) | collective-permute-done | bytes 53280 | tf_op jit(solution)/shard_map/ppermute | solution.py:29
  53.9 0.6 %unpack.1 = (f32[3,7,64]{2,1,0:T(8,128)}, f32[64,128]{1,0:T(8,128)}, f32[8,128]{1,0:T(8,128)}, f32[8,128]{1,0:T(8,128)}) custom-call(f32[104,128]{1,0:T(8,128)S(1)} %add.15.one_ref, f32[104,128]{1,0:T(8,128)S(1)} %collective-permute-done.8.two_ref), custom_call_target="tpu_custom_call" | custom-call | flops 100000000 | bytes 1000000 | tf_op jit(solution)/shard_map/unpack/pallas_call | solution.py:469
  (26 shorter events, 0.1 us)
Async XLA Ops:
  0.6 10.3 %copy-start.11 = (bf16[64,128]{1,0:T(8,128)(2,1)S(1)}, bf16[64,128]{1,0:T(8,128)(2,1)}, u32[]{:S(2)}) copy-start(bf16[64,128]{1,0:T(8,128)(2,1)} %long_ref.1) | copy-start | bytes 49156
  3.8 14.3 %collective-permute-start = (bf16[160,1024]{1,0:T(8,128)(2,1)}, bf16[160,1024]{1,0:T(8,128)(2,1)S(1)}, u32[]{:S(2)}, u32[]{:S(2)}) collective-permute-start(bf16[160,1024]{1,0:T(8,128)(2,1)} %get-tuple-element.57.sent_ref), channel_id=1, source_target_pairs={{0,4},{4,8},{8,12},{12,16},{16,20},{20,24},{24,28},{28,0},{1,5},{5... | collective-permute-start | bytes 983048 | tf_op jit(solution)/shard_map/ppermute | solution.py:25
  6.8 11.3 %collective-permute-start.1 = (bf16[16,1024]{1,0:T(8,128)(2,1)}, bf16[16,1024]{1,0:T(8,128)(2,1)S(1)}, u32[]{:S(2)}, u32[]{:S(2)}) collective-permute-start(bf16[16,1024]{1,0:T(8,128)(2,1)} %get-tuple-element.56), channel_id=1, source_target_pairs={{0,8},{4,12},{8,16},{12,20},{16,24},{20,28},{24,0},{28,4},{1,9},{5... | collective-permute-start | bytes 98312 | tf_op jit(solution)/shard_map/ppermute | solution.py:25
  8.4 0.7 %copy-start.10 = (bf16[64,128]{1,0:T(8,128)(2,1)S(1)}, bf16[64,128]{1,0:T(8,128)(2,1)}, u32[]{:S(2)}) copy-start(bf16[64,128]{1,0:T(8,128)(2,1)} %long_ref.1) | copy-start | bytes 49156
  10.9 1.8 %copy-start.3 = (bf16[128,1024]{1,0:T(8,128)(2,1)S(1)}, bf16[128,1024]{1,0:T(8,128)(2,1)}, u32[]{:S(2)}) copy-start(bf16[128,1024]{1,0:T(8,128)(2,1)} %q_ref.5) | copy-start | bytes 786436
  10.9 1.8 %copy-start.4 = (f32[24,1024]{1,0:T(8,128)S(1)}, f32[24,1024]{1,0:T(8,128)}, u32[]{:S(2)}) copy-start(f32[24,1024]{1,0:T(8,128)} %get-tuple-element.52.taps_ref) | copy-start | bytes 294916
  10.9 1.8 %copy-start.5 = (bf16[160,1024]{1,0:T(8,128)(2,1)S(1)}, bf16[160,1024]{1,0:T(8,128)(2,1)}, u32[]{:S(2)}) copy-start(bf16[160,1024]{1,0:T(8,128)(2,1)} %get-tuple-element.57.sent_ref) | copy-start | bytes 983044
  11.0 1.8 %copy-start.8 = (s32[8]{0:T(128)S(1)}, s32[8]{0:T(128)}, u32[]{:S(2)}) copy-start(s32[8]{0:T(128)} %len_ref.13) | copy-start | bytes 100
  11.0 1.8 %copy-start.9 = (f32[1024]{0:T(1024)S(1)}, f32[1024]{0:T(1024)}, u32[]{:S(2)}) copy-start(f32[1024]{0:T(1024)} %param.17) | copy-start | bytes 12292
  12.7 5.5 %copy-start = (bf16[128,1024]{1,0:T(8,128)(2,1)S(1)}, bf16[128,1024]{1,0:T(8,128)(2,1)}, u32[]{:S(2)}) copy-start(bf16[128,1024]{1,0:T(8,128)(2,1)} %k_ref.5) | copy-start | bytes 786436
  12.7 5.5 %copy-start.1 = (bf16[128,1024]{1,0:T(8,128)(2,1)S(1)}, bf16[128,1024]{1,0:T(8,128)(2,1)}, u32[]{:S(2)}) copy-start(bf16[128,1024]{1,0:T(8,128)(2,1)} %v_ref.5) | copy-start | bytes 786436
  12.7 5.5 %copy-start.2 = (bf16[128,1024]{1,0:T(8,128)(2,1)S(1)}, bf16[128,1024]{1,0:T(8,128)(2,1)}, u32[]{:S(2)}) copy-start(bf16[128,1024]{1,0:T(8,128)(2,1)} %cot_ref.5) | copy-start | bytes 786436
  12.7 5.5 %copy-start.6 = (bf16[128,1024]{1,0:T(8,128)(2,1)S(1)}, bf16[128,1024]{1,0:T(8,128)(2,1)}, u32[]{:S(2)}) copy-start(bf16[128,1024]{1,0:T(8,128)(2,1)} %resid_ref.1) | copy-start | bytes 786436
  12.7 5.4 %copy-start.7 = (f32[1024]{0:T(1024)S(1)}, f32[1024]{0:T(1024)}, u32[]{:S(2)}) copy-start(f32[1024]{0:T(1024)} %param.18) | copy-start | bytes 12292
  20.3 1.2 %collective-permute-start.2 = (f32[2,128]{1,0:T(2,128)S(1)}, f32[2,128]{1,0:T(2,128)S(1)}, u32[]{:S(2)}, u32[]{:S(2)}) collective-permute-start(f32[2,128]{1,0:T(2,128)S(1)} %get-tuple-element.63), channel_id=1, source_target_pairs={{0,1},{1,0},{2,3},{3,2},{4,5},{5,4},{6,7},{7,6},{8,9},{9,8},{10,11... | collective-permute-start | bytes 3080 | tf_op jit(solution)/shard_map/ppermute | solution.py:29
  21.5 3.6 %collective-permute-start.3 = (f32[2,128]{1,0:T(2,128)S(1)}, f32[2,128]{1,0:T(2,128)S(1)}, u32[]{:S(2)}, u32[]{:S(2)}) collective-permute-start(f32[2,128]{1,0:T(2,128)S(1)} %add.12), channel_id=1, source_target_pairs={{0,2},{1,3},{2,0},{3,1},{4,6},{5,7},{6,4},{7,5},{8,10},{9,11},{10,... | collective-permute-start | bytes 3080 | tf_op jit(solution)/shard_map/ppermute | solution.py:29
  25.6 9.8 %collective-permute-start.4 = (bf16[128,1024]{1,0:T(8,128)(2,1)S(1)}, bf16[128,1024]{1,0:T(8,128)(2,1)S(1)}, u32[]{:S(2)}, u32[]{:S(2)}) collective-permute-start(bf16[128,1024]{1,0:T(8,128)(2,1)S(1)} %get-tuple-element.70.gm_ref), channel_id=1, source_target_pairs={{4,0},{8,4},{12,8},{16,12},{20,16},{24,20},{28,24},{5,1},{9,5},{13... | collective-permute-start | bytes 786440 | tf_op jit(solution)/shard_map/ppermute | solution.py:25
  38.7 7.5 %collective-permute-start.5 = (bf16[32,1024]{1,0:T(8,128)(2,1)S(1)}, bf16[32,1024]{1,0:T(8,128)(2,1)S(1)}, u32[]{:S(2)}, u32[]{:S(2)}) collective-permute-start(bf16[32,1024]{1,0:T(8,128)(2,1)S(1)} %get-tuple-element.80), channel_id=1, source_target_pairs={{0,28},{4,0},{8,4},{12,8},{16,12},{20,16},{24,20},{28,24},{1,29},{... | collective-permute-start | bytes 196616 | tf_op jit(solution)/shard_map/ppermute | solution.py:25
  39.4 4.2 %collective-permute-start.6 = (f32[104,128]{1,0:T(8,128)S(1)}, f32[104,128]{1,0:T(8,128)S(1)}, u32[]{:S(2)}, u32[]{:S(2)}) collective-permute-start(f32[104,128]{1,0:T(8,128)S(1)} %get-tuple-element.81), channel_id=1, source_target_pairs={{0,4},{4,0},{8,12},{12,8},{16,20},{20,16},{24,28},{28,24},{1,5},{5... | collective-permute-start | bytes 159752 | tf_op jit(solution)/shard_map/ppermute | solution.py:29
  43.6 5.2 %collective-permute-start.7 = (f32[104,128]{1,0:T(8,128)S(1)}, f32[104,128]{1,0:T(8,128)S(1)}, u32[]{:S(2)}, u32[]{:S(2)}) collective-permute-start(f32[104,128]{1,0:T(8,128)S(1)} %add.14), channel_id=1, source_target_pairs={{0,8},{4,12},{8,0},{12,4},{16,24},{20,28},{24,16},{28,20},{1,9},{5... | collective-permute-start | bytes 159752 | tf_op jit(solution)/shard_map/ppermute | solution.py:29
  48.8 5.1 %collective-permute-start.8 = (f32[104,128]{1,0:T(8,128)S(1)}, f32[104,128]{1,0:T(8,128)S(1)}, u32[]{:S(2)}, u32[]{:S(2)}) collective-permute-start(f32[104,128]{1,0:T(8,128)S(1)} %add.15.one_ref), channel_id=1, source_target_pairs={{0,16},{4,20},{8,24},{12,28},{16,0},{20,4},{24,8},{28,12},{1,17},{... | collective-permute-start | bytes 159752 | tf_op jit(solution)/shard_map/ppermute | solution.py:29

commit v12 on v11

--- a/solution.py
+++ b/solution.py
@@ -362,7 +362,7 @@
         q_ext = join(rim_of(came_ref, Q_LAST, ls), q_ref[:, ls].astype(F32))
         cols_ref[:, ls] = tap_lines(gq_ref[:, ls].astype(F32), q_ext, after)
 
-    each_chunk(cot_ref.shape[1], body, 2)
+    each_chunk(cot_ref.shape[1], body, 4)
 
 
 def gate_kernel(
@@ -409,29 +409,26 @@
     return grad.astype(BF16)
 
 
-def main_qk_kernel(len_ref, taps_ref, tails_ref, gq_ref, gks_ref, oq_ref, ok_ref):
+def mains_kernel(len_ref, taps_ref, tails_ref, gq_ref, gks_ref, gvs_ref, oq_ref, ok_ref, ov_ref):
     after = follows(len_ref, first_row(), K + RIM)
 
     def body(q):
         ls = lanes_of(q)
         oq_ref[:, ls] = back_short(0, after, ls, taps_ref, gq_ref, tails_ref)
         ok_ref[:, ls] = back_short(1, after, ls, taps_ref, gks_ref, tails_ref)
+        ov_ref[:, ls] = back_short(2, after, ls, taps_ref, gvs_ref, tails_ref)
 
     each_chunk(gq_ref.shape[1], body)
 
 
-def main_v_kernel(
-    total, len_ref, taps_ref, tails_ref, gvs_ref, summed_ref, gain_ref, sums_ref, ov_ref, normed_ref
-):
-    after = follows(len_ref, first_row(), K + RIM)
+def normed_kernel(total, summed_ref, gain_ref, sums_ref, normed_ref):
     inverse = inverse_of(sums_ref, total)
 
     def body(q):
         ls = lanes_of(q)
         normed_ref[:, ls] = (gain_ref[:, ls] * summed_ref[:, ls] * inverse).astype(BF16)
-        ov_ref[:, ls] = back_short(2, after, ls, taps_ref, gvs_ref, tails_ref)
-
-    each_chunk(gvs_ref.shape[1], body)
+
+    each_chunk(summed_ref.shape[1], body)
 
 
 def unpack_kernel(one_ref, two_ref, short_ref, long_ref, skip_ref, gain_ref):
@@ -559,22 +556,25 @@
         ],
         [pltpu.VMEM((24, channels), F32)], flops=10**9, moved=5 * 10**6,
     )
+    count = lax.axis_size("ctx")
+    packed, summed = lax.optimization_barrier((packed, summed))
+    packed = packed + swapped(packed, "ctx", 1)
+    (normed,) = call(
+        "normed", functools.partial(normed_kernel, wide), [full_bf], [summed, gain2, sums],
+        flops=10**9, moved=5 * 10**6,
+    )
+    normed, tails, packed = lax.optimization_barrier((normed, tails, packed))
     tails = shifted(tails, "ctx", -1)
-    grad_q, grad_k = call(
-        "main_qk", main_qk_kernel, [full_bf] * 2, [lengths, taps, tails, grad_qs, grad_ks],
-        flops=10**9, moved=5 * 10**6,
-    )
-    count = lax.axis_size("ctx")
-    step = 1
+    step = 2
     while 2 * step < count:
         packed = packed + swapped(packed, "ctx", step)
         step *= 2
-    packed, grad_q, grad_k, grad_vs = lax.optimization_barrier((packed, grad_q, grad_k, grad_vs))
-    grad_v, normed = call(
-        "main_v", functools.partial(main_v_kernel, wide), [full_bf] * 2,
-        [lengths, taps, tails, grad_vs, summed, gain2, sums], flops=10**9, moved=5 * 10**6,
-    )
+    packed, tails = lax.optimization_barrier((packed, tails))
     other = swapped(packed, "ctx", step)
+    grad_q, grad_k, grad_v = call(
+        "mains", mains_kernel, [full_bf] * 3,
+        [lengths, taps, tails, grad_qs, grad_ks, grad_vs], flops=10**9, moved=5 * 10**6,
+    )
     grad_short, grad_long, grad_skip, grad_gain = call(
         "unpack", unpack_kernel,
         [

time: 54.8 us -> 55 us (level)
  Pallas kernels: 27.2 us -> 26.5 us
    pallas_call x12, Pallas kernels: 27.2 us -> 26.5 us  [call(): pl.pallas_call(kernel, out_shape=outs, in_specs=[far_off] * len(ins) if h...]
  transfers between devices with their start and end apart: 9 -> 9, of which waited for: 6 -> 7; matrix products, arithmetic and copies ran while one was open for 0% -> 0% of each run, Pallas kernels for 32% -> 31%
where the time goes in v12:
time: 55 us; the launch traced here: 54.7 us
  Pallas kernels  26.5 us (48%)
  starting transfers between devices  13.4 us (24%)
  waiting for transfers between devices  13.2 us (24%)
  between operations  0.9 us (2%)
  local copies, waits for them, and re-layouts  0.78 us (1%)
    pallas_call x12, Pallas kernels, call(): pl.pallas_call(kernel, out_shape=outs, in_specs=[far_off] * len(ins) if h...  26.5 us
    ppermute x4, starting transfers between devices, shifted(): lax.ppermute(x, axis, [p for p in pairs if wrap or p[1] - p[0] == by])  7.07 us
    ppermute x5, waiting for transfers between devices, swapped(): lax.ppermute(x, axis, [(i, i ^ step) for i in range(lax.axis_size(axis))])  6.66 us
    ppermute x4, waiting for transfers between devices, shifted(): lax.ppermute(x, axis, [p for p in pairs if wrap or p[1] - p[0] == by])  6.55 us
    ppermute x5, starting transfers between devices, swapped(): lax.ppermute(x, axis, [(i, i ^ step) for i in range(lax.axis_size(axis))])  6.3 us
  transfers between devices with their start and end apart: 9, of which 7 were waited for; matrix products, arithmetic and copies ran while one was open for 0% of the time, Pallas kernels for 31%

profile of v12, /device:TPU:0, one launch (start us, length us, event | category | flops | bytes accessed | tf_op | source)
XLA Modules:
  0.0 54.7 jit_solution(7756424994562350415)
XLA Ops:
  0.6 0.0 copy-start.11
  0.6 3.1 %first.1 = (f32[24,1024]{1,0:T(8,128)}, bf16[160,1024]{1,0:T(8,128)(2,1)}, bf16[16,1024]{1,0:T(8,128)(2,1)}) custom-call(s32[8]{0:T(128)} %len_ref.11, bf16[3,7,64]{2,1,0:T(8,128)(2,1)} %bitcast.12, bf16[128,1024]{1,0:T(8,128)(2,1)} %q_ref.5, bf16[128,1024]{1,0:T(8,128)(2,1)} %k_ref.5, bf16[128,1024]{1,0:T(8,128)(2,1)} %v_ref.5), custom_call_target="tpu_custom_call" | custom-call | flops 100000000 | bytes 1000000 | tf_op jit(solution)/shard_map/first/pallas_call | solution.py:466
  3.8 3.0 %collective-permute-start = (bf16[160,1024]{1,0:T(8,128)(2,1)}, bf16[160,1024]{1,0:T(8,128)(2,1)S(1)}, u32[]{:S(2)}, u32[]{:S(2)}) collective-permute-start(bf16[160,1024]{1,0:T(8,128)(2,1)} %get-tuple-element.59.sent_ref), channel_id=1, source_target_pairs={{0,4},{4,8},{8,12},{12,16},{16,20},{20,24},{24,28},{28,0},{1,5},{5... | collective-permute-start | bytes 983048 | tf_op jit(solution)/shard_map/ppermute | solution.py:25
  6.8 1.6 %collective-permute-start.1 = (bf16[16,1024]{1,0:T(8,128)(2,1)}, bf16[16,1024]{1,0:T(8,128)(2,1)S(1)}, u32[]{:S(2)}, u32[]{:S(2)}) collective-permute-start(bf16[16,1024]{1,0:T(8,128)(2,1)} %get-tuple-element.57), channel_id=1, source_target_pairs={{0,8},{4,12},{8,16},{12,20},{16,24},{20,28},{24,0},{28,4},{1,9},{5... | collective-permute-start | bytes 98312 | tf_op jit(solution)/shard_map/ppermute | solution.py:25
  8.4 0.7 %copy-done.10 = bf16[64,128]{1,0:T(8,128)(2,1)S(1)} copy-done((bf16[64,128]{1,0:T(8,128)(2,1)S(1)}, bf16[64,128]{1,0:T(8,128)(2,1)}, u32[]{:S(2)}) %copy-start.10) | copy-done | bytes 16408
  9.1 1.8 %circulants.3.fwd_ref = bf16[128,8192]{1,0:T(8,128)(2,1)S(1)} custom-call(bf16[64,128]{1,0:T(8,128)(2,1)S(1)} %copy-done.10), custom_call_target="tpu_custom_call" | custom-call | flops 1000000000 | bytes 4000000 | tf_op jit(solution)/shard_map/circulants/pallas_call | solution.py:466
  10.9 0.0 copy-start.4
  11.0 0.0 copy-start.8
  11.0 1.7 %circulants.2.bwd_ref = bf16[128,8192]{1,0:T(8,128)(2,1)S(1)} custom-call(bf16[64,128]{1,0:T(8,128)(2,1)S(1)} %copy-done.11), custom_call_target="tpu_custom_call" | custom-call | flops 1000000000 | bytes 4000000 | tf_op jit(solution)/shard_map/circulants/pallas_call | solution.py:466
  12.8 2.6 %current.1 = (f32[128,1024]{1,0:T(8,128)S(1)}, f32[128,1024]{1,0:T(8,128)S(1)}, bf16[128,1024]{1,0:T(8,128)(2,1)S(1)}) custom-call(s32[8]{0:T(128)S(1)} %copy-done.8, bf16[128,1024]{1,0:T(8,128)(2,1)S(1)} %copy-done.3, f32[24,1024]{1,0:T(8,128)S(1)} %copy-done.4, bf16[160,1024]{1,0:T(8,128)(2,1)S(1)} %copy-done.5, bf16[128,8192]{1,0:T(8,128)(2,1)S(1)} %circulants.3.fwd_ref, ...), custom_call_target="tpu_custom_call" | custom-call | flops 1000000000 | bytes 5000000 | tf_op jit(solution)/shard_map/current/pallas_call | solution.py:466
  15.4 2.8 %collective-permute-done.came_ref = bf16[160,1024]{1,0:T(8,128)(2,1)S(1)} collective-permute-done((bf16[160,1024]{1,0:T(8,128)(2,1)}, bf16[160,1024]{1,0:T(8,128)(2,1)S(1)}, u32[]{:S(2)}, u32[]{:S(2)}) %collective-permute-start) | collective-permute-done | bytes 327712 | tf_op jit(solution)/shard_map/ppermute | solution.py:25
  18.2 2.2 %summed.1 = (f32[128,1024]{1,0:T(8,128)S(1)}, bf16[128,1024]{1,0:T(8,128)(2,1)S(1)}, bf16[128,1024]{1,0:T(8,128)(2,1)S(1)}, f32[128,1024]{1,0:T(8,128)S(1)}, f32...) custom-call(s32[8]{0:T(128)S(1)} %copy-done.8, bf16[160,1024]{1,0:T(8,128)(2,1)S(1)} %collective-permute-done.came_ref, ...), custom_call_target="tpu_custom_call" | custom-call | flops 1000000000 | bytes 5000000 | tf_op jit(solution)/shard_map/summed/pallas_call | solution.py:466
  20.3 0.1 collective-permute-start.2
  20.4 1.1 %collective-permute-done.2 = f32[2,128]{1,0:T(2,128)S(1)} collective-permute-done((f32[2,128]{1,0:T(2,128)S(1)}, f32[2,128]{1,0:T(2,128)S(1)}, u32[]{:S(2)}, u32[]{:S(2)}) %collective-permute-start.2) | collective-permute-done | bytes 1056 | tf_op jit(solution)/shard_map/ppermute | solution.py:29
  21.5 1.5 %collective-permute-start.3 = (f32[2,128]{1,0:T(2,128)S(1)}, f32[2,128]{1,0:T(2,128)S(1)}, u32[]{:S(2)}, u32[]{:S(2)}) collective-permute-start(f32[2,128]{1,0:T(2,128)S(1)} %add.12), channel_id=1, source_target_pairs={{0,2},{1,3},{2,0},{3,1},{4,6},{5,7},{6,4},{7,5},{8,10},{9,11},{10,... | collective-permute-start | bytes 3080 | tf_op jit(solution)/shard_map/ppermute | solution.py:29
  23.0 1.9 %gates.1 = (f32[128,1024]{1,0:T(8,128)S(1)}, f32[128,1024]{1,0:T(8,128)S(1)}) custom-call(s32[8]{0:T(128)S(1)} %copy-done.8, bf16[128,1024]{1,0:T(8,128)(2,1)S(1)} %copy-done, bf16[128,1024]{1,0:T(8,128)(2,1)S(1)} %copy-done.1, bf16[160,1024]{1,0:T(8,128)(2,1)S(1)} %collective-permute-done.came_ref, f32[24,1024]{1,0:T(8,128)S(1)} %copy-done.4), custom_call_target="tpu_custom_call" | custom-call | flops 100000000 | bytes 2000000 | tf_op jit(solution)/shard_map/gates/pallas_call | solution.py:466
  24.9 0.2 collective-permute-done.3
  25.1 0.5 grads.1
  25.6 1.3 %collective-permute-start.4 = (bf16[128,1024]{1,0:T(8,128)(2,1)S(1)}, bf16[128,1024]{1,0:T(8,128)(2,1)S(1)}, u32[]{:S(2)}, u32[]{:S(2)}) collective-permute-start(bf16[128,1024]{1,0:T(8,128)(2,1)S(1)} %get-tuple-element.72.gm_ref), channel_id=1, source_target_pairs={{4,0},{8,4},{12,8},{16,12},{20,16},{24,20},{28,24},{5,1},{9,5},{13... | collective-permute-start | bytes 786440 | tf_op jit(solution)/shard_map/ppermute | solution.py:25
  26.9 4.7 %beside.1 = (f32[80,128]{1,0:T(8,128)S(1)}, f32[128,1024]{1,0:T(8,128)S(1)}, f32[8,1024]{1,0:T(8,128)S(1)}) custom-call(s32[8]{0:T(128)S(1)} %copy-done.8, f32[128,1024]{1,0:T(8,128)S(1)} %get-tuple-element.83.summed_ref, bf16[128,1024]{1,0:T(8,128)(2,1)S(1)} %copy-done.2, f32[2,128]{1,0:T(2,128)S(1)} %add.13.sums_ref, ...), custom_call_target="tpu_custom_call" | custom-call | flops 4000000000 | bytes 5000000 | tf_op jit(solution)/shard_map/beside/pallas_call | solution.py:466
  31.7 3.8 %collective-permute-done.4.after_ref = bf16[128,1024]{1,0:T(8,128)(2,1)S(1)} collective-permute-done((bf16[128,1024]{1,0:T(8,128)(2,1)S(1)}, bf16[128,1024]{1,0:T(8,128)(2,1)S(1)}, u32[]{:S(2)}, u32[]{:S(2)}) %collective-permute-start.4) | collective-permute-done | bytes 262176 | tf_op jit(solution)/shard_map/ppermute | solution.py:25
  35.5 3.2 %gate.1 = (bf16[128,1024]{1,0:T(8,128)(2,1)S(1)}, bf16[128,1024]{1,0:T(8,128)(2,1)S(1)}, bf16[32,1024]{1,0:T(8,128)(2,1)S(1)}, f32[104,128]{1,0:T(8,128)S(1)}) custom-call(s32[8]{0:T(128)S(1)} %copy-done.8, f32[128,1024]{1,0:T(8,128)S(1)} %get-tuple-element.77.part_ref, bf16[128,1024]{1,0:T(8,128)(2,1)S(1)} %collective-permute-done.4.after_ref, ...), custom_call_target="tpu_custom_call" | custom-call | flops 1000000000 | bytes 5000000 | tf_op jit(solution)/shard_map/gate/pallas_call | solution.py:466
  38.7 1.9 %collective-permute-start.5 = (f32[104,128]{1,0:T(8,128)S(1)}, f32[104,128]{1,0:T(8,128)S(1)}, u32[]{:S(2)}, u32[]{:S(2)}) collective-permute-start(f32[104,128]{1,0:T(8,128)S(1)} %get-tuple-element.85), channel_id=1, source_target_pairs={{0,4},{4,0},{8,12},{12,8},{16,20},{20,16},{24,28},{28,24},{1,5},{5... | collective-permute-start | bytes 159752 | tf_op jit(solution)/shard_map/ppermute | solution.py:29
  40.5 0.9 %normed.1 = bf16[128,1024]{1,0:T(8,128)(2,1)} custom-call(f32[128,1024]{1,0:T(8,128)S(1)} %get-tuple-element.83.summed_ref, f32[1,1024]{1,0:T(1,128)S(1)} %bitcast.8, f32[2,128]{1,0:T(2,128)S(1)} %add.13.sums_ref), custom_call_target="tpu_custom_call" | custom-call | flops 1000000000 | bytes 5000000 | tf_op jit(solution)/shard_map/normed/pallas_call | solution.py:466
  41.5 1.4 %collective-permute-done.5 = f32[104,128]{1,0:T(8,128)S(1)} collective-permute-done((f32[104,128]{1,0:T(8,128)S(1)}, f32[104,128]{1,0:T(8,128)S(1)}, u32[]{:S(2)}, u32[]{:S(2)}) %collective-permute-start.5) | collective-permute-done | bytes 53280 | tf_op jit(solution)/shard_map/ppermute | solution.py:29
  42.9 1.2 %collective-permute-start.7 = (bf16[32,1024]{1,0:T(8,128)(2,1)S(1)}, bf16[32,1024]{1,0:T(8,128)(2,1)S(1)}, u32[]{:S(2)}, u32[]{:S(2)}) collective-permute-start(bf16[32,1024]{1,0:T(8,128)(2,1)S(1)} %get-tuple-element.88), channel_id=1, source_target_pairs={{0,28},{4,0},{8,4},{12,8},{16,12},{20,16},{24,20},{28,24},{1,29},{... | collective-permute-start | bytes 196616 | tf_op jit(solution)/shard_map/ppermute | solution.py:25
  44.0 2.1 %collective-permute-start.6 = (f32[104,128]{1,0:T(8,128)S(1)}, f32[104,128]{1,0:T(8,128)S(1)}, u32[]{:S(2)}, u32[]{:S(2)}) collective-permute-start(f32[104,128]{1,0:T(8,128)S(1)} %add.14), channel_id=1, source_target_pairs={{0,8},{4,12},{8,0},{12,4},{16,24},{20,28},{24,16},{28,20},{1,9},{5... | collective-permute-start | bytes 159752 | tf_op jit(solution)/shard_map/ppermute | solution.py:29
  46.2 2.8 %collective-permute-done.6 = f32[104,128]{1,0:T(8,128)S(1)} collective-permute-done((f32[104,128]{1,0:T(8,128)S(1)}, f32[104,128]{1,0:T(8,128)S(1)}, u32[]{:S(2)}, u32[]{:S(2)}) %collective-permute-start.6) | collective-permute-done | bytes 53280 | tf_op jit(solution)/shard_map/ppermute | solution.py:29
  49.0 0.7 %collective-permute-start.8 = (f32[104,128]{1,0:T(8,128)S(1)}, f32[104,128]{1,0:T(8,128)S(1)}, u32[]{:S(2)}, u32[]{:S(2)}) collective-permute-start(f32[104,128]{1,0:T(8,128)S(1)} %add.15.one_ref), channel_id=1, source_target_pairs={{0,16},{4,20},{8,24},{12,28},{16,0},{20,4},{24,8},{28,12},{1,17},{... | collective-permute-start | bytes 159752 | tf_op jit(solution)/shard_map/ppermute | solution.py:29
  49.8 3.2 %mains.1 = (bf16[128,1024]{1,0:T(8,128)(2,1)}, bf16[128,1024]{1,0:T(8,128)(2,1)}, bf16[128,1024]{1,0:T(8,128)(2,1)}) custom-call(s32[8]{0:T(128)S(1)} %copy-done.8, f32[24,1024]{1,0:T(8,128)S(1)} %copy-done.4, bf16[32,1024]{1,0:T(8,128)(2,1)S(1)} %collective-permute-done.7.tails_ref, bf16[128,1024]{1,0:T(8,128)(2,1)S(1)} %get-tuple-element.73.gq_ref, ...), custom_call_target="tpu_custom_call" | custom-call | flops 1000000000 | bytes 5000000 | tf_op jit(solution)/shard_map/mains/pallas_call | solution.py:466
  53.0 1.1 %collective-permute-done.8.two_ref = f32[104,128]{1,0:T(8,128)S(1)} collective-permute-done((f32[104,128]{1,0:T(8,128)S(1)}, f32[104,128]{1,0:T(8,128)S(1)}, u32[]{:S(2)}, u32[]{:S(2)}) %collective-permute-start.8) | collective-permute-done | bytes 53280 | tf_op jit(solution)/shard_map/ppermute | solution.py:29
  54.1 0.6 %unpack.1 = (f32[3,7,64]{2,1,0:T(8,128)}, f32[64,128]{1,0:T(8,128)}, f32[8,128]{1,0:T(8,128)}, f32[8,128]{1,0:T(8,128)}) custom-call(f32[104,128]{1,0:T(8,128)S(1)} %add.15.one_ref, f32[104,128]{1,0:T(8,128)S(1)} %collective-permute-done.8.two_ref), custom_call_target="tpu_custom_call" | custom-call | flops 100000000 | bytes 1000000 | tf_op jit(solution)/shard_map/unpack/pallas_call | solution.py:466
  (26 shorter events, 0.1 us)
Async XLA Ops:
  0.6 10.3 %copy-start.11 = (bf16[64,128]{1,0:T(8,128)(2,1)S(1)}, bf16[64,128]{1,0:T(8,128)(2,1)}, u32[]{:S(2)}) copy-start(bf16[64,128]{1,0:T(8,128)(2,1)} %long_ref.1) | copy-start | bytes 49156
  3.8 14.3 %collective-permute-start = (bf16[160,1024]{1,0:T(8,128)(2,1)}, bf16[160,1024]{1,0:T(8,128)(2,1)S(1)}, u32[]{:S(2)}, u32[]{:S(2)}) collective-permute-start(bf16[160,1024]{1,0:T(8,128)(2,1)} %get-tuple-element.59.sent_ref), channel_id=1, source_target_pairs={{0,4},{4,8},{8,12},{12,16},{16,20},{20,24},{24,28},{28,0},{1,5},{5... | collective-permute-start | bytes 983048 | tf_op jit(solution)/shard_map/ppermute | solution.py:25
  6.8 11.3 %collective-permute-start.1 = (bf16[16,1024]{1,0:T(8,128)(2,1)}, bf16[16,1024]{1,0:T(8,128)(2,1)S(1)}, u32[]{:S(2)}, u32[]{:S(2)}) collective-permute-start(bf16[16,1024]{1,0:T(8,128)(2,1)} %get-tuple-element.57), channel_id=1, source_target_pairs={{0,8},{4,12},{8,16},{12,20},{16,24},{20,28},{24,0},{28,4},{1,9},{5... | collective-permute-start | bytes 98312 | tf_op jit(solution)/shard_map/ppermute | solution.py:25
  8.4 0.7 %copy-start.10 = (bf16[64,128]{1,0:T(8,128)(2,1)S(1)}, bf16[64,128]{1,0:T(8,128)(2,1)}, u32[]{:S(2)}) copy-start(bf16[64,128]{1,0:T(8,128)(2,1)} %long_ref.1) | copy-start | bytes 49156
  10.9 1.8 %copy-start.3 = (bf16[128,1024]{1,0:T(8,128)(2,1)S(1)}, bf16[128,1024]{1,0:T(8,128)(2,1)}, u32[]{:S(2)}) copy-start(bf16[128,1024]{1,0:T(8,128)(2,1)} %q_ref.5) | copy-start | bytes 786436
  10.9 1.8 %copy-start.4 = (f32[24,1024]{1,0:T(8,128)S(1)}, f32[24,1024]{1,0:T(8,128)}, u32[]{:S(2)}) copy-start(f32[24,1024]{1,0:T(8,128)} %get-tuple-element.58.taps_ref) | copy-start | bytes 294916
  10.9 1.8 %copy-start.5 = (bf16[160,1024]{1,0:T(8,128)(2,1)S(1)}, bf16[160,1024]{1,0:T(8,128)(2,1)}, u32[]{:S(2)}) copy-start(bf16[160,1024]{1,0:T(8,128)(2,1)} %get-tuple-element.59.sent_ref) | copy-start | bytes 983044
  11.0 1.8 %copy-start.8 = (s32[8]{0:T(128)S(1)}, s32[8]{0:T(128)}, u32[]{:S(2)}) copy-start(s32[8]{0:T(128)} %len_ref.11) | copy-start | bytes 100
  11.0 1.8 %copy-start.9 = (f32[1024]{0:T(1024)S(1)}, f32[1024]{0:T(1024)}, u32[]{:S(2)}) copy-start(f32[1024]{0:T(1024)} %param.17) | copy-start | bytes 12292
  12.7 5.5 %copy-start = (bf16[128,1024]{1,0:T(8,128)(2,1)S(1)}, bf16[128,1024]{1,0:T(8,128)(2,1)}, u32[]{:S(2)}) copy-start(bf16[128,1024]{1,0:T(8,128)(2,1)} %k_ref.5) | copy-start | bytes 786436
  12.7 5.5 %copy-start.1 = (bf16[128,1024]{1,0:T(8,128)(2,1)S(1)}, bf16[128,1024]{1,0:T(8,128)(2,1)}, u32[]{:S(2)}) copy-start(bf16[128,1024]{1,0:T(8,128)(2,1)} %v_ref.5) | copy-start | bytes 786436
  12.7 5.5 %copy-start.2 = (bf16[128,1024]{1,0:T(8,128)(2,1)S(1)}, bf16[128,1024]{1,0:T(8,128)(2,1)}, u32[]{:S(2)}) copy-start(bf16[128,1024]{1,0:T(8,128)(2,1)} %cot_ref.5) | copy-start | bytes 786436
  12.7 5.5 %copy-start.6 = (bf16[128,1024]{1,0:T(8,128)(2,1)S(1)}, bf16[128,1024]{1,0:T(8,128)(2,1)}, u32[]{:S(2)}) copy-start(bf16[128,1024]{1,0:T(8,128)(2,1)} %resid_ref.1) | copy-start | bytes 786436
  12.7 5.4 %copy-start.7 = (f32[1024]{0:T(1024)S(1)}, f32[1024]{0:T(1024)}, u32[]{:S(2)}) copy-start(f32[1024]{0:T(1024)} %param.18) | copy-start | bytes 12292
  20.3 1.2 %collective-permute-start.2 = (f32[2,128]{1,0:T(2,128)S(1)}, f32[2,128]{1,0:T(2,128)S(1)}, u32[]{:S(2)}, u32[]{:S(2)}) collective-permute-start(f32[2,128]{1,0:T(2,128)S(1)} %get-tuple-element.65), channel_id=1, source_target_pairs={{0,1},{1,0},{2,3},{3,2},{4,5},{5,4},{6,7},{7,6},{8,9},{9,8},{10,11... | collective-permute-start | bytes 3080 | tf_op jit(solution)/shard_map/ppermute | solution.py:29
  21.5 3.6 %collective-permute-start.3 = (f32[2,128]{1,0:T(2,128)S(1)}, f32[2,128]{1,0:T(2,128)S(1)}, u32[]{:S(2)}, u32[]{:S(2)}) collective-permute-start(f32[2,128]{1,0:T(2,128)S(1)} %add.12), channel_id=1, source_target_pairs={{0,2},{1,3},{2,0},{3,1},{4,6},{5,7},{6,4},{7,5},{8,10},{9,11},{10,... | collective-permute-start | bytes 3080 | tf_op jit(solution)/shard_map/ppermute | solution.py:29
  25.6 9.8 %collective-permute-start.4 = (bf16[128,1024]{1,0:T(8,128)(2,1)S(1)}, bf16[128,1024]{1,0:T(8,128)(2,1)S(1)}, u32[]{:S(2)}, u32[]{:S(2)}) collective-permute-start(bf16[128,1024]{1,0:T(8,128)(2,1)S(1)} %get-tuple-element.72.gm_ref), channel_id=1, source_target_pairs={{4,0},{8,4},{12,8},{16,12},{20,16},{24,20},{28,24},{5,1},{9,5},{13... | collective-permute-start | bytes 786440 | tf_op jit(solution)/shard_map/ppermute | solution.py:25
  38.7 4.2 %collective-permute-start.5 = (f32[104,128]{1,0:T(8,128)S(1)}, f32[104,128]{1,0:T(8,128)S(1)}, u32[]{:S(2)}, u32[]{:S(2)}) collective-permute-start(f32[104,128]{1,0:T(8,128)S(1)} %get-tuple-element.85), channel_id=1, source_target_pairs={{0,4},{4,0},{8,12},{12,8},{16,20},{20,16},{24,28},{28,24},{1,5},{5... | collective-permute-start | bytes 159752 | tf_op jit(solution)/shard_map/ppermute | solution.py:29
  42.9 6.1 %collective-permute-start.7 = (bf16[32,1024]{1,0:T(8,128)(2,1)S(1)}, bf16[32,1024]{1,0:T(8,128)(2,1)S(1)}, u32[]{:S(2)}, u32[]{:S(2)}) collective-permute-start(bf16[32,1024]{1,0:T(8,128)(2,1)S(1)} %get-tuple-element.88), channel_id=1, source_target_pairs={{0,28},{4,0},{8,4},{12,8},{16,12},{20,16},{24,20},{28,24},{1,29},{... | collective-permute-start | bytes 196616 | tf_op jit(solution)/shard_map/ppermute | solution.py:25
  44.0 4.9 %collective-permute-start.6 = (f32[104,128]{1,0:T(8,128)S(1)}, f32[104,128]{1,0:T(8,128)S(1)}, u32[]{:S(2)}, u32[]{:S(2)}) collective-permute-start(f32[104,128]{1,0:T(8,128)S(1)} %add.14), channel_id=1, source_target_pairs={{0,8},{4,12},{8,0},{12,4},{16,24},{20,28},{24,16},{28,20},{1,9},{5... | collective-permute-start | bytes 159752 | tf_op jit(solution)/shard_map/ppermute | solution.py:29
  49.0 5.1 %collective-permute-start.8 = (f32[104,128]{1,0:T(8,128)S(1)}, f32[104,128]{1,0:T(8,128)S(1)}, u32[]{:S(2)}, u32[]{:S(2)}) collective-permute-start(f32[104,128]{1,0:T(8,128)S(1)} %add.15.one_ref), channel_id=1, source_target_pairs={{0,16},{4,20},{8,24},{12,28},{16,0},{20,4},{24,8},{28,12},{1,17},{... | collective-permute-start | bytes 159752 | tf_op jit(solution)/shard_map/ppermute | solution.py:29

commit v13 on v12

--- a/solution.py
+++ b/solution.py
@@ -569,7 +569,7 @@
     while 2 * step < count:
         packed = packed + swapped(packed, "ctx", step)
         step *= 2
-    packed, tails = lax.optimization_barrier((packed, tails))
+    packed, grad_qs = lax.optimization_barrier((packed, grad_qs))
     other = swapped(packed, "ctx", step)
     grad_q, grad_k, grad_v = call(
         "mains", mains_kernel, [full_bf] * 3,

time: 55 us -> 55 us (level)
  no operation moved by 1% of the time
where the time goes in v13:
time: 55 us; the launch traced here: 54.7 us
  Pallas kernels  26.5 us (48%)
  starting transfers between devices  13.4 us (24%)
  waiting for transfers between devices  13.2 us (24%)
  between operations  0.89 us (2%)
  local copies, waits for them, and re-layouts  0.78 us (1%)
    pallas_call x12, Pallas kernels, call(): pl.pallas_call(kernel, out_shape=outs, in_specs=[far_off] * len(ins) if h...  26.5 us
    ppermute x4, starting transfers between devices, shifted(): lax.ppermute(x, axis, [p for p in pairs if wrap or p[1] - p[0] == by])  7.07 us
    ppermute x5, waiting for transfers between devices, swapped(): lax.ppermute(x, axis, [(i, i ^ step) for i in range(lax.axis_size(axis))])  6.65 us
    ppermute x4, waiting for transfers between devices, shifted(): lax.ppermute(x, axis, [p for p in pairs if wrap or p[1] - p[0] == by])  6.55 us
    ppermute x5, starting transfers between devices, swapped(): lax.ppermute(x, axis, [(i, i ^ step) for i in range(lax.axis_size(axis))])  6.3 us
  transfers between devices with their start and end apart: 9, of which 7 were waited for; matrix products, arithmetic and copies ran while one was open for 0% of the time, Pallas kernels for 31%

profile of v13, /device:TPU:0, one launch (start us, length us, event | category | flops | bytes accessed | tf_op | source)
XLA Modules:
  0.0 54.7 jit_solution(3976503761406530297)
XLA Ops:
  0.6 0.0 copy-start.11
  0.6 3.1 %first.1 = (f32[24,1024]{1,0:T(8,128)}, bf16[160,1024]{1,0:T(8,128)(2,1)}, bf16[16,1024]{1,0:T(8,128)(2,1)}) custom-call(s32[8]{0:T(128)} %len_ref.11, bf16[3,7,64]{2,1,0:T(8,128)(2,1)} %bitcast.12, bf16[128,1024]{1,0:T(8,128)(2,1)} %q_ref.5, bf16[128,1024]{1,0:T(8,128)(2,1)} %k_ref.5, bf16[128,1024]{1,0:T(8,128)(2,1)} %v_ref.5), custom_call_target="tpu_custom_call" | custom-call | flops 100000000 | bytes 1000000 | tf_op jit(solution)/shard_map/first/pallas_call | solution.py:466
  3.8 3.0 %collective-permute-start = (bf16[160,1024]{1,0:T(8,128)(2,1)}, bf16[160,1024]{1,0:T(8,128)(2,1)S(1)}, u32[]{:S(2)}, u32[]{:S(2)}) collective-permute-start(bf16[160,1024]{1,0:T(8,128)(2,1)} %get-tuple-element.59.sent_ref), channel_id=1, source_target_pairs={{0,4},{4,8},{8,12},{12,16},{16,20},{20,24},{24,28},{28,0},{1,5},{5... | collective-permute-start | bytes 983048 | tf_op jit(solution)/shard_map/ppermute | solution.py:25
  6.8 1.6 %collective-permute-start.1 = (bf16[16,1024]{1,0:T(8,128)(2,1)}, bf16[16,1024]{1,0:T(8,128)(2,1)S(1)}, u32[]{:S(2)}, u32[]{:S(2)}) collective-permute-start(bf16[16,1024]{1,0:T(8,128)(2,1)} %get-tuple-element.57), channel_id=1, source_target_pairs={{0,8},{4,12},{8,16},{12,20},{16,24},{20,28},{24,0},{28,4},{1,9},{5... | collective-permute-start | bytes 98312 | tf_op jit(solution)/shard_map/ppermute | solution.py:25
  8.4 0.7 %copy-done.10 = bf16[64,128]{1,0:T(8,128)(2,1)S(1)} copy-done((bf16[64,128]{1,0:T(8,128)(2,1)S(1)}, bf16[64,128]{1,0:T(8,128)(2,1)}, u32[]{:S(2)}) %copy-start.10) | copy-done | bytes 16408
  9.1 1.8 %circulants.3.fwd_ref = bf16[128,8192]{1,0:T(8,128)(2,1)S(1)} custom-call(bf16[64,128]{1,0:T(8,128)(2,1)S(1)} %copy-done.10), custom_call_target="tpu_custom_call" | custom-call | flops 1000000000 | bytes 4000000 | tf_op jit(solution)/shard_map/circulants/pallas_call | solution.py:466
  10.9 0.0 copy-start.4
  11.0 0.0 copy-start.8
  11.0 1.7 %circulants.2.bwd_ref = bf16[128,8192]{1,0:T(8,128)(2,1)S(1)} custom-call(bf16[64,128]{1,0:T(8,128)(2,1)S(1)} %copy-done.11), custom_call_target="tpu_custom_call" | custom-call | flops 1000000000 | bytes 4000000 | tf_op jit(solution)/shard_map/circulants/pallas_call | solution.py:466
  12.8 2.6 %current.1 = (f32[128,1024]{1,0:T(8,128)S(1)}, f32[128,1024]{1,0:T(8,128)S(1)}, bf16[128,1024]{1,0:T(8,128)(2,1)S(1)}) custom-call(s32[8]{0:T(128)S(1)} %copy-done.8, bf16[128,1024]{1,0:T(8,128)(2,1)S(1)} %copy-done.3, f32[24,1024]{1,0:T(8,128)S(1)} %copy-done.4, bf16[160,1024]{1,0:T(8,128)(2,1)S(1)} %copy-done.5, bf16[128,8192]{1,0:T(8,128)(2,1)S(1)} %circulants.3.fwd_ref, ...), custom_call_target="tpu_custom_call" | custom-call | flops 1000000000 | bytes 5000000 | tf_op jit(solution)/shard_map/current/pallas_call | solution.py:466
  15.4 2.8 %collective-permute-done.came_ref = bf16[160,1024]{1,0:T(8,128)(2,1)S(1)} collective-permute-done((bf16[160,1024]{1,0:T(8,128)(2,1)}, bf16[160,1024]{1,0:T(8,128)(2,1)S(1)}, u32[]{:S(2)}, u32[]{:S(2)}) %collective-permute-start) | collective-permute-done | bytes 327712 | tf_op jit(solution)/shard_map/ppermute | solution.py:25
  18.2 2.2 %summed.1 = (f32[128,1024]{1,0:T(8,128)S(1)}, bf16[128,1024]{1,0:T(8,128)(2,1)S(1)}, bf16[128,1024]{1,0:T(8,128)(2,1)S(1)}, f32[128,1024]{1,0:T(8,128)S(1)}, f32...) custom-call(s32[8]{0:T(128)S(1)} %copy-done.8, bf16[160,1024]{1,0:T(8,128)(2,1)S(1)} %collective-permute-done.came_ref, ...), custom_call_target="tpu_custom_call" | custom-call | flops 1000000000 | bytes 5000000 | tf_op jit(solution)/shard_map/summed/pallas_call | solution.py:466
  20.3 0.1 collective-permute-start.2
  20.4 1.1 %collective-permute-done.2 = f32[2,128]{1,0:T(2,128)S(1)} collective-permute-done((f32[2,128]{1,0:T(2,128)S(1)}, f32[2,128]{1,0:T(2,128)S(1)}, u32[]{:S(2)}, u32[]{:S(2)}) %collective-permute-start.2) | collective-permute-done | bytes 1056 | tf_op jit(solution)/shard_map/ppermute | solution.py:29
  21.5 1.5 %collective-permute-start.3 = (f32[2,128]{1,0:T(2,128)S(1)}, f32[2,128]{1,0:T(2,128)S(1)}, u32[]{:S(2)}, u32[]{:S(2)}) collective-permute-start(f32[2,128]{1,0:T(2,128)S(1)} %add.12), channel_id=1, source_target_pairs={{0,2},{1,3},{2,0},{3,1},{4,6},{5,7},{6,4},{7,5},{8,10},{9,11},{10,... | collective-permute-start | bytes 3080 | tf_op jit(solution)/shard_map/ppermute | solution.py:29
  23.0 1.9 %gates.1 = (f32[128,1024]{1,0:T(8,128)S(1)}, f32[128,1024]{1,0:T(8,128)S(1)}) custom-call(s32[8]{0:T(128)S(1)} %copy-done.8, bf16[128,1024]{1,0:T(8,128)(2,1)S(1)} %copy-done, bf16[128,1024]{1,0:T(8,128)(2,1)S(1)} %copy-done.1, bf16[160,1024]{1,0:T(8,128)(2,1)S(1)} %collective-permute-done.came_ref, f32[24,1024]{1,0:T(8,128)S(1)} %copy-done.4), custom_call_target="tpu_custom_call" | custom-call | flops 100000000 | bytes 2000000 | tf_op jit(solution)/shard_map/gates/pallas_call | solution.py:466
  24.9 0.2 collective-permute-done.3
  25.1 0.5 grads.1
  25.6 1.3 %collective-permute-start.4 = (bf16[128,1024]{1,0:T(8,128)(2,1)S(1)}, bf16[128,1024]{1,0:T(8,128)(2,1)S(1)}, u32[]{:S(2)}, u32[]{:S(2)}) collective-permute-start(bf16[128,1024]{1,0:T(8,128)(2,1)S(1)} %get-tuple-element.72.gm_ref), channel_id=1, source_target_pairs={{4,0},{8,4},{12,8},{16,12},{20,16},{24,20},{28,24},{5,1},{9,5},{13... | collective-permute-start | bytes 786440 | tf_op jit(solution)/shard_map/ppermute | solution.py:25
  26.9 4.7 %beside.1 = (f32[80,128]{1,0:T(8,128)S(1)}, f32[128,1024]{1,0:T(8,128)S(1)}, f32[8,1024]{1,0:T(8,128)S(1)}) custom-call(s32[8]{0:T(128)S(1)} %copy-done.8, f32[128,1024]{1,0:T(8,128)S(1)} %get-tuple-element.83.summed_ref, bf16[128,1024]{1,0:T(8,128)(2,1)S(1)} %copy-done.2, f32[2,128]{1,0:T(2,128)S(1)} %add.13.sums_ref, ...), custom_call_target="tpu_custom_call" | custom-call | flops 4000000000 | bytes 5000000 | tf_op jit(solution)/shard_map/beside/pallas_call | solution.py:466
  31.7 3.8 %collective-permute-done.4.after_ref = bf16[128,1024]{1,0:T(8,128)(2,1)S(1)} collective-permute-done((bf16[128,1024]{1,0:T(8,128)(2,1)S(1)}, bf16[128,1024]{1,0:T(8,128)(2,1)S(1)}, u32[]{:S(2)}, u32[]{:S(2)}) %collective-permute-start.4) | collective-permute-done | bytes 262176 | tf_op jit(solution)/shard_map/ppermute | solution.py:25
  35.5 3.2 %gate.1 = (bf16[128,1024]{1,0:T(8,128)(2,1)S(1)}, bf16[128,1024]{1,0:T(8,128)(2,1)S(1)}, bf16[32,1024]{1,0:T(8,128)(2,1)S(1)}, f32[104,128]{1,0:T(8,128)S(1)}) custom-call(s32[8]{0:T(128)S(1)} %copy-done.8, f32[128,1024]{1,0:T(8,128)S(1)} %get-tuple-element.77.part_ref, bf16[128,1024]{1,0:T(8,128)(2,1)S(1)} %collective-permute-done.4.after_ref, ...), custom_call_target="tpu_custom_call" | custom-call | flops 1000000000 | bytes 5000000 | tf_op jit(solution)/shard_map/gate/pallas_call | solution.py:466
  38.7 1.9 %collective-permute-start.5 = (f32[104,128]{1,0:T(8,128)S(1)}, f32[104,128]{1,0:T(8,128)S(1)}, u32[]{:S(2)}, u32[]{:S(2)}) collective-permute-start(f32[104,128]{1,0:T(8,128)S(1)} %get-tuple-element.85), channel_id=1, source_target_pairs={{0,4},{4,0},{8,12},{12,8},{16,20},{20,16},{24,28},{28,24},{1,5},{5... | collective-permute-start | bytes 159752 | tf_op jit(solution)/shard_map/ppermute | solution.py:29
  40.5 0.9 %normed.1 = bf16[128,1024]{1,0:T(8,128)(2,1)} custom-call(f32[128,1024]{1,0:T(8,128)S(1)} %get-tuple-element.83.summed_ref, f32[1,1024]{1,0:T(1,128)S(1)} %bitcast.8, f32[2,128]{1,0:T(2,128)S(1)} %add.13.sums_ref), custom_call_target="tpu_custom_call" | custom-call | flops 1000000000 | bytes 5000000 | tf_op jit(solution)/shard_map/normed/pallas_call | solution.py:466
  41.5 1.4 %collective-permute-done.5 = f32[104,128]{1,0:T(8,128)S(1)} collective-permute-done((f32[104,128]{1,0:T(8,128)S(1)}, f32[104,128]{1,0:T(8,128)S(1)}, u32[]{:S(2)}, u32[]{:S(2)}) %collective-permute-start.5) | collective-permute-done | bytes 53280 | tf_op jit(solution)/shard_map/ppermute | solution.py:29
  42.9 1.2 %collective-permute-start.6 = (bf16[32,1024]{1,0:T(8,128)(2,1)S(1)}, bf16[32,1024]{1,0:T(8,128)(2,1)S(1)}, u32[]{:S(2)}, u32[]{:S(2)}) collective-permute-start(bf16[32,1024]{1,0:T(8,128)(2,1)S(1)} %get-tuple-element.87), channel_id=1, source_target_pairs={{0,28},{4,0},{8,4},{12,8},{16,12},{20,16},{24,20},{28,24},{1,29},{... | collective-permute-start | bytes 196616 | tf_op jit(solution)/shard_map/ppermute | solution.py:25
  44.0 2.1 %collective-permute-start.7 = (f32[104,128]{1,0:T(8,128)S(1)}, f32[104,128]{1,0:T(8,128)S(1)}, u32[]{:S(2)}, u32[]{:S(2)}) collective-permute-start(f32[104,128]{1,0:T(8,128)S(1)} %add.14), channel_id=1, source_target_pairs={{0,8},{4,12},{8,0},{12,4},{16,24},{20,28},{24,16},{28,20},{1,9},{5... | collective-permute-start | bytes 159752 | tf_op jit(solution)/shard_map/ppermute | solution.py:29
  46.2 2.8 %collective-permute-done.7 = f32[104,128]{1,0:T(8,128)S(1)} collective-permute-done((f32[104,128]{1,0:T(8,128)S(1)}, f32[104,128]{1,0:T(8,128)S(1)}, u32[]{:S(2)}, u32[]{:S(2)}) %collective-permute-start.7) | collective-permute-done | bytes 53280 | tf_op jit(solution)/shard_map/ppermute | solution.py:29
  49.0 0.7 %collective-permute-start.8 = (f32[104,128]{1,0:T(8,128)S(1)}, f32[104,128]{1,0:T(8,128)S(1)}, u32[]{:S(2)}, u32[]{:S(2)}) collective-permute-start(f32[104,128]{1,0:T(8,128)S(1)} %add.15.one_ref), channel_id=1, source_target_pairs={{0,16},{4,20},{8,24},{12,28},{16,0},{20,4},{24,8},{28,12},{1,17},{... | collective-permute-start | bytes 159752 | tf_op jit(solution)/shard_map/ppermute | solution.py:29
  49.7 3.2 %mains.1 = (bf16[128,1024]{1,0:T(8,128)(2,1)}, bf16[128,1024]{1,0:T(8,128)(2,1)}, bf16[128,1024]{1,0:T(8,128)(2,1)}) custom-call(s32[8]{0:T(128)S(1)} %copy-done.8, f32[24,1024]{1,0:T(8,128)S(1)} %copy-done.4, bf16[32,1024]{1,0:T(8,128)(2,1)S(1)} %collective-permute-done.6.tails_ref, bf16[128,1024]{1,0:T(8,128)(2,1)S(1)} %get-tuple-element.89.gq_ref, ...), custom_call_target="tpu_custom_call" | custom-call | flops 1000000000 | bytes 5000000 | tf_op jit(solution)/shard_map/mains/pallas_call | solution.py:466
  53.0 1.1 %collective-permute-done.8.two_ref = f32[104,128]{1,0:T(8,128)S(1)} collective-permute-done((f32[104,128]{1,0:T(8,128)S(1)}, f32[104,128]{1,0:T(8,128)S(1)}, u32[]{:S(2)}, u32[]{:S(2)}) %collective-permute-start.8) | collective-permute-done | bytes 53280 | tf_op jit(solution)/shard_map/ppermute | solution.py:29
  54.1 0.6 %unpack.1 = (f32[3,7,64]{2,1,0:T(8,128)}, f32[64,128]{1,0:T(8,128)}, f32[8,128]{1,0:T(8,128)}, f32[8,128]{1,0:T(8,128)}) custom-call(f32[104,128]{1,0:T(8,128)S(1)} %add.15.one_ref, f32[104,128]{1,0:T(8,128)S(1)} %collective-permute-done.8.two_ref), custom_call_target="tpu_custom_call" | custom-call | flops 100000000 | bytes 1000000 | tf_op jit(solution)/shard_map/unpack/pallas_call | solution.py:466
  (26 shorter events, 0.1 us)
Async XLA Ops:
  0.6 10.3 %copy-start.11 = (bf16[64,128]{1,0:T(8,128)(2,1)S(1)}, bf16[64,128]{1,0:T(8,128)(2,1)}, u32[]{:S(2)}) copy-start(bf16[64,128]{1,0:T(8,128)(2,1)} %long_ref.1) | copy-start | bytes 49156
  3.8 14.3 %collective-permute-start = (bf16[160,1024]{1,0:T(8,128)(2,1)}, bf16[160,1024]{1,0:T(8,128)(2,1)S(1)}, u32[]{:S(2)}, u32[]{:S(2)}) collective-permute-start(bf16[160,1024]{1,0:T(8,128)(2,1)} %get-tuple-element.59.sent_ref), channel_id=1, source_target_pairs={{0,4},{4,8},{8,12},{12,16},{16,20},{20,24},{24,28},{28,0},{1,5},{5... | collective-permute-start | bytes 983048 | tf_op jit(solution)/shard_map/ppermute | solution.py:25
  6.8 11.3 %collective-permute-start.1 = (bf16[16,1024]{1,0:T(8,128)(2,1)}, bf16[16,1024]{1,0:T(8,128)(2,1)S(1)}, u32[]{:S(2)}, u32[]{:S(2)}) collective-permute-start(bf16[16,1024]{1,0:T(8,128)(2,1)} %get-tuple-element.57), channel_id=1, source_target_pairs={{0,8},{4,12},{8,16},{12,20},{16,24},{20,28},{24,0},{28,4},{1,9},{5... | collective-permute-start | bytes 98312 | tf_op jit(solution)/shard_map/ppermute | solution.py:25
  8.4 0.7 %copy-start.10 = (bf16[64,128]{1,0:T(8,128)(2,1)S(1)}, bf16[64,128]{1,0:T(8,128)(2,1)}, u32[]{:S(2)}) copy-start(bf16[64,128]{1,0:T(8,128)(2,1)} %long_ref.1) | copy-start | bytes 49156
  10.9 1.8 %copy-start.3 = (bf16[128,1024]{1,0:T(8,128)(2,1)S(1)}, bf16[128,1024]{1,0:T(8,128)(2,1)}, u32[]{:S(2)}) copy-start(bf16[128,1024]{1,0:T(8,128)(2,1)} %q_ref.5) | copy-start | bytes 786436
  10.9 1.8 %copy-start.4 = (f32[24,1024]{1,0:T(8,128)S(1)}, f32[24,1024]{1,0:T(8,128)}, u32[]{:S(2)}) copy-start(f32[24,1024]{1,0:T(8,128)} %get-tuple-element.58.taps_ref) | copy-start | bytes 294916
  10.9 1.8 %copy-start.5 = (bf16[160,1024]{1,0:T(8,128)(2,1)S(1)}, bf16[160,1024]{1,0:T(8,128)(2,1)}, u32[]{:S(2)}) copy-start(bf16[160,1024]{1,0:T(8,128)(2,1)} %get-tuple-element.59.sent_ref) | copy-start | bytes 983044
  11.0 1.8 %copy-start.8 = (s32[8]{0:T(128)S(1)}, s32[8]{0:T(128)}, u32[]{:S(2)}) copy-start(s32[8]{0:T(128)} %len_ref.11) | copy-start | bytes 100
  11.0 1.8 %copy-start.9 = (f32[1024]{0:T(1024)S(1)}, f32[1024]{0:T(1024)}, u32[]{:S(2)}) copy-start(f32[1024]{0:T(1024)} %param.17) | copy-start | bytes 12292
  12.7 5.5 %copy-start = (bf16[128,1024]{1,0:T(8,128)(2,1)S(1)}, bf16[128,1024]{1,0:T(8,128)(2,1)}, u32[]{:S(2)}) copy-start(bf16[128,1024]{1,0:T(8,128)(2,1)} %k_ref.5) | copy-start | bytes 786436
  12.7 5.5 %copy-start.1 = (bf16[128,1024]{1,0:T(8,128)(2,1)S(1)}, bf16[128,1024]{1,0:T(8,128)(2,1)}, u32[]{:S(2)}) copy-start(bf16[128,1024]{1,0:T(8,128)(2,1)} %v_ref.5) | copy-start | bytes 786436
  12.7 5.5 %copy-start.2 = (bf16[128,1024]{1,0:T(8,128)(2,1)S(1)}, bf16[128,1024]{1,0:T(8,128)(2,1)}, u32[]{:S(2)}) copy-start(bf16[128,1024]{1,0:T(8,128)(2,1)} %cot_ref.5) | copy-start | bytes 786436
  12.7 5.5 %copy-start.6 = (bf16[128,1024]{1,0:T(8,128)(2,1)S(1)}, bf16[128,1024]{1,0:T(8,128)(2,1)}, u32[]{:S(2)}) copy-start(bf16[128,1024]{1,0:T(8,128)(2,1)} %resid_ref.1) | copy-start | bytes 786436
  12.7 5.4 %copy-start.7 = (f32[1024]{0:T(1024)S(1)}, f32[1024]{0:T(1024)}, u32[]{:S(2)}) copy-start(f32[1024]{0:T(1024)} %param.18) | copy-start | bytes 12292
  20.3 1.2 %collective-permute-start.2 = (f32[2,128]{1,0:T(2,128)S(1)}, f32[2,128]{1,0:T(2,128)S(1)}, u32[]{:S(2)}, u32[]{:S(2)}) collective-permute-start(f32[2,128]{1,0:T(2,128)S(1)} %get-tuple-element.65), channel_id=1, source_target_pairs={{0,1},{1,0},{2,3},{3,2},{4,5},{5,4},{6,7},{7,6},{8,9},{9,8},{10,11... | collective-permute-start | bytes 3080 | tf_op jit(solution)/shard_map/ppermute | solution.py:29
  21.5 3.6 %collective-permute-start.3 = (f32[2,128]{1,0:T(2,128)S(1)}, f32[2,128]{1,0:T(2,128)S(1)}, u32[]{:S(2)}, u32[]{:S(2)}) collective-permute-start(f32[2,128]{1,0:T(2,128)S(1)} %add.12), channel_id=1, source_target_pairs={{0,2},{1,3},{2,0},{3,1},{4,6},{5,7},{6,4},{7,5},{8,10},{9,11},{10,... | collective-permute-start | bytes 3080 | tf_op jit(solution)/shard_map/ppermute | solution.py:29
  25.6 9.8 %collective-permute-start.4 = (bf16[128,1024]{1,0:T(8,128)(2,1)S(1)}, bf16[128,1024]{1,0:T(8,128)(2,1)S(1)}, u32[]{:S(2)}, u32[]{:S(2)}) collective-permute-start(bf16[128,1024]{1,0:T(8,128)(2,1)S(1)} %get-tuple-element.72.gm_ref), channel_id=1, source_target_pairs={{4,0},{8,4},{12,8},{16,12},{20,16},{24,20},{28,24},{5,1},{9,5},{13... | collective-permute-start | bytes 786440 | tf_op jit(solution)/shard_map/ppermute | solution.py:25
  38.7 4.2 %collective-permute-start.5 = (f32[104,128]{1,0:T(8,128)S(1)}, f32[104,128]{1,0:T(8,128)S(1)}, u32[]{:S(2)}, u32[]{:S(2)}) collective-permute-start(f32[104,128]{1,0:T(8,128)S(1)} %get-tuple-element.85), channel_id=1, source_target_pairs={{0,4},{4,0},{8,12},{12,8},{16,20},{20,16},{24,28},{28,24},{1,5},{5... | collective-permute-start | bytes 159752 | tf_op jit(solution)/shard_map/ppermute | solution.py:29
  42.9 6.9 %collective-permute-start.6 = (bf16[32,1024]{1,0:T(8,128)(2,1)S(1)}, bf16[32,1024]{1,0:T(8,128)(2,1)S(1)}, u32[]{:S(2)}, u32[]{:S(2)}) collective-permute-start(bf16[32,1024]{1,0:T(8,128)(2,1)S(1)} %get-tuple-element.87), channel_id=1, source_target_pairs={{0,28},{4,0},{8,4},{12,8},{16,12},{20,16},{24,20},{28,24},{1,29},{... | collective-permute-start | bytes 196616 | tf_op jit(solution)/shard_map/ppermute | solution.py:25
  44.0 4.9 %collective-permute-start.7 = (f32[104,128]{1,0:T(8,128)S(1)}, f32[104,128]{1,0:T(8,128)S(1)}, u32[]{:S(2)}, u32[]{:S(2)}) collective-permute-start(f32[104,128]{1,0:T(8,128)S(1)} %add.14), channel_id=1, source_target_pairs={{0,8},{4,12},{8,0},{12,4},{16,24},{20,28},{24,16},{28,20},{1,9},{5... | collective-permute-start | bytes 159752 | tf_op jit(solution)/shard_map/ppermute | solution.py:29
  49.0 5.1 %collective-permute-start.8 = (f32[104,128]{1,0:T(8,128)S(1)}, f32[104,128]{1,0:T(8,128)S(1)}, u32[]{:S(2)}, u32[]{:S(2)}) collective-permute-start(f32[104,128]{1,0:T(8,128)S(1)} %add.15.one_ref), channel_id=1, source_target_pairs={{0,16},{4,20},{8,24},{12,28},{16,0},{20,4},{24,8},{28,12},{1,17},{... | collective-permute-start | bytes 159752 | tf_op jit(solution)/shard_map/ppermute | solution.py:29

commit v14 on v11

--- a/solution.py
+++ b/solution.py
@@ -362,7 +362,7 @@
         q_ext = join(rim_of(came_ref, Q_LAST, ls), q_ref[:, ls].astype(F32))
         cols_ref[:, ls] = tap_lines(gq_ref[:, ls].astype(F32), q_ext, after)
 
-    each_chunk(cot_ref.shape[1], body, 2)
+    each_chunk(cot_ref.shape[1], body, 4)
 
 
 def gate_kernel(
@@ -396,7 +396,9 @@
 
     each_chunk(channels, body)
     packed_ref[0:kept] = stats_ref[...]
-    packed_ref[kept:] = group_sums(cols_ref[...])
+    sums = group_sums(cols_ref[...])
+    packed_ref[kept : kept + 8] = sums[:8] + pltpu.roll(sums[8:16], LANES // 2, 1)
+    packed_ref[kept + 8 :] = sums[16:]
 
 
 def back_short(which, after, ls, taps_ref, grad_ref, tails_ref):
@@ -441,9 +443,10 @@
     long_ref[...] = total[:groups]
     skip_ref[...] = total[groups : groups + rows]
     gain_ref[...] = total[groups + rows : groups + 2 * rows]
-    for i in range(3):
-        at = groups + 2 * rows + i * 8
-        short_ref[i] = total[at : at + KS, :groups]
+    taps = total[groups + 2 * rows :]
+    short_ref[0] = taps[:KS, :groups]
+    short_ref[1] = pltpu.roll(taps[:8], LANES // 2, 1)[:KS, :groups]
+    short_ref[2] = taps[8 : 8 + KS, :groups]
 
 
 def shards(
@@ -453,7 +456,7 @@
     groups = channels // GS
     wide = channels * lax.axis_size("tp")
     rows = groups // PER
-    packed_rows = groups + 2 * rows + 24
+    packed_rows = groups + 2 * rows + 16
 
     def arr(shape, dtype):
         return jax.ShapeDtypeStruct(shape, dtype)

time: 54.8 us -> 54.8 us (level)
  no operation moved by 1% of the time
where the time goes in v14:
time: 54.8 us; the launch traced here: 54.5 us
  Pallas kernels  27.2 us (50%)
  starting transfers between devices  12.8 us (23%)
  waiting for transfers between devices  12.8 us (23%)
  between operations  0.89 us (2%)
  local copies, waits for them, and re-layouts  0.78 us (1%)
    pallas_call x12, Pallas kernels, call(): pl.pallas_call(kernel, out_shape=outs, in_specs=[far_off] * len(ins) if h...  27.2 us
    ppermute x4, starting transfers between devices, shifted(): lax.ppermute(x, axis, [p for p in pairs if wrap or p[1] - p[0] == by])  6.56 us
    ppermute x4, waiting for transfers between devices, shifted(): lax.ppermute(x, axis, [p for p in pairs if wrap or p[1] - p[0] == by])  6.55 us
    ppermute x5, starting transfers between devices, swapped(): lax.ppermute(x, axis, [(i, i ^ step) for i in range(lax.axis_size(axis))])  6.27 us
    ppermute x5, waiting for transfers between devices, swapped(): lax.ppermute(x, axis, [(i, i ^ step) for i in range(lax.axis_size(axis))])  6.23 us
  transfers between devices with their start and end apart: 9, of which 6 were waited for; matrix products, arithmetic and copies ran while one was open for 0% of the time, Pallas kernels for 32%

profile of v14, /device:TPU:0, one launch (start us, length us, event | category | flops | bytes accessed | tf_op | source)
XLA Modules:
  0.0 54.5 jit_solution(10487851535400094151)
XLA Ops:
  0.6 3.1 %first.1 = (f32[24,1024]{1,0:T(8,128)}, bf16[160,1024]{1,0:T(8,128)(2,1)}, bf16[16,1024]{1,0:T(8,128)(2,1)}) custom-call(s32[8]{0:T(128)} %len_ref.13, bf16[3,7,64]{2,1,0:T(8,128)(2,1)} %bitcast.12, bf16[128,1024]{1,0:T(8,128)(2,1)} %q_ref.5, bf16[128,1024]{1,0:T(8,128)(2,1)} %k_ref.5, bf16[128,1024]{1,0:T(8,128)(2,1)} %v_ref.5), custom_call_target="tpu_custom_call" | custom-call | flops 100000000 | bytes 1000000 | tf_op jit(solution)/shard_map/first/pallas_call | solution.py:472
  3.8 3.0 %collective-permute-start = (bf16[160,1024]{1,0:T(8,128)(2,1)}, bf16[160,1024]{1,0:T(8,128)(2,1)S(1)}, u32[]{:S(2)}, u32[]{:S(2)}) collective-permute-start(bf16[160,1024]{1,0:T(8,128)(2,1)} %get-tuple-element.57.sent_ref), channel_id=1, source_target_pairs={{0,4},{4,8},{8,12},{12,16},{16,20},{20,24},{24,28},{28,0},{1,5},{5... | collective-permute-start | bytes 983048 | tf_op jit(solution)/shard_map/ppermute | solution.py:25
  6.8 1.6 %collective-permute-start.1 = (bf16[16,1024]{1,0:T(8,128)(2,1)}, bf16[16,1024]{1,0:T(8,128)(2,1)S(1)}, u32[]{:S(2)}, u32[]{:S(2)}) collective-permute-start(bf16[16,1024]{1,0:T(8,128)(2,1)} %get-tuple-element.56), channel_id=1, source_target_pairs={{0,8},{4,12},{8,16},{12,20},{16,24},{20,28},{24,0},{28,4},{1,9},{5... | collective-permute-start | bytes 98312 | tf_op jit(solution)/shard_map/ppermute | solution.py:25
  8.4 0.7 %copy-done.10 = bf16[64,128]{1,0:T(8,128)(2,1)S(1)} copy-done((bf16[64,128]{1,0:T(8,128)(2,1)S(1)}, bf16[64,128]{1,0:T(8,128)(2,1)}, u32[]{:S(2)}) %copy-start.10) | copy-done | bytes 16408
  9.1 1.8 %circulants.3.fwd_ref = bf16[128,8192]{1,0:T(8,128)(2,1)S(1)} custom-call(bf16[64,128]{1,0:T(8,128)(2,1)S(1)} %copy-done.10), custom_call_target="tpu_custom_call" | custom-call | flops 1000000000 | bytes 4000000 | tf_op jit(solution)/shard_map/circulants/pallas_call | solution.py:472
  10.9 0.0 copy-start.3
  11.0 0.0 copy-start.9
  11.0 1.7 %circulants.2.bwd_ref = bf16[128,8192]{1,0:T(8,128)(2,1)S(1)} custom-call(bf16[64,128]{1,0:T(8,128)(2,1)S(1)} %copy-done.11), custom_call_target="tpu_custom_call" | custom-call | flops 1000000000 | bytes 4000000 | tf_op jit(solution)/shard_map/circulants/pallas_call | solution.py:472
  12.7 0.0 copy-start
  12.7 0.0 copy-start.1
  12.8 2.6 %current.1 = (f32[128,1024]{1,0:T(8,128)S(1)}, f32[128,1024]{1,0:T(8,128)S(1)}, bf16[128,1024]{1,0:T(8,128)(2,1)S(1)}) custom-call(s32[8]{0:T(128)S(1)} %copy-done.8, bf16[128,1024]{1,0:T(8,128)(2,1)S(1)} %copy-done.3, f32[24,1024]{1,0:T(8,128)S(1)} %copy-done.4, bf16[160,1024]{1,0:T(8,128)(2,1)S(1)} %copy-done.5, bf16[128,8192]{1,0:T(8,128)(2,1)S(1)} %circulants.3.fwd_ref, ...), custom_call_target="tpu_custom_call" | custom-call | flops 1000000000 | bytes 5000000 | tf_op jit(solution)/shard_map/current/pallas_call | solution.py:472
  15.4 2.8 %collective-permute-done.came_ref = bf16[160,1024]{1,0:T(8,128)(2,1)S(1)} collective-permute-done((bf16[160,1024]{1,0:T(8,128)(2,1)}, bf16[160,1024]{1,0:T(8,128)(2,1)S(1)}, u32[]{:S(2)}, u32[]{:S(2)}) %collective-permute-start) | collective-permute-done | bytes 327712 | tf_op jit(solution)/shard_map/ppermute | solution.py:25
  18.2 2.2 %summed.1 = (f32[128,1024]{1,0:T(8,128)S(1)}, bf16[128,1024]{1,0:T(8,128)(2,1)S(1)}, bf16[128,1024]{1,0:T(8,128)(2,1)S(1)}, f32[128,1024]{1,0:T(8,128)S(1)}, f32...) custom-call(s32[8]{0:T(128)S(1)} %copy-done.8, bf16[160,1024]{1,0:T(8,128)(2,1)S(1)} %collective-permute-done.came_ref, ...), custom_call_target="tpu_custom_call" | custom-call | flops 1000000000 | bytes 5000000 | tf_op jit(solution)/shard_map/summed/pallas_call | solution.py:472
  20.3 0.1 collective-permute-start.2
  20.4 1.1 %collective-permute-done.2 = f32[2,128]{1,0:T(2,128)S(1)} collective-permute-done((f32[2,128]{1,0:T(2,128)S(1)}, f32[2,128]{1,0:T(2,128)S(1)}, u32[]{:S(2)}, u32[]{:S(2)}) %collective-permute-start.2) | collective-permute-done | bytes 1056 | tf_op jit(solution)/shard_map/ppermute | solution.py:29
  21.5 1.5 %collective-permute-start.3 = (f32[2,128]{1,0:T(2,128)S(1)}, f32[2,128]{1,0:T(2,128)S(1)}, u32[]{:S(2)}, u32[]{:S(2)}) collective-permute-start(f32[2,128]{1,0:T(2,128)S(1)} %add.12), channel_id=1, source_target_pairs={{0,2},{1,3},{2,0},{3,1},{4,6},{5,7},{6,4},{7,5},{8,10},{9,11},{10,... | collective-permute-start | bytes 3080 | tf_op jit(solution)/shard_map/ppermute | solution.py:29
  23.0 1.9 %gates.1 = (f32[128,1024]{1,0:T(8,128)S(1)}, f32[128,1024]{1,0:T(8,128)S(1)}) custom-call(s32[8]{0:T(128)S(1)} %copy-done.8, bf16[128,1024]{1,0:T(8,128)(2,1)S(1)} %copy-done, bf16[128,1024]{1,0:T(8,128)(2,1)S(1)} %copy-done.1, bf16[160,1024]{1,0:T(8,128)(2,1)S(1)} %collective-permute-done.came_ref, f32[24,1024]{1,0:T(8,128)S(1)} %copy-done.4), custom_call_target="tpu_custom_call" | custom-call | flops 100000000 | bytes 2000000 | tf_op jit(solution)/shard_map/gates/pallas_call | solution.py:472
  24.9 0.2 collective-permute-done.3
  25.1 0.5 grads.1
  25.6 1.3 %collective-permute-start.4 = (bf16[128,1024]{1,0:T(8,128)(2,1)S(1)}, bf16[128,1024]{1,0:T(8,128)(2,1)S(1)}, u32[]{:S(2)}, u32[]{:S(2)}) collective-permute-start(bf16[128,1024]{1,0:T(8,128)(2,1)S(1)} %get-tuple-element.70.gm_ref), channel_id=1, source_target_pairs={{4,0},{8,4},{12,8},{16,12},{20,16},{24,20},{28,24},{5,1},{9,5},{13... | collective-permute-start | bytes 786440 | tf_op jit(solution)/shard_map/ppermute | solution.py:25
  26.9 4.7 %beside.1 = (f32[80,128]{1,0:T(8,128)S(1)}, f32[128,1024]{1,0:T(8,128)S(1)}, f32[8,1024]{1,0:T(8,128)S(1)}) custom-call(s32[8]{0:T(128)S(1)} %copy-done.8, f32[128,1024]{1,0:T(8,128)S(1)} %get-tuple-element.62.summed_ref, bf16[128,1024]{1,0:T(8,128)(2,1)S(1)} %copy-done.2, f32[2,128]{1,0:T(2,128)S(1)} %add.13.sums_ref, ...), custom_call_target="tpu_custom_call" | custom-call | flops 4000000000 | bytes 5000000 | tf_op jit(solution)/shard_map/beside/pallas_call | solution.py:472
  31.7 3.8 %collective-permute-done.4.after_ref = bf16[128,1024]{1,0:T(8,128)(2,1)S(1)} collective-permute-done((bf16[128,1024]{1,0:T(8,128)(2,1)S(1)}, bf16[128,1024]{1,0:T(8,128)(2,1)S(1)}, u32[]{:S(2)}, u32[]{:S(2)}) %collective-permute-start.4) | collective-permute-done | bytes 262176 | tf_op jit(solution)/shard_map/ppermute | solution.py:25
  35.5 3.3 %gate.1 = (bf16[128,1024]{1,0:T(8,128)(2,1)S(1)}, bf16[128,1024]{1,0:T(8,128)(2,1)S(1)}, bf16[32,1024]{1,0:T(8,128)(2,1)S(1)}, f32[96,128]{1,0:T(8,128)S(1)}) custom-call(s32[8]{0:T(128)S(1)} %copy-done.8, f32[128,1024]{1,0:T(8,128)S(1)} %get-tuple-element.75.part_ref, bf16[128,1024]{1,0:T(8,128)(2,1)S(1)} %collective-permute-done.4.after_ref, ...), custom_call_target="tpu_custom_call" | custom-call | flops 1000000000 | bytes 5000000 | tf_op jit(solution)/shard_map/gate/pallas_call | solution.py:472
  38.7 0.7 %collective-permute-start.5 = (bf16[32,1024]{1,0:T(8,128)(2,1)S(1)}, bf16[32,1024]{1,0:T(8,128)(2,1)S(1)}, u32[]{:S(2)}, u32[]{:S(2)}) collective-permute-start(bf16[32,1024]{1,0:T(8,128)(2,1)S(1)} %get-tuple-element.80), channel_id=1, source_target_pairs={{0,28},{4,0},{8,4},{12,8},{16,12},{20,16},{24,20},{28,24},{1,29},{... | collective-permute-start | bytes 196616 | tf_op jit(solution)/shard_map/ppermute | solution.py:25
  39.4 1.4 %collective-permute-start.6 = (f32[96,128]{1,0:T(8,128)S(1)}, f32[96,128]{1,0:T(8,128)S(1)}, u32[]{:S(2)}, u32[]{:S(2)}) collective-permute-start(f32[96,128]{1,0:T(8,128)S(1)} %get-tuple-element.81), channel_id=1, source_target_pairs={{0,4},{4,0},{8,12},{12,8},{16,20},{20,16},{24,28},{28,24},{1,5},{5... | collective-permute-start | bytes 147464 | tf_op jit(solution)/shard_map/ppermute | solution.py:29
  40.7 2.8 %collective-permute-done.6 = f32[96,128]{1,0:T(8,128)S(1)} collective-permute-done((f32[96,128]{1,0:T(8,128)S(1)}, f32[96,128]{1,0:T(8,128)S(1)}, u32[]{:S(2)}, u32[]{:S(2)}) %collective-permute-start.6) | collective-permute-done | bytes 49184 | tf_op jit(solution)/shard_map/ppermute | solution.py:29
  43.5 2.6 %collective-permute-start.7 = (f32[96,128]{1,0:T(8,128)S(1)}, f32[96,128]{1,0:T(8,128)S(1)}, u32[]{:S(2)}, u32[]{:S(2)}) collective-permute-start(f32[96,128]{1,0:T(8,128)S(1)} %add.14), channel_id=1, source_target_pairs={{0,8},{4,12},{8,0},{12,4},{16,24},{20,28},{24,16},{28,20},{1,9},{5... | collective-permute-start | bytes 147464 | tf_op jit(solution)/shard_map/ppermute | solution.py:29
  46.1 2.6 %main_qk.1 = (bf16[128,1024]{1,0:T(8,128)(2,1)}, bf16[128,1024]{1,0:T(8,128)(2,1)}) custom-call(s32[8]{0:T(128)S(1)} %copy-done.8, f32[24,1024]{1,0:T(8,128)S(1)} %copy-done.4, bf16[32,1024]{1,0:T(8,128)(2,1)S(1)} %collective-permute-done.5.tails_ref, bf16[128,1024]{1,0:T(8,128)(2,1)S(1)} %get-tuple-element.71.gq_ref, ...), custom_call_target="tpu_custom_call" | custom-call | flops 1000000000 | bytes 5000000 | tf_op jit(solution)/shard_map/main_qk/pallas_call | solution.py:472
  48.8 0.7 %collective-permute-start.8 = (f32[96,128]{1,0:T(8,128)S(1)}, f32[96,128]{1,0:T(8,128)S(1)}, u32[]{:S(2)}, u32[]{:S(2)}) collective-permute-start(f32[96,128]{1,0:T(8,128)S(1)} %add.15.one_ref), channel_id=1, source_target_pairs={{0,16},{4,20},{8,24},{12,28},{16,0},{20,4},{24,8},{28,12},{1,17},{... | collective-permute-start | bytes 147464 | tf_op jit(solution)/shard_map/ppermute | solution.py:29
  49.5 2.2 %main_v.1 = (bf16[128,1024]{1,0:T(8,128)(2,1)}, bf16[128,1024]{1,0:T(8,128)(2,1)}) custom-call(s32[8]{0:T(128)S(1)} %copy-done.8, f32[24,1024]{1,0:T(8,128)S(1)} %copy-done.4, bf16[32,1024]{1,0:T(8,128)(2,1)S(1)} %collective-permute-done.5.tails_ref, bf16[128,1024]{1,0:T(8,128)(2,1)S(1)} %get-tuple-element.86.gvs_ref, ...), custom_call_target="tpu_custom_call" | custom-call | flops 1000000000 | bytes 5000000 | tf_op jit(solution)/shard_map/main_v/pallas_call | solution.py:472
  51.7 2.1 %collective-permute-done.8.two_ref = f32[96,128]{1,0:T(8,128)S(1)} collective-permute-done((f32[96,128]{1,0:T(8,128)S(1)}, f32[96,128]{1,0:T(8,128)S(1)}, u32[]{:S(2)}, u32[]{:S(2)}) %collective-permute-start.8) | collective-permute-done | bytes 49184 | tf_op jit(solution)/shard_map/ppermute | solution.py:29
  53.8 0.7 %unpack.1 = (f32[3,7,64]{2,1,0:T(8,128)}, f32[64,128]{1,0:T(8,128)}, f32[8,128]{1,0:T(8,128)}, f32[8,128]{1,0:T(8,128)}) custom-call(f32[96,128]{1,0:T(8,128)S(1)} %add.15.one_ref, f32[96,128]{1,0:T(8,128)S(1)} %collective-permute-done.8.two_ref), custom_call_target="tpu_custom_call" | custom-call | flops 100000000 | bytes 1000000 | tf_op jit(solution)/shard_map/unpack/pallas_call | solution.py:472
  (26 shorter events, 0.1 us)
Async XLA Ops:
  0.6 10.3 %copy-start.11 = (bf16[64,128]{1,0:T(8,128)(2,1)S(1)}, bf16[64,128]{1,0:T(8,128)(2,1)}, u32[]{:S(2)}) copy-start(bf16[64,128]{1,0:T(8,128)(2,1)} %long_ref.1) | copy-start | bytes 49156
  3.8 14.3 %collective-permute-start = (bf16[160,1024]{1,0:T(8,128)(2,1)}, bf16[160,1024]{1,0:T(8,128)(2,1)S(1)}, u32[]{:S(2)}, u32[]{:S(2)}) collective-permute-start(bf16[160,1024]{1,0:T(8,128)(2,1)} %get-tuple-element.57.sent_ref), channel_id=1, source_target_pairs={{0,4},{4,8},{8,12},{12,16},{16,20},{20,24},{24,28},{28,0},{1,5},{5... | collective-permute-start | bytes 983048 | tf_op jit(solution)/shard_map/ppermute | solution.py:25
  6.8 11.3 %collective-permute-start.1 = (bf16[16,1024]{1,0:T(8,128)(2,1)}, bf16[16,1024]{1,0:T(8,128)(2,1)S(1)}, u32[]{:S(2)}, u32[]{:S(2)}) collective-permute-start(bf16[16,1024]{1,0:T(8,128)(2,1)} %get-tuple-element.56), channel_id=1, source_target_pairs={{0,8},{4,12},{8,16},{12,20},{16,24},{20,28},{24,0},{28,4},{1,9},{5... | collective-permute-start | bytes 98312 | tf_op jit(solution)/shard_map/ppermute | solution.py:25
  8.4 0.7 %copy-start.10 = (bf16[64,128]{1,0:T(8,128)(2,1)S(1)}, bf16[64,128]{1,0:T(8,128)(2,1)}, u32[]{:S(2)}) copy-start(bf16[64,128]{1,0:T(8,128)(2,1)} %long_ref.1) | copy-start | bytes 49156
  10.9 1.8 %copy-start.3 = (bf16[128,1024]{1,0:T(8,128)(2,1)S(1)}, bf16[128,1024]{1,0:T(8,128)(2,1)}, u32[]{:S(2)}) copy-start(bf16[128,1024]{1,0:T(8,128)(2,1)} %q_ref.5) | copy-start | bytes 786436
  10.9 1.8 %copy-start.4 = (f32[24,1024]{1,0:T(8,128)S(1)}, f32[24,1024]{1,0:T(8,128)}, u32[]{:S(2)}) copy-start(f32[24,1024]{1,0:T(8,128)} %get-tuple-element.52.taps_ref) | copy-start | bytes 294916
  10.9 1.8 %copy-start.5 = (bf16[160,1024]{1,0:T(8,128)(2,1)S(1)}, bf16[160,1024]{1,0:T(8,128)(2,1)}, u32[]{:S(2)}) copy-start(bf16[160,1024]{1,0:T(8,128)(2,1)} %get-tuple-element.57.sent_ref) | copy-start | bytes 983044
  11.0 1.8 %copy-start.8 = (s32[8]{0:T(128)S(1)}, s32[8]{0:T(128)}, u32[]{:S(2)}) copy-start(s32[8]{0:T(128)} %len_ref.13) | copy-start | bytes 100
  11.0 1.8 %copy-start.9 = (f32[1024]{0:T(1024)S(1)}, f32[1024]{0:T(1024)}, u32[]{:S(2)}) copy-start(f32[1024]{0:T(1024)} %param.17) | copy-start | bytes 12292
  12.7 5.5 %copy-start = (bf16[128,1024]{1,0:T(8,128)(2,1)S(1)}, bf16[128,1024]{1,0:T(8,128)(2,1)}, u32[]{:S(2)}) copy-start(bf16[128,1024]{1,0:T(8,128)(2,1)} %k_ref.5) | copy-start | bytes 786436
  12.7 5.5 %copy-start.1 = (bf16[128,1024]{1,0:T(8,128)(2,1)S(1)}, bf16[128,1024]{1,0:T(8,128)(2,1)}, u32[]{:S(2)}) copy-start(bf16[128,1024]{1,0:T(8,128)(2,1)} %v_ref.5) | copy-start | bytes 786436
  12.7 5.5 %copy-start.2 = (bf16[128,1024]{1,0:T(8,128)(2,1)S(1)}, bf16[128,1024]{1,0:T(8,128)(2,1)}, u32[]{:S(2)}) copy-start(bf16[128,1024]{1,0:T(8,128)(2,1)} %cot_ref.5) | copy-start | bytes 786436
  12.7 5.5 %copy-start.6 = (bf16[128,1024]{1,0:T(8,128)(2,1)S(1)}, bf16[128,1024]{1,0:T(8,128)(2,1)}, u32[]{:S(2)}) copy-start(bf16[128,1024]{1,0:T(8,128)(2,1)} %resid_ref.1) | copy-start | bytes 786436
  12.7 5.4 %copy-start.7 = (f32[1024]{0:T(1024)S(1)}, f32[1024]{0:T(1024)}, u32[]{:S(2)}) copy-start(f32[1024]{0:T(1024)} %param.18) | copy-start | bytes 12292
  20.3 1.2 %collective-permute-start.2 = (f32[2,128]{1,0:T(2,128)S(1)}, f32[2,128]{1,0:T(2,128)S(1)}, u32[]{:S(2)}, u32[]{:S(2)}) collective-permute-start(f32[2,128]{1,0:T(2,128)S(1)} %get-tuple-element.63), channel_id=1, source_target_pairs={{0,1},{1,0},{2,3},{3,2},{4,5},{5,4},{6,7},{7,6},{8,9},{9,8},{10,11... | collective-permute-start | bytes 3080 | tf_op jit(solution)/shard_map/ppermute | solution.py:29
  21.5 3.6 %collective-permute-start.3 = (f32[2,128]{1,0:T(2,128)S(1)}, f32[2,128]{1,0:T(2,128)S(1)}, u32[]{:S(2)}, u32[]{:S(2)}) collective-permute-start(f32[2,128]{1,0:T(2,128)S(1)} %add.12), channel_id=1, source_target_pairs={{0,2},{1,3},{2,0},{3,1},{4,6},{5,7},{6,4},{7,5},{8,10},{9,11},{10,... | collective-permute-start | bytes 3080 | tf_op jit(solution)/shard_map/ppermute | solution.py:29
  25.6 9.8 %collective-permute-start.4 = (bf16[128,1024]{1,0:T(8,128)(2,1)S(1)}, bf16[128,1024]{1,0:T(8,128)(2,1)S(1)}, u32[]{:S(2)}, u32[]{:S(2)}) collective-permute-start(bf16[128,1024]{1,0:T(8,128)(2,1)S(1)} %get-tuple-element.70.gm_ref), channel_id=1, source_target_pairs={{4,0},{8,4},{12,8},{16,12},{20,16},{24,20},{28,24},{5,1},{9,5},{13... | collective-permute-start | bytes 786440 | tf_op jit(solution)/shard_map/ppermute | solution.py:25
  38.7 7.4 %collective-permute-start.5 = (bf16[32,1024]{1,0:T(8,128)(2,1)S(1)}, bf16[32,1024]{1,0:T(8,128)(2,1)S(1)}, u32[]{:S(2)}, u32[]{:S(2)}) collective-permute-start(bf16[32,1024]{1,0:T(8,128)(2,1)S(1)} %get-tuple-element.80), channel_id=1, source_target_pairs={{0,28},{4,0},{8,4},{12,8},{16,12},{20,16},{24,20},{28,24},{1,29},{... | collective-permute-start | bytes 196616 | tf_op jit(solution)/shard_map/ppermute | solution.py:25
  39.4 4.1 %collective-permute-start.6 = (f32[96,128]{1,0:T(8,128)S(1)}, f32[96,128]{1,0:T(8,128)S(1)}, u32[]{:S(2)}, u32[]{:S(2)}) collective-permute-start(f32[96,128]{1,0:T(8,128)S(1)} %get-tuple-element.81), channel_id=1, source_target_pairs={{0,4},{4,0},{8,12},{12,8},{16,20},{20,16},{24,28},{28,24},{1,5},{5... | collective-permute-start | bytes 147464 | tf_op jit(solution)/shard_map/ppermute | solution.py:29
  43.5 5.2 %collective-permute-start.7 = (f32[96,128]{1,0:T(8,128)S(1)}, f32[96,128]{1,0:T(8,128)S(1)}, u32[]{:S(2)}, u32[]{:S(2)}) collective-permute-start(f32[96,128]{1,0:T(8,128)S(1)} %add.14), channel_id=1, source_target_pairs={{0,8},{4,12},{8,0},{12,4},{16,24},{20,28},{24,16},{28,20},{1,9},{5... | collective-permute-start | bytes 147464 | tf_op jit(solution)/shard_map/ppermute | solution.py:29
  48.8 5.1 %collective-permute-start.8 = (f32[96,128]{1,0:T(8,128)S(1)}, f32[96,128]{1,0:T(8,128)S(1)}, u32[]{:S(2)}, u32[]{:S(2)}) collective-permute-start(f32[96,128]{1,0:T(8,128)S(1)} %add.15.one_ref), channel_id=1, source_target_pairs={{0,16},{4,20},{8,24},{12,28},{16,0},{20,4},{24,8},{28,12},{1,17},{... | collective-permute-start | bytes 147464 | tf_op jit(solution)/shard_map/ppermute | solution.py:29

commit v15 on v11

--- a/solution.py
+++ b/solution.py
@@ -535,7 +535,7 @@
         "grads", functools.partial(grads_kernel, wide), [full_bf, full_bf],
         [summed, mixed, q_short, cotangent, gain2, sums],
     )
-    after = shifted(grad_mixed, "ctx", -1, wrap=False)
+    after = shifted(grad_mixed, "ctx", -1)
     stats, part, qcols = call(
         "beside", functools.partial(beside_kernel, wide),
         [

time: 54.8 us -> 56.5 us (1.031)
  waiting for transfers between devices: 12.7 us -> 14.2 us
    ppermute x4, starting transfers between devices: 6.61 us -> 11.4 us  [shifted(): lax.ppermute(x, axis, [p for p in pairs if wrap or p[1] - p[0] == by])]
    ppermute x5, starting transfers between devices: 6.28 us -> 1.7 us  [swapped(): lax.ppermute(x, axis, [(i, i ^ step) for i in range(lax.axis_size(axis))])]
    ppermute x5, waiting for transfers between devices: 6.32 us -> 10.4 us  [swapped(): lax.ppermute(x, axis, [(i, i ^ step) for i in range(lax.axis_size(axis))])]
    ppermute x4, waiting for transfers between devices: 6.41 us -> 3.81 us  [shifted(): lax.ppermute(x, axis, [p for p in pairs if wrap or p[1] - p[0] == by])]
  transfers between devices with their start and end apart: 9 -> 9, of which waited for: 6 -> 7; matrix products, arithmetic and copies ran while one was open for 0% -> 0% of each run, Pallas kernels for 32% -> 31%
where the time goes in v15:
time: 56.5 us; the launch traced here: 56.2 us
  Pallas kernels  27.2 us (48%)
  waiting for transfers between devices  14.2 us (25%)
  starting transfers between devices  13.1 us (23%)
  between operations  0.91 us (2%)
  local copies, waits for them, and re-layouts  0.78 us (1%)
    pallas_call x12, Pallas kernels, call(): pl.pallas_call(kernel, out_shape=outs, in_specs=[far_off] * len(ins) if h...  27.2 us
    ppermute x4, starting transfers between devices, shifted(): lax.ppermute(x, axis, [p for p in pairs if wrap or p[1] - p[0] == by])  11.4 us
    ppermute x5, waiting for transfers between devices, swapped(): lax.ppermute(x, axis, [(i, i ^ step) for i in range(lax.axis_size(axis))])  10.4 us
    ppermute x4, waiting for transfers between devices, shifted(): lax.ppermute(x, axis, [p for p in pairs if wrap or p[1] - p[0] == by])  3.81 us
    ppermute x5, starting transfers between devices, swapped(): lax.ppermute(x, axis, [(i, i ^ step) for i in range(lax.axis_size(axis))])  1.7 us
  transfers between devices with their start and end apart: 9, of which 7 were waited for; matrix products, arithmetic and copies ran while one was open for 0% of the time, Pallas kernels for 31%

profile of v15, /device:TPU:0, one launch (start us, length us, event | category | flops | bytes accessed | tf_op | source)
XLA Modules:
  0.0 56.2 jit_solution(2712822666900233928)
XLA Ops:
  0.6 0.0 copy-start.11
  0.6 3.1 %first.1 = (f32[24,1024]{1,0:T(8,128)}, bf16[160,1024]{1,0:T(8,128)(2,1)}, bf16[16,1024]{1,0:T(8,128)(2,1)}) custom-call(s32[8]{0:T(128)} %len_ref.13, bf16[3,7,64]{2,1,0:T(8,128)(2,1)} %bitcast.12, bf16[128,1024]{1,0:T(8,128)(2,1)} %q_ref.5, bf16[128,1024]{1,0:T(8,128)(2,1)} %k_ref.5, bf16[128,1024]{1,0:T(8,128)(2,1)} %v_ref.5), custom_call_target="tpu_custom_call" | custom-call | flops 100000000 | bytes 1000000 | tf_op jit(solution)/shard_map/first/pallas_call | solution.py:469
  3.8 3.0 %collective-permute-start = (bf16[160,1024]{1,0:T(8,128)(2,1)}, bf16[160,1024]{1,0:T(8,128)(2,1)S(1)}, u32[]{:S(2)}, u32[]{:S(2)}) collective-permute-start(bf16[160,1024]{1,0:T(8,128)(2,1)} %get-tuple-element.57.sent_ref), channel_id=1, source_target_pairs={{0,4},{4,8},{8,12},{12,16},{16,20},{20,24},{24,28},{28,0},{1,5},{5... | collective-permute-start | bytes 983048 | tf_op jit(solution)/shard_map/ppermute | solution.py:25
  6.8 1.6 %collective-permute-start.1 = (bf16[16,1024]{1,0:T(8,128)(2,1)}, bf16[16,1024]{1,0:T(8,128)(2,1)S(1)}, u32[]{:S(2)}, u32[]{:S(2)}) collective-permute-start(bf16[16,1024]{1,0:T(8,128)(2,1)} %get-tuple-element.56), channel_id=1, source_target_pairs={{0,8},{4,12},{8,16},{12,20},{16,24},{20,28},{24,0},{28,4},{1,9},{5... | collective-permute-start | bytes 98312 | tf_op jit(solution)/shard_map/ppermute | solution.py:25
  8.4 0.7 %copy-done.10 = bf16[64,128]{1,0:T(8,128)(2,1)S(1)} copy-done((bf16[64,128]{1,0:T(8,128)(2,1)S(1)}, bf16[64,128]{1,0:T(8,128)(2,1)}, u32[]{:S(2)}) %copy-start.10) | copy-done | bytes 16408
  9.1 1.8 %circulants.3.fwd_ref = bf16[128,8192]{1,0:T(8,128)(2,1)S(1)} custom-call(bf16[64,128]{1,0:T(8,128)(2,1)S(1)} %copy-done.10), custom_call_target="tpu_custom_call" | custom-call | flops 1000000000 | bytes 4000000 | tf_op jit(solution)/shard_map/circulants/pallas_call | solution.py:469
  10.9 0.0 copy-start.4
  11.0 0.0 copy-start.8
  11.0 1.7 %circulants.2.bwd_ref = bf16[128,8192]{1,0:T(8,128)(2,1)S(1)} custom-call(bf16[64,128]{1,0:T(8,128)(2,1)S(1)} %copy-done.11), custom_call_target="tpu_custom_call" | custom-call | flops 1000000000 | bytes 4000000 | tf_op jit(solution)/shard_map/circulants/pallas_call | solution.py:469
  12.7 0.0 copy-start.1
  12.8 2.6 %current.1 = (f32[128,1024]{1,0:T(8,128)S(1)}, f32[128,1024]{1,0:T(8,128)S(1)}, bf16[128,1024]{1,0:T(8,128)(2,1)S(1)}) custom-call(s32[8]{0:T(128)S(1)} %copy-done.8, bf16[128,1024]{1,0:T(8,128)(2,1)S(1)} %copy-done.3, f32[24,1024]{1,0:T(8,128)S(1)} %copy-done.4, bf16[160,1024]{1,0:T(8,128)(2,1)S(1)} %copy-done.5, bf16[128,8192]{1,0:T(8,128)(2,1)S(1)} %circulants.3.fwd_ref, ...), custom_call_target="tpu_custom_call" | custom-call | flops 1000000000 | bytes 5000000 | tf_op jit(solution)/shard_map/current/pallas_call | solution.py:469
  15.4 2.8 %collective-permute-done.came_ref = bf16[160,1024]{1,0:T(8,128)(2,1)S(1)} collective-permute-done((bf16[160,1024]{1,0:T(8,128)(2,1)}, bf16[160,1024]{1,0:T(8,128)(2,1)S(1)}, u32[]{:S(2)}, u32[]{:S(2)}) %collective-permute-start) | collective-permute-done | bytes 327712 | tf_op jit(solution)/shard_map/ppermute | solution.py:25
  18.2 2.2 %summed.1 = (f32[128,1024]{1,0:T(8,128)S(1)}, bf16[128,1024]{1,0:T(8,128)(2,1)S(1)}, bf16[128,1024]{1,0:T(8,128)(2,1)S(1)}, f32[128,1024]{1,0:T(8,128)S(1)}, f32...) custom-call(s32[8]{0:T(128)S(1)} %copy-done.8, bf16[160,1024]{1,0:T(8,128)(2,1)S(1)} %collective-permute-done.came_ref, ...), custom_call_target="tpu_custom_call" | custom-call | flops 1000000000 | bytes 5000000 | tf_op jit(solution)/shard_map/summed/pallas_call | solution.py:469
  20.3 0.1 collective-permute-start.2
  20.4 1.1 %collective-permute-done.2 = f32[2,128]{1,0:T(2,128)S(1)} collective-permute-done((f32[2,128]{1,0:T(2,128)S(1)}, f32[2,128]{1,0:T(2,128)S(1)}, u32[]{:S(2)}, u32[]{:S(2)}) %collective-permute-start.2) | collective-permute-done | bytes 1056 | tf_op jit(solution)/shard_map/ppermute | solution.py:29
  21.5 1.5 %collective-permute-start.3 = (f32[2,128]{1,0:T(2,128)S(1)}, f32[2,128]{1,0:T(2,128)S(1)}, u32[]{:S(2)}, u32[]{:S(2)}) collective-permute-start(f32[2,128]{1,0:T(2,128)S(1)} %add.12), channel_id=1, source_target_pairs={{0,2},{1,3},{2,0},{3,1},{4,6},{5,7},{6,4},{7,5},{8,10},{9,11},{10,... | collective-permute-start | bytes 3080 | tf_op jit(solution)/shard_map/ppermute | solution.py:29
  23.0 1.9 %gates.1 = (f32[128,1024]{1,0:T(8,128)S(1)}, f32[128,1024]{1,0:T(8,128)S(1)}) custom-call(s32[8]{0:T(128)S(1)} %copy-done.8, bf16[128,1024]{1,0:T(8,128)(2,1)S(1)} %copy-done, bf16[128,1024]{1,0:T(8,128)(2,1)S(1)} %copy-done.1, bf16[160,1024]{1,0:T(8,128)(2,1)S(1)} %collective-permute-done.came_ref, f32[24,1024]{1,0:T(8,128)S(1)} %copy-done.4), custom_call_target="tpu_custom_call" | custom-call | flops 100000000 | bytes 2000000 | tf_op jit(solution)/shard_map/gates/pallas_call | solution.py:469
  24.9 0.2 collective-permute-done.3
  25.1 0.5 grads.1
  25.6 2.1 %collective-permute-start.4 = (bf16[128,1024]{1,0:T(8,128)(2,1)S(1)}, bf16[128,1024]{1,0:T(8,128)(2,1)S(1)}, u32[]{:S(2)}, u32[]{:S(2)}) collective-permute-start(bf16[128,1024]{1,0:T(8,128)(2,1)S(1)} %get-tuple-element.70.gm_ref), channel_id=1, source_target_pairs={{0,28},{4,0},{8,4},{12,8},{16,12},{20,16},{24,20},{28,24},{1,29},{... | collective-permute-start | bytes 786440 | tf_op jit(solution)/shard_map/ppermute | solution.py:25
  27.7 4.9 %beside.1 = (f32[80,128]{1,0:T(8,128)S(1)}, f32[128,1024]{1,0:T(8,128)S(1)}, f32[8,1024]{1,0:T(8,128)S(1)}) custom-call(s32[8]{0:T(128)S(1)} %copy-done.8, f32[128,1024]{1,0:T(8,128)S(1)} %get-tuple-element.62.summed_ref, bf16[128,1024]{1,0:T(8,128)(2,1)S(1)} %copy-done.2, f32[2,128]{1,0:T(2,128)S(1)} %add.13.sums_ref, ...), custom_call_target="tpu_custom_call" | custom-call | flops 4000000000 | bytes 5000000 | tf_op jit(solution)/shard_map/beside/pallas_call | solution.py:469
  32.6 1.0 %collective-permute-done.4.after_ref = bf16[128,1024]{1,0:T(8,128)(2,1)S(1)} collective-permute-done((bf16[128,1024]{1,0:T(8,128)(2,1)S(1)}, bf16[128,1024]{1,0:T(8,128)(2,1)S(1)}, u32[]{:S(2)}, u32[]{:S(2)}) %collective-permute-start.4) | collective-permute-done | bytes 262176 | tf_op jit(solution)/shard_map/ppermute | solution.py:25
  33.6 3.2 %gate.1 = (bf16[128,1024]{1,0:T(8,128)(2,1)S(1)}, bf16[128,1024]{1,0:T(8,128)(2,1)S(1)}, bf16[32,1024]{1,0:T(8,128)(2,1)S(1)}, f32[104,128]{1,0:T(8,128)S(1)}) custom-call(s32[8]{0:T(128)S(1)} %copy-done.8, f32[128,1024]{1,0:T(8,128)S(1)} %get-tuple-element.75.part_ref, bf16[128,1024]{1,0:T(8,128)(2,1)S(1)} %collective-permute-done.4.after_ref, ...), custom_call_target="tpu_custom_call" | custom-call | flops 1000000000 | bytes 5000000 | tf_op jit(solution)/shard_map/gate/pallas_call | solution.py:469
  36.8 4.8 %collective-permute-start.5 = (bf16[32,1024]{1,0:T(8,128)(2,1)S(1)}, bf16[32,1024]{1,0:T(8,128)(2,1)S(1)}, u32[]{:S(2)}, u32[]{:S(2)}) collective-permute-start(bf16[32,1024]{1,0:T(8,128)(2,1)S(1)} %get-tuple-element.80), channel_id=1, source_target_pairs={{0,28},{4,0},{8,4},{12,8},{16,12},{20,16},{24,20},{28,24},{1,29},{... | collective-permute-start | bytes 196616 | tf_op jit(solution)/shard_map/ppermute | solution.py:25
  41.6 4.1 %collective-permute-done.6 = f32[104,128]{1,0:T(8,128)S(1)} collective-permute-done((f32[104,128]{1,0:T(8,128)S(1)}, f32[104,128]{1,0:T(8,128)S(1)}, u32[]{:S(2)}, u32[]{:S(2)}) %collective-permute-start.6) | collective-permute-done | bytes 53280 | tf_op jit(solution)/shard_map/ppermute | solution.py:29
  45.7 0.1 collective-permute-start.7
  45.8 2.6 %main_qk.1 = (bf16[128,1024]{1,0:T(8,128)(2,1)}, bf16[128,1024]{1,0:T(8,128)(2,1)}) custom-call(s32[8]{0:T(128)S(1)} %copy-done.8, f32[24,1024]{1,0:T(8,128)S(1)} %copy-done.4, bf16[32,1024]{1,0:T(8,128)(2,1)S(1)} %collective-permute-done.5.tails_ref, bf16[128,1024]{1,0:T(8,128)(2,1)S(1)} %get-tuple-element.71.gq_ref, ...), custom_call_target="tpu_custom_call" | custom-call | flops 1000000000 | bytes 5000000 | tf_op jit(solution)/shard_map/main_qk/pallas_call | solution.py:469
  48.4 2.1 %collective-permute-done.7 = f32[104,128]{1,0:T(8,128)S(1)} collective-permute-done((f32[104,128]{1,0:T(8,128)S(1)}, f32[104,128]{1,0:T(8,128)S(1)}, u32[]{:S(2)}, u32[]{:S(2)}) %collective-permute-start.7) | collective-permute-done | bytes 53280 | tf_op jit(solution)/shard_map/ppermute | solution.py:29
  50.5 0.1 collective-permute-start.8
  50.6 2.2 %main_v.1 = (bf16[128,1024]{1,0:T(8,128)(2,1)}, bf16[128,1024]{1,0:T(8,128)(2,1)}) custom-call(s32[8]{0:T(128)S(1)} %copy-done.8, f32[24,1024]{1,0:T(8,128)S(1)} %copy-done.4, bf16[32,1024]{1,0:T(8,128)(2,1)S(1)} %collective-permute-done.5.tails_ref, bf16[128,1024]{1,0:T(8,128)(2,1)S(1)} %get-tuple-element.86.gvs_ref, ...), custom_call_target="tpu_custom_call" | custom-call | flops 1000000000 | bytes 5000000 | tf_op jit(solution)/shard_map/main_v/pallas_call | solution.py:469
  52.8 2.8 %collective-permute-done.8.two_ref = f32[104,128]{1,0:T(8,128)S(1)} collective-permute-done((f32[104,128]{1,0:T(8,128)S(1)}, f32[104,128]{1,0:T(8,128)S(1)}, u32[]{:S(2)}, u32[]{:S(2)}) %collective-permute-start.8) | collective-permute-done | bytes 53280 | tf_op jit(solution)/shard_map/ppermute | solution.py:29
  55.6 0.6 %unpack.1 = (f32[3,7,64]{2,1,0:T(8,128)}, f32[64,128]{1,0:T(8,128)}, f32[8,128]{1,0:T(8,128)}, f32[8,128]{1,0:T(8,128)}) custom-call(f32[104,128]{1,0:T(8,128)S(1)} %add.15.one_ref, f32[104,128]{1,0:T(8,128)S(1)} %collective-permute-done.8.two_ref), custom_call_target="tpu_custom_call" | custom-call | flops 100000000 | bytes 1000000 | tf_op jit(solution)/shard_map/unpack/pallas_call | solution.py:469
  (26 shorter events, 0.1 us)
Async XLA Ops:
  0.6 10.3 %copy-start.11 = (bf16[64,128]{1,0:T(8,128)(2,1)S(1)}, bf16[64,128]{1,0:T(8,128)(2,1)}, u32[]{:S(2)}) copy-start(bf16[64,128]{1,0:T(8,128)(2,1)} %long_ref.1) | copy-start | bytes 49156
  3.8 14.3 %collective-permute-start = (bf16[160,1024]{1,0:T(8,128)(2,1)}, bf16[160,1024]{1,0:T(8,128)(2,1)S(1)}, u32[]{:S(2)}, u32[]{:S(2)}) collective-permute-start(bf16[160,1024]{1,0:T(8,128)(2,1)} %get-tuple-element.57.sent_ref), channel_id=1, source_target_pairs={{0,4},{4,8},{8,12},{12,16},{16,20},{20,24},{24,28},{28,0},{1,5},{5... | collective-permute-start | bytes 983048 | tf_op jit(solution)/shard_map/ppermute | solution.py:25
  6.8 11.3 %collective-permute-start.1 = (bf16[16,1024]{1,0:T(8,128)(2,1)}, bf16[16,1024]{1,0:T(8,128)(2,1)S(1)}, u32[]{:S(2)}, u32[]{:S(2)}) collective-permute-start(bf16[16,1024]{1,0:T(8,128)(2,1)} %get-tuple-element.56), channel_id=1, source_target_pairs={{0,8},{4,12},{8,16},{12,20},{16,24},{20,28},{24,0},{28,4},{1,9},{5... | collective-permute-start | bytes 98312 | tf_op jit(solution)/shard_map/ppermute | solution.py:25
  8.4 0.7 %copy-start.10 = (bf16[64,128]{1,0:T(8,128)(2,1)S(1)}, bf16[64,128]{1,0:T(8,128)(2,1)}, u32[]{:S(2)}) copy-start(bf16[64,128]{1,0:T(8,128)(2,1)} %long_ref.1) | copy-start | bytes 49156
  10.9 1.8 %copy-start.3 = (bf16[128,1024]{1,0:T(8,128)(2,1)S(1)}, bf16[128,1024]{1,0:T(8,128)(2,1)}, u32[]{:S(2)}) copy-start(bf16[128,1024]{1,0:T(8,128)(2,1)} %q_ref.5) | copy-start | bytes 786436
  10.9 1.8 %copy-start.4 = (f32[24,1024]{1,0:T(8,128)S(1)}, f32[24,1024]{1,0:T(8,128)}, u32[]{:S(2)}) copy-start(f32[24,1024]{1,0:T(8,128)} %get-tuple-element.52.taps_ref) | copy-start | bytes 294916
  10.9 1.8 %copy-start.5 = (bf16[160,1024]{1,0:T(8,128)(2,1)S(1)}, bf16[160,1024]{1,0:T(8,128)(2,1)}, u32[]{:S(2)}) copy-start(bf16[160,1024]{1,0:T(8,128)(2,1)} %get-tuple-element.57.sent_ref) | copy-start | bytes 983044
  11.0 1.8 %copy-start.8 = (s32[8]{0:T(128)S(1)}, s32[8]{0:T(128)}, u32[]{:S(2)}) copy-start(s32[8]{0:T(128)} %len_ref.13) | copy-start | bytes 100
  11.0 1.8 %copy-start.9 = (f32[1024]{0:T(1024)S(1)}, f32[1024]{0:T(1024)}, u32[]{:S(2)}) copy-start(f32[1024]{0:T(1024)} %param.17) | copy-start | bytes 12292
  12.7 5.5 %copy-start = (bf16[128,1024]{1,0:T(8,128)(2,1)S(1)}, bf16[128,1024]{1,0:T(8,128)(2,1)}, u32[]{:S(2)}) copy-start(bf16[128,1024]{1,0:T(8,128)(2,1)} %k_ref.5) | copy-start | bytes 786436
  12.7 5.5 %copy-start.1 = (bf16[128,1024]{1,0:T(8,128)(2,1)S(1)}, bf16[128,1024]{1,0:T(8,128)(2,1)}, u32[]{:S(2)}) copy-start(bf16[128,1024]{1,0:T(8,128)(2,1)} %v_ref.5) | copy-start | bytes 786436
  12.7 5.5 %copy-start.2 = (bf16[128,1024]{1,0:T(8,128)(2,1)S(1)}, bf16[128,1024]{1,0:T(8,128)(2,1)}, u32[]{:S(2)}) copy-start(bf16[128,1024]{1,0:T(8,128)(2,1)} %cot_ref.5) | copy-start | bytes 786436
  12.7 5.5 %copy-start.6 = (bf16[128,1024]{1,0:T(8,128)(2,1)S(1)}, bf16[128,1024]{1,0:T(8,128)(2,1)}, u32[]{:S(2)}) copy-start(bf16[128,1024]{1,0:T(8,128)(2,1)} %resid_ref.1) | copy-start | bytes 786436
  12.7 5.4 %copy-start.7 = (f32[1024]{0:T(1024)S(1)}, f32[1024]{0:T(1024)}, u32[]{:S(2)}) copy-start(f32[1024]{0:T(1024)} %param.18) | copy-start | bytes 12292
  20.3 1.2 %collective-permute-start.2 = (f32[2,128]{1,0:T(2,128)S(1)}, f32[2,128]{1,0:T(2,128)S(1)}, u32[]{:S(2)}, u32[]{:S(2)}) collective-permute-start(f32[2,128]{1,0:T(2,128)S(1)} %get-tuple-element.63), channel_id=1, source_target_pairs={{0,1},{1,0},{2,3},{3,2},{4,5},{5,4},{6,7},{7,6},{8,9},{9,8},{10,11... | collective-permute-start | bytes 3080 | tf_op jit(solution)/shard_map/ppermute | solution.py:29
  21.5 3.6 %collective-permute-start.3 = (f32[2,128]{1,0:T(2,128)S(1)}, f32[2,128]{1,0:T(2,128)S(1)}, u32[]{:S(2)}, u32[]{:S(2)}) collective-permute-start(f32[2,128]{1,0:T(2,128)S(1)} %add.12), channel_id=1, source_target_pairs={{0,2},{1,3},{2,0},{3,1},{4,6},{5,7},{6,4},{7,5},{8,10},{9,11},{10,... | collective-permute-start | bytes 3080 | tf_op jit(solution)/shard_map/ppermute | solution.py:29
  25.6 8.0 %collective-permute-start.4 = (bf16[128,1024]{1,0:T(8,128)(2,1)S(1)}, bf16[128,1024]{1,0:T(8,128)(2,1)S(1)}, u32[]{:S(2)}, u32[]{:S(2)}) collective-permute-start(bf16[128,1024]{1,0:T(8,128)(2,1)S(1)} %get-tuple-element.70.gm_ref), channel_id=1, source_target_pairs={{0,28},{4,0},{8,4},{12,8},{16,12},{20,16},{24,20},{28,24},{1,29},{... | collective-permute-start | bytes 786440 | tf_op jit(solution)/shard_map/ppermute | solution.py:25
  36.8 9.0 %collective-permute-start.5 = (bf16[32,1024]{1,0:T(8,128)(2,1)S(1)}, bf16[32,1024]{1,0:T(8,128)(2,1)S(1)}, u32[]{:S(2)}, u32[]{:S(2)}) collective-permute-start(bf16[32,1024]{1,0:T(8,128)(2,1)S(1)} %get-tuple-element.80), channel_id=1, source_target_pairs={{0,28},{4,0},{8,4},{12,8},{16,12},{20,16},{24,20},{28,24},{1,29},{... | collective-permute-start | bytes 196616 | tf_op jit(solution)/shard_map/ppermute | solution.py:25
  41.6 4.1 %collective-permute-start.6 = (f32[104,128]{1,0:T(8,128)S(1)}, f32[104,128]{1,0:T(8,128)S(1)}, u32[]{:S(2)}, u32[]{:S(2)}) collective-permute-start(f32[104,128]{1,0:T(8,128)S(1)} %get-tuple-element.81), channel_id=1, source_target_pairs={{0,4},{4,0},{8,12},{12,8},{16,20},{20,16},{24,28},{28,24},{1,5},{5... | collective-permute-start | bytes 159752 | tf_op jit(solution)/shard_map/ppermute | solution.py:29
  45.7 4.8 %collective-permute-start.7 = (f32[104,128]{1,0:T(8,128)S(1)}, f32[104,128]{1,0:T(8,128)S(1)}, u32[]{:S(2)}, u32[]{:S(2)}) collective-permute-start(f32[104,128]{1,0:T(8,128)S(1)} %add.14), channel_id=1, source_target_pairs={{0,8},{4,12},{8,0},{12,4},{16,24},{20,28},{24,16},{28,20},{1,9},{5... | collective-permute-start | bytes 159752 | tf_op jit(solution)/shard_map/ppermute | solution.py:29
  50.5 5.1 %collective-permute-start.8 = (f32[104,128]{1,0:T(8,128)S(1)}, f32[104,128]{1,0:T(8,128)S(1)}, u32[]{:S(2)}, u32[]{:S(2)}) collective-permute-start(f32[104,128]{1,0:T(8,128)S(1)} %add.15.one_ref), channel_id=1, source_target_pairs={{0,16},{4,20},{8,24},{12,28},{16,0},{20,4},{24,8},{28,12},{1,17},{... | collective-permute-start | bytes 159752 | tf_op jit(solution)/shard_map/ppermute | solution.py:29
